TPU v7x, 32 devices: a whole 2x2x4 slice. The times are simulated.
32 devices in a mesh: seq: 4 (over y, x), expert: 8 (over z, core).
Axes of the slice: x: 2, y: 2, z: 4, core: 2. Of those that a mesh axis runs over, the one named last changes fastest.
Arguments:
- query_rows: bfloat16 [8, 512, 2048], P('expert', 'seq'), may hold values from -2000 to 2000
- key_rows: bfloat16 [8, 512, 2048], P('expert', 'seq'), may hold values from -4 to 4
- value_rows: bfloat16 [8, 512, 2048], P('expert', 'seq'), may hold values from -48 to 48
- norm_gain: float32 [2048], replicated, may hold values from 0.1 to 1.9
- expert_ids: int32 [8, 512, 2], P('expert', 'seq'), may hold values from 0 to 7, all different within a row; in each aligned block of 128 rows (0 to 127, 128 to 255, ..., all dimensions but the last counted through in order) at most 32 rows name the same one
- gate_weights: float32 [8, 512, 2], P('expert', 'seq'), may hold values from 0.1 to 1
- w_gate: bfloat16 [8, 2048, 768], P('expert'), may hold values from -0.125 to 0.125
- w_up: bfloat16 [8, 2048, 768], P('expert'), may hold values from -0.125 to 0.125
- w_down: bfloat16 [8, 768, 2048], P('expert'), may hold values from -0.21875 to 0.21875
Outputs:
- layer_out: bfloat16 [8, 512, 2048], P('expert', 'seq')
Inputs may be any that keep to these rules, and one draw needn't show every extreme that they name: `expert_ids`: within the tokens of one device (aligned blocks of 128 tokens of a sequence) no expert is named by more than 32 choices, a bound that some block reaches; a token's two ids differ.
All inputs are finite; a program needn't handle non-finite values.
Results may differ from a plain program's by a relative error of at most 0.017.
Values may be sent and summed in bfloat16 or wider, within the bound.
No kernel may reach another device: no remote copies, remote signals or barrier semaphores. Data moves between devices by JAX's collectives and lax.ppermute only.
A program may use at most 128 MiB of HBM per device.

v0:
```python
import jax
import jax.numpy as jnp
from jax import lax
from jax.sharding import PartitionSpec as P

HEADS = 16
CAP = 32


def head_attention(operands):
    query_head, key_head, value_head = operands
    head_size = query_head.shape[-1]
    scores = jnp.dot(query_head, key_head.T, preferred_element_type=jnp.float32) * head_size ** (
        -0.5
    )
    row_peak = jnp.max(scores, axis=-1, keepdims=True)
    exponentials = jnp.exp(scores - row_peak)
    totals = jnp.sum(exponentials, axis=-1, keepdims=True)
    weighted = jnp.dot(
        exponentials.astype(jnp.bfloat16), value_head, preferred_element_type=jnp.float32
    )
    return (weighted / totals).astype(jnp.bfloat16)


def local(
    query_rows, key_rows, value_rows, norm_gain, expert_ids, gate_weights, w_gate, w_up, w_down
):
    tokens = query_rows.shape[1]
    feature_width = query_rows.shape[2]
    head_count = HEADS
    head_size = feature_width // head_count
    groups = lax.axis_size("seq")
    per_group = head_count // groups

    def regroup(block):
        return block.reshape(1, tokens, groups, per_group, head_size)

    query_all = lax.all_to_all(regroup(query_rows), "seq", split_axis=2, concat_axis=1, tiled=True)
    key_all = lax.all_to_all(regroup(key_rows), "seq", split_axis=2, concat_axis=1, tiled=True)
    value_all = lax.all_to_all(regroup(value_rows), "seq", split_axis=2, concat_axis=1, tiled=True)
    stacked = lax.map(
        head_attention,
        (
            query_all[0, :, 0].transpose(1, 0, 2),
            key_all[0, :, 0].transpose(1, 0, 2),
            value_all[0, :, 0].transpose(1, 0, 2),
        ),
    )
    exchanged = stacked.transpose(1, 0, 2)[None, :, None]
    restored = lax.all_to_all(exchanged, "seq", split_axis=1, concat_axis=2, tiled=True)
    attended = restored.reshape(1, tokens, feature_width)
    widened = attended[0].astype(jnp.float32)
    normed = (
        widened * lax.rsqrt(jnp.mean(widened * widened, axis=-1, keepdims=True) + 1e-06) * norm_gain
    ).astype(jnp.bfloat16)
    choice_ids = expert_ids[0]
    experts = lax.axis_size("expert")
    capacity = CAP
    matches = (
        choice_ids[:, :, None] == jnp.arange(experts, dtype=jnp.int32)[None, None, :]
    ).astype(jnp.int32)
    flat_matches = matches.reshape(tokens * 2, experts)
    before = jnp.cumsum(flat_matches, axis=0) - flat_matches
    order_rank = jnp.sum(before * flat_matches, axis=1).reshape(tokens, 2)
    slot_index = choice_ids * capacity + order_rank
    slot_range = jnp.arange(experts * capacity, dtype=jnp.int32)
    select = (
        (slot_index[None, :, 0] == slot_range[:, None])
        | (slot_index[None, :, 1] == slot_range[:, None])
    ).astype(jnp.bfloat16)
    outgoing = jnp.dot(select, normed, preferred_element_type=jnp.float32).astype(jnp.bfloat16)
    outgoing = outgoing.reshape(experts, capacity, feature_width)
    incoming = lax.all_to_all(outgoing, "expert", split_axis=0, concat_axis=0, tiled=True)
    sources = incoming.shape[0]
    item_count = incoming.shape[1]
    flat_rows = incoming.reshape(sources * item_count, feature_width)
    gate_part = jnp.dot(flat_rows, w_gate[0], preferred_element_type=jnp.float32)
    up_part = jnp.dot(flat_rows, w_up[0], preferred_element_type=jnp.float32)
    hidden = (jax.nn.silu(gate_part) * up_part).astype(jnp.bfloat16)
    produced = jnp.dot(hidden, w_down[0], preferred_element_type=jnp.float32).astype(jnp.bfloat16)
    processed = produced.reshape(sources, item_count, feature_width)
    returned = lax.all_to_all(processed, "expert", split_axis=0, concat_axis=0, tiled=True)
    returned = returned.reshape(experts * capacity, feature_width)
    picked = returned[slot_index.reshape(-1)].reshape(tokens, 2, feature_width).astype(jnp.float32)
    mixture = jnp.sum(gate_weights[0][:, :, None] * picked, axis=1)
    return (widened + mixture).astype(jnp.bfloat16)[None]


def solution(mesh):
    placed = (
        P("expert", "seq", None),
        P("expert", "seq", None),
        P("expert", "seq", None),
        P(),
        P("expert", "seq", None),
        P("expert", "seq", None),
        P("expert", None, None),
        P("expert", None, None),
        P("expert", None, None),
    )
    return jax.shard_map(
        local, mesh=mesh, in_specs=placed, out_specs=P("expert", "seq", None), check_vma=False
    )
```

profile of v0, /device:TPU:0, one launch (start us, length us, event | category | flops | bytes accessed | tf_op | source)
XLA Modules:
  0.0 161.8 jit_solution(8536008157500413310)
XLA Ops:
  0.0 2.2 %copy.104 = bf16[1,128,2048]{1,2,0:T(8,128)(2,1)} copy(bf16[1,128,2048]{2,1,0:T(8,128)(2,1)} %param.11) | data formatting | bytes 1048576 | tf_op args[0]
  2.2 2.1 %copy.105 = bf16[1,128,4,4,128]{4,1,3,0,2:T(8,128)(2,1)} copy(bf16[1,128,4,4,128]{1,4,3,2,0:T(8,128)(2,1)} %bitcast.113) | data formatting | bytes 1048576 | tf_op jit(solution)/shard_map/reshape | solution.py:36
  4.3 5.2 %all-to-all-start = ((bf16[1,128,4,4,128]{4,1,3,0,2:T(8,128)(2,1)}), bf16[1,128,4,4,128]{4,1,3,0,2:T(8,128)(2,1)}, u32[]{:S(2)}, u32[]{:S(2)}) async-start(bf16[1,128,4,4,128]{4,1,3,0,2:T(8,128)(2,1)} %copy.105), calls=%async_computation | async-start | bytes 1048576 | tf_op jit(solution)/shard_map/all_to_all | solution.py:38
  9.4 2.1 %copy.107 = bf16[1,128,2048]{1,2,0:T(8,128)(2,1)} copy(bf16[1,128,2048]{2,1,0:T(8,128)(2,1)} %param.12) | data formatting | bytes 1048576 | tf_op args[1]
  11.5 2.1 %copy.108 = bf16[1,128,4,4,128]{4,1,3,0,2:T(8,128)(2,1)} copy(bf16[1,128,4,4,128]{1,4,3,2,0:T(8,128)(2,1)} %bitcast.114) | data formatting | bytes 1048576 | tf_op jit(solution)/shard_map/reshape | solution.py:36
  13.5 4.5 %all-to-all-done = bf16[1,128,4,4,128]{4,1,3,0,2:T(8,128)(2,1)} async-done(((bf16[1,128,4,4,128]{4,1,3,0,2:T(8,128)(2,1)}), bf16[1,128,4,4,128]{4,1,3,0,2:T(8,128)(2,1)}, u32[]{:S(2)}, u32[]{:S(2)}) %all-to-all-start) | async-done | bytes 524320 | tf_op jit(solution)/shard_map/all_to_all | solution.py:38
  18.0 4.1 %all-to-all-start.1 = ((bf16[1,128,4,4,128]{4,1,3,0,2:T(8,128)(2,1)}), bf16[1,128,4,4,128]{4,1,3,0,2:T(8,128)(2,1)}, u32[]{:S(2)}, u32[]{:S(2)}) async-start(bf16[1,128,4,4,128]{4,1,3,0,2:T(8,128)(2,1)} %copy.108), calls=%async_computation.1 | async-start | bytes 1048576 | tf_op jit(solution)/shard_map/all_to_all | solution.py:39
  22.1 2.0 %copy.110 = bf16[1,128,2048]{1,2,0:T(8,128)(2,1)} copy(bf16[1,128,2048]{2,1,0:T(8,128)(2,1)} %param.13) | data formatting | bytes 1048576 | tf_op args[2]
  24.2 2.0 %copy.111 = bf16[1,128,4,4,128]{4,1,3,0,2:T(8,128)(2,1)} copy(bf16[1,128,4,4,128]{1,4,3,2,0:T(8,128)(2,1)} %bitcast.115) | data formatting | bytes 1048576 | tf_op jit(solution)/shard_map/reshape | solution.py:36
  26.2 3.6 %all-to-all-done.1 = bf16[1,128,4,4,128]{4,1,3,0,2:T(8,128)(2,1)} async-done(((bf16[1,128,4,4,128]{4,1,3,0,2:T(8,128)(2,1)}), bf16[1,128,4,4,128]{4,1,3,0,2:T(8,128)(2,1)}, u32[]{:S(2)}, u32[]{:S(2)}) %all-to-all-start.1) | async-done | bytes 524320 | tf_op jit(solution)/shard_map/all_to_all | solution.py:39
  29.8 4.1 %all-to-all-start.2 = ((bf16[1,128,4,4,128]{4,1,3,0,2:T(8,128)(2,1)}), bf16[1,128,4,4,128]{4,1,3,0,2:T(8,128)(2,1)}, u32[]{:S(2)}, u32[]{:S(2)}) async-start(bf16[1,128,4,4,128]{4,1,3,0,2:T(8,128)(2,1)} %copy.111), calls=%async_computation.2 | async-start | bytes 1048576 | tf_op jit(solution)/shard_map/all_to_all | solution.py:40
  34.4 0.6 reduce-window.6
  35.0 0.2 slice_reduce_fusion.2
  35.3 1.9 %copy.106 = bf16[1,128,4,4,128]{4,1,2,3,0:T(8,128)(2,1)} copy(bf16[1,128,4,4,128]{4,1,3,0,2:T(8,128)(2,1)} %all-to-all-done) | data formatting | bytes 1048576 | tf_op jit(solution)/shard_map/all_to_all | solution.py:38
  37.2 1.9 %copy.109 = bf16[1,128,4,4,128]{4,1,2,3,0:T(8,128)(2,1)} copy(bf16[1,128,4,4,128]{4,1,3,0,2:T(8,128)(2,1)} %all-to-all-done.1) | data formatting | bytes 1048576 | tf_op jit(solution)/shard_map/all_to_all | solution.py:39
  39.1 1.8 %all-to-all-done.2 = bf16[1,128,4,4,128]{4,1,3,0,2:T(8,128)(2,1)} async-done(((bf16[1,128,4,4,128]{4,1,3,0,2:T(8,128)(2,1)}), bf16[1,128,4,4,128]{4,1,3,0,2:T(8,128)(2,1)}, u32[]{:S(2)}, u32[]{:S(2)}) %all-to-all-start.2) | async-done | bytes 524320 | tf_op jit(solution)/shard_map/all_to_all | solution.py:40
  40.9 1.9 %copy.112 = bf16[1,128,4,4,128]{4,1,2,3,0:T(8,128)(2,1)} copy(bf16[1,128,4,4,128]{4,1,3,0,2:T(8,128)(2,1)} %all-to-all-done.2) | data formatting | bytes 1048576 | tf_op jit(solution)/shard_map/all_to_all | solution.py:40
  42.8 13.6 %while.10 = (s32[]{:T(128)}, bf16[4,512,128]{2,1,0:T(8,128)(2,1)}, bf16[4,512,128]{2,1,0:T(8,128)(2,1)}, bf16[4,512,128]{2,1,0:T(8,128)(2,1)}, bf16[4,512,128]{2,1,0:T(8,128)(2,1)}, /*index=5*/s32[]{:T(128)}) while((s32[]{:T(128)}, bf16[4,512,128]{2,1,0:T(8,128)(2,1)}, bf16[4,512,128]{2,1,0:T(8,128)(2,1)}, bf16[4,512,128]{2,1,0:T(8,128)(2,1)}, ...), condition=%wide.region_3.4_spmd, body=%wide.region_0.3_spmd.sunk | while | flops 135920640 | bytes 3682381 | solution.py:41
  42.8 1.3 fusion.55
  44.1 0.2 fusion.56
  44.3 1.9 %fusion.57 = bf16[4,512,128]{2,1,0:T(8,128)(2,1)} fusion(bf16[4,512,128]{2,1,0:T(8,128)(2,1)} %get-tuple-element.89, s32[]{:T(128)S(6)} %copy.130, f32[512,512]{0,1:T(8,128)S(1)} %get-tuple-element.80, f32[512]{0:T(512)S(1)} %get-tuple-element.81, f32[512]{0:T(512)S(1)} %fusion.56, bf16[4,512,128]{2,1,0:T(8,128)(2,1)} %get-tuple-element.98), kind=kOutput, calls=%fused_computation.5.clone.1 | convolution fusion | flops 67764224 | bytes 1315840 | tf_op jit(solution)/shard_map/while/body/eval_jaxpr/dot_general | solution.py:19
  46.2 1.3 fusion.55
  47.5 0.2 fusion.56
  47.7 1.9 %fusion.57 = bf16[4,512,128]{2,1,0:T(8,128)(2,1)} fusion(bf16[4,512,128]{2,1,0:T(8,128)(2,1)} %get-tuple-element.89, s32[]{:T(128)S(6)} %copy.130, f32[512,512]{0,1:T(8,128)S(1)} %get-tuple-element.80, f32[512]{0:T(512)S(1)} %get-tuple-element.81, f32[512]{0:T(512)S(1)} %fusion.56, bf16[4,512,128]{2,1,0:T(8,128)(2,1)} %get-tuple-element.98), kind=kOutput, calls=%fused_computation.5.clone.1 | convolution fusion | flops 67764224 | bytes 1315840 | tf_op jit(solution)/shard_map/while/body/eval_jaxpr/dot_general | solution.py:19
  49.6 1.3 fusion.55
  50.9 0.2 fusion.56
  51.1 1.9 %fusion.57 = bf16[4,512,128]{2,1,0:T(8,128)(2,1)} fusion(bf16[4,512,128]{2,1,0:T(8,128)(2,1)} %get-tuple-element.89, s32[]{:T(128)S(6)} %copy.130, f32[512,512]{0,1:T(8,128)S(1)} %get-tuple-element.80, f32[512]{0:T(512)S(1)} %get-tuple-element.81, f32[512]{0:T(512)S(1)} %fusion.56, bf16[4,512,128]{2,1,0:T(8,128)(2,1)} %get-tuple-element.98), kind=kOutput, calls=%fused_computation.5.clone.1 | convolution fusion | flops 67764224 | bytes 1315840 | tf_op jit(solution)/shard_map/while/body/eval_jaxpr/dot_general | solution.py:19
  53.0 1.3 fusion.55
  54.5 1.9 %fusion.57 = bf16[4,512,128]{2,1,0:T(8,128)(2,1)} fusion(bf16[4,512,128]{2,1,0:T(8,128)(2,1)} %get-tuple-element.89, s32[]{:T(128)S(6)} %copy.130, f32[512,512]{0,1:T(8,128)S(1)} %get-tuple-element.80, f32[512]{0:T(512)S(1)} %get-tuple-element.81, f32[512]{0:T(512)S(1)} %fusion.56, bf16[4,512,128]{2,1,0:T(8,128)(2,1)} %get-tuple-element.98), kind=kOutput, calls=%fused_computation.5.clone.1 | convolution fusion | flops 67764224 | bytes 1315840 | tf_op jit(solution)/shard_map/while/body/eval_jaxpr/dot_general | solution.py:19
  56.4 2.3 %copy.126 = bf16[4,512,128]{2,0,1:T(4,128)(2,1)} copy(bf16[4,512,128]{2,1,0:T(8,128)(2,1)} %get-tuple-element.32) | data formatting | bytes 1048576 | tf_op jit(solution)/shard_map/while | solution.py:41
  58.7 4.1 %all-to-all-start.3 = ((bf16[1,512,1,4,128]{4,3,2,0,1:T(4,128)(2,1)}), bf16[1,512,1,4,128]{4,3,2,0,1:T(4,128)(2,1)}, u32[]{:S(2)}, u32[]{:S(2)}) async-start(bf16[1,512,1,4,128]{4,3,2,0,1:T(4,128)(2,1)} %bitcast.112), calls=%async_computation.3 | async-start | bytes 1048576 | tf_op jit(solution)/shard_map/all_to_all | solution.py:50
  63.2 6.2 %all-to-all-done.3 = bf16[1,512,1,4,128]{4,3,2,0,1:T(4,128)(2,1)} async-done(((bf16[1,512,1,4,128]{4,3,2,0,1:T(4,128)(2,1)}), bf16[1,512,1,4,128]{4,3,2,0,1:T(4,128)(2,1)}, u32[]{:S(2)}, u32[]{:S(2)}) %all-to-all-start.3) | async-done | bytes 524320 | tf_op jit(solution)/shard_map/all_to_all | solution.py:50
  69.4 1.2 multiply_reduce_fusion.1
  70.7 2.1 %copy_convert_fusion = f32[1,512,1,4,128]{4,1,3,2,0:T(8,128)} fusion(bf16[1,512,1,4,128]{4,3,2,0,1:T(4,128)(2,1)} %all-to-all-done.3), kind=kLoop, calls=%fused_computation.35 | loop fusion | flops 262144 | bytes 1572864 | tf_op jit(solution)/shard_map/convert_element_type | solution.py:52
  72.8 2.5 %copy.115 = f32[1,128,4,1,4,128]{1,5,4,2,3,0:T(8,128)} copy(f32[1,128,4,1,4,128]{5,1,2,4,3,0:T(8,128)} %bitcast.109) | data formatting | bytes 2097152 | tf_op jit(solution)/shard_map/convert_element_type | solution.py:52
  75.4 1.7 %fusion.32 = bf16[128,2048]{0,1:T(8,128)(2,1)S(1)} fusion(f32[1,128,4,1,4,128]{1,5,4,2,3,0:T(8,128)} %copy.115, f32[2048]{0:T(1024)S(1)} %copy-done.3, f32[128]{0:T(128)S(1)} %add_rsqrt_fusion), kind=kLoop, calls=%fused_computation.33 | loop fusion | flops 786432 | bytes 1581568 | tf_op jit(solution)/shard_map/convert_element_type | solution.py:55
  77.1 0.4 convolution_convert_fusion
  77.6 31.1 %all_to_all.64 = bf16[8,32,2048]{2,1,0:T(8,128)(2,1)S(1)} all-to-all(bf16[8,32,2048]{2,1,0:T(8,128)(2,1)S(1)} %bitcast.108), channel_id=1, replica_groups=mesh['seq'=4,'expert'=8] {'expert'}, dimensions={0} | all-to-all | bytes 2097152 | tf_op jit(solution)/shard_map/all_to_all | solution.py:73
  108.7 1.0 copy-done.2
  109.7 1.9 %fusion.19 = f32[256,768]{1,0:T(8,128)} fusion(bf16[256,2048]{1,0:T(8,128)(2,1)S(1)} %bitcast.117, bf16[1,2048,768]{2,1,0:T(8,128)(2,1)S(1)} %copy-done.6), kind=kOutput, calls=%fused_computation.22 | convolution fusion | flops 805306368 | bytes 4980736 | tf_op jit(solution)/shard_map/dot_general | solution.py:77
  111.6 5.5 %fusion.21 = bf16[256,2048]{1,0:T(8,128)(2,1)} fusion(bf16[1,768,2048]{2,1,0:T(8,128)(2,1)S(1)} %copy-done, bf16[256,2048]{1,0:T(8,128)(2,1)} %bitcast.118, bf16[1,2048,768]{2,1,0:T(8,128)(2,1)} %param.18, f32[256,768]{1,0:T(8,128)} %fusion.19), kind=kOutput, calls=%fused_computation.25 | convolution fusion | flops 1612316672 | bytes 9175040 | tf_op jit(solution)/shard_map/dot_general | solution.py:80
  117.1 4.4 %all-to-all-start.5 = ((bf16[8,32,2048]{2,1,0:T(8,128)(2,1)}), bf16[8,32,2048]{2,1,0:T(8,128)(2,1)}, u32[]{:S(2)}, u32[]{:S(2)}) async-start(bf16[8,32,2048]{2,1,0:T(8,128)(2,1)} %bitcast.116), calls=%async_computation.5 | async-start | bytes 2097152 | tf_op jit(solution)/shard_map/all_to_all | solution.py:82
  121.8 2.6 %copy.121 = f32[1,128,2048]{2,1,0:T(8,128)} copy(f32[1,128,2048]{1,2,0:T(8,128)} %bitcast.107) | data formatting | bytes 2097152 | tf_op jit(solution)/shard_map/convert_element_type | solution.py:52
  124.4 23.5 %all-to-all-done.5 = bf16[8,32,2048]{2,1,0:T(8,128)(2,1)} async-done(((bf16[8,32,2048]{2,1,0:T(8,128)(2,1)}), bf16[8,32,2048]{2,1,0:T(8,128)(2,1)}, u32[]{:S(2)}, u32[]{:S(2)}) %all-to-all-start.5) | async-done | bytes 1048608 | tf_op jit(solution)/shard_map/all_to_all | solution.py:82
  147.9 4.7 %gather_fusion = bf16[256,2048]{1,0:T(8,128)(2,1)} fusion(bf16[256,2048]{1,0:T(8,128)(2,1)} %bitcast.37, s32[1024]{0:T(1024)S(1)} %pad_clamp_fusion), kind=kCustom, calls=%fused_computation | custom fusion | bytes 2098176 | tf_op jit(solution)/shard_map/gather | solution.py:84
  152.6 3.3 %reshape.138 = f32[128,2,2048]{2,1,0:T(2,128)} reshape(bf16[256,2048]{1,0:T(8,128)(2,1)} %gather_fusion) | data formatting | bytes 3145728 | tf_op jit(solution)/shard_map/convert_element_type | solution.py:84
  156.0 4.9 %multiply_reduce_fusion = f32[128,2048]{1,0:T(8,128)S(1)} fusion(f32[128,2,2048]{2,1,0:T(2,128)} %reshape.138, f32[128,2]{1,0:T(8,128)S(1)} %copy.116), kind=kLoop, calls=%fused_computation.26 | loop fusion | flops 786432 | bytes 3146752 | tf_op jit(solution)/shard_map/reduce_sum | solution.py:85
  160.9 0.9 fusion.30
  (32 shorter events, 1.4 us)
Async XLA Ops:
  0.0 111.6 %copy-start = (bf16[1,768,2048]{2,1,0:T(8,128)(2,1)S(1)}, bf16[1,768,2048]{2,1,0:T(8,128)(2,1)}, u32[]{:S(2)}) copy-start(bf16[1,768,2048]{2,1,0:T(8,128)(2,1)} %param.19) | copy-start | bytes 9437188
  4.3 13.7 %all-to-all-start = ((bf16[1,128,4,4,128]{4,1,3,0,2:T(8,128)(2,1)}), bf16[1,128,4,4,128]{4,1,3,0,2:T(8,128)(2,1)}, u32[]{:S(2)}, u32[]{:S(2)}) async-start(bf16[1,128,4,4,128]{4,1,3,0,2:T(8,128)(2,1)} %copy.105), calls=%async_computation | async-start | bytes 1048576 | tf_op jit(solution)/shard_map/all_to_all | solution.py:38
  9.4 24.6 %copy-start.4 = (s32[1,128,2]{1,2,0:T(2,128)S(1)}, s32[1,128,2]{1,2,0:T(2,128)}, u32[]{:S(2)}) copy-start(s32[1,128,2]{1,2,0:T(2,128)} %param.15) | copy-start | bytes 3076
  18.0 11.9 %all-to-all-start.1 = ((bf16[1,128,4,4,128]{4,1,3,0,2:T(8,128)(2,1)}), bf16[1,128,4,4,128]{4,1,3,0,2:T(8,128)(2,1)}, u32[]{:S(2)}, u32[]{:S(2)}) async-start(bf16[1,128,4,4,128]{4,1,3,0,2:T(8,128)(2,1)} %copy.108), calls=%async_computation.1 | async-start | bytes 1048576 | tf_op jit(solution)/shard_map/all_to_all | solution.py:39
  29.8 11.0 %all-to-all-start.2 = ((bf16[1,128,4,4,128]{4,1,3,0,2:T(8,128)(2,1)}), bf16[1,128,4,4,128]{4,1,3,0,2:T(8,128)(2,1)}, u32[]{:S(2)}, u32[]{:S(2)}) async-start(bf16[1,128,4,4,128]{4,1,3,0,2:T(8,128)(2,1)} %copy.111), calls=%async_computation.2 | async-start | bytes 1048576 | tf_op jit(solution)/shard_map/all_to_all | solution.py:40
  56.4 19.0 %copy-start.3 = (f32[2048]{0:T(1024)S(1)}, f32[2048]{0:T(1024)}, u32[]{:S(2)}) copy-start(f32[2048]{0:T(1024)} %param.14) | copy-start | bytes 24580
  58.7 10.8 %all-to-all-start.3 = ((bf16[1,512,1,4,128]{4,3,2,0,1:T(4,128)(2,1)}), bf16[1,512,1,4,128]{4,3,2,0,1:T(4,128)(2,1)}, u32[]{:S(2)}, u32[]{:S(2)}) async-start(bf16[1,512,1,4,128]{4,3,2,0,1:T(4,128)(2,1)} %bitcast.112), calls=%async_computation.3 | async-start | bytes 1048576 | tf_op jit(solution)/shard_map/all_to_all | solution.py:50
  75.4 34.3 %copy-start.6 = (bf16[1,2048,768]{2,1,0:T(8,128)(2,1)S(1)}, bf16[1,2048,768]{2,1,0:T(8,128)(2,1)}, u32[]{:S(2)}) copy-start(bf16[1,2048,768]{2,1,0:T(8,128)(2,1)} %param.17) | copy-start | bytes 9437188
  108.7 1.0 copy-start.2
  111.6 10.1 %copy-start.5 = (f32[1,128,2]{1,2,0:T(2,128)S(1)}, f32[1,128,2]{1,2,0:T(2,128)}, u32[]{:S(2)}) copy-start(f32[1,128,2]{1,2,0:T(2,128)} %param.16) | copy-start | bytes 3076
  117.1 30.8 %all-to-all-start.5 = ((bf16[8,32,2048]{2,1,0:T(8,128)(2,1)}), bf16[8,32,2048]{2,1,0:T(8,128)(2,1)}, u32[]{:S(2)}, u32[]{:S(2)}) async-start(bf16[8,32,2048]{2,1,0:T(8,128)(2,1)} %bitcast.116), calls=%async_computation.5 | async-start | bytes 2097152 | tf_op jit(solution)/shard_map/all_to_all | solution.py:82
  156.0 4.9 %copy-start.1 = (f32[1,128,2048]{2,1,0:T(8,128)S(1)}, f32[1,128,2048]{2,1,0:T(8,128)}, u32[]{:S(2)}) copy-start(f32[1,128,2048]{2,1,0:T(8,128)} %copy.121) | copy-start | bytes 3145732
where the time goes:
time: 163 us; the launch traced here: 162 us
  waiting for transfers between devices  39.6 us (24%)
  local copies, waits for them, and re-layouts  35.8 us (22%)
  blocking collectives  31.1 us (19%)
  starting transfers between devices  22 us (13%)
  matrix products  20.6 us (13%)
  other arithmetic  12.4 us (8%)
    all_to_all x1, blocking collectives, local(): lax.all_to_all(outgoing, 'expert', split_axis=0, concat_axis=0, tiled=True)  31.1 us
    all_to_all x1, waiting for transfers between devices, local(): lax.all_to_all(processed, 'expert', split_axis=0, concat_axis=0, tiled=True)  23.5 us
    dot_general x4, matrix products, head_attention(): jnp.dot(exponentials.astype(jnp.bfloat16), value_head, preferred_element_...  7.7 us
    unnamed x18, local copies, waits for them, and re-layouts  7.45 us
    all_to_all x1, waiting for transfers between devices, local(): lax.all_to_all(exchanged, 'seq', split_axis=1, concat_axis=2, tiled=True)  6.21 us
    reshape x3, local copies, waits for them, and re-layouts, regroup(): return block.reshape(1, tokens, groups, per_group, head_size)  6.16 us
    dot_general x1, matrix products, local(): jnp.dot(hidden, w_down[0], preferred_element_type=jnp.float32)  5.52 us
    all_to_all x1, starting transfers between devices, local(): lax.all_to_all(regroup(query_rows), 'seq', split_axis=2, concat_axis=1, t...  5.16 us
  transfers between devices with their start and end apart: 5, of which 5 were waited for; matrix products, arithmetic and copies ran while one was open for 10% of the time, Pallas kernels for 0%

commit v1 on v0

v1 whole, which is shorter than its diff:
```python
import functools

import jax
import jax.numpy as jnp
from jax import lax
from jax.experimental import pallas as pl
from jax.experimental.pallas import tpu as pltpu
from jax.sharding import PartitionSpec as P

HEADS = 16
CAP = 32
CHUNKS = 1
F32 = jnp.float32
BF16 = jnp.bfloat16
ANY = pl.BlockSpec(memory_space=pl.ANY)
VMEM = pl.BlockSpec(memory_space=pltpu.VMEM)


def swap(x, axis, distance):
    size = lax.axis_size(axis)
    return lax.ppermute(x, axis, [(i, i ^ distance) for i in range(size)])


def params(mib):
    return pltpu.CompilerParams(vmem_limit_bytes=mib << 20)


def cost(flops, moved):
    return pl.CostEstimate(flops=flops, bytes_accessed=moved, transcendentals=0)


def pack_kernel(groups, group_width, start, width, q_ref, k_ref, v_ref, *rest):
    outs, sems = rest[:-1], rest[-1]
    me = lax.axis_index("seq")
    copies = []
    for distance in range(1, groups):
        column = pl.multiple_of((me ^ distance) * group_width + start, 128)
        for i, ref in enumerate((q_ref, k_ref, v_ref)):
            copies.append(
                pltpu.make_async_copy(
                    ref.at[0, :, pl.ds(column, width)],
                    outs[distance - 1].at[i],
                    sems.at[3 * (distance - 1) + i],
                )
            )
    for copy in copies:
        copy.start()
    for copy in copies:
        copy.wait()


def pack(groups, group_width, start, width, q, k, v):
    tokens = q.shape[1]
    return pl.pallas_call(
        functools.partial(pack_kernel, groups, group_width, start, width),
        out_shape=[jax.ShapeDtypeStruct((3, tokens, width), BF16)] * (groups - 1),
        in_specs=[ANY] * 3,
        out_specs=[ANY] * (groups - 1),
        scratch_shapes=[pltpu.SemaphoreType.DMA((3 * (groups - 1),))],
        compiler_params=params(8),
        cost_estimate=cost(0, 2 * 3 * (groups - 1) * tokens * width * 2),
        name="pack_heads",
    )(q, k, v)


def attend_kernel(groups, group_width, start, width, head_size, q_ref, k_ref, v_ref, *rest):
    received, outs = rest[: groups - 1], rest[groups - 1 : 2 * groups - 1]
    q_all, k_all, v_all, sems = rest[2 * groups - 1 :]
    tokens = outs[0].shape[0]
    me = lax.axis_index("seq")
    column = pl.multiple_of(me * group_width + start, 128)
    copies = []
    for i, (ref, held) in enumerate(((q_ref, q_all), (k_ref, k_all), (v_ref, v_all))):
        copies.append(
            pltpu.make_async_copy(
                ref.at[0, :, pl.ds(column, width)], held.at[pl.ds(0, tokens)], sems.at[i]
            )
        )
        for j in range(groups - 1):
            copies.append(
                pltpu.make_async_copy(
                    received[j].at[i],
                    held.at[pl.ds((j + 1) * tokens, tokens)],
                    sems.at[3 * (j + 1) + i],
                )
            )
    for copy in copies:
        copy.start()
    for copy in copies:
        copy.wait()
    for head in range(width // head_size):
        lanes = slice(head * head_size, (head + 1) * head_size)
        keys, values = k_all[:, lanes], v_all[:, lanes]
        for block in range(groups):
            rows = slice(block * tokens, (block + 1) * tokens)
            scores = lax.dot_general(
                q_all[rows, lanes], keys, (((1,), (1,)), ((), ())), preferred_element_type=F32
            ) * (head_size**-0.5)
            peak = jnp.max(scores, axis=-1, keepdims=True)
            exponentials = jnp.exp(scores - peak)
            totals = jnp.sum(exponentials, axis=-1, keepdims=True)
            weighted = jnp.dot(exponentials.astype(BF16), values, preferred_element_type=F32)
            outs[block][:, lanes] = (weighted / totals).astype(BF16)


def attend(groups, group_width, start, width, head_size, q, k, v, received):
    tokens = q.shape[1]
    total = groups * tokens
    return pl.pallas_call(
        functools.partial(attend_kernel, groups, group_width, start, width, head_size),
        out_shape=[jax.ShapeDtypeStruct((tokens, width), BF16)] * groups,
        in_specs=[ANY] * (3 + groups - 1),
        out_specs=[VMEM] * groups,
        scratch_shapes=[pltpu.VMEM((total, width), BF16)] * 3
        + [pltpu.SemaphoreType.DMA((3 * groups,))],
        compiler_params=params(32),
        cost_estimate=cost(16 * total * total * width, 8 * total * width),
        name="attend",
    )(q, k, v, *received)


def slot_matrix(experts, ids):
    tokens = ids.shape[1]
    me = lax.axis_index("expert")
    named = lax.broadcasted_iota(jnp.int32, (experts, tokens), 0) ^ me
    matches = jnp.where((ids[0:1, :] == named) | (ids[1:2, :] == named), 1.0, 0.0)
    earlier = jnp.where(
        lax.broadcasted_iota(jnp.int32, (tokens, tokens), 0)
        < lax.broadcasted_iota(jnp.int32, (tokens, tokens), 1),
        1.0,
        0.0,
    )
    rank = jnp.dot(matches.astype(BF16), earlier.astype(BF16), preferred_element_type=F32)
    rank = jnp.where(matches > 0.0, rank, -1.0).astype(jnp.int32)
    slots = lax.broadcasted_iota(jnp.int32, (CAP, tokens), 0)
    return [slots == rank[d : d + 1, :] for d in range(experts)], named


def select_kernel(groups, experts, width, ids_ref, *rest):
    blocks, outs = rest[:groups], rest[groups : groups + experts]
    kept, sems = rest[groups + experts :]
    me = lax.axis_index("seq")
    copies = []
    for d in range(groups):
        column = pl.multiple_of((me ^ d) * width, 128)
        copies.append(
            pltpu.make_async_copy(blocks[d], kept.at[:, pl.ds(column, width)], sems.at[d])
        )
    for copy in copies:
        copy.start()
    hits, _ = slot_matrix(experts, ids_ref[...])
    chosen = jnp.concatenate([jnp.where(h, 1.0, 0.0).astype(BF16) for h in hits], axis=0)
    for copy in copies:
        copy.wait()
    picked = jnp.dot(chosen, kept[...], preferred_element_type=F32).astype(BF16)
    for d in range(experts):
        outs[d][...] = picked[d * CAP : (d + 1) * CAP]


def select(groups, experts, ids, blocks):
    tokens, width = blocks[0].shape
    full = groups * width
    return pl.pallas_call(
        functools.partial(select_kernel, groups, experts, width),
        out_shape=[jax.ShapeDtypeStruct((CAP, full), BF16)] * experts
        + [jax.ShapeDtypeStruct((tokens, full), BF16)],
        in_specs=[VMEM] + [ANY] * groups,
        out_specs=[VMEM] * (experts + 1),
        scratch_shapes=[pltpu.SemaphoreType.DMA((groups,))],
        compiler_params=params(16),
        cost_estimate=cost(2 * experts * CAP * tokens * full, 8 * tokens * full),
        name="select_rows",
    )(ids, *blocks)


def experts_kernel(groups, count, widths, gain_ref, gate_ref, up_ref, down_ref, *rest):
    chunks = len(widths)
    blocks, outs = rest[: count * chunks], rest[count * chunks : count * chunks + count]
    rows_ref, total_ref = rest[count * chunks + count :]
    step = pl.program_id(0)

    @pl.when(step == 0)
    def _():
        stride = sum(widths)
        for i in range(count):
            parts = []
            for g in range(groups):
                for c, w in enumerate(widths):
                    parts.append(blocks[i * chunks + c][:, g * w : (g + 1) * w].astype(F32))
            row = jnp.concatenate(parts, axis=1) if len(parts) > 1 else parts[0]
            scale = lax.rsqrt(jnp.mean(row * row, axis=-1, keepdims=True) + 1e-06)
            rows_ref[i * CAP : (i + 1) * CAP, :] = (row * scale * gain_ref[...]).astype(BF16)
        del stride

    rows = rows_ref[...]
    gate = jnp.dot(rows, gate_ref[0], preferred_element_type=F32)
    up = jnp.dot(rows, up_ref[0], preferred_element_type=F32)
    hidden = (gate / (1.0 + jnp.exp(-gate)) * up).astype(BF16)
    part = jnp.dot(hidden, down_ref[0], preferred_element_type=F32)

    @pl.when(step == 0)
    def _():
        total_ref[...] = part

    @pl.when(step > 0)
    def _():
        total_ref[...] += part

    @pl.when(step == pl.num_programs(0) - 1)
    def _():
        for i in range(count):
            outs[i][...] = total_ref[i * CAP : (i + 1) * CAP, :].astype(BF16)


def run_experts(groups, widths, gain, w_gate, w_up, w_down, blocks):
    count = len(blocks)
    features, units = w_gate.shape[1:]
    tile = 256 if units % 256 == 0 else 128
    flat = [part for block in blocks for part in block]
    return pl.pallas_call(
        functools.partial(experts_kernel, groups, count, widths),
        grid=(units // tile,),
        out_shape=[jax.ShapeDtypeStruct((CAP, features), BF16)] * count,
        in_specs=[
            pl.BlockSpec((1, features), lambda i: (0, 0)),
            pl.BlockSpec((1, features, tile), lambda i: (0, 0, i)),
            pl.BlockSpec((1, features, tile), lambda i: (0, 0, i)),
            pl.BlockSpec((1, tile, features), lambda i: (0, i, 0)),
        ]
        + [pl.BlockSpec(part.shape, lambda i: (0, 0)) for part in flat],
        out_specs=[pl.BlockSpec((CAP, features), lambda i: (0, 0))] * count,
        scratch_shapes=[
            pltpu.VMEM((count * CAP, features), BF16),
            pltpu.VMEM((count * CAP, features), F32),
        ],
        compiler_params=params(32),
        cost_estimate=cost(6 * count * CAP * features * units, 6 * features * units),
        name="experts",
    )(gain, w_gate, w_up, w_down, *flat)


def combine_kernel(groups, experts, widths, ids_ref, gates_ref, *rest):
    chunks = len(widths)
    kept, blocks, out_ref = rest[:chunks], rest[chunks : chunks + experts], rest[-1]
    ids, gates = ids_ref[...], gates_ref[...]
    hits, named = slot_matrix(experts, ids)
    weight = jnp.where(ids[0:1, :] == named, gates[0:1, :], 0.0) + jnp.where(
        ids[1:2, :] == named, gates[1:2, :], 0.0
    )
    coarse = weight.astype(BF16).astype(F32)
    fine = weight - coarse
    spread = []
    for part in (coarse, fine):
        for d in range(experts):
            spread.append(jnp.where(hits[d], part[d : d + 1, :], 0.0).astype(BF16))
    spread = jnp.concatenate(spread, axis=0)
    rows = jnp.concatenate([block[...] for block in blocks], axis=0)
    mixture = lax.dot_general(
        spread,
        jnp.concatenate([rows, rows], axis=0),
        (((0,), (0,)), ((), ())),
        preferred_element_type=F32,
    )
    column = 0
    for g in range(groups):
        for c, w in enumerate(widths):
            part = kept[c][:, g * w : (g + 1) * w].astype(F32)
            out_ref[0, :, column : column + w] = (part + mixture[:, column : column + w]).astype(
                BF16
            )
            column += w


def combine(groups, widths, ids, gates, kept, blocks):
    tokens, features = ids.shape[1], blocks[0].shape[1]
    experts = len(blocks)
    return pl.pallas_call(
        functools.partial(combine_kernel, groups, experts, widths),
        out_shape=jax.ShapeDtypeStruct((1, tokens, features), BF16),
        in_specs=[VMEM] * (2 + len(widths) + experts),
        out_specs=VMEM,
        compiler_params=params(32),
        cost_estimate=cost(4 * experts * CAP * tokens * features, 8 * tokens * features),
        name="combine",
    )(ids, gates, *kept, *blocks)


def local(
    query_rows, key_rows, value_rows, norm_gain, expert_ids, gate_weights, w_gate, w_up, w_down
):
    features = query_rows.shape[2]
    head_size = features // HEADS
    groups, experts = lax.axis_size("seq"), lax.axis_size("expert")
    per_group = HEADS // groups
    group_width = per_group * head_size
    chunks = CHUNKS if per_group % CHUNKS == 0 else 1
    width = group_width // chunks
    widths = (width,) * chunks
    ids, gates = expert_ids[0].T, gate_weights[0].T
    gain = norm_gain.reshape(1, features)

    received = []
    for c in range(chunks):
        packed = pack(groups, group_width, c * width, width, query_rows, key_rows, value_rows)
        received.append([swap(packed[d - 1], "seq", d) for d in range(1, groups)])
    kept, arrived = [], []
    for c in range(chunks):
        heads = attend(
            groups, group_width, c * width, width, head_size,
            query_rows, key_rows, value_rows, received[c],
        )
        blocks = [heads[0]] + [swap(heads[d], "seq", d) for d in range(1, groups)]
        *rows, own = select(groups, experts, ids, blocks)
        kept.append(own)
        arrived.append([rows[0]] + [None] * (experts - 1))
        for d in list(range(experts // 2, experts)) + list(range(1, experts // 2)):
            arrived[c][d] = swap(rows[d], "expert", d)
    half, quarter = experts // 2, experts // 4
    returned = [None] * experts
    for members in (
        range(half, half + quarter),
        range(half + quarter, experts),
        range(half),
    ):
        produced = run_experts(
            groups, widths, gain, w_gate, w_up, w_down,
            [[arrived[c][d] for c in range(chunks)] for d in members],
        )
        for d, block in zip(members, produced):
            returned[d] = block if d == 0 else swap(block, "expert", d)
    return combine(groups, widths, ids, gates, kept, returned)


def solution(mesh):
    rows = P("expert", "seq", None)
    weights = P("expert", None, None)
    return jax.shard_map(
        local,
        mesh=mesh,
        in_specs=(rows, rows, rows, P(), rows, rows, weights, weights, weights),
        out_specs=rows,
        check_vma=False,
    )
```

time: 163 us -> 96.4 us (0.59)
  the two profiles are of different devices: /device:TPU:0 before, /device:TPU:11 now
where the time goes in v1:
time: 96.4 us; the launch traced here: 95.7 us
  waiting for transfers between devices  43.2 us (45%)
  starting transfers between devices  28.4 us (29%)
  Pallas kernels  17.7 us (18%)
  local copies, waits for them, and re-layouts  6.27 us (7%)
    ppermute x20, waiting for transfers between devices, swap(): return lax.ppermute(x, axis, [(i, i ^ distance) for i in range(size)])  43.2 us
    ppermute x20, starting transfers between devices, swap(): return lax.ppermute(x, axis, [(i, i ^ distance) for i in range(size)])  28.4 us
    pallas_call x3, Pallas kernels, run_experts(): pl.pallas_call(functools.partial(experts_kernel, groups, count, widths),...  9.24 us
    unnamed x24, local copies, waits for them, and re-layouts  6.27 us
    pallas_call x1, Pallas kernels, attend(): pl.pallas_call(functools.partial(attend_kernel, groups, group_width, star...  6.1 us
  transfers between devices with their start and end apart: 20, of which 11 were waited for; matrix products, arithmetic and copies ran while one was open for 0% of the time, Pallas kernels for 10%

profile of v1, /device:TPU:11, one launch (start us, length us, event | category | flops | bytes accessed | tf_op | source)
XLA Modules:
  0.0 95.7 jit_solution(9512225499796438671)
XLA Ops:
  0.0 1.0 %copy-done.3 = bf16[1,128,2048]{2,1,0:T(8,128)(2,1)S(1)} copy-done((bf16[1,128,2048]{2,1,0:T(8,128)(2,1)S(1)}, bf16[1,128,2048]{2,1,0:T(8,128)(2,1)}, u32[]{:S(2)}) %copy-start.3) | copy-done | bytes 524312
  1.0 1.0 %copy-done.5 = bf16[1,128,2048]{2,1,0:T(8,128)(2,1)S(1)} copy-done((bf16[1,128,2048]{2,1,0:T(8,128)(2,1)S(1)}, bf16[1,128,2048]{2,1,0:T(8,128)(2,1)}, u32[]{:S(2)}) %copy-start.5) | copy-done | bytes 524312
  2.1 1.0 %copy-done.7 = bf16[1,128,2048]{2,1,0:T(8,128)(2,1)S(1)} copy-done((bf16[1,128,2048]{2,1,0:T(8,128)(2,1)S(1)}, bf16[1,128,2048]{2,1,0:T(8,128)(2,1)}, u32[]{:S(2)}) %copy-start.7) | copy-done | bytes 524312
  3.1 0.3 pack_heads.1
  3.4 0.3 collective-permute-start
  3.7 1.2 %collective-permute-start.1 = (bf16[3,128,512]{2,1,0:T(8,128)(2,1)S(1)}, bf16[3,128,512]{2,1,0:T(8,128)(2,1)S(1)}, u32[]{:S(2)}, u32[]{:S(2)}) collective-permute-start(bf16[3,128,512]{2,1,0:T(8,128)(2,1)S(1)} %get-tuple-element.30), channel_id=1, source_target_pairs={{0,16},{8,24},{16,0},{24,8},{1,17},{9,25},{17,1},{25,9},{2,18},{10... | collective-permute-start | bytes 1179656 | tf_op jit(solution)/shard_map/ppermute | solution.py:21
  5.0 1.2 %collective-permute-start.2 = (bf16[3,128,512]{2,1,0:T(8,128)(2,1)S(1)}, bf16[3,128,512]{2,1,0:T(8,128)(2,1)S(1)}, u32[]{:S(2)}, u32[]{:S(2)}) collective-permute-start(bf16[3,128,512]{2,1,0:T(8,128)(2,1)S(1)} %get-tuple-element.31), channel_id=1, source_target_pairs={{0,24},{8,16},{16,8},{24,0},{1,25},{9,17},{17,9},{25,1},{2,26},{10... | collective-permute-start | bytes 1179656 | tf_op jit(solution)/shard_map/ppermute | solution.py:21
  6.1 7.3 %collective-permute-done.rest_0_ = bf16[3,128,512]{2,1,0:T(8,128)(2,1)S(1)} collective-permute-done((bf16[3,128,512]{2,1,0:T(8,128)(2,1)S(1)}, bf16[3,128,512]{2,1,0:T(8,128)(2,1)S(1)}, u32[]{:S(2)}, u32[]{:S(2)}) %collective-permute-start) | collective-permute-done | bytes 393248 | tf_op jit(solution)/shard_map/ppermute | solution.py:21
  13.5 0.0 collective-permute-done.1.rest_1_
  13.5 9.4 %collective-permute-done.2.rest_2_ = bf16[3,128,512]{2,1,0:T(8,128)(2,1)S(1)} collective-permute-done((bf16[3,128,512]{2,1,0:T(8,128)(2,1)S(1)}, bf16[3,128,512]{2,1,0:T(8,128)(2,1)S(1)}, u32[]{:S(2)}, u32[]{:S(2)}) %collective-permute-start.2) | collective-permute-done | bytes 393248 | tf_op jit(solution)/shard_map/ppermute | solution.py:21
  22.8 1.0 %copy-done.4 = bf16[1,128,2048]{2,1,0:T(8,128)(2,1)S(1)} copy-done((bf16[1,128,2048]{2,1,0:T(8,128)(2,1)S(1)}, bf16[1,128,2048]{2,1,0:T(8,128)(2,1)}, u32[]{:S(2)}) %copy-start.4) | copy-done | bytes 524312
  23.9 1.0 %copy-done.6 = bf16[1,128,2048]{2,1,0:T(8,128)(2,1)S(1)} copy-done((bf16[1,128,2048]{2,1,0:T(8,128)(2,1)S(1)}, bf16[1,128,2048]{2,1,0:T(8,128)(2,1)}, u32[]{:S(2)}) %copy-start.6) | copy-done | bytes 524312
  24.9 1.0 %copy-done.8 = bf16[1,128,2048]{2,1,0:T(8,128)(2,1)S(1)} copy-done((bf16[1,128,2048]{2,1,0:T(8,128)(2,1)S(1)}, bf16[1,128,2048]{2,1,0:T(8,128)(2,1)}, u32[]{:S(2)}) %copy-start.8) | copy-done | bytes 524312
  26.0 6.1 %attend.1 = (bf16[128,512]{1,0:T(8,128)(2,1)S(1)}, bf16[128,512]{1,0:T(8,128)(2,1)S(1)}, bf16[128,512]{1,0:T(8,128)(2,1)S(1)}, bf16[128,512]{1,0:T(8,128)(2,1)S(1)}) custom-call(bf16[1,128,2048]{2,1,0:T(8,128)(2,1)S(1)} %copy-done.4, bf16[1,128,2048]{2,1,0:T(8,128)(2,1)S(1)} %copy-done.6, bf16[1,128,2048]{2,1,0:T(8,128)(2,1)S(1)} %copy-done.8, ...), custom_call_target="tpu_custom_call" | custom-call | flops 2147483648 | bytes 2097152 | tf_op jit(solution)/shard_map/attend/pallas_call | solution.py:109
  32.1 0.4 collective-permute-start.3
  32.5 0.2 collective-permute-start.4
  32.7 2.1 %collective-permute-start.5 = (bf16[128,512]{1,0:T(8,128)(2,1)S(1)}, bf16[128,512]{1,0:T(8,128)(2,1)S(1)}, u32[]{:S(2)}, u32[]{:S(2)}) collective-permute-start(bf16[128,512]{1,0:T(8,128)(2,1)S(1)} %get-tuple-element.35), channel_id=1, source_target_pairs={{0,24},{8,16},{16,8},{24,0},{1,25},{9,17},{17,9},{25,1},{2,26},{10... | collective-permute-start | bytes 393224 | tf_op jit(solution)/shard_map/ppermute | solution.py:21
  34.8 1.2 %collective-permute-done.3.rest_1_ = bf16[128,512]{1,0:T(8,128)(2,1)S(1)} collective-permute-done((bf16[128,512]{1,0:T(8,128)(2,1)S(1)}, bf16[128,512]{1,0:T(8,128)(2,1)S(1)}, u32[]{:S(2)}, u32[]{:S(2)}) %collective-permute-start.3) | collective-permute-done | bytes 131104 | tf_op jit(solution)/shard_map/ppermute | solution.py:21
  36.0 1.7 %collective-permute-done.4.rest_2_ = bf16[128,512]{1,0:T(8,128)(2,1)S(1)} collective-permute-done((bf16[128,512]{1,0:T(8,128)(2,1)S(1)}, bf16[128,512]{1,0:T(8,128)(2,1)S(1)}, u32[]{:S(2)}, u32[]{:S(2)}) %collective-permute-start.4) | collective-permute-done | bytes 131104 | tf_op jit(solution)/shard_map/ppermute | solution.py:21
  37.7 0.4 collective-permute-done.5.rest_3_
  38.1 0.7 select_rows.1
  38.8 3.8 %collective-permute-start.6 = (bf16[32,2048]{1,0:T(8,128)(2,1)S(1)}, bf16[32,2048]{1,0:T(8,128)(2,1)S(1)}, u32[]{:S(2)}, u32[]{:S(2)}) collective-permute-start(bf16[32,2048]{1,0:T(8,128)(2,1)S(1)} %get-tuple-element.38), channel_id=1, source_target_pairs={{0,1},{1,0},{2,3},{3,2},{4,5},{5,4},{6,7},{7,6},{8,9},{9,8},{10,11... | collective-permute-start | bytes 393224 | tf_op jit(solution)/shard_map/ppermute | solution.py:21
  42.6 0.2 collective-permute-start.7
  42.8 1.5 %collective-permute-start.8 = (bf16[32,2048]{1,0:T(8,128)(2,1)S(1)}, bf16[32,2048]{1,0:T(8,128)(2,1)S(1)}, u32[]{:S(2)}, u32[]{:S(2)}) collective-permute-start(bf16[32,2048]{1,0:T(8,128)(2,1)S(1)} %get-tuple-element.40), channel_id=1, source_target_pairs={{0,3},{1,2},{2,1},{3,0},{4,7},{5,6},{6,5},{7,4},{8,11},{9,10},{10,... | collective-permute-start | bytes 393224 | tf_op jit(solution)/shard_map/ppermute | solution.py:21
  44.3 2.3 %collective-permute-start.12 = (bf16[32,2048]{1,0:T(8,128)(2,1)S(1)}, bf16[32,2048]{1,0:T(8,128)(2,1)S(1)}, u32[]{:S(2)}, u32[]{:S(2)}) collective-permute-start(bf16[32,2048]{1,0:T(8,128)(2,1)S(1)} %get-tuple-element.45), channel_id=1, source_target_pairs={{0,4},{1,5},{2,6},{3,7},{4,0},{5,1},{6,2},{7,3},{8,12},{9,13},{10,... | collective-permute-start | bytes 393224 | tf_op jit(solution)/shard_map/ppermute | solution.py:21
  46.7 0.4 collective-permute-start.13
  47.0 0.0 collective-permute-done.6.rest_1_
  47.0 1.3 %collective-permute-start.16 = (bf16[32,2048]{1,0:T(8,128)(2,1)S(1)}, bf16[32,2048]{1,0:T(8,128)(2,1)S(1)}, u32[]{:S(2)}, u32[]{:S(2)}) collective-permute-start(bf16[32,2048]{1,0:T(8,128)(2,1)S(1)} %get-tuple-element.49), channel_id=1, source_target_pairs={{0,6},{1,7},{2,4},{3,5},{4,2},{5,3},{6,0},{7,1},{8,14},{9,15},{10,... | collective-permute-start | bytes 393224 | tf_op jit(solution)/shard_map/ppermute | solution.py:21
  48.3 0.0 collective-permute-done.7.rest_2_
  48.3 3.4 %collective-permute-start.17 = (bf16[32,2048]{1,0:T(8,128)(2,1)S(1)}, bf16[32,2048]{1,0:T(8,128)(2,1)S(1)}, u32[]{:S(2)}, u32[]{:S(2)}) collective-permute-start(bf16[32,2048]{1,0:T(8,128)(2,1)S(1)} %get-tuple-element.50), channel_id=1, source_target_pairs={{0,7},{1,6},{2,5},{3,4},{4,3},{5,2},{6,1},{7,0},{8,15},{9,14},{10,... | collective-permute-start | bytes 393224 | tf_op jit(solution)/shard_map/ppermute | solution.py:21
  51.7 1.9 %collective-permute-done.8.rest_3_ = bf16[32,2048]{1,0:T(8,128)(2,1)S(1)} collective-permute-done((bf16[32,2048]{1,0:T(8,128)(2,1)S(1)}, bf16[32,2048]{1,0:T(8,128)(2,1)S(1)}, u32[]{:S(2)}, u32[]{:S(2)}) %collective-permute-start.8) | collective-permute-done | bytes 131104 | tf_op jit(solution)/shard_map/ppermute | solution.py:21
  53.6 3.2 %experts.3 = (bf16[32,2048]{1,0:T(8,128)(2,1)S(1)}, bf16[32,2048]{1,0:T(8,128)(2,1)S(1)}, bf16[32,2048]{1,0:T(8,128)(2,1)S(1)}, bf16[32,2048]{1,0:T(8,128)(2,1)S(1)}) custom-call(f32[1,2048]{1,0:T(1,128)S(1)} %bitcast.7, bf16[1,2048,768]{2,1,0:T(8,128)(2,1)S(1)} %copy-done, bf16[1,2048,768]{2,1,0:T(8,128)(2,1)S(1)} %copy-done.1, ...), custom_call_target="tpu_custom_call" | custom-call | flops 1207959552 | bytes 9437184 | tf_op jit(solution)/shard_map/experts/pallas_call | solution.py:220
  56.8 0.9 collective-permute-start.9
  57.7 1.9 %collective-permute-start.10 = (bf16[32,2048]{1,0:T(8,128)(2,1)S(1)}, bf16[32,2048]{1,0:T(8,128)(2,1)S(1)}, u32[]{:S(2)}, u32[]{:S(2)}) collective-permute-start(bf16[32,2048]{1,0:T(8,128)(2,1)S(1)} %get-tuple-element.43), channel_id=1, source_target_pairs={{0,2},{1,3},{2,0},{3,1},{4,6},{5,7},{6,4},{7,5},{8,10},{9,11},{10,... | collective-permute-start | bytes 393224 | tf_op jit(solution)/shard_map/ppermute | solution.py:21
  59.6 3.9 %collective-permute-done.13.rest_1_ = bf16[32,2048]{1,0:T(8,128)(2,1)S(1)} collective-permute-done((bf16[32,2048]{1,0:T(8,128)(2,1)S(1)}, bf16[32,2048]{1,0:T(8,128)(2,1)S(1)}, u32[]{:S(2)}, u32[]{:S(2)}) %collective-permute-start.13) | collective-permute-done | bytes 131104 | tf_op jit(solution)/shard_map/ppermute | solution.py:21
  63.5 1.7 %collective-permute-start.11 = (bf16[32,2048]{1,0:T(8,128)(2,1)S(1)}, bf16[32,2048]{1,0:T(8,128)(2,1)S(1)}, u32[]{:S(2)}, u32[]{:S(2)}) collective-permute-start(bf16[32,2048]{1,0:T(8,128)(2,1)S(1)} %get-tuple-element.44), channel_id=1, source_target_pairs={{0,3},{1,2},{2,1},{3,0},{4,7},{5,6},{6,5},{7,4},{8,11},{9,10},{10,... | collective-permute-start | bytes 393224 | tf_op jit(solution)/shard_map/ppermute | solution.py:21
  65.2 3.0 %experts.4 = (bf16[32,2048]{1,0:T(8,128)(2,1)S(1)}, bf16[32,2048]{1,0:T(8,128)(2,1)S(1)}) custom-call(f32[1,2048]{1,0:T(1,128)S(1)} %bitcast.8, bf16[1,2048,768]{2,1,0:T(8,128)(2,1)S(1)} %copy-done, bf16[1,2048,768]{2,1,0:T(8,128)(2,1)S(1)} %copy-done.1, bf16[1,768,2048]{2,1,0:T(8,128)(2,1)S(1)} %copy-done.2, ...), custom_call_target="tpu_custom_call" | custom-call | flops 603979776 | bytes 9437184 | tf_op jit(solution)/shard_map/experts/pallas_call | solution.py:220
  68.3 0.0 collective-permute-done.16.rest_0_
  68.3 2.3 %collective-permute-start.14 = (bf16[32,2048]{1,0:T(8,128)(2,1)S(1)}, bf16[32,2048]{1,0:T(8,128)(2,1)S(1)}, u32[]{:S(2)}, u32[]{:S(2)}) collective-permute-start(bf16[32,2048]{1,0:T(8,128)(2,1)S(1)} %get-tuple-element.47), channel_id=1, source_target_pairs={{0,4},{1,5},{2,6},{3,7},{4,0},{5,1},{6,2},{7,3},{8,12},{9,13},{10,... | collective-permute-start | bytes 393224 | tf_op jit(solution)/shard_map/ppermute | solution.py:21
  70.6 0.0 collective-permute-done.17.rest_1_
  70.6 0.4 collective-permute-start.15
  71.0 3.0 %experts.5 = (bf16[32,2048]{1,0:T(8,128)(2,1)S(1)}, bf16[32,2048]{1,0:T(8,128)(2,1)S(1)}) custom-call(f32[1,2048]{1,0:T(1,128)S(1)} %bitcast.9, bf16[1,2048,768]{2,1,0:T(8,128)(2,1)S(1)} %copy-done, bf16[1,2048,768]{2,1,0:T(8,128)(2,1)S(1)} %copy-done.1, bf16[1,768,2048]{2,1,0:T(8,128)(2,1)S(1)} %copy-done.2, ...), custom_call_target="tpu_custom_call" | custom-call | flops 603979776 | bytes 9437184 | tf_op jit(solution)/shard_map/experts/pallas_call | solution.py:220
  74.0 2.9 %collective-permute-start.18 = (bf16[32,2048]{1,0:T(8,128)(2,1)S(1)}, bf16[32,2048]{1,0:T(8,128)(2,1)S(1)}, u32[]{:S(2)}, u32[]{:S(2)}) collective-permute-start(bf16[32,2048]{1,0:T(8,128)(2,1)S(1)} %get-tuple-element.51), channel_id=1, source_target_pairs={{0,6},{1,7},{2,4},{3,5},{4,2},{5,3},{6,0},{7,1},{8,14},{9,15},{10,... | collective-permute-start | bytes 393224 | tf_op jit(solution)/shard_map/ppermute | solution.py:21
  76.9 8.1 %collective-permute-done.14.rest_5_ = bf16[32,2048]{1,0:T(8,128)(2,1)S(1)} collective-permute-done((bf16[32,2048]{1,0:T(8,128)(2,1)S(1)}, bf16[32,2048]{1,0:T(8,128)(2,1)S(1)}, u32[]{:S(2)}, u32[]{:S(2)}) %collective-permute-start.14) | collective-permute-done | bytes 131104 | tf_op jit(solution)/shard_map/ppermute | solution.py:21
  85.1 2.8 %collective-permute-done.15.rest_6_ = bf16[32,2048]{1,0:T(8,128)(2,1)S(1)} collective-permute-done((bf16[32,2048]{1,0:T(8,128)(2,1)S(1)}, bf16[32,2048]{1,0:T(8,128)(2,1)S(1)}, u32[]{:S(2)}, u32[]{:S(2)}) %collective-permute-start.15) | collective-permute-done | bytes 131104 | tf_op jit(solution)/shard_map/ppermute | solution.py:21
  87.9 3.6 %collective-permute-done.18.rest_7_ = bf16[32,2048]{1,0:T(8,128)(2,1)S(1)} collective-permute-done((bf16[32,2048]{1,0:T(8,128)(2,1)S(1)}, bf16[32,2048]{1,0:T(8,128)(2,1)S(1)}, u32[]{:S(2)}, u32[]{:S(2)}) %collective-permute-start.18) | collective-permute-done | bytes 131104 | tf_op jit(solution)/shard_map/ppermute | solution.py:21
  91.5 2.8 %collective-permute-done.19.rest_8_ = bf16[32,2048]{1,0:T(8,128)(2,1)S(1)} collective-permute-done((bf16[32,2048]{1,0:T(8,128)(2,1)S(1)}, bf16[32,2048]{1,0:T(8,128)(2,1)S(1)}, u32[]{:S(2)}, u32[]{:S(2)}) %collective-permute-start.19) | collective-permute-done | bytes 131104 | tf_op jit(solution)/shard_map/ppermute | solution.py:21
  94.3 1.4 %combine.1 = bf16[1,128,2048]{2,1,0:T(8,128)(2,1)} custom-call(s32[2,128]{1,0:T(2,128)S(1)} %bitcast.11, f32[2,128]{1,0:T(2,128)S(1)} %bitcast.12, bf16[128,2048]{1,0:T(8,128)(2,1)S(1)} %get-tuple-element.36.rest_0_, bf16[32,2048]{1,0:T(8,128)(2,1)S(1)} %get-tuple-element.41.rest_1_, bf16[32,2048]{1,0:T(8,128)(2,1)S(1)} %collective-permute-done.9.rest_2_, ...), custom_call_target="tpu_custom_call" | custom-call | flops 268435456 | bytes 2097152 | tf_op jit(solution)/shard_map/combine/pallas_call | solution.py:277
  (23 shorter events, 0.0 us)
Async XLA Ops:
  0.0 1.0 %copy-start.3 = (bf16[1,128,2048]{2,1,0:T(8,128)(2,1)S(1)}, bf16[1,128,2048]{2,1,0:T(8,128)(2,1)}, u32[]{:S(2)}) copy-start(bf16[1,128,2048]{2,1,0:T(8,128)(2,1)} %q_ref.3) | copy-start | bytes 1572868
  1.0 1.0 %copy-start.5 = (bf16[1,128,2048]{2,1,0:T(8,128)(2,1)S(1)}, bf16[1,128,2048]{2,1,0:T(8,128)(2,1)}, u32[]{:S(2)}) copy-start(bf16[1,128,2048]{2,1,0:T(8,128)(2,1)} %k_ref.3) | copy-start | bytes 1572868
  2.1 1.0 %copy-start.7 = (bf16[1,128,2048]{2,1,0:T(8,128)(2,1)S(1)}, bf16[1,128,2048]{2,1,0:T(8,128)(2,1)}, u32[]{:S(2)}) copy-start(bf16[1,128,2048]{2,1,0:T(8,128)(2,1)} %v_ref.3) | copy-start | bytes 1572868
  3.1 50.5 %copy-start.2 = (bf16[1,768,2048]{2,1,0:T(8,128)(2,1)S(1)}, bf16[1,768,2048]{2,1,0:T(8,128)(2,1)}, u32[]{:S(2)}) copy-start(bf16[1,768,2048]{2,1,0:T(8,128)(2,1)} %down_ref.5) | copy-start | bytes 9437188
  3.4 10.0 %collective-permute-start = (bf16[3,128,512]{2,1,0:T(8,128)(2,1)S(1)}, bf16[3,128,512]{2,1,0:T(8,128)(2,1)S(1)}, u32[]{:S(2)}, u32[]{:S(2)}) collective-permute-start(bf16[3,128,512]{2,1,0:T(8,128)(2,1)S(1)} %get-tuple-element.29), channel_id=1, source_target_pairs={{0,8},{8,0},{16,24},{24,16},{1,9},{9,1},{17,25},{25,17},{2,10},{10... | collective-permute-start | bytes 1179656 | tf_op jit(solution)/shard_map/ppermute | solution.py:21
  3.7 9.7 %collective-permute-start.1 = (bf16[3,128,512]{2,1,0:T(8,128)(2,1)S(1)}, bf16[3,128,512]{2,1,0:T(8,128)(2,1)S(1)}, u32[]{:S(2)}, u32[]{:S(2)}) collective-permute-start(bf16[3,128,512]{2,1,0:T(8,128)(2,1)S(1)} %get-tuple-element.30), channel_id=1, source_target_pairs={{0,16},{8,24},{16,0},{24,8},{1,17},{9,25},{17,1},{25,9},{2,18},{10... | collective-permute-start | bytes 1179656 | tf_op jit(solution)/shard_map/ppermute | solution.py:21
  5.0 48.6 %copy-start = (bf16[1,2048,768]{2,1,0:T(8,128)(2,1)S(1)}, bf16[1,2048,768]{2,1,0:T(8,128)(2,1)}, u32[]{:S(2)}) copy-start(bf16[1,2048,768]{2,1,0:T(8,128)(2,1)} %gate_ref.5) | copy-start | bytes 9437188
  5.0 48.6 %copy-start.1 = (bf16[1,2048,768]{2,1,0:T(8,128)(2,1)S(1)}, bf16[1,2048,768]{2,1,0:T(8,128)(2,1)}, u32[]{:S(2)}) copy-start(bf16[1,2048,768]{2,1,0:T(8,128)(2,1)} %up_ref.5) | copy-start | bytes 9437188
  5.0 17.9 %collective-permute-start.2 = (bf16[3,128,512]{2,1,0:T(8,128)(2,1)S(1)}, bf16[3,128,512]{2,1,0:T(8,128)(2,1)S(1)}, u32[]{:S(2)}, u32[]{:S(2)}) collective-permute-start(bf16[3,128,512]{2,1,0:T(8,128)(2,1)S(1)} %get-tuple-element.31), channel_id=1, source_target_pairs={{0,24},{8,16},{16,8},{24,0},{1,25},{9,17},{17,9},{25,1},{2,26},{10... | collective-permute-start | bytes 1179656 | tf_op jit(solution)/shard_map/ppermute | solution.py:21
  22.8 1.0 %copy-start.4 = (bf16[1,128,2048]{2,1,0:T(8,128)(2,1)S(1)}, bf16[1,128,2048]{2,1,0:T(8,128)(2,1)}, u32[]{:S(2)}) copy-start(bf16[1,128,2048]{2,1,0:T(8,128)(2,1)} %q_ref.3) | copy-start | bytes 1572868
  23.9 1.0 %copy-start.6 = (bf16[1,128,2048]{2,1,0:T(8,128)(2,1)S(1)}, bf16[1,128,2048]{2,1,0:T(8,128)(2,1)}, u32[]{:S(2)}) copy-start(bf16[1,128,2048]{2,1,0:T(8,128)(2,1)} %k_ref.3) | copy-start | bytes 1572868
  24.9 1.0 %copy-start.8 = (bf16[1,128,2048]{2,1,0:T(8,128)(2,1)S(1)}, bf16[1,128,2048]{2,1,0:T(8,128)(2,1)}, u32[]{:S(2)}) copy-start(bf16[1,128,2048]{2,1,0:T(8,128)(2,1)} %v_ref.3) | copy-start | bytes 1572868
  26.0 12.1 %copy-start.10 = (s32[1,128,2]{1,2,0:T(2,128)S(1)}, s32[1,128,2]{1,2,0:T(2,128)}, u32[]{:S(2)}) copy-start(s32[1,128,2]{1,2,0:T(2,128)} %param.13) | copy-start | bytes 3076
  26.0 27.6 %copy-start.9 = (f32[2048]{0:T(1024)S(1)}, f32[2048]{0:T(1024)}, u32[]{:S(2)}) copy-start(f32[2048]{0:T(1024)} %param.12) | copy-start | bytes 24580
  32.1 3.9 %collective-permute-start.3 = (bf16[128,512]{1,0:T(8,128)(2,1)S(1)}, bf16[128,512]{1,0:T(8,128)(2,1)S(1)}, u32[]{:S(2)}, u32[]{:S(2)}) collective-permute-start(bf16[128,512]{1,0:T(8,128)(2,1)S(1)} %get-tuple-element.33), channel_id=1, source_target_pairs={{0,8},{8,0},{16,24},{24,16},{1,9},{9,1},{17,25},{25,17},{2,10},{10... | collective-permute-start | bytes 393224 | tf_op jit(solution)/shard_map/ppermute | solution.py:21
  32.5 5.2 %collective-permute-start.4 = (bf16[128,512]{1,0:T(8,128)(2,1)S(1)}, bf16[128,512]{1,0:T(8,128)(2,1)S(1)}, u32[]{:S(2)}, u32[]{:S(2)}) collective-permute-start(bf16[128,512]{1,0:T(8,128)(2,1)S(1)} %get-tuple-element.34), channel_id=1, source_target_pairs={{0,16},{8,24},{16,0},{24,8},{1,17},{9,25},{17,1},{25,9},{2,18},{10... | collective-permute-start | bytes 393224 | tf_op jit(solution)/shard_map/ppermute | solution.py:21
  32.7 5.4 %collective-permute-start.5 = (bf16[128,512]{1,0:T(8,128)(2,1)S(1)}, bf16[128,512]{1,0:T(8,128)(2,1)S(1)}, u32[]{:S(2)}, u32[]{:S(2)}) collective-permute-start(bf16[128,512]{1,0:T(8,128)(2,1)S(1)} %get-tuple-element.35), channel_id=1, source_target_pairs={{0,24},{8,16},{16,8},{24,0},{1,25},{9,17},{17,9},{25,1},{2,26},{10... | collective-permute-start | bytes 393224 | tf_op jit(solution)/shard_map/ppermute | solution.py:21
  38.8 8.2 %collective-permute-start.6 = (bf16[32,2048]{1,0:T(8,128)(2,1)S(1)}, bf16[32,2048]{1,0:T(8,128)(2,1)S(1)}, u32[]{:S(2)}, u32[]{:S(2)}) collective-permute-start(bf16[32,2048]{1,0:T(8,128)(2,1)S(1)} %get-tuple-element.38), channel_id=1, source_target_pairs={{0,1},{1,0},{2,3},{3,2},{4,5},{5,4},{6,7},{7,6},{8,9},{9,8},{10,11... | collective-permute-start | bytes 393224 | tf_op jit(solution)/shard_map/ppermute | solution.py:21
  42.6 5.7 %collective-permute-start.7 = (bf16[32,2048]{1,0:T(8,128)(2,1)S(1)}, bf16[32,2048]{1,0:T(8,128)(2,1)S(1)}, u32[]{:S(2)}, u32[]{:S(2)}) collective-permute-start(bf16[32,2048]{1,0:T(8,128)(2,1)S(1)} %get-tuple-element.39), channel_id=1, source_target_pairs={{0,2},{1,3},{2,0},{3,1},{4,6},{5,7},{6,4},{7,5},{8,10},{9,11},{10,... | collective-permute-start | bytes 393224 | tf_op jit(solution)/shard_map/ppermute | solution.py:21
  42.8 10.8 %collective-permute-start.8 = (bf16[32,2048]{1,0:T(8,128)(2,1)S(1)}, bf16[32,2048]{1,0:T(8,128)(2,1)S(1)}, u32[]{:S(2)}, u32[]{:S(2)}) collective-permute-start(bf16[32,2048]{1,0:T(8,128)(2,1)S(1)} %get-tuple-element.40), channel_id=1, source_target_pairs={{0,3},{1,2},{2,1},{3,0},{4,7},{5,6},{6,5},{7,4},{8,11},{9,10},{10,... | collective-permute-start | bytes 393224 | tf_op jit(solution)/shard_map/ppermute | solution.py:21
  44.3 13.4 %collective-permute-start.12 = (bf16[32,2048]{1,0:T(8,128)(2,1)S(1)}, bf16[32,2048]{1,0:T(8,128)(2,1)S(1)}, u32[]{:S(2)}, u32[]{:S(2)}) collective-permute-start(bf16[32,2048]{1,0:T(8,128)(2,1)S(1)} %get-tuple-element.45), channel_id=1, source_target_pairs={{0,4},{1,5},{2,6},{3,7},{4,0},{5,1},{6,2},{7,3},{8,12},{9,13},{10,... | collective-permute-start | bytes 393224 | tf_op jit(solution)/shard_map/ppermute | solution.py:21
  46.7 16.9 %collective-permute-start.13 = (bf16[32,2048]{1,0:T(8,128)(2,1)S(1)}, bf16[32,2048]{1,0:T(8,128)(2,1)S(1)}, u32[]{:S(2)}, u32[]{:S(2)}) collective-permute-start(bf16[32,2048]{1,0:T(8,128)(2,1)S(1)} %get-tuple-element.46), channel_id=1, source_target_pairs={{0,5},{1,4},{2,7},{3,6},{4,1},{5,0},{6,3},{7,2},{8,13},{9,12},{10,... | collective-permute-start | bytes 393224 | tf_op jit(solution)/shard_map/ppermute | solution.py:21
  47.0 21.3 %collective-permute-start.16 = (bf16[32,2048]{1,0:T(8,128)(2,1)S(1)}, bf16[32,2048]{1,0:T(8,128)(2,1)S(1)}, u32[]{:S(2)}, u32[]{:S(2)}) collective-permute-start(bf16[32,2048]{1,0:T(8,128)(2,1)S(1)} %get-tuple-element.49), channel_id=1, source_target_pairs={{0,6},{1,7},{2,4},{3,5},{4,2},{5,3},{6,0},{7,1},{8,14},{9,15},{10,... | collective-permute-start | bytes 393224 | tf_op jit(solution)/shard_map/ppermute | solution.py:21
  48.3 22.3 %collective-permute-start.17 = (bf16[32,2048]{1,0:T(8,128)(2,1)S(1)}, bf16[32,2048]{1,0:T(8,128)(2,1)S(1)}, u32[]{:S(2)}, u32[]{:S(2)}) collective-permute-start(bf16[32,2048]{1,0:T(8,128)(2,1)S(1)} %get-tuple-element.50), channel_id=1, source_target_pairs={{0,7},{1,6},{2,5},{3,4},{4,3},{5,2},{6,1},{7,0},{8,15},{9,14},{10,... | collective-permute-start | bytes 393224 | tf_op jit(solution)/shard_map/ppermute | solution.py:21
  56.8 17.2 %collective-permute-start.9 = (bf16[32,2048]{1,0:T(8,128)(2,1)S(1)}, bf16[32,2048]{1,0:T(8,128)(2,1)S(1)}, u32[]{:S(2)}, u32[]{:S(2)}) collective-permute-start(bf16[32,2048]{1,0:T(8,128)(2,1)S(1)} %get-tuple-element.42), channel_id=1, source_target_pairs={{0,1},{1,0},{2,3},{3,2},{4,5},{5,4},{6,7},{7,6},{8,9},{9,8},{10,11... | collective-permute-start | bytes 393224 | tf_op jit(solution)/shard_map/ppermute | solution.py:21
  57.7 19.2 %collective-permute-start.10 = (bf16[32,2048]{1,0:T(8,128)(2,1)S(1)}, bf16[32,2048]{1,0:T(8,128)(2,1)S(1)}, u32[]{:S(2)}, u32[]{:S(2)}) collective-permute-start(bf16[32,2048]{1,0:T(8,128)(2,1)S(1)} %get-tuple-element.43), channel_id=1, source_target_pairs={{0,2},{1,3},{2,0},{3,1},{4,6},{5,7},{6,4},{7,5},{8,10},{9,11},{10,... | collective-permute-start | bytes 393224 | tf_op jit(solution)/shard_map/ppermute | solution.py:21
  63.5 13.4 %collective-permute-start.11 = (bf16[32,2048]{1,0:T(8,128)(2,1)S(1)}, bf16[32,2048]{1,0:T(8,128)(2,1)S(1)}, u32[]{:S(2)}, u32[]{:S(2)}) collective-permute-start(bf16[32,2048]{1,0:T(8,128)(2,1)S(1)} %get-tuple-element.44), channel_id=1, source_target_pairs={{0,3},{1,2},{2,1},{3,0},{4,7},{5,6},{6,5},{7,4},{8,11},{9,10},{10,... | collective-permute-start | bytes 393224 | tf_op jit(solution)/shard_map/ppermute | solution.py:21
  68.3 16.8 %collective-permute-start.14 = (bf16[32,2048]{1,0:T(8,128)(2,1)S(1)}, bf16[32,2048]{1,0:T(8,128)(2,1)S(1)}, u32[]{:S(2)}, u32[]{:S(2)}) collective-permute-start(bf16[32,2048]{1,0:T(8,128)(2,1)S(1)} %get-tuple-element.47), channel_id=1, source_target_pairs={{0,4},{1,5},{2,6},{3,7},{4,0},{5,1},{6,2},{7,3},{8,12},{9,13},{10,... | collective-permute-start | bytes 393224 | tf_op jit(solution)/shard_map/ppermute | solution.py:21
  70.6 23.7 %copy-start.11 = (f32[1,128,2]{1,2,0:T(2,128)S(1)}, f32[1,128,2]{1,2,0:T(2,128)}, u32[]{:S(2)}) copy-start(f32[1,128,2]{1,2,0:T(2,128)} %param.14) | copy-start | bytes 3076
  70.6 17.3 %collective-permute-start.15 = (bf16[32,2048]{1,0:T(8,128)(2,1)S(1)}, bf16[32,2048]{1,0:T(8,128)(2,1)S(1)}, u32[]{:S(2)}, u32[]{:S(2)}) collective-permute-start(bf16[32,2048]{1,0:T(8,128)(2,1)S(1)} %get-tuple-element.48), channel_id=1, source_target_pairs={{0,5},{1,4},{2,7},{3,6},{4,1},{5,0},{6,3},{7,2},{8,13},{9,12},{10,... | collective-permute-start | bytes 393224 | tf_op jit(solution)/shard_map/ppermute | solution.py:21
  74.0 17.5 %collective-permute-start.18 = (bf16[32,2048]{1,0:T(8,128)(2,1)S(1)}, bf16[32,2048]{1,0:T(8,128)(2,1)S(1)}, u32[]{:S(2)}, u32[]{:S(2)}) collective-permute-start(bf16[32,2048]{1,0:T(8,128)(2,1)S(1)} %get-tuple-element.51), channel_id=1, source_target_pairs={{0,6},{1,7},{2,4},{3,5},{4,2},{5,3},{6,0},{7,1},{8,14},{9,15},{10,... | collective-permute-start | bytes 393224 | tf_op jit(solution)/shard_map/ppermute | solution.py:21
  76.9 17.4 %collective-permute-start.19 = (bf16[32,2048]{1,0:T(8,128)(2,1)S(1)}, bf16[32,2048]{1,0:T(8,128)(2,1)S(1)}, u32[]{:S(2)}, u32[]{:S(2)}) collective-permute-start(bf16[32,2048]{1,0:T(8,128)(2,1)S(1)} %get-tuple-element.52), channel_id=1, source_target_pairs={{0,7},{1,6},{2,5},{3,4},{4,3},{5,2},{6,1},{7,0},{8,15},{9,14},{10,... | collective-permute-start | bytes 393224 | tf_op jit(solution)/shard_map/ppermute | solution.py:21

commit v2 on v1

v2 whole, which is shorter than its diff:
```python
import functools
import math

import jax
import jax.numpy as jnp
from jax import lax
from jax.experimental import pallas as pl
from jax.experimental.pallas import tpu as pltpu
from jax.sharding import PartitionSpec as P

HEADS = 16
CAP = 32
CHUNKS = 2
PACK_MIB = 56
F32 = jnp.float32
BF16 = jnp.bfloat16
HBM = pl.BlockSpec(memory_space=pltpu.HBM)
VMEM = pl.BlockSpec(memory_space=pltpu.VMEM)


def swap(x, axis, distance):
    size = lax.axis_size(axis)
    return lax.ppermute(x, axis, [(i, i ^ distance) for i in range(size)])


def params(mib):
    return pltpu.CompilerParams(vmem_limit_bytes=mib << 20)


def cost(flops, moved):
    return pl.CostEstimate(flops=flops, bytes_accessed=moved, transcendentals=0)


def pack_kernel(groups, chunks, c, width, q_ref, k_ref, v_ref, *rest):
    outs, sems = rest[:-1], rest[-1]
    me = lax.axis_index("seq")
    copies = []
    for distance in range(groups):
        column = pl.multiple_of(((me ^ distance) * chunks + c) * width, 128)
        for i, ref in enumerate((q_ref, k_ref, v_ref)):
            copies.append(
                pltpu.make_async_copy(
                    ref.at[0, :, pl.ds(column, width)], outs[distance].at[i], sems.at[len(copies)]
                )
            )
    for copy in copies:
        copy.start()
    for copy in copies:
        copy.wait()


def pack(groups, chunks, c, width, q, k, v):
    tokens = q.shape[1]
    count = groups
    return pl.pallas_call(
        functools.partial(pack_kernel, groups, chunks, c, width),
        out_shape=[jax.ShapeDtypeStruct((3, tokens, width), BF16)] * count,
        in_specs=[HBM] * 3,
        out_specs=[VMEM] * count,
        scratch_shapes=[pltpu.SemaphoreType.DMA((3 * count,))],
        compiler_params=params(PACK_MIB if c == 0 else 8),
        cost_estimate=cost(0, 2 * 3 * count * tokens * width * 2),
        name="pack_heads",
    )(q, k, v)


def attend_kernel(groups, width, head_size, *rest):
    blocks, outs = rest[:groups], rest[groups : 2 * groups]
    q_all, k_all, v_all, sems = rest[2 * groups :]
    tokens = outs[0].shape[0]
    copies = []
    for i, held in enumerate((q_all, k_all, v_all)):
        for j in range(groups):
            copies.append(
                pltpu.make_async_copy(
                    blocks[j].at[i], held.at[pl.ds(j * tokens, tokens)], sems.at[len(copies)]
                )
            )
    for copy in copies:
        copy.start()
    for copy in copies:
        copy.wait()
    scale = head_size**-0.5 * math.log2(math.e)
    for head in range(width // head_size):
        lanes = slice(head * head_size, (head + 1) * head_size)
        keys, values = k_all[:, lanes], v_all[:, lanes]
        for block in range(groups):
            rows = slice(block * tokens, (block + 1) * tokens)
            scores = lax.dot_general(
                q_all[rows, lanes], keys, (((1,), (1,)), ((), ())), preferred_element_type=F32
            )
            peak = jnp.max(scores, axis=-1, keepdims=True)
            exponentials = jnp.exp2((scores - peak) * scale)
            totals = jnp.sum(exponentials, axis=-1, keepdims=True)
            weighted = jnp.dot(exponentials.astype(BF16), values, preferred_element_type=F32)
            outs[block][:, lanes] = (weighted / totals).astype(BF16)


def attend(width, head_size, blocks):
    groups, tokens = len(blocks), blocks[0].shape[1]
    total = groups * tokens
    return pl.pallas_call(
        functools.partial(attend_kernel, groups, width, head_size),
        out_shape=[jax.ShapeDtypeStruct((tokens, width), BF16)] * groups,
        in_specs=[HBM] * groups,
        out_specs=[VMEM] * groups,
        scratch_shapes=[pltpu.VMEM((total, width), BF16)] * 3
        + [pltpu.SemaphoreType.DMA((3 * groups,))],
        compiler_params=params(32),
        cost_estimate=cost(160 * total * total * width, 80 * total * width),
        name="attend",
    )(*blocks)


def slot_matrix(experts, ids):
    tokens = ids.shape[1]
    me = lax.axis_index("expert")
    named = lax.broadcasted_iota(jnp.int32, (experts, tokens), 0) ^ me
    matches = jnp.where((ids[0:1, :] == named) | (ids[1:2, :] == named), 1.0, 0.0)
    earlier = jnp.where(
        lax.broadcasted_iota(jnp.int32, (tokens, tokens), 0)
        < lax.broadcasted_iota(jnp.int32, (tokens, tokens), 1),
        1.0,
        0.0,
    )
    rank = jnp.dot(matches.astype(BF16), earlier.astype(BF16), preferred_element_type=F32)
    rank = jnp.where(matches > 0.0, rank, -1.0).astype(jnp.int32)
    slots = lax.broadcasted_iota(jnp.int32, (CAP, tokens), 0)
    return [slots == rank[d : d + 1, :] for d in range(experts)], named


def select_kernel(groups, experts, width, earlier, last, ids_ref, *rest):
    blocks, before = rest[:groups], rest[groups : groups + earlier]
    half, middle = experts // 2, experts // 2 + experts // 4
    count = experts if last else middle - half
    outs = rest[groups + earlier : groups + earlier + count]
    kept, sems = rest[groups + earlier + count :]
    me = lax.axis_index("seq")
    copies = []
    for d in range(groups):
        column = pl.multiple_of((me ^ d) * width, 128)
        copies.append(
            pltpu.make_async_copy(blocks[d], kept.at[:, pl.ds(column, width)], sems.at[d])
        )
    for copy in copies:
        copy.start()
    hits, _ = slot_matrix(experts, ids_ref[...])
    chosen = [jnp.where(h, 1.0, 0.0).astype(BF16) for h in hits]
    for copy in copies:
        copy.wait()

    def pick(distances, rows, first):
        picked = jnp.dot(
            jnp.concatenate([chosen[d] for d in distances], axis=0),
            rows,
            preferred_element_type=F32,
        ).astype(BF16)
        for i in range(len(distances)):
            outs[first + i][...] = picked[i * CAP : (i + 1) * CAP]

    pick(range(half, middle), kept[...], 0)
    if last:
        parts = [ref[...] for ref in before] + [kept[...]]
        full = jnp.concatenate(parts, axis=1) if earlier else parts[0]
        pick([*range(middle, experts), *range(half)], full, middle - half)


def select(groups, experts, ids, blocks, before, last):
    tokens, width = blocks[0].shape
    part = groups * width
    whole = part * (len(before) + 1)
    quarter = experts // 4
    shapes = [(CAP, part)] * quarter
    if last:
        shapes += [(CAP, whole)] * (experts - quarter)
    shapes.append((tokens, part))
    return pl.pallas_call(
        functools.partial(select_kernel, groups, experts, width, len(before), last),
        out_shape=[jax.ShapeDtypeStruct(shape, BF16) for shape in shapes],
        in_specs=[VMEM] + [HBM] * groups + [VMEM] * len(before),
        out_specs=[VMEM] * len(shapes),
        scratch_shapes=[pltpu.SemaphoreType.DMA((groups,))],
        compiler_params=params(16),
        cost_estimate=cost(2 * experts * CAP * tokens * part, 8 * tokens * part),
        name="select_rows",
    )(ids, *blocks, *before)


def experts_kernel(
    groups, chunks, width, count, held, gain_ref, gate_ref, up_ref, down_ref, *rest
):
    blocks, outs = rest[: count * held], rest[count * held : count * held + count]
    rows_ref, total_ref = rest[count * held + count :]
    step = pl.program_id(0)

    @pl.when(step == 0)
    def _():
        for i in range(count):
            mine = [blocks[k][...] for k in range(i * held, (i + 1) * held)]
            row = jnp.concatenate(mine, axis=1) if held > 1 else mine[0]
            parts = []
            for g in range(groups):
                for c in range(chunks):
                    first = (c * groups + g) * width
                    parts.append(row[:, first : first + width].astype(F32))
            row = jnp.concatenate(parts, axis=1)
            scale = lax.rsqrt(jnp.mean(row * row, axis=-1, keepdims=True) + 1e-06)
            rows_ref[i * CAP : (i + 1) * CAP, :] = (row * scale * gain_ref[...]).astype(BF16)

    rows = rows_ref[...]
    gate = jnp.dot(rows, gate_ref[0], preferred_element_type=F32)
    up = jnp.dot(rows, up_ref[0], preferred_element_type=F32)
    hidden = (gate / (1.0 + jnp.exp(-gate)) * up).astype(BF16)
    part = jnp.dot(hidden, down_ref[0], preferred_element_type=F32)

    @pl.when(step == 0)
    def _():
        total_ref[...] = part

    @pl.when(step > 0)
    def _():
        total_ref[...] += part

    @pl.when(step == pl.num_programs(0) - 1)
    def _():
        for i in range(count):
            outs[i][...] = total_ref[i * CAP : (i + 1) * CAP, :].astype(BF16)


def run_experts(groups, chunks, width, gain, w_gate, w_up, w_down, blocks):
    count, held = len(blocks), len(blocks[0])
    features, units = w_gate.shape[1:]
    tile = 256 if units % 256 == 0 else 128
    flat = [part for block in blocks for part in block]
    return pl.pallas_call(
        functools.partial(experts_kernel, groups, chunks, width, count, held),
        grid=(units // tile,),
        out_shape=[jax.ShapeDtypeStruct((CAP, features), BF16)] * count,
        in_specs=[
            pl.BlockSpec((1, features), lambda i: (0, 0)),
            pl.BlockSpec((1, features, tile), lambda i: (0, 0, i)),
            pl.BlockSpec((1, features, tile), lambda i: (0, 0, i)),
            pl.BlockSpec((1, tile, features), lambda i: (0, i, 0)),
        ]
        + [pl.BlockSpec(part.shape, lambda i: (0, 0)) for part in flat],
        out_specs=[pl.BlockSpec((CAP, features), lambda i: (0, 0))] * count,
        scratch_shapes=[
            pltpu.VMEM((count * CAP, features), BF16),
            pltpu.VMEM((count * CAP, features), F32),
        ],
        compiler_params=params(32),
        cost_estimate=cost(count * CAP * features, features * units // 100),
        name="experts",
    )(gain, w_gate, w_up, w_down, *flat)


def combine_kernel(groups, experts, widths, ids_ref, gates_ref, *rest):
    chunks = len(widths)
    kept, blocks, out_ref = rest[:chunks], rest[chunks : chunks + experts], rest[-1]
    ids, gates = ids_ref[...], gates_ref[...]
    hits, named = slot_matrix(experts, ids)
    weight = jnp.where(ids[0:1, :] == named, gates[0:1, :], 0.0) + jnp.where(
        ids[1:2, :] == named, gates[1:2, :], 0.0
    )
    coarse = weight.astype(BF16).astype(F32)
    fine = weight - coarse
    spread = []
    for part in (coarse, fine):
        for d in range(experts):
            spread.append(jnp.where(hits[d], part[d : d + 1, :], 0.0).astype(BF16))
    spread = jnp.concatenate(spread, axis=0)
    rows = jnp.concatenate([block[...] for block in blocks], axis=0)
    mixture = lax.dot_general(
        spread,
        jnp.concatenate([rows, rows], axis=0),
        (((0,), (0,)), ((), ())),
        preferred_element_type=F32,
    )
    column = 0
    for g in range(groups):
        for c, w in enumerate(widths):
            part = kept[c][:, g * w : (g + 1) * w].astype(F32)
            out_ref[0, :, column : column + w] = (part + mixture[:, column : column + w]).astype(
                BF16
            )
            column += w


def combine(groups, widths, ids, gates, kept, blocks):
    tokens, features = ids.shape[1], blocks[0].shape[1]
    experts = len(blocks)
    return pl.pallas_call(
        functools.partial(combine_kernel, groups, experts, widths),
        out_shape=jax.ShapeDtypeStruct((1, tokens, features), BF16),
        in_specs=[VMEM] * (2 + len(widths) + experts),
        out_specs=VMEM,
        compiler_params=params(32),
        cost_estimate=cost(4 * experts * CAP * tokens * features, 8 * tokens * features),
        name="combine",
    )(ids, gates, *kept, *blocks)


def after(values, *earlier):
    return lax.optimization_barrier((values, earlier))[0]


def local(
    query_rows, key_rows, value_rows, norm_gain, expert_ids, gate_weights, w_gate, w_up, w_down
):
    features = query_rows.shape[2]
    head_size = features // HEADS
    groups, experts = lax.axis_size("seq"), lax.axis_size("expert")
    per_group = HEADS // groups
    group_width = per_group * head_size
    chunks = CHUNKS if per_group % CHUNKS == 0 else 1
    width = group_width // chunks
    ids, gates = expert_ids[0].T, gate_weights[0].T
    gain = norm_gain.reshape(1, features)
    half = experts // 2
    middle = half + experts // 4

    def exchange(blocks, name):
        with jax.named_scope(name):
            return [blocks[0]] + [swap(blocks[d], "seq", d) for d in range(1, groups)]

    def send(block, distance, name):
        with jax.named_scope(f"{name}{distance}"):
            return swap(block, "expert", distance)

    received = [
        exchange(pack(groups, chunks, c, width, query_rows, key_rows, value_rows), f"qkv{c}_")
        for c in range(chunks)
    ]
    heads = [attend(width, head_size, received[c]) for c in range(chunks)]
    kept, arrived = [], [[] for _ in range(experts)]
    for c in range(chunks):
        last = c == chunks - 1
        out = heads[c] if c == 0 else after(heads[c], kept[-1])
        *rows, own = select(groups, experts, ids, exchange(out, f"heads{c}_"), kept, last)
        kept.append(own)
        for d in range(half, middle):
            row = rows[d - half] if c == 0 else after(rows[d - half], arrived[d][-1])
            arrived[d].append(send(row, d, f"rows{c}_"))
    whole = rows[middle - half :]
    for d in range(middle, experts):
        arrived[d].append(send(whole[d - middle], d, "rows_"))
    whole = whole[experts - middle :]
    arrived[0].append(whole[0])
    for d in range(1, half):
        arrived[d].append(send(whole[d], d, "rows_"))
    returned = [None] * experts
    for members in (range(half, middle), range(middle, experts), range(half)):
        produced = run_experts(
            groups, chunks, width, gain, w_gate, w_up, w_down,
            [arrived[d] for d in members],
        )
        for d, block in zip(members, produced):
            returned[d] = block if d == 0 else send(block, d, "back_")
    return combine(groups, (width,) * chunks, ids, gates, kept, returned)


def solution(mesh):
    rows = P("expert", "seq", None)
    weights = P("expert", None, None)
    return jax.shard_map(
        local,
        mesh=mesh,
        in_specs=(rows, rows, rows, P(), rows, rows, weights, weights, weights),
        out_specs=rows,
        check_vma=False,
    )
```

time: 96.4 us -> 84.6 us (0.88)
  waiting for transfers between devices: 43.2 us -> 24.4 us
  starting transfers between devices: 28.4 us -> 34.8 us
  Pallas kernels: 17.7 us -> 20.8 us
  local copies, waits for them, and re-layouts: 6.27 us -> 4.07 us
    ppermute x20 -> x28, waiting for transfers between devices: 43.2 us -> 24.4 us  [swap(): return lax.ppermute(x, axis, [(i, i ^ distance) for i in range(size)])]
    ppermute x20 -> x28, starting transfers between devices: 28.4 us -> 34.8 us  [swap(): return lax.ppermute(x, axis, [(i, i ^ distance) for i in range(size)])]
    pallas_call x6 -> x9, Pallas kernels: 16.3 us -> 19.4 us  [the longest x3 9.23 us: run_experts(): pl.pallas_call(functools.partial(experts_kernel, groups, chunks, width, c...]
    unnamed x24 -> x20, local copies, waits for them, and re-layouts: 6.27 us -> 4.07 us
  transfers between devices with their start and end apart: 20 -> 28, of which waited for: 11 -> 9; matrix products, arithmetic and copies ran while one was open for 0% -> 0% of each run, Pallas kernels for 10% -> 20%
where the time goes in v2:
time: 84.6 us; the launch traced here: 84.3 us
  starting transfers between devices  34.8 us (41%)
  waiting for transfers between devices  24.4 us (29%)
  Pallas kernels  20.8 us (25%)
  local copies, waits for them, and re-layouts  4.07 us (5%)
    ppermute x28, starting transfers between devices, swap(): return lax.ppermute(x, axis, [(i, i ^ distance) for i in range(size)])  34.8 us
    ppermute x28, waiting for transfers between devices, swap(): return lax.ppermute(x, axis, [(i, i ^ distance) for i in range(size)])  24.4 us
    pallas_call x3, Pallas kernels, run_experts(): pl.pallas_call(functools.partial(experts_kernel, groups, chunks, width, c...  9.23 us
    pallas_call x2, Pallas kernels, attend(): pl.pallas_call(functools.partial(attend_kernel, groups, width, head_size)...  6.72 us
    unnamed x20, local copies, waits for them, and re-layouts  4.07 us
    pallas_call x2, Pallas kernels, pack(): pl.pallas_call(functools.partial(pack_kernel, groups, chunks, c, width),...  2.39 us
  transfers between devices with their start and end apart: 28, of which 9 were waited for; matrix products, arithmetic and copies ran while one was open for 0% of the time, Pallas kernels for 20%

profile of v2, /device:TPU:11, one launch (start us, length us, event | category | flops | bytes accessed | tf_op | source)
XLA Modules:
  0.0 84.3 jit_solution(3939451555317425773)
XLA Ops:
  0.0 2.1 %pack_heads.2 = (bf16[3,128,256]{2,1,0:T(8,128)(2,1)}, bf16[3,128,256]{2,1,0:T(8,128)(2,1)}, bf16[3,128,256]{2,1,0:T(8,128)(2,1)}, bf16[3,128,256]{2,1,0:T(8,128)(2,1)}) custom-call(bf16[1,128,2048]{2,1,0:T(8,128)(2,1)} %q_ref.3, bf16[1,128,2048]{2,1,0:T(8,128)(2,1)} %k_ref.3, bf16[1,128,2048]{2,1,0:T(8,128)(2,1)} %v_ref.3), custom_call_target="tpu_custom_call" | custom-call | bytes 1572864 | tf_op jit(solution)/shard_map/pack_heads/pallas_call | solution.py:55
  2.1 0.3 collective-permute-start
  2.5 1.2 %collective-permute-start.1 = (bf16[3,128,256]{2,1,0:T(8,128)(2,1)}, bf16[3,128,256]{2,1,0:T(8,128)(2,1)S(1)}, u32[]{:S(2)}, u32[]{:S(2)}) collective-permute-start(bf16[3,128,256]{2,1,0:T(8,128)(2,1)} %get-tuple-element.49), channel_id=1, source_target_pairs={{0,16},{8,24},{16,0},{24,8},{1,17},{9,25},{17,1},{25,9},{2,18},{10... | collective-permute-start | bytes 589832 | tf_op jit(solution)/shard_map/qkv0_/ppermute | solution.py:23
  3.7 1.2 %collective-permute-start.2 = (bf16[3,128,256]{2,1,0:T(8,128)(2,1)}, bf16[3,128,256]{2,1,0:T(8,128)(2,1)S(1)}, u32[]{:S(2)}, u32[]{:S(2)}) collective-permute-start(bf16[3,128,256]{2,1,0:T(8,128)(2,1)} %get-tuple-element.50), channel_id=1, source_target_pairs={{0,24},{8,16},{16,8},{24,0},{1,25},{9,17},{17,9},{25,1},{2,26},{10... | collective-permute-start | bytes 589832 | tf_op jit(solution)/shard_map/qkv0_/ppermute | solution.py:23
  4.9 1.0 %copy-done.3 = bf16[1,128,2048]{2,1,0:T(8,128)(2,1)S(1)} copy-done((bf16[1,128,2048]{2,1,0:T(8,128)(2,1)S(1)}, bf16[1,128,2048]{2,1,0:T(8,128)(2,1)}, u32[]{:S(2)}) %copy-start.3) | copy-done | bytes 524312
  5.9 1.0 %copy-done.4 = bf16[1,128,2048]{2,1,0:T(8,128)(2,1)S(1)} copy-done((bf16[1,128,2048]{2,1,0:T(8,128)(2,1)S(1)}, bf16[1,128,2048]{2,1,0:T(8,128)(2,1)}, u32[]{:S(2)}) %copy-start.4) | copy-done | bytes 524312
  6.9 1.0 %copy-done.5 = bf16[1,128,2048]{2,1,0:T(8,128)(2,1)S(1)} copy-done((bf16[1,128,2048]{2,1,0:T(8,128)(2,1)S(1)}, bf16[1,128,2048]{2,1,0:T(8,128)(2,1)}, u32[]{:S(2)}) %copy-start.5) | copy-done | bytes 524312
  8.0 0.2 pack_heads.3
  8.2 0.3 collective-permute-start.6
  8.6 1.2 %collective-permute-start.7 = (bf16[3,128,256]{2,1,0:T(8,128)(2,1)S(1)}, bf16[3,128,256]{2,1,0:T(8,128)(2,1)S(1)}, u32[]{:S(2)}, u32[]{:S(2)}) collective-permute-start(bf16[3,128,256]{2,1,0:T(8,128)(2,1)S(1)} %get-tuple-element.58), channel_id=1, source_target_pairs={{0,16},{8,24},{16,0},{24,8},{1,17},{9,25},{17,1},{25,9},{2,18},{10... | collective-permute-start | bytes 589832 | tf_op jit(solution)/shard_map/qkv1_/ppermute | solution.py:23
  9.8 1.2 %collective-permute-start.8 = (bf16[3,128,256]{2,1,0:T(8,128)(2,1)S(1)}, bf16[3,128,256]{2,1,0:T(8,128)(2,1)S(1)}, u32[]{:S(2)}, u32[]{:S(2)}) collective-permute-start(bf16[3,128,256]{2,1,0:T(8,128)(2,1)S(1)} %get-tuple-element.59), channel_id=1, source_target_pairs={{0,24},{8,16},{16,8},{24,0},{1,25},{9,17},{17,9},{25,1},{2,26},{10... | collective-permute-start | bytes 589832 | tf_op jit(solution)/shard_map/qkv1_/ppermute | solution.py:23
  11.0 2.4 %collective-permute-done.2.rest_3_ = bf16[3,128,256]{2,1,0:T(8,128)(2,1)S(1)} collective-permute-done((bf16[3,128,256]{2,1,0:T(8,128)(2,1)}, bf16[3,128,256]{2,1,0:T(8,128)(2,1)S(1)}, u32[]{:S(2)}, u32[]{:S(2)}) %collective-permute-start.2) | collective-permute-done | bytes 196640 | tf_op jit(solution)/shard_map/qkv0_/ppermute | solution.py:23
  13.4 0.9 %copy-done.9 = bf16[3,128,256]{2,1,0:T(8,128)(2,1)S(1)} copy-done((bf16[3,128,256]{2,1,0:T(8,128)(2,1)S(1)}, bf16[3,128,256]{2,1,0:T(8,128)(2,1)}, u32[]{:S(2)}) %copy-start.9) | copy-done | bytes 196632
  14.3 3.3 %attend.2 = (bf16[128,256]{1,0:T(8,128)(2,1)S(1)}, bf16[128,256]{1,0:T(8,128)(2,1)S(1)}, bf16[128,256]{1,0:T(8,128)(2,1)S(1)}, bf16[128,256]{1,0:T(8,128)(2,1)S(1)}) custom-call(bf16[3,128,256]{2,1,0:T(8,128)(2,1)S(1)} %copy-done.9, bf16[3,128,256]{2,1,0:T(8,128)(2,1)S(1)} %collective-permute-done.rest_1_, ...), custom_call_target="tpu_custom_call" | custom-call | flops 10737418240 | bytes 10485760 | tf_op jit(solution)/shard_map/attend/pallas_call | solution.py:102
  17.7 0.3 collective-permute-start.3
  18.0 0.2 collective-permute-start.4
  18.2 2.2 %collective-permute-start.5 = (bf16[128,256]{1,0:T(8,128)(2,1)S(1)}, bf16[128,256]{1,0:T(8,128)(2,1)S(1)}, u32[]{:S(2)}, u32[]{:S(2)}) collective-permute-start(bf16[128,256]{1,0:T(8,128)(2,1)S(1)} %get-tuple-element.54), channel_id=1, source_target_pairs={{0,24},{8,16},{16,8},{24,0},{1,25},{9,17},{17,9},{25,1},{2,26},{10... | collective-permute-start | bytes 196616 | tf_op jit(solution)/shard_map/heads0_/ppermute | solution.py:23
  20.4 1.4 %collective-permute-done.8.rest_3_ = bf16[3,128,256]{2,1,0:T(8,128)(2,1)S(1)} collective-permute-done((bf16[3,128,256]{2,1,0:T(8,128)(2,1)S(1)}, bf16[3,128,256]{2,1,0:T(8,128)(2,1)S(1)}, u32[]{:S(2)}, u32[]{:S(2)}) %collective-permute-start.8) | collective-permute-done | bytes 196640 | tf_op jit(solution)/shard_map/qkv1_/ppermute | solution.py:23
  21.9 3.4 %attend.3 = (bf16[128,256]{1,0:T(8,128)(2,1)S(1)}, bf16[128,256]{1,0:T(8,128)(2,1)S(1)}, bf16[128,256]{1,0:T(8,128)(2,1)S(1)}, bf16[128,256]{1,0:T(8,128)(2,1)S(1)}) custom-call(bf16[3,128,256]{2,1,0:T(8,128)(2,1)S(1)} %get-tuple-element.56.rest_0_, bf16[3,128,256]{2,1,0:T(8,128)(2,1)S(1)} %collective-permute-done.6.rest_1_, ...), custom_call_target="tpu_custom_call" | custom-call | flops 10737418240 | bytes 10485760 | tf_op jit(solution)/shard_map/attend/pallas_call | solution.py:102
  25.3 0.4 select_rows.2
  25.7 0.4 collective-permute-start.9
  26.1 0.4 collective-permute-start.10
  26.5 2.0 %collective-permute-start.11 = (bf16[128,256]{1,0:T(8,128)(2,1)S(1)}, bf16[128,256]{1,0:T(8,128)(2,1)S(1)}, u32[]{:S(2)}, u32[]{:S(2)}) collective-permute-start(bf16[128,256]{1,0:T(8,128)(2,1)S(1)} %get-tuple-element.67), channel_id=1, source_target_pairs={{0,24},{8,16},{16,8},{24,0},{1,25},{9,17},{17,9},{25,1},{2,26},{10... | collective-permute-start | bytes 196616 | tf_op jit(solution)/shard_map/heads1_/ppermute | solution.py:23
  28.4 2.3 %collective-permute-start.18 = (bf16[32,1024]{1,0:T(8,128)(2,1)S(1)}, bf16[32,1024]{1,0:T(8,128)(2,1)S(1)}, u32[]{:S(2)}, u32[]{:S(2)}) collective-permute-start(bf16[32,1024]{1,0:T(8,128)(2,1)S(1)} %get-tuple-element.77), channel_id=1, source_target_pairs={{0,4},{1,5},{2,6},{3,7},{4,0},{5,1},{6,2},{7,3},{8,12},{9,13},{10,... | collective-permute-start | bytes 196616 | tf_op jit(solution)/shard_map/rows0_4/ppermute | solution.py:23
  30.7 3.8 %collective-permute-start.20 = (bf16[32,1024]{1,0:T(8,128)(2,1)S(1)}, bf16[32,1024]{1,0:T(8,128)(2,1)S(1)}, u32[]{:S(2)}, u32[]{:S(2)}) collective-permute-start(bf16[32,1024]{1,0:T(8,128)(2,1)S(1)} %get-tuple-element.80), channel_id=1, source_target_pairs={{0,5},{1,4},{2,7},{3,6},{4,1},{5,0},{6,3},{7,2},{8,13},{9,12},{10,... | collective-permute-start | bytes 196616 | tf_op jit(solution)/shard_map/rows0_5/ppermute | solution.py:23
  34.5 0.6 select_rows.3
  35.1 1.7 %collective-permute-start.12 = (bf16[32,2048]{1,0:T(8,128)(2,1)S(1)}, bf16[32,2048]{1,0:T(8,128)(2,1)S(1)}, u32[]{:S(2)}, u32[]{:S(2)}) collective-permute-start(bf16[32,2048]{1,0:T(8,128)(2,1)S(1)} %get-tuple-element.70), channel_id=1, source_target_pairs={{0,1},{1,0},{2,3},{3,2},{4,5},{5,4},{6,7},{7,6},{8,9},{9,8},{10,11... | collective-permute-start | bytes 393224 | tf_op jit(solution)/shard_map/rows_1/ppermute | solution.py:23
  37.1 1.4 %collective-permute-done.20.rest_2_ = bf16[32,1024]{1,0:T(8,128)(2,1)S(1)} collective-permute-done((bf16[32,1024]{1,0:T(8,128)(2,1)S(1)}, bf16[32,1024]{1,0:T(8,128)(2,1)S(1)}, u32[]{:S(2)}, u32[]{:S(2)}) %collective-permute-start.20) | collective-permute-done | bytes 65568 | tf_op jit(solution)/shard_map/rows0_5/ppermute | solution.py:23
  38.5 3.4 %collective-permute-start.21 = (bf16[32,1024]{1,0:T(8,128)(2,1)S(1)}, bf16[32,1024]{1,0:T(8,128)(2,1)S(1)}, u32[]{:S(2)}, u32[]{:S(2)}) collective-permute-start(bf16[32,1024]{1,0:T(8,128)(2,1)S(1)} %get-tuple-element.82), channel_id=1, source_target_pairs={{0,5},{1,4},{2,7},{3,6},{4,1},{5,0},{6,3},{7,2},{8,13},{9,12},{10,... | collective-permute-start | bytes 196616 | tf_op jit(solution)/shard_map/rows1_5/ppermute | solution.py:23
  41.8 0.2 collective-permute-start.19
  42.1 1.0 %collective-permute-start.14 = (bf16[32,2048]{1,0:T(8,128)(2,1)S(1)}, bf16[32,2048]{1,0:T(8,128)(2,1)S(1)}, u32[]{:S(2)}, u32[]{:S(2)}) collective-permute-start(bf16[32,2048]{1,0:T(8,128)(2,1)S(1)} %get-tuple-element.72), channel_id=1, source_target_pairs={{0,3},{1,2},{2,1},{3,0},{4,7},{5,6},{6,5},{7,4},{8,11},{9,10},{10,... | collective-permute-start | bytes 393224 | tf_op jit(solution)/shard_map/rows_3/ppermute | solution.py:23
  43.1 1.7 %collective-permute-done.21.rest_3_ = bf16[32,1024]{1,0:T(8,128)(2,1)S(1)} collective-permute-done((bf16[32,1024]{1,0:T(8,128)(2,1)S(1)}, bf16[32,1024]{1,0:T(8,128)(2,1)S(1)}, u32[]{:S(2)}, u32[]{:S(2)}) %collective-permute-start.21) | collective-permute-done | bytes 65568 | tf_op jit(solution)/shard_map/rows1_5/ppermute | solution.py:23
  44.8 1.2 %collective-permute-start.24 = (bf16[32,2048]{1,0:T(8,128)(2,1)S(1)}, bf16[32,2048]{1,0:T(8,128)(2,1)S(1)}, u32[]{:S(2)}, u32[]{:S(2)}) collective-permute-start(bf16[32,2048]{1,0:T(8,128)(2,1)S(1)} %get-tuple-element.85), channel_id=1, source_target_pairs={{0,6},{1,7},{2,4},{3,5},{4,2},{5,3},{6,0},{7,1},{8,14},{9,15},{10,... | collective-permute-start | bytes 393224 | tf_op jit(solution)/shard_map/rows_6/ppermute | solution.py:23
  46.0 0.7 collective-permute-done.19.rest_1_
  46.7 1.2 %collective-permute-start.25 = (bf16[32,2048]{1,0:T(8,128)(2,1)S(1)}, bf16[32,2048]{1,0:T(8,128)(2,1)S(1)}, u32[]{:S(2)}, u32[]{:S(2)}) collective-permute-start(bf16[32,2048]{1,0:T(8,128)(2,1)S(1)} %get-tuple-element.86), channel_id=1, source_target_pairs={{0,7},{1,6},{2,5},{3,4},{4,3},{5,2},{6,1},{7,0},{8,15},{9,14},{10,... | collective-permute-start | bytes 393224 | tf_op jit(solution)/shard_map/rows_7/ppermute | solution.py:23
  48.0 3.1 %experts.4 = (bf16[32,2048]{1,0:T(8,128)(2,1)S(1)}, bf16[32,2048]{1,0:T(8,128)(2,1)S(1)}) custom-call(f32[1,2048]{1,0:T(1,128)S(1)} %bitcast.7, bf16[1,2048,768]{2,1,0:T(8,128)(2,1)S(1)} %copy-done, bf16[1,2048,768]{2,1,0:T(8,128)(2,1)S(1)} %copy-done.1, bf16[1,768,2048]{2,1,0:T(8,128)(2,1)S(1)} %copy-done.2, ...), custom_call_target="tpu_custom_call" | custom-call | flops 131072 | bytes 15728 | tf_op jit(solution)/shard_map/experts/pallas_call | solution.py:235
  51.0 4.4 %collective-permute-start.22 = (bf16[32,2048]{1,0:T(8,128)(2,1)S(1)}, bf16[32,2048]{1,0:T(8,128)(2,1)S(1)}, u32[]{:S(2)}, u32[]{:S(2)}) collective-permute-start(bf16[32,2048]{1,0:T(8,128)(2,1)S(1)} %get-tuple-element.83), channel_id=1, source_target_pairs={{0,4},{1,5},{2,6},{3,7},{4,0},{5,1},{6,2},{7,3},{8,12},{9,13},{10,... | collective-permute-start | bytes 393224 | tf_op jit(solution)/shard_map/back_4/ppermute | solution.py:23
  55.6 3.1 %experts.3 = (bf16[32,2048]{1,0:T(8,128)(2,1)S(1)}, bf16[32,2048]{1,0:T(8,128)(2,1)S(1)}, bf16[32,2048]{1,0:T(8,128)(2,1)S(1)}, bf16[32,2048]{1,0:T(8,128)(2,1)S(1)}) custom-call(f32[1,2048]{1,0:T(1,128)S(1)} %bitcast.8, bf16[1,2048,768]{2,1,0:T(8,128)(2,1)S(1)} %copy-done, bf16[1,2048,768]{2,1,0:T(8,128)(2,1)S(1)} %copy-done.1, ...), custom_call_target="tpu_custom_call" | custom-call | flops 262144 | bytes 15728 | tf_op jit(solution)/shard_map/experts/pallas_call | solution.py:235
  58.8 0.4 collective-permute-start.15
  59.2 2.2 %collective-permute-start.16 = (bf16[32,2048]{1,0:T(8,128)(2,1)S(1)}, bf16[32,2048]{1,0:T(8,128)(2,1)S(1)}, u32[]{:S(2)}, u32[]{:S(2)}) collective-permute-start(bf16[32,2048]{1,0:T(8,128)(2,1)S(1)} %get-tuple-element.75), channel_id=1, source_target_pairs={{0,2},{1,3},{2,0},{3,1},{4,6},{5,7},{6,4},{7,5},{8,10},{9,11},{10,... | collective-permute-start | bytes 393224 | tf_op jit(solution)/shard_map/back_2/ppermute | solution.py:23
  61.4 4.5 %collective-permute-done.25.rest_1_ = bf16[32,2048]{1,0:T(8,128)(2,1)S(1)} collective-permute-done((bf16[32,2048]{1,0:T(8,128)(2,1)S(1)}, bf16[32,2048]{1,0:T(8,128)(2,1)S(1)}, u32[]{:S(2)}, u32[]{:S(2)}) %collective-permute-start.25) | collective-permute-done | bytes 131104 | tf_op jit(solution)/shard_map/rows_7/ppermute | solution.py:23
  65.9 3.0 %experts.5 = (bf16[32,2048]{1,0:T(8,128)(2,1)S(1)}, bf16[32,2048]{1,0:T(8,128)(2,1)S(1)}) custom-call(f32[1,2048]{1,0:T(1,128)S(1)} %bitcast.9, bf16[1,2048,768]{2,1,0:T(8,128)(2,1)S(1)} %copy-done, bf16[1,2048,768]{2,1,0:T(8,128)(2,1)S(1)} %copy-done.1, bf16[1,768,2048]{2,1,0:T(8,128)(2,1)S(1)} %copy-done.2, ...), custom_call_target="tpu_custom_call" | custom-call | flops 131072 | bytes 15728 | tf_op jit(solution)/shard_map/experts/pallas_call | solution.py:235
  68.9 0.6 collective-permute-start.26
  69.5 1.3 %collective-permute-start.27 = (bf16[32,2048]{1,0:T(8,128)(2,1)S(1)}, bf16[32,2048]{1,0:T(8,128)(2,1)S(1)}, u32[]{:S(2)}, u32[]{:S(2)}) collective-permute-start(bf16[32,2048]{1,0:T(8,128)(2,1)S(1)} %get-tuple-element.88), channel_id=1, source_target_pairs={{0,7},{1,6},{2,5},{3,4},{4,3},{5,2},{6,1},{7,0},{8,15},{9,14},{10,... | collective-permute-start | bytes 393224 | tf_op jit(solution)/shard_map/back_7/ppermute | solution.py:23
  70.8 8.0 %collective-permute-done.17.rest_5_ = bf16[32,2048]{1,0:T(8,128)(2,1)S(1)} collective-permute-done((bf16[32,2048]{1,0:T(8,128)(2,1)S(1)}, bf16[32,2048]{1,0:T(8,128)(2,1)S(1)}, u32[]{:S(2)}, u32[]{:S(2)}) %collective-permute-start.17) | collective-permute-done | bytes 131104 | tf_op jit(solution)/shard_map/back_3/ppermute | solution.py:23
  78.8 1.3 %collective-permute-done.26.rest_8_ = bf16[32,2048]{1,0:T(8,128)(2,1)S(1)} collective-permute-done((bf16[32,2048]{1,0:T(8,128)(2,1)S(1)}, bf16[32,2048]{1,0:T(8,128)(2,1)S(1)}, u32[]{:S(2)}, u32[]{:S(2)}) %collective-permute-start.26) | collective-permute-done | bytes 131104 | tf_op jit(solution)/shard_map/back_6/ppermute | solution.py:23
  80.1 2.8 %collective-permute-done.27.rest_9_ = bf16[32,2048]{1,0:T(8,128)(2,1)S(1)} collective-permute-done((bf16[32,2048]{1,0:T(8,128)(2,1)S(1)}, bf16[32,2048]{1,0:T(8,128)(2,1)S(1)}, u32[]{:S(2)}, u32[]{:S(2)}) %collective-permute-start.27) | collective-permute-done | bytes 131104 | tf_op jit(solution)/shard_map/back_7/ppermute | solution.py:23
  82.9 1.4 %combine.1 = bf16[1,128,2048]{2,1,0:T(8,128)(2,1)} custom-call(s32[2,128]{1,0:T(2,128)S(1)} %bitcast.12, f32[2,128]{1,0:T(2,128)S(1)} %bitcast.13, bf16[128,1024]{1,0:T(8,128)(2,1)S(1)} %get-tuple-element.55.rest_4_.rest_0_, bf16[128,1024]{1,0:T(8,128)(2,1)S(1)} %get-tuple-element.68.rest_1_, bf16[32,2048]{1,0:T(8,128)(2,1)S(1)} %get-tuple-element.73.rest_2_, ...), custom_call_target="tpu_custom_call" | custom-call | flops 268435456 | bytes 2097152 | tf_op jit(solution)/shard_map/combine/pallas_call | solution.py:292
  (38 shorter events, 0.4 us)
Async XLA Ops:
  2.1 7.7 %collective-permute-start = (bf16[3,128,256]{2,1,0:T(8,128)(2,1)}, bf16[3,128,256]{2,1,0:T(8,128)(2,1)S(1)}, u32[]{:S(2)}, u32[]{:S(2)}) collective-permute-start(bf16[3,128,256]{2,1,0:T(8,128)(2,1)} %get-tuple-element.48), channel_id=1, source_target_pairs={{0,8},{8,0},{16,24},{24,16},{1,9},{9,1},{17,25},{25,17},{2,10},{10... | collective-permute-start | bytes 589832 | tf_op jit(solution)/shard_map/qkv0_/ppermute | solution.py:23
  2.5 8.5 %collective-permute-start.1 = (bf16[3,128,256]{2,1,0:T(8,128)(2,1)}, bf16[3,128,256]{2,1,0:T(8,128)(2,1)S(1)}, u32[]{:S(2)}, u32[]{:S(2)}) collective-permute-start(bf16[3,128,256]{2,1,0:T(8,128)(2,1)} %get-tuple-element.49), channel_id=1, source_target_pairs={{0,16},{8,24},{16,0},{24,8},{1,17},{9,25},{17,1},{25,9},{2,18},{10... | collective-permute-start | bytes 589832 | tf_op jit(solution)/shard_map/qkv0_/ppermute | solution.py:23
  3.7 9.7 %collective-permute-start.2 = (bf16[3,128,256]{2,1,0:T(8,128)(2,1)}, bf16[3,128,256]{2,1,0:T(8,128)(2,1)S(1)}, u32[]{:S(2)}, u32[]{:S(2)}) collective-permute-start(bf16[3,128,256]{2,1,0:T(8,128)(2,1)} %get-tuple-element.50), channel_id=1, source_target_pairs={{0,24},{8,16},{16,8},{24,0},{1,25},{9,17},{17,9},{25,1},{2,26},{10... | collective-permute-start | bytes 589832 | tf_op jit(solution)/shard_map/qkv0_/ppermute | solution.py:23
  4.9 1.0 %copy-start.3 = (bf16[1,128,2048]{2,1,0:T(8,128)(2,1)S(1)}, bf16[1,128,2048]{2,1,0:T(8,128)(2,1)}, u32[]{:S(2)}) copy-start(bf16[1,128,2048]{2,1,0:T(8,128)(2,1)} %q_ref.3) | copy-start | bytes 1572868
  5.9 1.0 %copy-start.4 = (bf16[1,128,2048]{2,1,0:T(8,128)(2,1)S(1)}, bf16[1,128,2048]{2,1,0:T(8,128)(2,1)}, u32[]{:S(2)}) copy-start(bf16[1,128,2048]{2,1,0:T(8,128)(2,1)} %k_ref.3) | copy-start | bytes 1572868
  6.9 1.0 %copy-start.5 = (bf16[1,128,2048]{2,1,0:T(8,128)(2,1)S(1)}, bf16[1,128,2048]{2,1,0:T(8,128)(2,1)}, u32[]{:S(2)}) copy-start(bf16[1,128,2048]{2,1,0:T(8,128)(2,1)} %v_ref.3) | copy-start | bytes 1572868
  8.2 10.0 %collective-permute-start.6 = (bf16[3,128,256]{2,1,0:T(8,128)(2,1)S(1)}, bf16[3,128,256]{2,1,0:T(8,128)(2,1)S(1)}, u32[]{:S(2)}, u32[]{:S(2)}) collective-permute-start(bf16[3,128,256]{2,1,0:T(8,128)(2,1)S(1)} %get-tuple-element.57), channel_id=1, source_target_pairs={{0,8},{8,0},{16,24},{24,16},{1,9},{9,1},{17,25},{25,17},{2,10},{10... | collective-permute-start | bytes 589832 | tf_op jit(solution)/shard_map/qkv1_/ppermute | solution.py:23
  8.6 11.8 %collective-permute-start.7 = (bf16[3,128,256]{2,1,0:T(8,128)(2,1)S(1)}, bf16[3,128,256]{2,1,0:T(8,128)(2,1)S(1)}, u32[]{:S(2)}, u32[]{:S(2)}) collective-permute-start(bf16[3,128,256]{2,1,0:T(8,128)(2,1)S(1)} %get-tuple-element.58), channel_id=1, source_target_pairs={{0,16},{8,24},{16,0},{24,8},{1,17},{9,25},{17,1},{25,9},{2,18},{10... | collective-permute-start | bytes 589832 | tf_op jit(solution)/shard_map/qkv1_/ppermute | solution.py:23
  9.8 12.0 %collective-permute-start.8 = (bf16[3,128,256]{2,1,0:T(8,128)(2,1)S(1)}, bf16[3,128,256]{2,1,0:T(8,128)(2,1)S(1)}, u32[]{:S(2)}, u32[]{:S(2)}) collective-permute-start(bf16[3,128,256]{2,1,0:T(8,128)(2,1)S(1)} %get-tuple-element.59), channel_id=1, source_target_pairs={{0,24},{8,16},{16,8},{24,0},{1,25},{9,17},{17,9},{25,1},{2,26},{10... | collective-permute-start | bytes 589832 | tf_op jit(solution)/shard_map/qkv1_/ppermute | solution.py:23
  13.4 0.9 %copy-start.9 = (bf16[3,128,256]{2,1,0:T(8,128)(2,1)S(1)}, bf16[3,128,256]{2,1,0:T(8,128)(2,1)}, u32[]{:S(2)}) copy-start(bf16[3,128,256]{2,1,0:T(8,128)(2,1)} %get-tuple-element.47.rest_0_) | copy-start | bytes 589828
  17.7 7.6 %collective-permute-start.3 = (bf16[128,256]{1,0:T(8,128)(2,1)S(1)}, bf16[128,256]{1,0:T(8,128)(2,1)S(1)}, u32[]{:S(2)}, u32[]{:S(2)}) collective-permute-start(bf16[128,256]{1,0:T(8,128)(2,1)S(1)} %get-tuple-element.52), channel_id=1, source_target_pairs={{0,8},{8,0},{16,24},{24,16},{1,9},{9,1},{17,25},{25,17},{2,10},{10... | collective-permute-start | bytes 196616 | tf_op jit(solution)/shard_map/heads0_/ppermute | solution.py:23
  18.0 7.2 %collective-permute-start.4 = (bf16[128,256]{1,0:T(8,128)(2,1)S(1)}, bf16[128,256]{1,0:T(8,128)(2,1)S(1)}, u32[]{:S(2)}, u32[]{:S(2)}) collective-permute-start(bf16[128,256]{1,0:T(8,128)(2,1)S(1)} %get-tuple-element.53), channel_id=1, source_target_pairs={{0,16},{8,24},{16,0},{24,8},{1,17},{9,25},{17,1},{25,9},{2,18},{10... | collective-permute-start | bytes 196616 | tf_op jit(solution)/shard_map/heads0_/ppermute | solution.py:23
  18.2 7.0 %collective-permute-start.5 = (bf16[128,256]{1,0:T(8,128)(2,1)S(1)}, bf16[128,256]{1,0:T(8,128)(2,1)S(1)}, u32[]{:S(2)}, u32[]{:S(2)}) collective-permute-start(bf16[128,256]{1,0:T(8,128)(2,1)S(1)} %get-tuple-element.54), channel_id=1, source_target_pairs={{0,24},{8,16},{16,8},{24,0},{1,25},{9,17},{17,9},{25,1},{2,26},{10... | collective-permute-start | bytes 196616 | tf_op jit(solution)/shard_map/heads0_/ppermute | solution.py:23
  21.8 3.4 %copy-start.7 = (s32[1,128,2]{1,2,0:T(2,128)S(1)}, s32[1,128,2]{1,2,0:T(2,128)}, u32[]{:S(2)}) copy-start(s32[1,128,2]{1,2,0:T(2,128)} %param.13) | copy-start | bytes 3076
  21.8 26.1 %copy-start = (bf16[1,2048,768]{2,1,0:T(8,128)(2,1)S(1)}, bf16[1,2048,768]{2,1,0:T(8,128)(2,1)}, u32[]{:S(2)}) copy-start(bf16[1,2048,768]{2,1,0:T(8,128)(2,1)} %gate_ref.5) | copy-start | bytes 9437188
  21.8 26.1 %copy-start.1 = (bf16[1,2048,768]{2,1,0:T(8,128)(2,1)S(1)}, bf16[1,2048,768]{2,1,0:T(8,128)(2,1)}, u32[]{:S(2)}) copy-start(bf16[1,2048,768]{2,1,0:T(8,128)(2,1)} %up_ref.5) | copy-start | bytes 9437188
  21.8 26.1 %copy-start.2 = (bf16[1,768,2048]{2,1,0:T(8,128)(2,1)S(1)}, bf16[1,768,2048]{2,1,0:T(8,128)(2,1)}, u32[]{:S(2)}) copy-start(bf16[1,768,2048]{2,1,0:T(8,128)(2,1)} %down_ref.5) | copy-start | bytes 9437188
  21.8 26.1 %copy-start.6 = (f32[2048]{0:T(1024)S(1)}, f32[2048]{0:T(1024)}, u32[]{:S(2)}) copy-start(f32[2048]{0:T(1024)} %param.12) | copy-start | bytes 24580
  25.7 8.8 %collective-permute-start.9 = (bf16[128,256]{1,0:T(8,128)(2,1)S(1)}, bf16[128,256]{1,0:T(8,128)(2,1)S(1)}, u32[]{:S(2)}, u32[]{:S(2)}) collective-permute-start(bf16[128,256]{1,0:T(8,128)(2,1)S(1)} %get-tuple-element.65), channel_id=1, source_target_pairs={{0,8},{8,0},{16,24},{24,16},{1,9},{9,1},{17,25},{25,17},{2,10},{10... | collective-permute-start | bytes 196616 | tf_op jit(solution)/shard_map/heads1_/ppermute | solution.py:23
  26.1 8.4 %collective-permute-start.10 = (bf16[128,256]{1,0:T(8,128)(2,1)S(1)}, bf16[128,256]{1,0:T(8,128)(2,1)S(1)}, u32[]{:S(2)}, u32[]{:S(2)}) collective-permute-start(bf16[128,256]{1,0:T(8,128)(2,1)S(1)} %get-tuple-element.66), channel_id=1, source_target_pairs={{0,16},{8,24},{16,0},{24,8},{1,17},{9,25},{17,1},{25,9},{2,18},{10... | collective-permute-start | bytes 196616 | tf_op jit(solution)/shard_map/heads1_/ppermute | solution.py:23
  26.5 8.0 %collective-permute-start.11 = (bf16[128,256]{1,0:T(8,128)(2,1)S(1)}, bf16[128,256]{1,0:T(8,128)(2,1)S(1)}, u32[]{:S(2)}, u32[]{:S(2)}) collective-permute-start(bf16[128,256]{1,0:T(8,128)(2,1)S(1)} %get-tuple-element.67), channel_id=1, source_target_pairs={{0,24},{8,16},{16,8},{24,0},{1,25},{9,17},{17,9},{25,1},{2,26},{10... | collective-permute-start | bytes 196616 | tf_op jit(solution)/shard_map/heads1_/ppermute | solution.py:23
  28.4 13.4 %collective-permute-start.18 = (bf16[32,1024]{1,0:T(8,128)(2,1)S(1)}, bf16[32,1024]{1,0:T(8,128)(2,1)S(1)}, u32[]{:S(2)}, u32[]{:S(2)}) collective-permute-start(bf16[32,1024]{1,0:T(8,128)(2,1)S(1)} %get-tuple-element.77), channel_id=1, source_target_pairs={{0,4},{1,5},{2,6},{3,7},{4,0},{5,1},{6,2},{7,3},{8,12},{9,13},{10,... | collective-permute-start | bytes 196616 | tf_op jit(solution)/shard_map/rows0_4/ppermute | solution.py:23
  30.7 7.7 %collective-permute-start.20 = (bf16[32,1024]{1,0:T(8,128)(2,1)S(1)}, bf16[32,1024]{1,0:T(8,128)(2,1)S(1)}, u32[]{:S(2)}, u32[]{:S(2)}) collective-permute-start(bf16[32,1024]{1,0:T(8,128)(2,1)S(1)} %get-tuple-element.80), channel_id=1, source_target_pairs={{0,5},{1,4},{2,7},{3,6},{4,1},{5,0},{6,3},{7,2},{8,13},{9,12},{10,... | collective-permute-start | bytes 196616 | tf_op jit(solution)/shard_map/rows0_5/ppermute | solution.py:23
  35.1 15.9 %collective-permute-start.12 = (bf16[32,2048]{1,0:T(8,128)(2,1)S(1)}, bf16[32,2048]{1,0:T(8,128)(2,1)S(1)}, u32[]{:S(2)}, u32[]{:S(2)}) collective-permute-start(bf16[32,2048]{1,0:T(8,128)(2,1)S(1)} %get-tuple-element.70), channel_id=1, source_target_pairs={{0,1},{1,0},{2,3},{3,2},{4,5},{5,4},{6,7},{7,6},{8,9},{9,8},{10,11... | collective-permute-start | bytes 393224 | tf_op jit(solution)/shard_map/rows_1/ppermute | solution.py:23
  36.9 18.6 %collective-permute-start.13 = (bf16[32,2048]{1,0:T(8,128)(2,1)S(1)}, bf16[32,2048]{1,0:T(8,128)(2,1)S(1)}, u32[]{:S(2)}, u32[]{:S(2)}) collective-permute-start(bf16[32,2048]{1,0:T(8,128)(2,1)S(1)} %get-tuple-element.71), channel_id=1, source_target_pairs={{0,2},{1,3},{2,0},{3,1},{4,6},{5,7},{6,4},{7,5},{8,10},{9,11},{10,... | collective-permute-start | bytes 393224 | tf_op jit(solution)/shard_map/rows_2/ppermute | solution.py:23
  38.5 6.3 %collective-permute-start.21 = (bf16[32,1024]{1,0:T(8,128)(2,1)S(1)}, bf16[32,1024]{1,0:T(8,128)(2,1)S(1)}, u32[]{:S(2)}, u32[]{:S(2)}) collective-permute-start(bf16[32,1024]{1,0:T(8,128)(2,1)S(1)} %get-tuple-element.82), channel_id=1, source_target_pairs={{0,5},{1,4},{2,7},{3,6},{4,1},{5,0},{6,3},{7,2},{8,13},{9,12},{10,... | collective-permute-start | bytes 196616 | tf_op jit(solution)/shard_map/rows1_5/ppermute | solution.py:23
  41.8 4.9 %collective-permute-start.19 = (bf16[32,1024]{1,0:T(8,128)(2,1)S(1)}, bf16[32,1024]{1,0:T(8,128)(2,1)S(1)}, u32[]{:S(2)}, u32[]{:S(2)}) collective-permute-start(bf16[32,1024]{1,0:T(8,128)(2,1)S(1)} %get-tuple-element.79), channel_id=1, source_target_pairs={{0,4},{1,5},{2,6},{3,7},{4,0},{5,1},{6,2},{7,3},{8,12},{9,13},{10,... | collective-permute-start | bytes 196616 | tf_op jit(solution)/shard_map/rows1_4/ppermute | solution.py:23
  42.1 13.6 %collective-permute-start.14 = (bf16[32,2048]{1,0:T(8,128)(2,1)S(1)}, bf16[32,2048]{1,0:T(8,128)(2,1)S(1)}, u32[]{:S(2)}, u32[]{:S(2)}) collective-permute-start(bf16[32,2048]{1,0:T(8,128)(2,1)S(1)} %get-tuple-element.72), channel_id=1, source_target_pairs={{0,3},{1,2},{2,1},{3,0},{4,7},{5,6},{6,5},{7,4},{8,11},{9,10},{10,... | collective-permute-start | bytes 393224 | tf_op jit(solution)/shard_map/rows_3/ppermute | solution.py:23
  44.8 14.4 %collective-permute-start.24 = (bf16[32,2048]{1,0:T(8,128)(2,1)S(1)}, bf16[32,2048]{1,0:T(8,128)(2,1)S(1)}, u32[]{:S(2)}, u32[]{:S(2)}) collective-permute-start(bf16[32,2048]{1,0:T(8,128)(2,1)S(1)} %get-tuple-element.85), channel_id=1, source_target_pairs={{0,6},{1,7},{2,4},{3,5},{4,2},{5,3},{6,0},{7,1},{8,14},{9,15},{10,... | collective-permute-start | bytes 393224 | tf_op jit(solution)/shard_map/rows_6/ppermute | solution.py:23
  46.7 19.2 %collective-permute-start.25 = (bf16[32,2048]{1,0:T(8,128)(2,1)S(1)}, bf16[32,2048]{1,0:T(8,128)(2,1)S(1)}, u32[]{:S(2)}, u32[]{:S(2)}) collective-permute-start(bf16[32,2048]{1,0:T(8,128)(2,1)S(1)} %get-tuple-element.86), channel_id=1, source_target_pairs={{0,7},{1,6},{2,5},{3,4},{4,3},{5,2},{6,1},{7,0},{8,15},{9,14},{10,... | collective-permute-start | bytes 393224 | tf_op jit(solution)/shard_map/rows_7/ppermute | solution.py:23
  51.0 17.9 %collective-permute-start.22 = (bf16[32,2048]{1,0:T(8,128)(2,1)S(1)}, bf16[32,2048]{1,0:T(8,128)(2,1)S(1)}, u32[]{:S(2)}, u32[]{:S(2)}) collective-permute-start(bf16[32,2048]{1,0:T(8,128)(2,1)S(1)} %get-tuple-element.83), channel_id=1, source_target_pairs={{0,4},{1,5},{2,6},{3,7},{4,0},{5,1},{6,2},{7,3},{8,12},{9,13},{10,... | collective-permute-start | bytes 393224 | tf_op jit(solution)/shard_map/back_4/ppermute | solution.py:23
  55.5 14.1 %collective-permute-start.23 = (bf16[32,2048]{1,0:T(8,128)(2,1)S(1)}, bf16[32,2048]{1,0:T(8,128)(2,1)S(1)}, u32[]{:S(2)}, u32[]{:S(2)}) collective-permute-start(bf16[32,2048]{1,0:T(8,128)(2,1)S(1)} %get-tuple-element.84), channel_id=1, source_target_pairs={{0,5},{1,4},{2,7},{3,6},{4,1},{5,0},{6,3},{7,2},{8,13},{9,12},{10,... | collective-permute-start | bytes 393224 | tf_op jit(solution)/shard_map/back_5/ppermute | solution.py:23
  58.8 12.0 %collective-permute-start.15 = (bf16[32,2048]{1,0:T(8,128)(2,1)S(1)}, bf16[32,2048]{1,0:T(8,128)(2,1)S(1)}, u32[]{:S(2)}, u32[]{:S(2)}) collective-permute-start(bf16[32,2048]{1,0:T(8,128)(2,1)S(1)} %get-tuple-element.74), channel_id=1, source_target_pairs={{0,1},{1,0},{2,3},{3,2},{4,5},{5,4},{6,7},{7,6},{8,9},{9,8},{10,11... | collective-permute-start | bytes 393224 | tf_op jit(solution)/shard_map/back_1/ppermute | solution.py:23
  59.2 11.6 %collective-permute-start.16 = (bf16[32,2048]{1,0:T(8,128)(2,1)S(1)}, bf16[32,2048]{1,0:T(8,128)(2,1)S(1)}, u32[]{:S(2)}, u32[]{:S(2)}) collective-permute-start(bf16[32,2048]{1,0:T(8,128)(2,1)S(1)} %get-tuple-element.75), channel_id=1, source_target_pairs={{0,2},{1,3},{2,0},{3,1},{4,6},{5,7},{6,4},{7,5},{8,10},{9,11},{10,... | collective-permute-start | bytes 393224 | tf_op jit(solution)/shard_map/back_2/ppermute | solution.py:23
  65.9 17.0 %copy-start.8 = (f32[1,128,2]{1,2,0:T(2,128)S(1)}, f32[1,128,2]{1,2,0:T(2,128)}, u32[]{:S(2)}) copy-start(f32[1,128,2]{1,2,0:T(2,128)} %param.14) | copy-start | bytes 3076
  65.9 12.9 %collective-permute-start.17 = (bf16[32,2048]{1,0:T(8,128)(2,1)S(1)}, bf16[32,2048]{1,0:T(8,128)(2,1)S(1)}, u32[]{:S(2)}, u32[]{:S(2)}) collective-permute-start(bf16[32,2048]{1,0:T(8,128)(2,1)S(1)} %get-tuple-element.76), channel_id=1, source_target_pairs={{0,3},{1,2},{2,1},{3,0},{4,7},{5,6},{6,5},{7,4},{8,11},{9,10},{10,... | collective-permute-start | bytes 393224 | tf_op jit(solution)/shard_map/back_3/ppermute | solution.py:23
  68.9 11.1 %collective-permute-start.26 = (bf16[32,2048]{1,0:T(8,128)(2,1)S(1)}, bf16[32,2048]{1,0:T(8,128)(2,1)S(1)}, u32[]{:S(2)}, u32[]{:S(2)}) collective-permute-start(bf16[32,2048]{1,0:T(8,128)(2,1)S(1)} %get-tuple-element.87), channel_id=1, source_target_pairs={{0,6},{1,7},{2,4},{3,5},{4,2},{5,3},{6,0},{7,1},{8,14},{9,15},{10,... | collective-permute-start | bytes 393224 | tf_op jit(solution)/shard_map/back_6/ppermute | solution.py:23
  69.5 13.3 %collective-permute-start.27 = (bf16[32,2048]{1,0:T(8,128)(2,1)S(1)}, bf16[32,2048]{1,0:T(8,128)(2,1)S(1)}, u32[]{:S(2)}, u32[]{:S(2)}) collective-permute-start(bf16[32,2048]{1,0:T(8,128)(2,1)S(1)} %get-tuple-element.88), channel_id=1, source_target_pairs={{0,7},{1,6},{2,5},{3,4},{4,3},{5,2},{6,1},{7,0},{8,15},{9,14},{10,... | collective-permute-start | bytes 393224 | tf_op jit(solution)/shard_map/back_7/ppermute | solution.py:23

commit v3 on v2

v3 whole, which is shorter than its diff:
```python
import functools
import math

import jax
import jax.numpy as jnp
from jax import lax
from jax.experimental import pallas as pl
from jax.experimental.pallas import tpu as pltpu
from jax.sharding import PartitionSpec as P

HEADS = 16
CAP = 32
CHUNKS = 2
PACK_MIB = 56
F32 = jnp.float32
BF16 = jnp.bfloat16
HBM = pl.BlockSpec(memory_space=pltpu.HBM)
VMEM = pl.BlockSpec(memory_space=pltpu.VMEM)


def swap(x, axis, distance):
    size = lax.axis_size(axis)
    return lax.ppermute(x, axis, [(i, i ^ distance) for i in range(size)])


def params(mib):
    return pltpu.CompilerParams(vmem_limit_bytes=mib << 20)


def cost(flops, moved):
    return pl.CostEstimate(flops=flops, bytes_accessed=moved, transcendentals=0)


def pack_kernel(groups, chunks, c, width, q_ref, k_ref, v_ref, *rest):
    outs, (in_sems, *staged) = rest[:groups], rest[groups:]
    me = lax.axis_index("seq")
    inward, outward = [], []
    for distance in [*range(1, groups), 0]:
        column = pl.multiple_of(((me ^ distance) * chunks + c) * width, 128)
        for i, ref in enumerate((q_ref, k_ref, v_ref)):
            n = len(inward)
            target = staged[0].at[n] if staged else outs[distance].at[i]
            inward.append(
                pltpu.make_async_copy(ref.at[0, :, pl.ds(column, width)], target, in_sems.at[n])
            )
            if staged:
                outward.append(
                    pltpu.make_async_copy(target, outs[distance].at[i], staged[1].at[n])
                )
    for copy in inward:
        copy.start()
    for n, copy in enumerate(inward):
        copy.wait()
        if staged:
            outward[n].start()
    for out in outward:
        out.wait()


def pack(groups, chunks, c, width, q, k, v):
    tokens = q.shape[1]
    count = 3 * groups
    staged = [pltpu.VMEM((count, tokens, width), BF16), pltpu.SemaphoreType.DMA((count,))]
    return pl.pallas_call(
        functools.partial(pack_kernel, groups, chunks, c, width),
        out_shape=[jax.ShapeDtypeStruct((3, tokens, width), BF16)] * groups,
        in_specs=[HBM] * 3,
        out_specs=[HBM if c == 0 else VMEM] * groups,
        scratch_shapes=[pltpu.SemaphoreType.DMA((count,))] + (staged if c == 0 else []),
        compiler_params=params(PACK_MIB if c == 0 else 8),
        cost_estimate=cost(0, 4 * count * tokens * width),
        name="pack_heads",
    )(q, k, v)


def attend_kernel(groups, width, head_size, *rest):
    blocks, outs = rest[:groups], rest[groups:]
    scale = head_size**-0.5 * math.log2(math.e)
    step = min(groups, 4)
    for head in range(width // head_size):
        lanes = slice(head * head_size, (head + 1) * head_size)
        keys = jnp.concatenate([block[1, :, lanes] for block in blocks], axis=0)
        values = jnp.concatenate([block[2, :, lanes] for block in blocks], axis=0)
        for first in range(0, groups, step):
            members = range(first, min(first + step, groups))
            scores = [
                lax.dot_general(
                    blocks[b][0, :, lanes], keys, (((1,), (1,)), ((), ())),
                    preferred_element_type=F32,
                )
                for b in members
            ]
            peaks = [jnp.max(part, axis=-1, keepdims=True) for part in scores]
            exponentials = [jnp.exp2((s - p) * scale) for s, p in zip(scores, peaks)]
            totals = [jnp.sum(part, axis=-1, keepdims=True) for part in exponentials]
            weighted = [
                jnp.dot(part.astype(BF16), values, preferred_element_type=F32)
                for part in exponentials
            ]
            for b, part, total in zip(members, weighted, totals):
                outs[b][:, lanes] = (part * (1.0 / total)).astype(BF16)


def attend(width, head_size, blocks):
    groups, tokens = len(blocks), blocks[0].shape[1]
    total = groups * tokens
    return pl.pallas_call(
        functools.partial(attend_kernel, groups, width, head_size),
        out_shape=[jax.ShapeDtypeStruct((tokens, width), BF16)] * groups,
        in_specs=[VMEM] * groups,
        out_specs=[VMEM] * groups,
        compiler_params=params(32),
        cost_estimate=cost(160 * total * total * width, 80 * total * width),
        name="attend",
    )(*blocks)


def slot_matrix(experts, ids):
    tokens = ids.shape[1]
    me = lax.axis_index("expert")
    named = lax.broadcasted_iota(jnp.int32, (experts, tokens), 0) ^ me
    matches = jnp.where((ids[0:1, :] == named) | (ids[1:2, :] == named), 1.0, 0.0)
    earlier = jnp.where(
        lax.broadcasted_iota(jnp.int32, (tokens, tokens), 0)
        < lax.broadcasted_iota(jnp.int32, (tokens, tokens), 1),
        1.0,
        0.0,
    )
    rank = jnp.dot(matches.astype(BF16), earlier.astype(BF16), preferred_element_type=F32)
    rank = jnp.where(matches > 0.0, rank, -1.0).astype(jnp.int32)
    slots = lax.broadcasted_iota(jnp.int32, (CAP, tokens), 0)
    return [slots == rank[d : d + 1, :] for d in range(experts)], named


def select_kernel(groups, experts, width, earlier, last, ids_ref, *rest):
    blocks, before = rest[:groups], rest[groups : groups + earlier]
    half, middle = experts // 2, experts // 2 + experts // 4
    count = experts if last else middle - half
    outs = rest[groups + earlier : groups + earlier + count]
    kept, sems = rest[groups + earlier + count :]
    me = lax.axis_index("seq")
    copies = []
    for d in range(groups):
        column = pl.multiple_of((me ^ d) * width, 128)
        copies.append(
            pltpu.make_async_copy(blocks[d], kept.at[:, pl.ds(column, width)], sems.at[d])
        )
    for copy in copies:
        copy.start()
    hits, _ = slot_matrix(experts, ids_ref[...])
    chosen = [jnp.where(h, 1.0, 0.0).astype(BF16) for h in hits]
    for copy in copies:
        copy.wait()

    def pick(distances, rows, first):
        picked = jnp.dot(
            jnp.concatenate([chosen[d] for d in distances], axis=0),
            rows,
            preferred_element_type=F32,
        ).astype(BF16)
        for i in range(len(distances)):
            outs[first + i][...] = picked[i * CAP : (i + 1) * CAP]

    pick(range(half, middle), kept[...], 0)
    if last:
        parts = [ref[...] for ref in before] + [kept[...]]
        full = jnp.concatenate(parts, axis=1) if earlier else parts[0]
        pick([*range(middle, experts), *range(half)], full, middle - half)


def select(groups, experts, ids, blocks, before, last):
    tokens, width = blocks[0].shape
    part = groups * width
    whole = part * (len(before) + 1)
    quarter = experts // 4
    shapes = [(CAP, part)] * quarter
    if last:
        shapes += [(CAP, whole)] * (experts - quarter)
    shapes.append((tokens, part))
    return pl.pallas_call(
        functools.partial(select_kernel, groups, experts, width, len(before), last),
        out_shape=[jax.ShapeDtypeStruct(shape, BF16) for shape in shapes],
        in_specs=[VMEM] + [HBM] * groups + [VMEM] * len(before),
        out_specs=[VMEM] * len(shapes),
        scratch_shapes=[pltpu.SemaphoreType.DMA((groups,))],
        compiler_params=params(16),
        cost_estimate=cost(2 * experts * CAP * tokens * part, 8 * tokens * part),
        name="select_rows",
    )(ids, *blocks, *before)


def experts_kernel(groups, chunks, width, held, gain_ref, gate_ref, up_ref, down_ref, *rest):
    inputs, count = sum(held), len(held)
    blocks, outs = rest[:inputs], rest[inputs : inputs + count]
    rows_ref, hidden_ref = rest[inputs + count :]
    used = 0
    for i in range(count):
        mine = [blocks[k][...] for k in range(used, used + held[i])]
        used += held[i]
        row = jnp.concatenate(mine, axis=1) if len(mine) > 1 else mine[0]
        parts = []
        for g in range(groups):
            for c in range(chunks):
                first = (c * groups + g) * width
                parts.append(row[:, first : first + width].astype(F32))
        row = jnp.concatenate(parts, axis=1)
        scale = lax.rsqrt(jnp.mean(row * row, axis=-1, keepdims=True) + 1e-06)
        rows_ref[i * CAP : (i + 1) * CAP, :] = (row * scale * gain_ref[...]).astype(BF16)
    units, features = down_ref.shape[1:]
    tile = 256 if units % 256 == 0 else 128
    for first in range(0, units, tile):
        lanes = slice(first, first + tile)
        gate = jnp.dot(rows_ref[...], gate_ref[0, :, lanes], preferred_element_type=F32)
        up = jnp.dot(rows_ref[...], up_ref[0, :, lanes], preferred_element_type=F32)
        hidden_ref[:, lanes] = (gate / (1.0 + jnp.exp(-gate)) * up).astype(BF16)
    for first in range(0, features, 512):
        lanes = slice(first, first + 512)
        made = jnp.dot(hidden_ref[...], down_ref[0, :, lanes], preferred_element_type=F32)
        for i in range(count):
            outs[i][:, lanes] = made[i * CAP : (i + 1) * CAP].astype(BF16)


def run_experts(groups, chunks, width, gain, w_gate, w_up, w_down, blocks):
    held = tuple(len(block) for block in blocks)
    count = len(held)
    features, units = w_gate.shape[1:]
    flat = [part for block in blocks for part in block]
    return pl.pallas_call(
        functools.partial(experts_kernel, groups, chunks, width, held),
        out_shape=[jax.ShapeDtypeStruct((CAP, features), BF16)] * count,
        in_specs=[VMEM] * (4 + len(flat)),
        out_specs=[VMEM] * count,
        scratch_shapes=[
            pltpu.VMEM((count * CAP, features), BF16),
            pltpu.VMEM((count * CAP, units), BF16),
        ],
        compiler_params=params(24),
        cost_estimate=cost(count * CAP * features, features * units // 100),
        name="experts",
    )(gain, w_gate, w_up, w_down, *flat)


def spread_kernel(experts, ids_ref, gates_ref, coarse_ref, fine_ref):
    ids, gates = ids_ref[...], gates_ref[...]
    hits, named = slot_matrix(experts, ids)
    weight = jnp.where(ids[0:1, :] == named, gates[0:1, :], 0.0) + jnp.where(
        ids[1:2, :] == named, gates[1:2, :], 0.0
    )
    coarse = weight.astype(BF16).astype(F32)
    for ref, part in ((coarse_ref, coarse), (fine_ref, weight - coarse)):
        slots = [jnp.where(hits[d], part[d : d + 1, :], 0.0) for d in range(experts)]
        ref[...] = jnp.concatenate(slots, axis=0).T.astype(BF16)


def spread(experts, ids, gates):
    tokens = ids.shape[1]
    return pl.pallas_call(
        functools.partial(spread_kernel, experts),
        out_shape=[jax.ShapeDtypeStruct((tokens, experts * CAP), BF16)] * 2,
        in_specs=[VMEM] * 2,
        out_specs=[VMEM] * 2,
        compiler_params=params(16),
        cost_estimate=cost(0, 4 * tokens * experts * CAP),
        name="spread_gates",
    )(ids, gates)


def combine_kernel(groups, experts, chunks, coarse_ref, fine_ref, *rest):
    kept, blocks = rest[:chunks], rest[chunks : chunks + experts]
    out_ref, made_ref, sems = rest[chunks + experts :]
    width = kept[0].shape[1] // groups
    copies = []
    for g in range(groups):
        span = slice(g * chunks * width, (g + 1) * chunks * width)
        rows = jnp.concatenate([block[:, span] for block in blocks], axis=0)
        total = jnp.concatenate(
            [ref[:, g * width : (g + 1) * width] for ref in kept], axis=1
        ).astype(F32)
        total += jnp.dot(coarse_ref[...], rows, preferred_element_type=F32)
        total += jnp.dot(fine_ref[...], rows, preferred_element_type=F32)
        made_ref[:, span] = total.astype(BF16)
        copies.append(
            pltpu.make_async_copy(made_ref.at[:, span], out_ref.at[0, :, span], sems.at[g])
        )
        copies[-1].start()
    for copy in copies:
        copy.wait()


def combine(groups, weights, kept, blocks):
    tokens, features = weights[0].shape[0], blocks[0].shape[1]
    experts = len(blocks)
    return pl.pallas_call(
        functools.partial(combine_kernel, groups, experts, len(kept)),
        out_shape=jax.ShapeDtypeStruct((1, tokens, features), BF16),
        in_specs=[VMEM] * (2 + len(kept) + experts),
        out_specs=HBM,
        scratch_shapes=[
            pltpu.VMEM((tokens, features), BF16),
            pltpu.SemaphoreType.DMA((groups,)),
        ],
        compiler_params=params(24),
        cost_estimate=cost(4 * experts * CAP * tokens * features, 8 * tokens * features),
        name="combine",
    )(*weights, *kept, *blocks)


def after(values, *earlier):
    return lax.optimization_barrier((values, earlier))[0]


def local(
    query_rows, key_rows, value_rows, norm_gain, expert_ids, gate_weights, w_gate, w_up, w_down
):
    features = query_rows.shape[2]
    head_size = features // HEADS
    groups, experts = lax.axis_size("seq"), lax.axis_size("expert")
    per_group = HEADS // groups
    group_width = per_group * head_size
    chunks = CHUNKS if per_group % CHUNKS == 0 else 1
    width = group_width // chunks
    ids, gates = expert_ids[0].T, gate_weights[0].T
    gain = norm_gain.reshape(1, features)
    half = experts // 2
    middle = half + experts // 4

    def exchange(blocks, name):
        with jax.named_scope(name):
            return [blocks[0]] + [swap(blocks[d], "seq", d) for d in range(1, groups)]

    def send(block, distance, name):
        with jax.named_scope(f"{name}{distance}"):
            return swap(block, "expert", distance)

    received = [
        exchange(pack(groups, chunks, c, width, query_rows, key_rows, value_rows), f"qkv{c}_")
        for c in range(chunks)
    ]
    weights = spread(experts, ids, gates)
    received[-1][0] = after(received[-1][0], weights)
    heads = [attend(width, head_size, received[c]) for c in range(chunks)]
    kept, arrived = [], [[] for _ in range(experts)]
    for c in range(chunks):
        last = c == chunks - 1
        out = heads[c] if c == 0 else after(heads[c], kept[-1])
        *rows, own = select(groups, experts, ids, exchange(out, f"heads{c}_"), kept, last)
        kept.append(own)
        for d in range(half, middle):
            row = rows[d - half] if c == 0 else after(rows[d - half], arrived[d][-1])
            arrived[d].append(send(row, d, f"rows{c}_"))
    whole = rows[middle - half :]
    for d in range(middle, experts):
        arrived[d].append(send(whole[d - middle], d, "rows_"))
    whole = whole[experts - middle :]
    arrived[0].append(whole[0])
    for d in range(1, half):
        arrived[d].append(send(whole[d], d, "rows_"))
    returned = [None] * experts
    for members in (range(half, middle), range(middle, experts), range(half)):
        produced = run_experts(
            groups, chunks, width, gain, w_gate, w_up, w_down,
            [arrived[d] for d in members],
        )
        for d, block in zip(members, produced):
            returned[d] = block if d == 0 else send(block, d, "back_")
    return combine(groups, weights, kept, returned)


def solution(mesh):
    rows = P("expert", "seq", None)
    weights = P("expert", None, None)
    return jax.shard_map(
        local,
        mesh=mesh,
        in_specs=(rows, rows, rows, P(), rows, rows, weights, weights, weights),
        out_specs=rows,
        check_vma=False,
    )
```

time: 84.6 us -> 81.8 us (0.967)
  waiting for transfers between devices: 24.4 us -> 34.9 us
  Pallas kernels: 20.8 us -> 12 us
  starting transfers between devices: 34.8 us -> 29.9 us
    ppermute x28, waiting for transfers between devices: 24.4 us -> 34.9 us  [swap(): return lax.ppermute(x, axis, [(i, i ^ distance) for i in range(size)])]
    ppermute x28, starting transfers between devices: 34.8 us -> 29.9 us  [swap(): return lax.ppermute(x, axis, [(i, i ^ distance) for i in range(size)])]
    pallas_call x2, Pallas kernels: 6.72 us -> 1.92 us  [attend(): pl.pallas_call(functools.partial(attend_kernel, groups, width, head_size)...]
    pallas_call x4 -> x5, Pallas kernels: 10.7 us -> 6.81 us  [the longest x3 5.42 us: run_experts(): pl.pallas_call(functools.partial(experts_kernel, groups, chunks, width, h...]
  transfers between devices with their start and end apart: 28 -> 28, of which waited for: 9 -> 13; matrix products, arithmetic and copies ran while one was open for 0% -> 0% of each run, Pallas kernels for 20% -> 10%
where the time goes in v3:
time: 81.8 us; the launch traced here: 81 us
  waiting for transfers between devices  34.9 us (43%)
  starting transfers between devices  29.9 us (37%)
  Pallas kernels  12 us (15%)
  local copies, waits for them, and re-layouts  4.07 us (5%)
    ppermute x28, waiting for transfers between devices, swap(): return lax.ppermute(x, axis, [(i, i ^ distance) for i in range(size)])  34.9 us
    ppermute x28, starting transfers between devices, swap(): return lax.ppermute(x, axis, [(i, i ^ distance) for i in range(size)])  29.9 us
    pallas_call x3, Pallas kernels, run_experts(): pl.pallas_call(functools.partial(experts_kernel, groups, chunks, width, h...  5.42 us
    unnamed x20, local copies, waits for them, and re-layouts  4.07 us
    pallas_call x2, Pallas kernels, pack(): pl.pallas_call(functools.partial(pack_kernel, groups, chunks, c, width),...  2.28 us
    pallas_call x2, Pallas kernels, attend(): pl.pallas_call(functools.partial(attend_kernel, groups, width, head_size)...  1.92 us
  transfers between devices with their start and end apart: 28, of which 13 were waited for; matrix products, arithmetic and copies ran while one was open for 0% of the time, Pallas kernels for 10%

profile of v3, /device:TPU:11, one launch (start us, length us, event | category | flops | bytes accessed | tf_op | source)
XLA Modules:
  0.0 81.0 jit_solution(8777638727802277525)
XLA Ops:
  0.0 2.0 %pack_heads.2 = (bf16[3,128,256]{2,1,0:T(8,128)(2,1)}, bf16[3,128,256]{2,1,0:T(8,128)(2,1)}, bf16[3,128,256]{2,1,0:T(8,128)(2,1)}, bf16[3,128,256]{2,1,0:T(8,128)(2,1)}) custom-call(bf16[1,128,2048]{2,1,0:T(8,128)(2,1)} %q_ref.3, bf16[1,128,2048]{2,1,0:T(8,128)(2,1)} %k_ref.3, bf16[1,128,2048]{2,1,0:T(8,128)(2,1)} %v_ref.3), custom_call_target="tpu_custom_call" | custom-call | bytes 1572864 | tf_op jit(solution)/shard_map/pack_heads/pallas_call | solution.py:64
  2.0 0.3 collective-permute-start
  2.4 1.2 %collective-permute-start.1 = (bf16[3,128,256]{2,1,0:T(8,128)(2,1)}, bf16[3,128,256]{2,1,0:T(8,128)(2,1)S(1)}, u32[]{:S(2)}, u32[]{:S(2)}) collective-permute-start(bf16[3,128,256]{2,1,0:T(8,128)(2,1)} %get-tuple-element.54), channel_id=1, source_target_pairs={{0,16},{8,24},{16,0},{24,8},{1,17},{9,25},{17,1},{25,9},{2,18},{10... | collective-permute-start | bytes 589832 | tf_op jit(solution)/shard_map/qkv0_/ppermute | solution.py:23
  3.6 1.2 %collective-permute-start.2 = (bf16[3,128,256]{2,1,0:T(8,128)(2,1)}, bf16[3,128,256]{2,1,0:T(8,128)(2,1)S(1)}, u32[]{:S(2)}, u32[]{:S(2)}) collective-permute-start(bf16[3,128,256]{2,1,0:T(8,128)(2,1)} %get-tuple-element.55), channel_id=1, source_target_pairs={{0,24},{8,16},{16,8},{24,0},{1,25},{9,17},{17,9},{25,1},{2,26},{10... | collective-permute-start | bytes 589832 | tf_op jit(solution)/shard_map/qkv0_/ppermute | solution.py:23
  4.8 1.0 %copy-done.3 = bf16[1,128,2048]{2,1,0:T(8,128)(2,1)S(1)} copy-done((bf16[1,128,2048]{2,1,0:T(8,128)(2,1)S(1)}, bf16[1,128,2048]{2,1,0:T(8,128)(2,1)}, u32[]{:S(2)}) %copy-start.3) | copy-done | bytes 524312
  5.8 1.0 %copy-done.4 = bf16[1,128,2048]{2,1,0:T(8,128)(2,1)S(1)} copy-done((bf16[1,128,2048]{2,1,0:T(8,128)(2,1)S(1)}, bf16[1,128,2048]{2,1,0:T(8,128)(2,1)}, u32[]{:S(2)}) %copy-start.4) | copy-done | bytes 524312
  6.8 1.0 %copy-done.5 = bf16[1,128,2048]{2,1,0:T(8,128)(2,1)S(1)} copy-done((bf16[1,128,2048]{2,1,0:T(8,128)(2,1)S(1)}, bf16[1,128,2048]{2,1,0:T(8,128)(2,1)}, u32[]{:S(2)}) %copy-start.5) | copy-done | bytes 524312
  7.9 0.2 pack_heads.3
  8.1 0.3 collective-permute-start.6
  8.5 1.2 %collective-permute-start.7 = (bf16[3,128,256]{2,1,0:T(8,128)(2,1)S(1)}, bf16[3,128,256]{2,1,0:T(8,128)(2,1)S(1)}, u32[]{:S(2)}, u32[]{:S(2)}) collective-permute-start(bf16[3,128,256]{2,1,0:T(8,128)(2,1)S(1)} %get-tuple-element.64), channel_id=1, source_target_pairs={{0,16},{8,24},{16,0},{24,8},{1,17},{9,25},{17,1},{25,9},{2,18},{10... | collective-permute-start | bytes 589832 | tf_op jit(solution)/shard_map/qkv1_/ppermute | solution.py:23
  10.0 1.2 %collective-permute-start.8 = (bf16[3,128,256]{2,1,0:T(8,128)(2,1)S(1)}, bf16[3,128,256]{2,1,0:T(8,128)(2,1)S(1)}, u32[]{:S(2)}, u32[]{:S(2)}) collective-permute-start(bf16[3,128,256]{2,1,0:T(8,128)(2,1)S(1)} %get-tuple-element.65), channel_id=1, source_target_pairs={{0,24},{8,16},{16,8},{24,0},{1,25},{9,17},{17,9},{25,1},{2,26},{10... | collective-permute-start | bytes 589832 | tf_op jit(solution)/shard_map/qkv1_/ppermute | solution.py:23
  11.2 2.1 %collective-permute-done.2.rest_3_ = bf16[3,128,256]{2,1,0:T(8,128)(2,1)S(1)} collective-permute-done((bf16[3,128,256]{2,1,0:T(8,128)(2,1)}, bf16[3,128,256]{2,1,0:T(8,128)(2,1)S(1)}, u32[]{:S(2)}, u32[]{:S(2)}) %collective-permute-start.2) | collective-permute-done | bytes 196640 | tf_op jit(solution)/shard_map/qkv0_/ppermute | solution.py:23
  13.3 0.9 %copy-done.9 = bf16[3,128,256]{2,1,0:T(8,128)(2,1)S(1)} copy-done((bf16[3,128,256]{2,1,0:T(8,128)(2,1)S(1)}, bf16[3,128,256]{2,1,0:T(8,128)(2,1)}, u32[]{:S(2)}) %copy-start.9) | copy-done | bytes 196632
  14.2 1.0 %attend.2 = (bf16[128,256]{1,0:T(8,128)(2,1)S(1)}, bf16[128,256]{1,0:T(8,128)(2,1)S(1)}, bf16[128,256]{1,0:T(8,128)(2,1)S(1)}, bf16[128,256]{1,0:T(8,128)(2,1)S(1)}) custom-call(bf16[3,128,256]{2,1,0:T(8,128)(2,1)S(1)} %copy-done.9, bf16[3,128,256]{2,1,0:T(8,128)(2,1)S(1)} %collective-permute-done.rest_1_, ...), custom_call_target="tpu_custom_call" | custom-call | flops 10737418240 | bytes 10485760 | tf_op jit(solution)/shard_map/attend/pallas_call | solution.py:107
  15.2 0.3 collective-permute-start.3
  15.7 0.8 %collective-permute-done.6.rest_1_ = bf16[3,128,256]{2,1,0:T(8,128)(2,1)S(1)} collective-permute-done((bf16[3,128,256]{2,1,0:T(8,128)(2,1)S(1)}, bf16[3,128,256]{2,1,0:T(8,128)(2,1)S(1)}, u32[]{:S(2)}, u32[]{:S(2)}) %collective-permute-start.6) | collective-permute-done | bytes 196640 | tf_op jit(solution)/shard_map/qkv1_/ppermute | solution.py:23
  16.6 1.4 %collective-permute-start.5 = (bf16[128,256]{1,0:T(8,128)(2,1)S(1)}, bf16[128,256]{1,0:T(8,128)(2,1)S(1)}, u32[]{:S(2)}, u32[]{:S(2)}) collective-permute-start(bf16[128,256]{1,0:T(8,128)(2,1)S(1)} %get-tuple-element.59), channel_id=1, source_target_pairs={{0,24},{8,16},{16,8},{24,0},{1,25},{9,17},{17,9},{25,1},{2,26},{10... | collective-permute-start | bytes 196616 | tf_op jit(solution)/shard_map/heads0_/ppermute | solution.py:23
  18.0 1.2 %collective-permute-done.7.rest_2_ = bf16[3,128,256]{2,1,0:T(8,128)(2,1)S(1)} collective-permute-done((bf16[3,128,256]{2,1,0:T(8,128)(2,1)S(1)}, bf16[3,128,256]{2,1,0:T(8,128)(2,1)S(1)}, u32[]{:S(2)}, u32[]{:S(2)}) %collective-permute-start.7) | collective-permute-done | bytes 196640 | tf_op jit(solution)/shard_map/qkv1_/ppermute | solution.py:23
  19.2 2.6 %collective-permute-done.8.rest_3_ = bf16[3,128,256]{2,1,0:T(8,128)(2,1)S(1)} collective-permute-done((bf16[3,128,256]{2,1,0:T(8,128)(2,1)S(1)}, bf16[3,128,256]{2,1,0:T(8,128)(2,1)S(1)}, u32[]{:S(2)}, u32[]{:S(2)}) %collective-permute-start.8) | collective-permute-done | bytes 196640 | tf_op jit(solution)/shard_map/qkv1_/ppermute | solution.py:23
  21.8 1.0 %attend.3 = (bf16[128,256]{1,0:T(8,128)(2,1)S(1)}, bf16[128,256]{1,0:T(8,128)(2,1)S(1)}, bf16[128,256]{1,0:T(8,128)(2,1)S(1)}, bf16[128,256]{1,0:T(8,128)(2,1)S(1)}) custom-call(bf16[3,128,256]{2,1,0:T(8,128)(2,1)S(1)} %get-tuple-element.62.rest_0_, bf16[3,128,256]{2,1,0:T(8,128)(2,1)S(1)} %collective-permute-done.6.rest_1_, ...), custom_call_target="tpu_custom_call" | custom-call | flops 10737418240 | bytes 10485760 | tf_op jit(solution)/shard_map/attend/pallas_call | solution.py:107
  22.8 1.8 %collective-permute-done.4.rest_2_ = bf16[128,256]{1,0:T(8,128)(2,1)S(1)} collective-permute-done((bf16[128,256]{1,0:T(8,128)(2,1)S(1)}, bf16[128,256]{1,0:T(8,128)(2,1)S(1)}, u32[]{:S(2)}, u32[]{:S(2)}) %collective-permute-start.4) | collective-permute-done | bytes 65568 | tf_op jit(solution)/shard_map/heads0_/ppermute | solution.py:23
  24.5 0.4 select_rows.2
  24.9 0.7 collective-permute-start.9
  25.6 0.5 collective-permute-start.10
  26.1 1.6 %collective-permute-start.11 = (bf16[128,256]{1,0:T(8,128)(2,1)S(1)}, bf16[128,256]{1,0:T(8,128)(2,1)S(1)}, u32[]{:S(2)}, u32[]{:S(2)}) collective-permute-start(bf16[128,256]{1,0:T(8,128)(2,1)S(1)} %get-tuple-element.73), channel_id=1, source_target_pairs={{0,24},{8,16},{16,8},{24,0},{1,25},{9,17},{17,9},{25,1},{2,26},{10... | collective-permute-start | bytes 196616 | tf_op jit(solution)/shard_map/heads1_/ppermute | solution.py:23
  27.7 2.3 %collective-permute-start.18 = (bf16[32,1024]{1,0:T(8,128)(2,1)S(1)}, bf16[32,1024]{1,0:T(8,128)(2,1)S(1)}, u32[]{:S(2)}, u32[]{:S(2)}) collective-permute-start(bf16[32,1024]{1,0:T(8,128)(2,1)S(1)} %get-tuple-element.83), channel_id=1, source_target_pairs={{0,4},{1,5},{2,6},{3,7},{4,0},{5,1},{6,2},{7,3},{8,12},{9,13},{10,... | collective-permute-start | bytes 196616 | tf_op jit(solution)/shard_map/rows0_4/ppermute | solution.py:23
  30.0 2.7 %collective-permute-start.20 = (bf16[32,1024]{1,0:T(8,128)(2,1)S(1)}, bf16[32,1024]{1,0:T(8,128)(2,1)S(1)}, u32[]{:S(2)}, u32[]{:S(2)}) collective-permute-start(bf16[32,1024]{1,0:T(8,128)(2,1)S(1)} %get-tuple-element.86), channel_id=1, source_target_pairs={{0,5},{1,4},{2,7},{3,6},{4,1},{5,0},{6,3},{7,2},{8,13},{9,12},{10,... | collective-permute-start | bytes 196616 | tf_op jit(solution)/shard_map/rows0_5/ppermute | solution.py:23
  32.7 0.6 select_rows.3
  33.3 1.7 %collective-permute-start.12 = (bf16[32,2048]{1,0:T(8,128)(2,1)S(1)}, bf16[32,2048]{1,0:T(8,128)(2,1)S(1)}, u32[]{:S(2)}, u32[]{:S(2)}) collective-permute-start(bf16[32,2048]{1,0:T(8,128)(2,1)S(1)} %get-tuple-element.76), channel_id=1, source_target_pairs={{0,1},{1,0},{2,3},{3,2},{4,5},{5,4},{6,7},{7,6},{8,9},{9,8},{10,11... | collective-permute-start | bytes 393224 | tf_op jit(solution)/shard_map/rows_1/ppermute | solution.py:23
  35.2 1.3 %collective-permute-done.20.rest_2_ = bf16[32,1024]{1,0:T(8,128)(2,1)S(1)} collective-permute-done((bf16[32,1024]{1,0:T(8,128)(2,1)S(1)}, bf16[32,1024]{1,0:T(8,128)(2,1)S(1)}, u32[]{:S(2)}, u32[]{:S(2)}) %collective-permute-start.20) | collective-permute-done | bytes 65568 | tf_op jit(solution)/shard_map/rows0_5/ppermute | solution.py:23
  36.5 3.4 %collective-permute-start.21 = (bf16[32,1024]{1,0:T(8,128)(2,1)S(1)}, bf16[32,1024]{1,0:T(8,128)(2,1)S(1)}, u32[]{:S(2)}, u32[]{:S(2)}) collective-permute-start(bf16[32,1024]{1,0:T(8,128)(2,1)S(1)} %get-tuple-element.88), channel_id=1, source_target_pairs={{0,5},{1,4},{2,7},{3,6},{4,1},{5,0},{6,3},{7,2},{8,13},{9,12},{10,... | collective-permute-start | bytes 196616 | tf_op jit(solution)/shard_map/rows1_5/ppermute | solution.py:23
  40.3 3.3 %collective-permute-done.21.rest_3_ = bf16[32,1024]{1,0:T(8,128)(2,1)S(1)} collective-permute-done((bf16[32,1024]{1,0:T(8,128)(2,1)S(1)}, bf16[32,1024]{1,0:T(8,128)(2,1)S(1)}, u32[]{:S(2)}, u32[]{:S(2)}) %collective-permute-start.21) | collective-permute-done | bytes 65568 | tf_op jit(solution)/shard_map/rows1_5/ppermute | solution.py:23
  43.7 1.4 %collective-permute-done.19.rest_1_ = bf16[32,1024]{1,0:T(8,128)(2,1)S(1)} collective-permute-done((bf16[32,1024]{1,0:T(8,128)(2,1)S(1)}, bf16[32,1024]{1,0:T(8,128)(2,1)S(1)}, u32[]{:S(2)}, u32[]{:S(2)}) %collective-permute-start.19) | collective-permute-done | bytes 65568 | tf_op jit(solution)/shard_map/rows1_4/ppermute | solution.py:23
  45.1 0.7 collective-permute-start.25
  45.8 1.9 %experts.4 = (bf16[32,2048]{1,0:T(8,128)(2,1)S(1)}, bf16[32,2048]{1,0:T(8,128)(2,1)S(1)}) custom-call(f32[1,2048]{1,0:T(1,128)S(1)} %bitcast.7, bf16[1,2048,768]{2,1,0:T(8,128)(2,1)S(1)} %copy-done, bf16[1,2048,768]{2,1,0:T(8,128)(2,1)S(1)} %copy-done.1, bf16[1,768,2048]{2,1,0:T(8,128)(2,1)S(1)} %copy-done.2, ...), custom_call_target="tpu_custom_call" | custom-call | flops 131072 | bytes 15728 | tf_op jit(solution)/shard_map/experts/pallas_call | solution.py:228
  47.7 4.9 %collective-permute-start.22 = (bf16[32,2048]{1,0:T(8,128)(2,1)S(1)}, bf16[32,2048]{1,0:T(8,128)(2,1)S(1)}, u32[]{:S(2)}, u32[]{:S(2)}) collective-permute-start(bf16[32,2048]{1,0:T(8,128)(2,1)S(1)} %get-tuple-element.89), channel_id=1, source_target_pairs={{0,4},{1,5},{2,6},{3,7},{4,0},{5,1},{6,2},{7,3},{8,12},{9,13},{10,... | collective-permute-start | bytes 393224 | tf_op jit(solution)/shard_map/back_4/ppermute | solution.py:23
  52.7 1.7 %experts.3 = (bf16[32,2048]{1,0:T(8,128)(2,1)S(1)}, bf16[32,2048]{1,0:T(8,128)(2,1)S(1)}, bf16[32,2048]{1,0:T(8,128)(2,1)S(1)}, bf16[32,2048]{1,0:T(8,128)(2,1)S(1)}) custom-call(f32[1,2048]{1,0:T(1,128)S(1)} %bitcast.8, bf16[1,2048,768]{2,1,0:T(8,128)(2,1)S(1)} %copy-done, bf16[1,2048,768]{2,1,0:T(8,128)(2,1)S(1)} %copy-done.1, ...), custom_call_target="tpu_custom_call" | custom-call | flops 262144 | bytes 15728 | tf_op jit(solution)/shard_map/experts/pallas_call | solution.py:228
  54.3 0.5 collective-permute-start.15
  54.9 1.4 %collective-permute-start.16 = (bf16[32,2048]{1,0:T(8,128)(2,1)S(1)}, bf16[32,2048]{1,0:T(8,128)(2,1)S(1)}, u32[]{:S(2)}, u32[]{:S(2)}) collective-permute-start(bf16[32,2048]{1,0:T(8,128)(2,1)S(1)} %get-tuple-element.81), channel_id=1, source_target_pairs={{0,2},{1,3},{2,0},{3,1},{4,6},{5,7},{6,4},{7,5},{8,10},{9,11},{10,... | collective-permute-start | bytes 393224 | tf_op jit(solution)/shard_map/back_2/ppermute | solution.py:23
  56.3 7.6 %collective-permute-done.25.rest_1_ = bf16[32,2048]{1,0:T(8,128)(2,1)S(1)} collective-permute-done((bf16[32,2048]{1,0:T(8,128)(2,1)S(1)}, bf16[32,2048]{1,0:T(8,128)(2,1)S(1)}, u32[]{:S(2)}, u32[]{:S(2)}) %collective-permute-start.25) | collective-permute-done | bytes 131104 | tf_op jit(solution)/shard_map/rows_7/ppermute | solution.py:23
  63.9 1.9 %experts.5 = (bf16[32,2048]{1,0:T(8,128)(2,1)S(1)}, bf16[32,2048]{1,0:T(8,128)(2,1)S(1)}) custom-call(f32[1,2048]{1,0:T(1,128)S(1)} %bitcast.9, bf16[1,2048,768]{2,1,0:T(8,128)(2,1)S(1)} %copy-done, bf16[1,2048,768]{2,1,0:T(8,128)(2,1)S(1)} %copy-done.1, bf16[1,768,2048]{2,1,0:T(8,128)(2,1)S(1)} %copy-done.2, ...), custom_call_target="tpu_custom_call" | custom-call | flops 131072 | bytes 15728 | tf_op jit(solution)/shard_map/experts/pallas_call | solution.py:228
  65.8 0.5 collective-permute-start.26
  66.3 1.4 %collective-permute-done.23.rest_7_ = bf16[32,2048]{1,0:T(8,128)(2,1)S(1)} collective-permute-done((bf16[32,2048]{1,0:T(8,128)(2,1)S(1)}, bf16[32,2048]{1,0:T(8,128)(2,1)S(1)}, u32[]{:S(2)}, u32[]{:S(2)}) %collective-permute-start.23) | collective-permute-done | bytes 131104 | tf_op jit(solution)/shard_map/back_5/ppermute | solution.py:23
  67.6 1.0 %collective-permute-start.27 = (bf16[32,2048]{1,0:T(8,128)(2,1)S(1)}, bf16[32,2048]{1,0:T(8,128)(2,1)S(1)}, u32[]{:S(2)}, u32[]{:S(2)}) collective-permute-start(bf16[32,2048]{1,0:T(8,128)(2,1)S(1)} %get-tuple-element.94), channel_id=1, source_target_pairs={{0,7},{1,6},{2,5},{3,4},{4,3},{5,2},{6,1},{7,0},{8,15},{9,14},{10,... | collective-permute-start | bytes 393224 | tf_op jit(solution)/shard_map/back_7/ppermute | solution.py:23
  68.7 7.6 %collective-permute-done.17.rest_5_ = bf16[32,2048]{1,0:T(8,128)(2,1)S(1)} collective-permute-done((bf16[32,2048]{1,0:T(8,128)(2,1)S(1)}, bf16[32,2048]{1,0:T(8,128)(2,1)S(1)}, u32[]{:S(2)}, u32[]{:S(2)}) %collective-permute-start.17) | collective-permute-done | bytes 131104 | tf_op jit(solution)/shard_map/back_3/ppermute | solution.py:23
  76.3 0.8 collective-permute-done.26.rest_8_
  77.1 2.8 %collective-permute-done.27.rest_9_ = bf16[32,2048]{1,0:T(8,128)(2,1)S(1)} collective-permute-done((bf16[32,2048]{1,0:T(8,128)(2,1)S(1)}, bf16[32,2048]{1,0:T(8,128)(2,1)S(1)}, u32[]{:S(2)}, u32[]{:S(2)}) %collective-permute-start.27) | collective-permute-done | bytes 131104 | tf_op jit(solution)/shard_map/back_7/ppermute | solution.py:23
  79.9 1.2 %combine.1 = bf16[1,128,2048]{2,1,0:T(8,128)(2,1)} custom-call(bf16[128,256]{1,0:T(8,128)(2,1)S(1)} %get-tuple-element.50.coarse_ref, bf16[128,256]{1,0:T(8,128)(2,1)S(1)} %get-tuple-element.51.fine_ref, bf16[128,1024]{1,0:T(8,128)(2,1)S(1)} %get-tuple-element.60.rest_4_.rest_0_, bf16[128,1024]{1,0:T(8,128)(2,1)S(1)} %get-tuple-element.74.rest_1_, ...), custom_call_target="tpu_custom_call" | custom-call | flops 268435456 | bytes 2097152 | tf_op jit(solution)/shard_map/combine/pallas_call | solution.py:293
  (39 shorter events, 1.1 us)
Async XLA Ops:
  0.0 9.7 %copy-start.8 = (f32[1,128,2]{1,2,0:T(2,128)S(1)}, f32[1,128,2]{1,2,0:T(2,128)}, u32[]{:S(2)}) copy-start(f32[1,128,2]{1,2,0:T(2,128)} %param.14) | copy-start | bytes 3076
  0.0 9.7 %copy-start.7 = (s32[1,128,2]{1,2,0:T(2,128)S(1)}, s32[1,128,2]{1,2,0:T(2,128)}, u32[]{:S(2)}) copy-start(s32[1,128,2]{1,2,0:T(2,128)} %param.13) | copy-start | bytes 3076
  2.0 7.9 %collective-permute-start = (bf16[3,128,256]{2,1,0:T(8,128)(2,1)}, bf16[3,128,256]{2,1,0:T(8,128)(2,1)S(1)}, u32[]{:S(2)}, u32[]{:S(2)}) collective-permute-start(bf16[3,128,256]{2,1,0:T(8,128)(2,1)} %get-tuple-element.53), channel_id=1, source_target_pairs={{0,8},{8,0},{16,24},{24,16},{1,9},{9,1},{17,25},{25,17},{2,10},{10... | collective-permute-start | bytes 589832 | tf_op jit(solution)/shard_map/qkv0_/ppermute | solution.py:23
  2.4 8.8 %collective-permute-start.1 = (bf16[3,128,256]{2,1,0:T(8,128)(2,1)}, bf16[3,128,256]{2,1,0:T(8,128)(2,1)S(1)}, u32[]{:S(2)}, u32[]{:S(2)}) collective-permute-start(bf16[3,128,256]{2,1,0:T(8,128)(2,1)} %get-tuple-element.54), channel_id=1, source_target_pairs={{0,16},{8,24},{16,0},{24,8},{1,17},{9,25},{17,1},{25,9},{2,18},{10... | collective-permute-start | bytes 589832 | tf_op jit(solution)/shard_map/qkv0_/ppermute | solution.py:23
  3.6 9.7 %collective-permute-start.2 = (bf16[3,128,256]{2,1,0:T(8,128)(2,1)}, bf16[3,128,256]{2,1,0:T(8,128)(2,1)S(1)}, u32[]{:S(2)}, u32[]{:S(2)}) collective-permute-start(bf16[3,128,256]{2,1,0:T(8,128)(2,1)} %get-tuple-element.55), channel_id=1, source_target_pairs={{0,24},{8,16},{16,8},{24,0},{1,25},{9,17},{17,9},{25,1},{2,26},{10... | collective-permute-start | bytes 589832 | tf_op jit(solution)/shard_map/qkv0_/ppermute | solution.py:23
  4.8 1.0 %copy-start.3 = (bf16[1,128,2048]{2,1,0:T(8,128)(2,1)S(1)}, bf16[1,128,2048]{2,1,0:T(8,128)(2,1)}, u32[]{:S(2)}) copy-start(bf16[1,128,2048]{2,1,0:T(8,128)(2,1)} %q_ref.3) | copy-start | bytes 1572868
  5.8 1.0 %copy-start.4 = (bf16[1,128,2048]{2,1,0:T(8,128)(2,1)S(1)}, bf16[1,128,2048]{2,1,0:T(8,128)(2,1)}, u32[]{:S(2)}) copy-start(bf16[1,128,2048]{2,1,0:T(8,128)(2,1)} %k_ref.3) | copy-start | bytes 1572868
  6.8 1.0 %copy-start.5 = (bf16[1,128,2048]{2,1,0:T(8,128)(2,1)S(1)}, bf16[1,128,2048]{2,1,0:T(8,128)(2,1)}, u32[]{:S(2)}) copy-start(bf16[1,128,2048]{2,1,0:T(8,128)(2,1)} %v_ref.3) | copy-start | bytes 1572868
  8.1 8.4 %collective-permute-start.6 = (bf16[3,128,256]{2,1,0:T(8,128)(2,1)S(1)}, bf16[3,128,256]{2,1,0:T(8,128)(2,1)S(1)}, u32[]{:S(2)}, u32[]{:S(2)}) collective-permute-start(bf16[3,128,256]{2,1,0:T(8,128)(2,1)S(1)} %get-tuple-element.63), channel_id=1, source_target_pairs={{0,8},{8,0},{16,24},{24,16},{1,9},{9,1},{17,25},{25,17},{2,10},{10... | collective-permute-start | bytes 589832 | tf_op jit(solution)/shard_map/qkv1_/ppermute | solution.py:23
  8.5 10.7 %collective-permute-start.7 = (bf16[3,128,256]{2,1,0:T(8,128)(2,1)S(1)}, bf16[3,128,256]{2,1,0:T(8,128)(2,1)S(1)}, u32[]{:S(2)}, u32[]{:S(2)}) collective-permute-start(bf16[3,128,256]{2,1,0:T(8,128)(2,1)S(1)} %get-tuple-element.64), channel_id=1, source_target_pairs={{0,16},{8,24},{16,0},{24,8},{1,17},{9,25},{17,1},{25,9},{2,18},{10... | collective-permute-start | bytes 589832 | tf_op jit(solution)/shard_map/qkv1_/ppermute | solution.py:23
  10.0 11.8 %collective-permute-start.8 = (bf16[3,128,256]{2,1,0:T(8,128)(2,1)S(1)}, bf16[3,128,256]{2,1,0:T(8,128)(2,1)S(1)}, u32[]{:S(2)}, u32[]{:S(2)}) collective-permute-start(bf16[3,128,256]{2,1,0:T(8,128)(2,1)S(1)} %get-tuple-element.65), channel_id=1, source_target_pairs={{0,24},{8,16},{16,8},{24,0},{1,25},{9,17},{17,9},{25,1},{2,26},{10... | collective-permute-start | bytes 589832 | tf_op jit(solution)/shard_map/qkv1_/ppermute | solution.py:23
  13.3 0.9 %copy-start.9 = (bf16[3,128,256]{2,1,0:T(8,128)(2,1)S(1)}, bf16[3,128,256]{2,1,0:T(8,128)(2,1)}, u32[]{:S(2)}) copy-start(bf16[3,128,256]{2,1,0:T(8,128)(2,1)} %get-tuple-element.52.rest_0_) | copy-start | bytes 589828
  15.2 7.6 %collective-permute-start.3 = (bf16[128,256]{1,0:T(8,128)(2,1)S(1)}, bf16[128,256]{1,0:T(8,128)(2,1)S(1)}, u32[]{:S(2)}, u32[]{:S(2)}) collective-permute-start(bf16[128,256]{1,0:T(8,128)(2,1)S(1)} %get-tuple-element.57), channel_id=1, source_target_pairs={{0,8},{8,0},{16,24},{24,16},{1,9},{9,1},{17,25},{25,17},{2,10},{10... | collective-permute-start | bytes 196616 | tf_op jit(solution)/shard_map/heads0_/ppermute | solution.py:23
  15.5 9.0 %collective-permute-start.4 = (bf16[128,256]{1,0:T(8,128)(2,1)S(1)}, bf16[128,256]{1,0:T(8,128)(2,1)S(1)}, u32[]{:S(2)}, u32[]{:S(2)}) collective-permute-start(bf16[128,256]{1,0:T(8,128)(2,1)S(1)} %get-tuple-element.58), channel_id=1, source_target_pairs={{0,16},{8,24},{16,0},{24,8},{1,17},{9,25},{17,1},{25,9},{2,18},{10... | collective-permute-start | bytes 196616 | tf_op jit(solution)/shard_map/heads0_/ppermute | solution.py:23
  16.6 29.3 %copy-start = (bf16[1,2048,768]{2,1,0:T(8,128)(2,1)S(1)}, bf16[1,2048,768]{2,1,0:T(8,128)(2,1)}, u32[]{:S(2)}) copy-start(bf16[1,2048,768]{2,1,0:T(8,128)(2,1)} %gate_ref.5) | copy-start | bytes 9437188
  16.6 29.3 %copy-start.1 = (bf16[1,2048,768]{2,1,0:T(8,128)(2,1)S(1)}, bf16[1,2048,768]{2,1,0:T(8,128)(2,1)}, u32[]{:S(2)}) copy-start(bf16[1,2048,768]{2,1,0:T(8,128)(2,1)} %up_ref.5) | copy-start | bytes 9437188
  16.6 29.3 %copy-start.2 = (bf16[1,768,2048]{2,1,0:T(8,128)(2,1)S(1)}, bf16[1,768,2048]{2,1,0:T(8,128)(2,1)}, u32[]{:S(2)}) copy-start(bf16[1,768,2048]{2,1,0:T(8,128)(2,1)} %down_ref.5) | copy-start | bytes 9437188
  16.6 29.3 %copy-start.6 = (f32[2048]{0:T(1024)S(1)}, f32[2048]{0:T(1024)}, u32[]{:S(2)}) copy-start(f32[2048]{0:T(1024)} %param.12) | copy-start | bytes 24580
  16.6 8.0 %collective-permute-start.5 = (bf16[128,256]{1,0:T(8,128)(2,1)S(1)}, bf16[128,256]{1,0:T(8,128)(2,1)S(1)}, u32[]{:S(2)}, u32[]{:S(2)}) collective-permute-start(bf16[128,256]{1,0:T(8,128)(2,1)S(1)} %get-tuple-element.59), channel_id=1, source_target_pairs={{0,24},{8,16},{16,8},{24,0},{1,25},{9,17},{17,9},{25,1},{2,26},{10... | collective-permute-start | bytes 196616 | tf_op jit(solution)/shard_map/heads0_/ppermute | solution.py:23
  24.9 7.7 %collective-permute-start.9 = (bf16[128,256]{1,0:T(8,128)(2,1)S(1)}, bf16[128,256]{1,0:T(8,128)(2,1)S(1)}, u32[]{:S(2)}, u32[]{:S(2)}) collective-permute-start(bf16[128,256]{1,0:T(8,128)(2,1)S(1)} %get-tuple-element.71), channel_id=1, source_target_pairs={{0,8},{8,0},{16,24},{24,16},{1,9},{9,1},{17,25},{25,17},{2,10},{10... | collective-permute-start | bytes 196616 | tf_op jit(solution)/shard_map/heads1_/ppermute | solution.py:23
  25.6 7.1 %collective-permute-start.10 = (bf16[128,256]{1,0:T(8,128)(2,1)S(1)}, bf16[128,256]{1,0:T(8,128)(2,1)S(1)}, u32[]{:S(2)}, u32[]{:S(2)}) collective-permute-start(bf16[128,256]{1,0:T(8,128)(2,1)S(1)} %get-tuple-element.72), channel_id=1, source_target_pairs={{0,16},{8,24},{16,0},{24,8},{1,17},{9,25},{17,1},{25,9},{2,18},{10... | collective-permute-start | bytes 196616 | tf_op jit(solution)/shard_map/heads1_/ppermute | solution.py:23
  26.1 6.6 %collective-permute-start.11 = (bf16[128,256]{1,0:T(8,128)(2,1)S(1)}, bf16[128,256]{1,0:T(8,128)(2,1)S(1)}, u32[]{:S(2)}, u32[]{:S(2)}) collective-permute-start(bf16[128,256]{1,0:T(8,128)(2,1)S(1)} %get-tuple-element.73), channel_id=1, source_target_pairs={{0,24},{8,16},{16,8},{24,0},{1,25},{9,17},{17,9},{25,1},{2,26},{10... | collective-permute-start | bytes 196616 | tf_op jit(solution)/shard_map/heads1_/ppermute | solution.py:23
  27.7 12.3 %collective-permute-start.18 = (bf16[32,1024]{1,0:T(8,128)(2,1)S(1)}, bf16[32,1024]{1,0:T(8,128)(2,1)S(1)}, u32[]{:S(2)}, u32[]{:S(2)}) collective-permute-start(bf16[32,1024]{1,0:T(8,128)(2,1)S(1)} %get-tuple-element.83), channel_id=1, source_target_pairs={{0,4},{1,5},{2,6},{3,7},{4,0},{5,1},{6,2},{7,3},{8,12},{9,13},{10,... | collective-permute-start | bytes 196616 | tf_op jit(solution)/shard_map/rows0_4/ppermute | solution.py:23
  30.0 6.6 %collective-permute-start.20 = (bf16[32,1024]{1,0:T(8,128)(2,1)S(1)}, bf16[32,1024]{1,0:T(8,128)(2,1)S(1)}, u32[]{:S(2)}, u32[]{:S(2)}) collective-permute-start(bf16[32,1024]{1,0:T(8,128)(2,1)S(1)} %get-tuple-element.86), channel_id=1, source_target_pairs={{0,5},{1,4},{2,7},{3,6},{4,1},{5,0},{6,3},{7,2},{8,13},{9,12},{10,... | collective-permute-start | bytes 196616 | tf_op jit(solution)/shard_map/rows0_5/ppermute | solution.py:23
  33.3 14.4 %collective-permute-start.12 = (bf16[32,2048]{1,0:T(8,128)(2,1)S(1)}, bf16[32,2048]{1,0:T(8,128)(2,1)S(1)}, u32[]{:S(2)}, u32[]{:S(2)}) collective-permute-start(bf16[32,2048]{1,0:T(8,128)(2,1)S(1)} %get-tuple-element.76), channel_id=1, source_target_pairs={{0,1},{1,0},{2,3},{3,2},{4,5},{5,4},{6,7},{7,6},{8,9},{9,8},{10,11... | collective-permute-start | bytes 393224 | tf_op jit(solution)/shard_map/rows_1/ppermute | solution.py:23
  35.0 17.6 %collective-permute-start.13 = (bf16[32,2048]{1,0:T(8,128)(2,1)S(1)}, bf16[32,2048]{1,0:T(8,128)(2,1)S(1)}, u32[]{:S(2)}, u32[]{:S(2)}) collective-permute-start(bf16[32,2048]{1,0:T(8,128)(2,1)S(1)} %get-tuple-element.77), channel_id=1, source_target_pairs={{0,2},{1,3},{2,0},{3,1},{4,6},{5,7},{6,4},{7,5},{8,10},{9,11},{10,... | collective-permute-start | bytes 393224 | tf_op jit(solution)/shard_map/rows_2/ppermute | solution.py:23
  36.5 7.1 %collective-permute-start.21 = (bf16[32,1024]{1,0:T(8,128)(2,1)S(1)}, bf16[32,1024]{1,0:T(8,128)(2,1)S(1)}, u32[]{:S(2)}, u32[]{:S(2)}) collective-permute-start(bf16[32,1024]{1,0:T(8,128)(2,1)S(1)} %get-tuple-element.88), channel_id=1, source_target_pairs={{0,5},{1,4},{2,7},{3,6},{4,1},{5,0},{6,3},{7,2},{8,13},{9,12},{10,... | collective-permute-start | bytes 196616 | tf_op jit(solution)/shard_map/rows1_5/ppermute | solution.py:23
  39.9 5.2 %collective-permute-start.19 = (bf16[32,1024]{1,0:T(8,128)(2,1)S(1)}, bf16[32,1024]{1,0:T(8,128)(2,1)S(1)}, u32[]{:S(2)}, u32[]{:S(2)}) collective-permute-start(bf16[32,1024]{1,0:T(8,128)(2,1)S(1)} %get-tuple-element.85), channel_id=1, source_target_pairs={{0,4},{1,5},{2,6},{3,7},{4,0},{5,1},{6,2},{7,3},{8,12},{9,13},{10,... | collective-permute-start | bytes 196616 | tf_op jit(solution)/shard_map/rows1_4/ppermute | solution.py:23
  40.1 12.5 %collective-permute-start.14 = (bf16[32,2048]{1,0:T(8,128)(2,1)S(1)}, bf16[32,2048]{1,0:T(8,128)(2,1)S(1)}, u32[]{:S(2)}, u32[]{:S(2)}) collective-permute-start(bf16[32,2048]{1,0:T(8,128)(2,1)S(1)} %get-tuple-element.78), channel_id=1, source_target_pairs={{0,3},{1,2},{2,1},{3,0},{4,7},{5,6},{6,5},{7,4},{8,11},{9,10},{10,... | collective-permute-start | bytes 393224 | tf_op jit(solution)/shard_map/rows_3/ppermute | solution.py:23
  43.7 11.2 %collective-permute-start.24 = (bf16[32,2048]{1,0:T(8,128)(2,1)S(1)}, bf16[32,2048]{1,0:T(8,128)(2,1)S(1)}, u32[]{:S(2)}, u32[]{:S(2)}) collective-permute-start(bf16[32,2048]{1,0:T(8,128)(2,1)S(1)} %get-tuple-element.91), channel_id=1, source_target_pairs={{0,6},{1,7},{2,4},{3,5},{4,2},{5,3},{6,0},{7,1},{8,14},{9,15},{10,... | collective-permute-start | bytes 393224 | tf_op jit(solution)/shard_map/rows_6/ppermute | solution.py:23
  45.1 18.8 %collective-permute-start.25 = (bf16[32,2048]{1,0:T(8,128)(2,1)S(1)}, bf16[32,2048]{1,0:T(8,128)(2,1)S(1)}, u32[]{:S(2)}, u32[]{:S(2)}) collective-permute-start(bf16[32,2048]{1,0:T(8,128)(2,1)S(1)} %get-tuple-element.92), channel_id=1, source_target_pairs={{0,7},{1,6},{2,5},{3,4},{4,3},{5,2},{6,1},{7,0},{8,15},{9,14},{10,... | collective-permute-start | bytes 393224 | tf_op jit(solution)/shard_map/rows_7/ppermute | solution.py:23
  47.7 18.1 %collective-permute-start.22 = (bf16[32,2048]{1,0:T(8,128)(2,1)S(1)}, bf16[32,2048]{1,0:T(8,128)(2,1)S(1)}, u32[]{:S(2)}, u32[]{:S(2)}) collective-permute-start(bf16[32,2048]{1,0:T(8,128)(2,1)S(1)} %get-tuple-element.89), channel_id=1, source_target_pairs={{0,4},{1,5},{2,6},{3,7},{4,0},{5,1},{6,2},{7,3},{8,12},{9,13},{10,... | collective-permute-start | bytes 393224 | tf_op jit(solution)/shard_map/back_4/ppermute | solution.py:23
  52.6 15.0 %collective-permute-start.23 = (bf16[32,2048]{1,0:T(8,128)(2,1)S(1)}, bf16[32,2048]{1,0:T(8,128)(2,1)S(1)}, u32[]{:S(2)}, u32[]{:S(2)}) collective-permute-start(bf16[32,2048]{1,0:T(8,128)(2,1)S(1)} %get-tuple-element.90), channel_id=1, source_target_pairs={{0,5},{1,4},{2,7},{3,6},{4,1},{5,0},{6,3},{7,2},{8,13},{9,12},{10,... | collective-permute-start | bytes 393224 | tf_op jit(solution)/shard_map/back_5/ppermute | solution.py:23
  54.3 14.3 %collective-permute-start.15 = (bf16[32,2048]{1,0:T(8,128)(2,1)S(1)}, bf16[32,2048]{1,0:T(8,128)(2,1)S(1)}, u32[]{:S(2)}, u32[]{:S(2)}) collective-permute-start(bf16[32,2048]{1,0:T(8,128)(2,1)S(1)} %get-tuple-element.80), channel_id=1, source_target_pairs={{0,1},{1,0},{2,3},{3,2},{4,5},{5,4},{6,7},{7,6},{8,9},{9,8},{10,11... | collective-permute-start | bytes 393224 | tf_op jit(solution)/shard_map/back_1/ppermute | solution.py:23
  54.9 13.8 %collective-permute-start.16 = (bf16[32,2048]{1,0:T(8,128)(2,1)S(1)}, bf16[32,2048]{1,0:T(8,128)(2,1)S(1)}, u32[]{:S(2)}, u32[]{:S(2)}) collective-permute-start(bf16[32,2048]{1,0:T(8,128)(2,1)S(1)} %get-tuple-element.81), channel_id=1, source_target_pairs={{0,2},{1,3},{2,0},{3,1},{4,6},{5,7},{6,4},{7,5},{8,10},{9,11},{10,... | collective-permute-start | bytes 393224 | tf_op jit(solution)/shard_map/back_2/ppermute | solution.py:23
  63.9 12.4 %collective-permute-start.17 = (bf16[32,2048]{1,0:T(8,128)(2,1)S(1)}, bf16[32,2048]{1,0:T(8,128)(2,1)S(1)}, u32[]{:S(2)}, u32[]{:S(2)}) collective-permute-start(bf16[32,2048]{1,0:T(8,128)(2,1)S(1)} %get-tuple-element.82), channel_id=1, source_target_pairs={{0,3},{1,2},{2,1},{3,0},{4,7},{5,6},{6,5},{7,4},{8,11},{9,10},{10,... | collective-permute-start | bytes 393224 | tf_op jit(solution)/shard_map/back_3/ppermute | solution.py:23
  65.8 11.3 %collective-permute-start.26 = (bf16[32,2048]{1,0:T(8,128)(2,1)S(1)}, bf16[32,2048]{1,0:T(8,128)(2,1)S(1)}, u32[]{:S(2)}, u32[]{:S(2)}) collective-permute-start(bf16[32,2048]{1,0:T(8,128)(2,1)S(1)} %get-tuple-element.93), channel_id=1, source_target_pairs={{0,6},{1,7},{2,4},{3,5},{4,2},{5,3},{6,0},{7,1},{8,14},{9,15},{10,... | collective-permute-start | bytes 393224 | tf_op jit(solution)/shard_map/back_6/ppermute | solution.py:23
  67.6 12.3 %collective-permute-start.27 = (bf16[32,2048]{1,0:T(8,128)(2,1)S(1)}, bf16[32,2048]{1,0:T(8,128)(2,1)S(1)}, u32[]{:S(2)}, u32[]{:S(2)}) collective-permute-start(bf16[32,2048]{1,0:T(8,128)(2,1)S(1)} %get-tuple-element.94), channel_id=1, source_target_pairs={{0,7},{1,6},{2,5},{3,4},{4,3},{5,2},{6,1},{7,0},{8,15},{9,14},{10,... | collective-permute-start | bytes 393224 | tf_op jit(solution)/shard_map/back_7/ppermute | solution.py:23

commit v4 on v3

--- a/solution.py
+++ b/solution.py
@@ -11,7 +11,7 @@
 HEADS = 16
 CAP = 32
 CHUNKS = 2
-PACK_MIB = 56
+PACK_MIB = 53
 F32 = jnp.float32
 BF16 = jnp.bfloat16
 HBM = pl.BlockSpec(memory_space=pltpu.HBM)
@@ -31,43 +31,34 @@
     return pl.CostEstimate(flops=flops, bytes_accessed=moved, transcendentals=0)
 
 
-def pack_kernel(groups, chunks, c, width, q_ref, k_ref, v_ref, *rest):
-    outs, (in_sems, *staged) = rest[:groups], rest[groups:]
+def pack_kernel(places, chunks, width, q_ref, k_ref, v_ref, *rest):
+    outs, sems = rest[:-1], rest[-1]
     me = lax.axis_index("seq")
-    inward, outward = [], []
-    for distance in [*range(1, groups), 0]:
+    copies = []
+    for out, (distance, c) in zip(outs, places):
         column = pl.multiple_of(((me ^ distance) * chunks + c) * width, 128)
         for i, ref in enumerate((q_ref, k_ref, v_ref)):
-            n = len(inward)
-            target = staged[0].at[n] if staged else outs[distance].at[i]
-            inward.append(
-                pltpu.make_async_copy(ref.at[0, :, pl.ds(column, width)], target, in_sems.at[n])
+            copies.append(
+                pltpu.make_async_copy(
+                    ref.at[0, :, pl.ds(column, width)], out.at[i], sems.at[len(copies)]
+                )
             )
-            if staged:
-                outward.append(
-                    pltpu.make_async_copy(target, outs[distance].at[i], staged[1].at[n])
-                )
-    for copy in inward:
+    for copy in copies:
         copy.start()
-    for n, copy in enumerate(inward):
+    for copy in copies:
         copy.wait()
-        if staged:
-            outward[n].start()
-    for out in outward:
-        out.wait()
-
-
-def pack(groups, chunks, c, width, q, k, v):
+
+
+def pack(places, chunks, width, mib, q, k, v):
     tokens = q.shape[1]
-    count = 3 * groups
-    staged = [pltpu.VMEM((count, tokens, width), BF16), pltpu.SemaphoreType.DMA((count,))]
-    return pl.pallas_call(
-        functools.partial(pack_kernel, groups, chunks, c, width),
-        out_shape=[jax.ShapeDtypeStruct((3, tokens, width), BF16)] * groups,
+    count = 3 * len(places)
+    return pl.pallas_call(
+        functools.partial(pack_kernel, places, chunks, width),
+        out_shape=[jax.ShapeDtypeStruct((3, tokens, width), BF16)] * len(places),
         in_specs=[HBM] * 3,
-        out_specs=[HBM if c == 0 else VMEM] * groups,
-        scratch_shapes=[pltpu.SemaphoreType.DMA((count,))] + (staged if c == 0 else []),
-        compiler_params=params(PACK_MIB if c == 0 else 8),
+        out_specs=[VMEM] * len(places),
+        scratch_shapes=[pltpu.SemaphoreType.DMA((count,))],
+        compiler_params=params(mib),
         cost_estimate=cost(0, 4 * count * tokens * width),
         name="pack_heads",
     )(q, k, v)
@@ -332,9 +323,13 @@
         with jax.named_scope(f"{name}{distance}"):
             return swap(block, "expert", distance)
 
+    first = [(d, 0) for d in range(1, groups)]
+    others = [(0, 0)] + [(d, c) for c in range(1, chunks) for d in range(groups)]
+    packed = pack(first, chunks, width, PACK_MIB, query_rows, key_rows, value_rows)
+    own, *rest = pack(others, chunks, width, 8, query_rows, key_rows, value_rows)
+    packed = [own, *packed, *rest]
     received = [
-        exchange(pack(groups, chunks, c, width, query_rows, key_rows, value_rows), f"qkv{c}_")
-        for c in range(chunks)
+        exchange(packed[c * groups : (c + 1) * groups], f"qkv{c}_") for c in range(chunks)
     ]
     weights = spread(experts, ids, gates)
     received[-1][0] = after(received[-1][0], weights)
@@ -342,7 +337,7 @@
     kept, arrived = [], [[] for _ in range(experts)]
     for c in range(chunks):
         last = c == chunks - 1
-        out = heads[c] if c == 0 else after(heads[c], kept[-1])
+        out = heads[c]
         *rows, own = select(groups, experts, ids, exchange(out, f"heads{c}_"), kept, last)
         kept.append(own)
         for d in range(half, middle):

time: 81.8 us -> 80.8 us (0.988)
  starting transfers between devices: 29.9 us -> 31.1 us
  waiting for transfers between devices: 34.9 us -> 33.8 us
  local copies, waits for them, and re-layouts: 4.07 us -> 3.15 us
    ppermute x28, starting transfers between devices: 29.9 us -> 31.1 us  [swap(): return lax.ppermute(x, axis, [(i, i ^ distance) for i in range(size)])]
    ppermute x28, waiting for transfers between devices: 34.9 us -> 33.8 us  [swap(): return lax.ppermute(x, axis, [(i, i ^ distance) for i in range(size)])]
    unnamed x20 -> x18, local copies, waits for them, and re-layouts: 4.07 us -> 3.15 us
  transfers between devices with their start and end apart: 28 -> 28, of which waited for: 13 -> 12; matrix products, arithmetic and copies ran while one was open for 0% -> 0% of each run, Pallas kernels for 10% -> 11%
where the time goes in v4:
time: 80.8 us; the launch traced here: 79.5 us
  waiting for transfers between devices  33.8 us (42%)
  starting transfers between devices  31.1 us (38%)
  Pallas kernels  11.3 us (14%)
  local copies, waits for them, and re-layouts  3.15 us (4%)
    ppermute x28, waiting for transfers between devices, swap(): return lax.ppermute(x, axis, [(i, i ^ distance) for i in range(size)])  33.8 us
    ppermute x28, starting transfers between devices, swap(): return lax.ppermute(x, axis, [(i, i ^ distance) for i in range(size)])  31.1 us
    pallas_call x3, Pallas kernels, run_experts(): pl.pallas_call(functools.partial(experts_kernel, groups, chunks, width, h...  5.41 us
    unnamed x18, local copies, waits for them, and re-layouts  3.15 us
    pallas_call x2, Pallas kernels, attend(): pl.pallas_call(functools.partial(attend_kernel, groups, width, head_size)...  1.93 us
  transfers between devices with their start and end apart: 28, of which 12 were waited for; matrix products, arithmetic and copies ran while one was open for 0% of the time, Pallas kernels for 11%

profile of v4, /device:TPU:11, one launch (start us, length us, event | category | flops | bytes accessed | tf_op | source)
XLA Modules:
  0.0 79.5 jit_solution(14098365185531594410)
XLA Ops:
  0.0 1.2 %pack_heads.3 = (bf16[3,128,256]{2,1,0:T(8,128)(2,1)S(1)}, bf16[3,128,256]{2,1,0:T(8,128)(2,1)S(1)}, bf16[3,128,256]{2,1,0:T(8,128)(2,1)S(1)}) custom-call(bf16[1,128,2048]{2,1,0:T(8,128)(2,1)} %q_ref.3, bf16[1,128,2048]{2,1,0:T(8,128)(2,1)} %k_ref.3, bf16[1,128,2048]{2,1,0:T(8,128)(2,1)} %v_ref.3), custom_call_target="tpu_custom_call" | custom-call | bytes 1179648 | tf_op jit(solution)/shard_map/pack_heads/pallas_call | solution.py:55
  1.2 0.3 collective-permute-start
  1.5 1.2 %collective-permute-start.1 = (bf16[3,128,256]{2,1,0:T(8,128)(2,1)S(1)}, bf16[3,128,256]{2,1,0:T(8,128)(2,1)S(1)}, u32[]{:S(2)}, u32[]{:S(2)}) collective-permute-start(bf16[3,128,256]{2,1,0:T(8,128)(2,1)S(1)} %get-tuple-element.50), channel_id=1, source_target_pairs={{0,16},{8,24},{16,0},{24,8},{1,17},{9,25},{17,1},{25,9},{2,18},{10... | collective-permute-start | bytes 589832 | tf_op jit(solution)/shard_map/qkv0_/ppermute | solution.py:23
  2.8 1.2 %collective-permute-start.2 = (bf16[3,128,256]{2,1,0:T(8,128)(2,1)S(1)}, bf16[3,128,256]{2,1,0:T(8,128)(2,1)S(1)}, u32[]{:S(2)}, u32[]{:S(2)}) collective-permute-start(bf16[3,128,256]{2,1,0:T(8,128)(2,1)S(1)} %get-tuple-element.51), channel_id=1, source_target_pairs={{0,24},{8,16},{16,8},{24,0},{1,25},{9,17},{17,9},{25,1},{2,26},{10... | collective-permute-start | bytes 589832 | tf_op jit(solution)/shard_map/qkv0_/ppermute | solution.py:23
  3.9 1.0 %copy-done.3 = bf16[1,128,2048]{2,1,0:T(8,128)(2,1)S(1)} copy-done((bf16[1,128,2048]{2,1,0:T(8,128)(2,1)S(1)}, bf16[1,128,2048]{2,1,0:T(8,128)(2,1)}, u32[]{:S(2)}) %copy-start.3) | copy-done | bytes 524312
  5.0 1.0 %copy-done.4 = bf16[1,128,2048]{2,1,0:T(8,128)(2,1)S(1)} copy-done((bf16[1,128,2048]{2,1,0:T(8,128)(2,1)S(1)}, bf16[1,128,2048]{2,1,0:T(8,128)(2,1)}, u32[]{:S(2)}) %copy-start.4) | copy-done | bytes 524312
  6.0 1.0 %copy-done.5 = bf16[1,128,2048]{2,1,0:T(8,128)(2,1)S(1)} copy-done((bf16[1,128,2048]{2,1,0:T(8,128)(2,1)S(1)}, bf16[1,128,2048]{2,1,0:T(8,128)(2,1)}, u32[]{:S(2)}) %copy-start.5) | copy-done | bytes 524312
  7.1 0.3 pack_heads.2
  7.4 0.3 collective-permute-start.6
  7.7 1.2 %collective-permute-start.7 = (bf16[3,128,256]{2,1,0:T(8,128)(2,1)S(1)}, bf16[3,128,256]{2,1,0:T(8,128)(2,1)S(1)}, u32[]{:S(2)}, u32[]{:S(2)}) collective-permute-start(bf16[3,128,256]{2,1,0:T(8,128)(2,1)S(1)} %get-tuple-element.60), channel_id=1, source_target_pairs={{0,16},{8,24},{16,0},{24,8},{1,17},{9,25},{17,1},{25,9},{2,18},{10... | collective-permute-start | bytes 589832 | tf_op jit(solution)/shard_map/qkv1_/ppermute | solution.py:23
  8.9 0.2 spread_gates.1
  9.2 1.2 %collective-permute-start.8 = (bf16[3,128,256]{2,1,0:T(8,128)(2,1)S(1)}, bf16[3,128,256]{2,1,0:T(8,128)(2,1)S(1)}, u32[]{:S(2)}, u32[]{:S(2)}) collective-permute-start(bf16[3,128,256]{2,1,0:T(8,128)(2,1)S(1)} %get-tuple-element.61), channel_id=1, source_target_pairs={{0,24},{8,16},{16,8},{24,0},{1,25},{9,17},{17,9},{25,1},{2,26},{10... | collective-permute-start | bytes 589832 | tf_op jit(solution)/shard_map/qkv1_/ppermute | solution.py:23
  10.4 1.8 %collective-permute-done.2.rest_3_ = bf16[3,128,256]{2,1,0:T(8,128)(2,1)S(1)} collective-permute-done((bf16[3,128,256]{2,1,0:T(8,128)(2,1)S(1)}, bf16[3,128,256]{2,1,0:T(8,128)(2,1)S(1)}, u32[]{:S(2)}, u32[]{:S(2)}) %collective-permute-start.2) | collective-permute-done | bytes 196640 | tf_op jit(solution)/shard_map/qkv0_/ppermute | solution.py:23
  12.3 1.0 %attend.2 = (bf16[128,256]{1,0:T(8,128)(2,1)S(1)}, bf16[128,256]{1,0:T(8,128)(2,1)S(1)}, bf16[128,256]{1,0:T(8,128)(2,1)S(1)}, bf16[128,256]{1,0:T(8,128)(2,1)S(1)}) custom-call(bf16[3,128,256]{2,1,0:T(8,128)(2,1)S(1)} %get-tuple-element.48.rest_0_, bf16[3,128,256]{2,1,0:T(8,128)(2,1)S(1)} %collective-permute-done.rest_1_, ...), custom_call_target="tpu_custom_call" | custom-call | flops 10737418240 | bytes 10485760 | tf_op jit(solution)/shard_map/attend/pallas_call | solution.py:98
  13.2 0.3 collective-permute-start.3
  13.6 0.2 collective-permute-start.4
  13.8 1.7 %collective-permute-done.6.rest_1_ = bf16[3,128,256]{2,1,0:T(8,128)(2,1)S(1)} collective-permute-done((bf16[3,128,256]{2,1,0:T(8,128)(2,1)S(1)}, bf16[3,128,256]{2,1,0:T(8,128)(2,1)S(1)}, u32[]{:S(2)}, u32[]{:S(2)}) %collective-permute-start.6) | collective-permute-done | bytes 196640 | tf_op jit(solution)/shard_map/qkv1_/ppermute | solution.py:23
  15.5 1.3 %collective-permute-start.5 = (bf16[128,256]{1,0:T(8,128)(2,1)S(1)}, bf16[128,256]{1,0:T(8,128)(2,1)S(1)}, u32[]{:S(2)}, u32[]{:S(2)}) collective-permute-start(bf16[128,256]{1,0:T(8,128)(2,1)S(1)} %get-tuple-element.55), channel_id=1, source_target_pairs={{0,24},{8,16},{16,8},{24,0},{1,25},{9,17},{17,9},{25,1},{2,26},{10... | collective-permute-start | bytes 196616 | tf_op jit(solution)/shard_map/heads0_/ppermute | solution.py:23
  16.8 1.4 %collective-permute-done.7.rest_2_ = bf16[3,128,256]{2,1,0:T(8,128)(2,1)S(1)} collective-permute-done((bf16[3,128,256]{2,1,0:T(8,128)(2,1)S(1)}, bf16[3,128,256]{2,1,0:T(8,128)(2,1)S(1)}, u32[]{:S(2)}, u32[]{:S(2)}) %collective-permute-start.7) | collective-permute-done | bytes 196640 | tf_op jit(solution)/shard_map/qkv1_/ppermute | solution.py:23
  18.2 2.5 %collective-permute-done.8.rest_3_ = bf16[3,128,256]{2,1,0:T(8,128)(2,1)S(1)} collective-permute-done((bf16[3,128,256]{2,1,0:T(8,128)(2,1)S(1)}, bf16[3,128,256]{2,1,0:T(8,128)(2,1)S(1)}, u32[]{:S(2)}, u32[]{:S(2)}) %collective-permute-start.8) | collective-permute-done | bytes 196640 | tf_op jit(solution)/shard_map/qkv1_/ppermute | solution.py:23
  20.7 1.0 %attend.3 = (bf16[128,256]{1,0:T(8,128)(2,1)S(1)}, bf16[128,256]{1,0:T(8,128)(2,1)S(1)}, bf16[128,256]{1,0:T(8,128)(2,1)S(1)}, bf16[128,256]{1,0:T(8,128)(2,1)S(1)}) custom-call(bf16[3,128,256]{2,1,0:T(8,128)(2,1)S(1)} %get-tuple-element.58.rest_0_, bf16[3,128,256]{2,1,0:T(8,128)(2,1)S(1)} %collective-permute-done.6.rest_1_, ...), custom_call_target="tpu_custom_call" | custom-call | flops 10737418240 | bytes 10485760 | tf_op jit(solution)/shard_map/attend/pallas_call | solution.py:98
  21.7 0.3 collective-permute-start.9
  22.0 0.4 collective-permute-start.10
  22.4 2.0 %collective-permute-start.11 = (bf16[128,256]{1,0:T(8,128)(2,1)S(1)}, bf16[128,256]{1,0:T(8,128)(2,1)S(1)}, u32[]{:S(2)}, u32[]{:S(2)}) collective-permute-start(bf16[128,256]{1,0:T(8,128)(2,1)S(1)} %get-tuple-element.65), channel_id=1, source_target_pairs={{0,24},{8,16},{16,8},{24,0},{1,25},{9,17},{17,9},{25,1},{2,26},{10... | collective-permute-start | bytes 196616 | tf_op jit(solution)/shard_map/heads1_/ppermute | solution.py:23
  24.4 0.4 select_rows.2
  24.8 2.4 %collective-permute-start.18 = (bf16[32,1024]{1,0:T(8,128)(2,1)S(1)}, bf16[32,1024]{1,0:T(8,128)(2,1)S(1)}, u32[]{:S(2)}, u32[]{:S(2)}) collective-permute-start(bf16[32,1024]{1,0:T(8,128)(2,1)S(1)} %get-tuple-element.75), channel_id=1, source_target_pairs={{0,4},{1,5},{2,6},{3,7},{4,0},{5,1},{6,2},{7,3},{8,12},{9,13},{10,... | collective-permute-start | bytes 196616 | tf_op jit(solution)/shard_map/rows0_4/ppermute | solution.py:23
  27.2 3.8 %collective-permute-start.20 = (bf16[32,1024]{1,0:T(8,128)(2,1)S(1)}, bf16[32,1024]{1,0:T(8,128)(2,1)S(1)}, u32[]{:S(2)}, u32[]{:S(2)}) collective-permute-start(bf16[32,1024]{1,0:T(8,128)(2,1)S(1)} %get-tuple-element.78), channel_id=1, source_target_pairs={{0,5},{1,4},{2,7},{3,6},{4,1},{5,0},{6,3},{7,2},{8,13},{9,12},{10,... | collective-permute-start | bytes 196616 | tf_op jit(solution)/shard_map/rows0_5/ppermute | solution.py:23
  31.0 0.6 select_rows.3
  31.7 1.8 %collective-permute-start.12 = (bf16[32,2048]{1,0:T(8,128)(2,1)S(1)}, bf16[32,2048]{1,0:T(8,128)(2,1)S(1)}, u32[]{:S(2)}, u32[]{:S(2)}) collective-permute-start(bf16[32,2048]{1,0:T(8,128)(2,1)S(1)} %get-tuple-element.68), channel_id=1, source_target_pairs={{0,1},{1,0},{2,3},{3,2},{4,5},{5,4},{6,7},{7,6},{8,9},{9,8},{10,11... | collective-permute-start | bytes 393224 | tf_op jit(solution)/shard_map/rows_1/ppermute | solution.py:23
  33.7 1.2 %collective-permute-done.20.rest_2_ = bf16[32,1024]{1,0:T(8,128)(2,1)S(1)} collective-permute-done((bf16[32,1024]{1,0:T(8,128)(2,1)S(1)}, bf16[32,1024]{1,0:T(8,128)(2,1)S(1)}, u32[]{:S(2)}, u32[]{:S(2)}) %collective-permute-start.20) | collective-permute-done | bytes 65568 | tf_op jit(solution)/shard_map/rows0_5/ppermute | solution.py:23
  34.9 3.4 %collective-permute-start.21 = (bf16[32,1024]{1,0:T(8,128)(2,1)S(1)}, bf16[32,1024]{1,0:T(8,128)(2,1)S(1)}, u32[]{:S(2)}, u32[]{:S(2)}) collective-permute-start(bf16[32,1024]{1,0:T(8,128)(2,1)S(1)} %get-tuple-element.80), channel_id=1, source_target_pairs={{0,5},{1,4},{2,7},{3,6},{4,1},{5,0},{6,3},{7,2},{8,13},{9,12},{10,... | collective-permute-start | bytes 196616 | tf_op jit(solution)/shard_map/rows1_5/ppermute | solution.py:23
  38.7 3.5 %collective-permute-done.21.rest_3_ = bf16[32,1024]{1,0:T(8,128)(2,1)S(1)} collective-permute-done((bf16[32,1024]{1,0:T(8,128)(2,1)S(1)}, bf16[32,1024]{1,0:T(8,128)(2,1)S(1)}, u32[]{:S(2)}, u32[]{:S(2)}) %collective-permute-start.21) | collective-permute-done | bytes 65568 | tf_op jit(solution)/shard_map/rows1_5/ppermute | solution.py:23
  42.2 1.4 %collective-permute-done.19.rest_1_ = bf16[32,1024]{1,0:T(8,128)(2,1)S(1)} collective-permute-done((bf16[32,1024]{1,0:T(8,128)(2,1)S(1)}, bf16[32,1024]{1,0:T(8,128)(2,1)S(1)}, u32[]{:S(2)}, u32[]{:S(2)}) %collective-permute-start.19) | collective-permute-done | bytes 65568 | tf_op jit(solution)/shard_map/rows1_4/ppermute | solution.py:23
  43.6 0.8 collective-permute-start.25
  44.4 1.9 %experts.4 = (bf16[32,2048]{1,0:T(8,128)(2,1)S(1)}, bf16[32,2048]{1,0:T(8,128)(2,1)S(1)}) custom-call(f32[1,2048]{1,0:T(1,128)S(1)} %bitcast.7, bf16[1,2048,768]{2,1,0:T(8,128)(2,1)S(1)} %copy-done, bf16[1,2048,768]{2,1,0:T(8,128)(2,1)S(1)} %copy-done.1, bf16[1,768,2048]{2,1,0:T(8,128)(2,1)S(1)} %copy-done.2, ...), custom_call_target="tpu_custom_call" | custom-call | flops 131072 | bytes 15728 | tf_op jit(solution)/shard_map/experts/pallas_call | solution.py:219
  46.3 4.9 %collective-permute-start.22 = (bf16[32,2048]{1,0:T(8,128)(2,1)S(1)}, bf16[32,2048]{1,0:T(8,128)(2,1)S(1)}, u32[]{:S(2)}, u32[]{:S(2)}) collective-permute-start(bf16[32,2048]{1,0:T(8,128)(2,1)S(1)} %get-tuple-element.81), channel_id=1, source_target_pairs={{0,4},{1,5},{2,6},{3,7},{4,0},{5,1},{6,2},{7,3},{8,12},{9,13},{10,... | collective-permute-start | bytes 393224 | tf_op jit(solution)/shard_map/back_4/ppermute | solution.py:23
  51.2 1.7 %experts.3 = (bf16[32,2048]{1,0:T(8,128)(2,1)S(1)}, bf16[32,2048]{1,0:T(8,128)(2,1)S(1)}, bf16[32,2048]{1,0:T(8,128)(2,1)S(1)}, bf16[32,2048]{1,0:T(8,128)(2,1)S(1)}) custom-call(f32[1,2048]{1,0:T(1,128)S(1)} %bitcast.8, bf16[1,2048,768]{2,1,0:T(8,128)(2,1)S(1)} %copy-done, bf16[1,2048,768]{2,1,0:T(8,128)(2,1)S(1)} %copy-done.1, ...), custom_call_target="tpu_custom_call" | custom-call | flops 262144 | bytes 15728 | tf_op jit(solution)/shard_map/experts/pallas_call | solution.py:219
  52.8 0.5 collective-permute-start.15
  53.4 1.4 %collective-permute-start.16 = (bf16[32,2048]{1,0:T(8,128)(2,1)S(1)}, bf16[32,2048]{1,0:T(8,128)(2,1)S(1)}, u32[]{:S(2)}, u32[]{:S(2)}) collective-permute-start(bf16[32,2048]{1,0:T(8,128)(2,1)S(1)} %get-tuple-element.73), channel_id=1, source_target_pairs={{0,2},{1,3},{2,0},{3,1},{4,6},{5,7},{6,4},{7,5},{8,10},{9,11},{10,... | collective-permute-start | bytes 393224 | tf_op jit(solution)/shard_map/back_2/ppermute | solution.py:23
  54.8 7.6 %collective-permute-done.25.rest_1_ = bf16[32,2048]{1,0:T(8,128)(2,1)S(1)} collective-permute-done((bf16[32,2048]{1,0:T(8,128)(2,1)S(1)}, bf16[32,2048]{1,0:T(8,128)(2,1)S(1)}, u32[]{:S(2)}, u32[]{:S(2)}) %collective-permute-start.25) | collective-permute-done | bytes 131104 | tf_op jit(solution)/shard_map/rows_7/ppermute | solution.py:23
  62.4 1.9 %experts.5 = (bf16[32,2048]{1,0:T(8,128)(2,1)S(1)}, bf16[32,2048]{1,0:T(8,128)(2,1)S(1)}) custom-call(f32[1,2048]{1,0:T(1,128)S(1)} %bitcast.9, bf16[1,2048,768]{2,1,0:T(8,128)(2,1)S(1)} %copy-done, bf16[1,2048,768]{2,1,0:T(8,128)(2,1)S(1)} %copy-done.1, bf16[1,768,2048]{2,1,0:T(8,128)(2,1)S(1)} %copy-done.2, ...), custom_call_target="tpu_custom_call" | custom-call | flops 131072 | bytes 15728 | tf_op jit(solution)/shard_map/experts/pallas_call | solution.py:219
  64.3 0.5 collective-permute-start.26
  64.8 1.4 %collective-permute-done.23.rest_7_ = bf16[32,2048]{1,0:T(8,128)(2,1)S(1)} collective-permute-done((bf16[32,2048]{1,0:T(8,128)(2,1)S(1)}, bf16[32,2048]{1,0:T(8,128)(2,1)S(1)}, u32[]{:S(2)}, u32[]{:S(2)}) %collective-permute-start.23) | collective-permute-done | bytes 131104 | tf_op jit(solution)/shard_map/back_5/ppermute | solution.py:23
  66.1 1.1 %collective-permute-start.27 = (bf16[32,2048]{1,0:T(8,128)(2,1)S(1)}, bf16[32,2048]{1,0:T(8,128)(2,1)S(1)}, u32[]{:S(2)}, u32[]{:S(2)}) collective-permute-start(bf16[32,2048]{1,0:T(8,128)(2,1)S(1)} %get-tuple-element.86), channel_id=1, source_target_pairs={{0,7},{1,6},{2,5},{3,4},{4,3},{5,2},{6,1},{7,0},{8,15},{9,14},{10,... | collective-permute-start | bytes 393224 | tf_op jit(solution)/shard_map/back_7/ppermute | solution.py:23
  67.2 7.6 %collective-permute-done.17.rest_5_ = bf16[32,2048]{1,0:T(8,128)(2,1)S(1)} collective-permute-done((bf16[32,2048]{1,0:T(8,128)(2,1)S(1)}, bf16[32,2048]{1,0:T(8,128)(2,1)S(1)}, u32[]{:S(2)}, u32[]{:S(2)}) %collective-permute-start.17) | collective-permute-done | bytes 131104 | tf_op jit(solution)/shard_map/back_3/ppermute | solution.py:23
  74.8 0.8 collective-permute-done.26.rest_8_
  75.6 2.8 %collective-permute-done.27.rest_9_ = bf16[32,2048]{1,0:T(8,128)(2,1)S(1)} collective-permute-done((bf16[32,2048]{1,0:T(8,128)(2,1)S(1)}, bf16[32,2048]{1,0:T(8,128)(2,1)S(1)}, u32[]{:S(2)}, u32[]{:S(2)}) %collective-permute-start.27) | collective-permute-done | bytes 131104 | tf_op jit(solution)/shard_map/back_7/ppermute | solution.py:23
  78.4 1.2 %combine.1 = bf16[1,128,2048]{2,1,0:T(8,128)(2,1)} custom-call(bf16[128,256]{1,0:T(8,128)(2,1)S(1)} %get-tuple-element.46.coarse_ref, bf16[128,256]{1,0:T(8,128)(2,1)S(1)} %get-tuple-element.47.fine_ref, bf16[128,1024]{1,0:T(8,128)(2,1)S(1)} %get-tuple-element.56.rest_4_.rest_0_, bf16[128,1024]{1,0:T(8,128)(2,1)S(1)} %get-tuple-element.66.rest_1_, ...), custom_call_target="tpu_custom_call" | custom-call | flops 268435456 | bytes 2097152 | tf_op jit(solution)/shard_map/combine/pallas_call | solution.py:284
  (37 shorter events, 0.7 us)
Async XLA Ops:
  0.0 8.9 %copy-start.8 = (f32[1,128,2]{1,2,0:T(2,128)S(1)}, f32[1,128,2]{1,2,0:T(2,128)}, u32[]{:S(2)}) copy-start(f32[1,128,2]{1,2,0:T(2,128)} %param.14) | copy-start | bytes 3076
  0.0 8.9 %copy-start.7 = (s32[1,128,2]{1,2,0:T(2,128)S(1)}, s32[1,128,2]{1,2,0:T(2,128)}, u32[]{:S(2)}) copy-start(s32[1,128,2]{1,2,0:T(2,128)} %param.13) | copy-start | bytes 3076
  1.2 8.0 %collective-permute-start = (bf16[3,128,256]{2,1,0:T(8,128)(2,1)S(1)}, bf16[3,128,256]{2,1,0:T(8,128)(2,1)S(1)}, u32[]{:S(2)}, u32[]{:S(2)}) collective-permute-start(bf16[3,128,256]{2,1,0:T(8,128)(2,1)S(1)} %get-tuple-element.49), channel_id=1, source_target_pairs={{0,8},{8,0},{16,24},{24,16},{1,9},{9,1},{17,25},{25,17},{2,10},{10... | collective-permute-start | bytes 589832 | tf_op jit(solution)/shard_map/qkv0_/ppermute | solution.py:23
  1.5 8.9 %collective-permute-start.1 = (bf16[3,128,256]{2,1,0:T(8,128)(2,1)S(1)}, bf16[3,128,256]{2,1,0:T(8,128)(2,1)S(1)}, u32[]{:S(2)}, u32[]{:S(2)}) collective-permute-start(bf16[3,128,256]{2,1,0:T(8,128)(2,1)S(1)} %get-tuple-element.50), channel_id=1, source_target_pairs={{0,16},{8,24},{16,0},{24,8},{1,17},{9,25},{17,1},{25,9},{2,18},{10... | collective-permute-start | bytes 589832 | tf_op jit(solution)/shard_map/qkv0_/ppermute | solution.py:23
  2.8 9.5 %collective-permute-start.2 = (bf16[3,128,256]{2,1,0:T(8,128)(2,1)S(1)}, bf16[3,128,256]{2,1,0:T(8,128)(2,1)S(1)}, u32[]{:S(2)}, u32[]{:S(2)}) collective-permute-start(bf16[3,128,256]{2,1,0:T(8,128)(2,1)S(1)} %get-tuple-element.51), channel_id=1, source_target_pairs={{0,24},{8,16},{16,8},{24,0},{1,25},{9,17},{17,9},{25,1},{2,26},{10... | collective-permute-start | bytes 589832 | tf_op jit(solution)/shard_map/qkv0_/ppermute | solution.py:23
  3.9 1.0 %copy-start.3 = (bf16[1,128,2048]{2,1,0:T(8,128)(2,1)S(1)}, bf16[1,128,2048]{2,1,0:T(8,128)(2,1)}, u32[]{:S(2)}) copy-start(bf16[1,128,2048]{2,1,0:T(8,128)(2,1)} %q_ref.3) | copy-start | bytes 1572868
  5.0 1.0 %copy-start.4 = (bf16[1,128,2048]{2,1,0:T(8,128)(2,1)S(1)}, bf16[1,128,2048]{2,1,0:T(8,128)(2,1)}, u32[]{:S(2)}) copy-start(bf16[1,128,2048]{2,1,0:T(8,128)(2,1)} %k_ref.3) | copy-start | bytes 1572868
  6.0 1.0 %copy-start.5 = (bf16[1,128,2048]{2,1,0:T(8,128)(2,1)S(1)}, bf16[1,128,2048]{2,1,0:T(8,128)(2,1)}, u32[]{:S(2)}) copy-start(bf16[1,128,2048]{2,1,0:T(8,128)(2,1)} %v_ref.3) | copy-start | bytes 1572868
  7.4 8.1 %collective-permute-start.6 = (bf16[3,128,256]{2,1,0:T(8,128)(2,1)S(1)}, bf16[3,128,256]{2,1,0:T(8,128)(2,1)S(1)}, u32[]{:S(2)}, u32[]{:S(2)}) collective-permute-start(bf16[3,128,256]{2,1,0:T(8,128)(2,1)S(1)} %get-tuple-element.59), channel_id=1, source_target_pairs={{0,8},{8,0},{16,24},{24,16},{1,9},{9,1},{17,25},{25,17},{2,10},{10... | collective-permute-start | bytes 589832 | tf_op jit(solution)/shard_map/qkv1_/ppermute | solution.py:23
  7.7 10.5 %collective-permute-start.7 = (bf16[3,128,256]{2,1,0:T(8,128)(2,1)S(1)}, bf16[3,128,256]{2,1,0:T(8,128)(2,1)S(1)}, u32[]{:S(2)}, u32[]{:S(2)}) collective-permute-start(bf16[3,128,256]{2,1,0:T(8,128)(2,1)S(1)} %get-tuple-element.60), channel_id=1, source_target_pairs={{0,16},{8,24},{16,0},{24,8},{1,17},{9,25},{17,1},{25,9},{2,18},{10... | collective-permute-start | bytes 589832 | tf_op jit(solution)/shard_map/qkv1_/ppermute | solution.py:23
  9.2 11.5 %collective-permute-start.8 = (bf16[3,128,256]{2,1,0:T(8,128)(2,1)S(1)}, bf16[3,128,256]{2,1,0:T(8,128)(2,1)S(1)}, u32[]{:S(2)}, u32[]{:S(2)}) collective-permute-start(bf16[3,128,256]{2,1,0:T(8,128)(2,1)S(1)} %get-tuple-element.61), channel_id=1, source_target_pairs={{0,24},{8,16},{16,8},{24,0},{1,25},{9,17},{17,9},{25,1},{2,26},{10... | collective-permute-start | bytes 589832 | tf_op jit(solution)/shard_map/qkv1_/ppermute | solution.py:23
  13.2 9.2 %collective-permute-start.3 = (bf16[128,256]{1,0:T(8,128)(2,1)S(1)}, bf16[128,256]{1,0:T(8,128)(2,1)S(1)}, u32[]{:S(2)}, u32[]{:S(2)}) collective-permute-start(bf16[128,256]{1,0:T(8,128)(2,1)S(1)} %get-tuple-element.53), channel_id=1, source_target_pairs={{0,8},{8,0},{16,24},{24,16},{1,9},{9,1},{17,25},{25,17},{2,10},{10... | collective-permute-start | bytes 196616 | tf_op jit(solution)/shard_map/heads0_/ppermute | solution.py:23
  13.6 10.9 %collective-permute-start.4 = (bf16[128,256]{1,0:T(8,128)(2,1)S(1)}, bf16[128,256]{1,0:T(8,128)(2,1)S(1)}, u32[]{:S(2)}, u32[]{:S(2)}) collective-permute-start(bf16[128,256]{1,0:T(8,128)(2,1)S(1)} %get-tuple-element.54), channel_id=1, source_target_pairs={{0,16},{8,24},{16,0},{24,8},{1,17},{9,25},{17,1},{25,9},{2,18},{10... | collective-permute-start | bytes 196616 | tf_op jit(solution)/shard_map/heads0_/ppermute | solution.py:23
  15.5 28.9 %copy-start = (bf16[1,2048,768]{2,1,0:T(8,128)(2,1)S(1)}, bf16[1,2048,768]{2,1,0:T(8,128)(2,1)}, u32[]{:S(2)}) copy-start(bf16[1,2048,768]{2,1,0:T(8,128)(2,1)} %gate_ref.5) | copy-start | bytes 9437188
  15.5 28.9 %copy-start.1 = (bf16[1,2048,768]{2,1,0:T(8,128)(2,1)S(1)}, bf16[1,2048,768]{2,1,0:T(8,128)(2,1)}, u32[]{:S(2)}) copy-start(bf16[1,2048,768]{2,1,0:T(8,128)(2,1)} %up_ref.5) | copy-start | bytes 9437188
  15.5 28.9 %copy-start.2 = (bf16[1,768,2048]{2,1,0:T(8,128)(2,1)S(1)}, bf16[1,768,2048]{2,1,0:T(8,128)(2,1)}, u32[]{:S(2)}) copy-start(bf16[1,768,2048]{2,1,0:T(8,128)(2,1)} %down_ref.5) | copy-start | bytes 9437188
  15.5 28.9 %copy-start.6 = (f32[2048]{0:T(1024)S(1)}, f32[2048]{0:T(1024)}, u32[]{:S(2)}) copy-start(f32[2048]{0:T(1024)} %param.12) | copy-start | bytes 24580
  15.5 8.9 %collective-permute-start.5 = (bf16[128,256]{1,0:T(8,128)(2,1)S(1)}, bf16[128,256]{1,0:T(8,128)(2,1)S(1)}, u32[]{:S(2)}, u32[]{:S(2)}) collective-permute-start(bf16[128,256]{1,0:T(8,128)(2,1)S(1)} %get-tuple-element.55), channel_id=1, source_target_pairs={{0,24},{8,16},{16,8},{24,0},{1,25},{9,17},{17,9},{25,1},{2,26},{10... | collective-permute-start | bytes 196616 | tf_op jit(solution)/shard_map/heads0_/ppermute | solution.py:23
  21.7 9.3 %collective-permute-start.9 = (bf16[128,256]{1,0:T(8,128)(2,1)S(1)}, bf16[128,256]{1,0:T(8,128)(2,1)S(1)}, u32[]{:S(2)}, u32[]{:S(2)}) collective-permute-start(bf16[128,256]{1,0:T(8,128)(2,1)S(1)} %get-tuple-element.63), channel_id=1, source_target_pairs={{0,8},{8,0},{16,24},{24,16},{1,9},{9,1},{17,25},{25,17},{2,10},{10... | collective-permute-start | bytes 196616 | tf_op jit(solution)/shard_map/heads1_/ppermute | solution.py:23
  22.0 9.0 %collective-permute-start.10 = (bf16[128,256]{1,0:T(8,128)(2,1)S(1)}, bf16[128,256]{1,0:T(8,128)(2,1)S(1)}, u32[]{:S(2)}, u32[]{:S(2)}) collective-permute-start(bf16[128,256]{1,0:T(8,128)(2,1)S(1)} %get-tuple-element.64), channel_id=1, source_target_pairs={{0,16},{8,24},{16,0},{24,8},{1,17},{9,25},{17,1},{25,9},{2,18},{10... | collective-permute-start | bytes 196616 | tf_op jit(solution)/shard_map/heads1_/ppermute | solution.py:23
  22.4 8.6 %collective-permute-start.11 = (bf16[128,256]{1,0:T(8,128)(2,1)S(1)}, bf16[128,256]{1,0:T(8,128)(2,1)S(1)}, u32[]{:S(2)}, u32[]{:S(2)}) collective-permute-start(bf16[128,256]{1,0:T(8,128)(2,1)S(1)} %get-tuple-element.65), channel_id=1, source_target_pairs={{0,24},{8,16},{16,8},{24,0},{1,25},{9,17},{17,9},{25,1},{2,26},{10... | collective-permute-start | bytes 196616 | tf_op jit(solution)/shard_map/heads1_/ppermute | solution.py:23
  24.8 13.4 %collective-permute-start.18 = (bf16[32,1024]{1,0:T(8,128)(2,1)S(1)}, bf16[32,1024]{1,0:T(8,128)(2,1)S(1)}, u32[]{:S(2)}, u32[]{:S(2)}) collective-permute-start(bf16[32,1024]{1,0:T(8,128)(2,1)S(1)} %get-tuple-element.75), channel_id=1, source_target_pairs={{0,4},{1,5},{2,6},{3,7},{4,0},{5,1},{6,2},{7,3},{8,12},{9,13},{10,... | collective-permute-start | bytes 196616 | tf_op jit(solution)/shard_map/rows0_4/ppermute | solution.py:23
  27.2 7.7 %collective-permute-start.20 = (bf16[32,1024]{1,0:T(8,128)(2,1)S(1)}, bf16[32,1024]{1,0:T(8,128)(2,1)S(1)}, u32[]{:S(2)}, u32[]{:S(2)}) collective-permute-start(bf16[32,1024]{1,0:T(8,128)(2,1)S(1)} %get-tuple-element.78), channel_id=1, source_target_pairs={{0,5},{1,4},{2,7},{3,6},{4,1},{5,0},{6,3},{7,2},{8,13},{9,12},{10,... | collective-permute-start | bytes 196616 | tf_op jit(solution)/shard_map/rows0_5/ppermute | solution.py:23
  31.7 14.6 %collective-permute-start.12 = (bf16[32,2048]{1,0:T(8,128)(2,1)S(1)}, bf16[32,2048]{1,0:T(8,128)(2,1)S(1)}, u32[]{:S(2)}, u32[]{:S(2)}) collective-permute-start(bf16[32,2048]{1,0:T(8,128)(2,1)S(1)} %get-tuple-element.68), channel_id=1, source_target_pairs={{0,1},{1,0},{2,3},{3,2},{4,5},{5,4},{6,7},{7,6},{8,9},{9,8},{10,11... | collective-permute-start | bytes 393224 | tf_op jit(solution)/shard_map/rows_1/ppermute | solution.py:23
  33.5 17.6 %collective-permute-start.13 = (bf16[32,2048]{1,0:T(8,128)(2,1)S(1)}, bf16[32,2048]{1,0:T(8,128)(2,1)S(1)}, u32[]{:S(2)}, u32[]{:S(2)}) collective-permute-start(bf16[32,2048]{1,0:T(8,128)(2,1)S(1)} %get-tuple-element.69), channel_id=1, source_target_pairs={{0,2},{1,3},{2,0},{3,1},{4,6},{5,7},{6,4},{7,5},{8,10},{9,11},{10,... | collective-permute-start | bytes 393224 | tf_op jit(solution)/shard_map/rows_2/ppermute | solution.py:23
  34.9 7.3 %collective-permute-start.21 = (bf16[32,1024]{1,0:T(8,128)(2,1)S(1)}, bf16[32,1024]{1,0:T(8,128)(2,1)S(1)}, u32[]{:S(2)}, u32[]{:S(2)}) collective-permute-start(bf16[32,1024]{1,0:T(8,128)(2,1)S(1)} %get-tuple-element.80), channel_id=1, source_target_pairs={{0,5},{1,4},{2,7},{3,6},{4,1},{5,0},{6,3},{7,2},{8,13},{9,12},{10,... | collective-permute-start | bytes 196616 | tf_op jit(solution)/shard_map/rows1_5/ppermute | solution.py:23
  38.3 5.3 %collective-permute-start.19 = (bf16[32,1024]{1,0:T(8,128)(2,1)S(1)}, bf16[32,1024]{1,0:T(8,128)(2,1)S(1)}, u32[]{:S(2)}, u32[]{:S(2)}) collective-permute-start(bf16[32,1024]{1,0:T(8,128)(2,1)S(1)} %get-tuple-element.77), channel_id=1, source_target_pairs={{0,4},{1,5},{2,6},{3,7},{4,0},{5,1},{6,2},{7,3},{8,12},{9,13},{10,... | collective-permute-start | bytes 196616 | tf_op jit(solution)/shard_map/rows1_4/ppermute | solution.py:23
  38.5 12.7 %collective-permute-start.14 = (bf16[32,2048]{1,0:T(8,128)(2,1)S(1)}, bf16[32,2048]{1,0:T(8,128)(2,1)S(1)}, u32[]{:S(2)}, u32[]{:S(2)}) collective-permute-start(bf16[32,2048]{1,0:T(8,128)(2,1)S(1)} %get-tuple-element.70), channel_id=1, source_target_pairs={{0,3},{1,2},{2,1},{3,0},{4,7},{5,6},{6,5},{7,4},{8,11},{9,10},{10,... | collective-permute-start | bytes 393224 | tf_op jit(solution)/shard_map/rows_3/ppermute | solution.py:23
  42.2 11.2 %collective-permute-start.24 = (bf16[32,2048]{1,0:T(8,128)(2,1)S(1)}, bf16[32,2048]{1,0:T(8,128)(2,1)S(1)}, u32[]{:S(2)}, u32[]{:S(2)}) collective-permute-start(bf16[32,2048]{1,0:T(8,128)(2,1)S(1)} %get-tuple-element.83), channel_id=1, source_target_pairs={{0,6},{1,7},{2,4},{3,5},{4,2},{5,3},{6,0},{7,1},{8,14},{9,15},{10,... | collective-permute-start | bytes 393224 | tf_op jit(solution)/shard_map/rows_6/ppermute | solution.py:23
  43.6 18.8 %collective-permute-start.25 = (bf16[32,2048]{1,0:T(8,128)(2,1)S(1)}, bf16[32,2048]{1,0:T(8,128)(2,1)S(1)}, u32[]{:S(2)}, u32[]{:S(2)}) collective-permute-start(bf16[32,2048]{1,0:T(8,128)(2,1)S(1)} %get-tuple-element.84), channel_id=1, source_target_pairs={{0,7},{1,6},{2,5},{3,4},{4,3},{5,2},{6,1},{7,0},{8,15},{9,14},{10,... | collective-permute-start | bytes 393224 | tf_op jit(solution)/shard_map/rows_7/ppermute | solution.py:23
  46.3 18.0 %collective-permute-start.22 = (bf16[32,2048]{1,0:T(8,128)(2,1)S(1)}, bf16[32,2048]{1,0:T(8,128)(2,1)S(1)}, u32[]{:S(2)}, u32[]{:S(2)}) collective-permute-start(bf16[32,2048]{1,0:T(8,128)(2,1)S(1)} %get-tuple-element.81), channel_id=1, source_target_pairs={{0,4},{1,5},{2,6},{3,7},{4,0},{5,1},{6,2},{7,3},{8,12},{9,13},{10,... | collective-permute-start | bytes 393224 | tf_op jit(solution)/shard_map/back_4/ppermute | solution.py:23
  51.2 15.0 %collective-permute-start.23 = (bf16[32,2048]{1,0:T(8,128)(2,1)S(1)}, bf16[32,2048]{1,0:T(8,128)(2,1)S(1)}, u32[]{:S(2)}, u32[]{:S(2)}) collective-permute-start(bf16[32,2048]{1,0:T(8,128)(2,1)S(1)} %get-tuple-element.82), channel_id=1, source_target_pairs={{0,5},{1,4},{2,7},{3,6},{4,1},{5,0},{6,3},{7,2},{8,13},{9,12},{10,... | collective-permute-start | bytes 393224 | tf_op jit(solution)/shard_map/back_5/ppermute | solution.py:23
  52.8 14.3 %collective-permute-start.15 = (bf16[32,2048]{1,0:T(8,128)(2,1)S(1)}, bf16[32,2048]{1,0:T(8,128)(2,1)S(1)}, u32[]{:S(2)}, u32[]{:S(2)}) collective-permute-start(bf16[32,2048]{1,0:T(8,128)(2,1)S(1)} %get-tuple-element.72), channel_id=1, source_target_pairs={{0,1},{1,0},{2,3},{3,2},{4,5},{5,4},{6,7},{7,6},{8,9},{9,8},{10,11... | collective-permute-start | bytes 393224 | tf_op jit(solution)/shard_map/back_1/ppermute | solution.py:23
  53.4 13.8 %collective-permute-start.16 = (bf16[32,2048]{1,0:T(8,128)(2,1)S(1)}, bf16[32,2048]{1,0:T(8,128)(2,1)S(1)}, u32[]{:S(2)}, u32[]{:S(2)}) collective-permute-start(bf16[32,2048]{1,0:T(8,128)(2,1)S(1)} %get-tuple-element.73), channel_id=1, source_target_pairs={{0,2},{1,3},{2,0},{3,1},{4,6},{5,7},{6,4},{7,5},{8,10},{9,11},{10,... | collective-permute-start | bytes 393224 | tf_op jit(solution)/shard_map/back_2/ppermute | solution.py:23
  62.4 12.4 %collective-permute-start.17 = (bf16[32,2048]{1,0:T(8,128)(2,1)S(1)}, bf16[32,2048]{1,0:T(8,128)(2,1)S(1)}, u32[]{:S(2)}, u32[]{:S(2)}) collective-permute-start(bf16[32,2048]{1,0:T(8,128)(2,1)S(1)} %get-tuple-element.74), channel_id=1, source_target_pairs={{0,3},{1,2},{2,1},{3,0},{4,7},{5,6},{6,5},{7,4},{8,11},{9,10},{10,... | collective-permute-start | bytes 393224 | tf_op jit(solution)/shard_map/back_3/ppermute | solution.py:23
  64.3 11.3 %collective-permute-start.26 = (bf16[32,2048]{1,0:T(8,128)(2,1)S(1)}, bf16[32,2048]{1,0:T(8,128)(2,1)S(1)}, u32[]{:S(2)}, u32[]{:S(2)}) collective-permute-start(bf16[32,2048]{1,0:T(8,128)(2,1)S(1)} %get-tuple-element.85), channel_id=1, source_target_pairs={{0,6},{1,7},{2,4},{3,5},{4,2},{5,3},{6,0},{7,1},{8,14},{9,15},{10,... | collective-permute-start | bytes 393224 | tf_op jit(solution)/shard_map/back_6/ppermute | solution.py:23
  66.1 12.2 %collective-permute-start.27 = (bf16[32,2048]{1,0:T(8,128)(2,1)S(1)}, bf16[32,2048]{1,0:T(8,128)(2,1)S(1)}, u32[]{:S(2)}, u32[]{:S(2)}) collective-permute-start(bf16[32,2048]{1,0:T(8,128)(2,1)S(1)} %get-tuple-element.86), channel_id=1, source_target_pairs={{0,7},{1,6},{2,5},{3,4},{4,3},{5,2},{6,1},{7,0},{8,15},{9,14},{10,... | collective-permute-start | bytes 393224 | tf_op jit(solution)/shard_map/back_7/ppermute | solution.py:23

commit v5 on v4

--- a/solution.py
+++ b/solution.py
@@ -123,43 +123,33 @@
     return [slots == rank[d : d + 1, :] for d in range(experts)], named
 
 
-def select_kernel(groups, experts, width, earlier, last, ids_ref, *rest):
+def select_kernel(groups, experts, width, earlier, last, chosen_ref, *rest):
     blocks, before = rest[:groups], rest[groups : groups + earlier]
     half, middle = experts // 2, experts // 2 + experts // 4
     count = experts if last else middle - half
     outs = rest[groups + earlier : groups + earlier + count]
-    kept, sems = rest[groups + earlier + count :]
+    kept = rest[groups + earlier + count]
     me = lax.axis_index("seq")
-    copies = []
     for d in range(groups):
         column = pl.multiple_of((me ^ d) * width, 128)
-        copies.append(
-            pltpu.make_async_copy(blocks[d], kept.at[:, pl.ds(column, width)], sems.at[d])
-        )
-    for copy in copies:
-        copy.start()
-    hits, _ = slot_matrix(experts, ids_ref[...])
-    chosen = [jnp.where(h, 1.0, 0.0).astype(BF16) for h in hits]
-    for copy in copies:
-        copy.wait()
-
-    def pick(distances, rows, first):
+        kept[:, pl.ds(column, width)] = blocks[d][...]
+
+    def pick(low, high, rows, targets):
         picked = jnp.dot(
-            jnp.concatenate([chosen[d] for d in distances], axis=0),
-            rows,
-            preferred_element_type=F32,
+            chosen_ref[low * CAP : high * CAP], rows, preferred_element_type=F32
         ).astype(BF16)
-        for i in range(len(distances)):
-            outs[first + i][...] = picked[i * CAP : (i + 1) * CAP]
-
-    pick(range(half, middle), kept[...], 0)
+        for i, target in enumerate(targets):
+            target[...] = picked[i * CAP : (i + 1) * CAP]
+
+    pick(half, middle, kept[...], outs[: middle - half])
     if last:
         parts = [ref[...] for ref in before] + [kept[...]]
         full = jnp.concatenate(parts, axis=1) if earlier else parts[0]
-        pick([*range(middle, experts), *range(half)], full, middle - half)
-
-
-def select(groups, experts, ids, blocks, before, last):
+        pick(middle, experts, full, outs[middle - half : experts - half])
+        pick(0, half, full, outs[experts - half :])
+
+
+def select(groups, experts, chosen, blocks, before, last):
     tokens, width = blocks[0].shape
     part = groups * width
     whole = part * (len(before) + 1)
@@ -171,13 +161,12 @@
     return pl.pallas_call(
         functools.partial(select_kernel, groups, experts, width, len(before), last),
         out_shape=[jax.ShapeDtypeStruct(shape, BF16) for shape in shapes],
-        in_specs=[VMEM] + [HBM] * groups + [VMEM] * len(before),
+        in_specs=[VMEM] * (1 + groups + len(before)),
         out_specs=[VMEM] * len(shapes),
-        scratch_shapes=[pltpu.SemaphoreType.DMA((groups,))],
         compiler_params=params(16),
         cost_estimate=cost(2 * experts * CAP * tokens * part, 8 * tokens * part),
         name="select_rows",
-    )(ids, *blocks, *before)
+    )(chosen, *blocks, *before)
 
 
 def experts_kernel(groups, chunks, width, held, gain_ref, gate_ref, up_ref, down_ref, *rest):
@@ -231,9 +220,11 @@
     )(gain, w_gate, w_up, w_down, *flat)
 
 
-def spread_kernel(experts, ids_ref, gates_ref, coarse_ref, fine_ref):
+def spread_kernel(experts, ids_ref, gates_ref, coarse_ref, fine_ref, chosen_ref):
     ids, gates = ids_ref[...], gates_ref[...]
     hits, named = slot_matrix(experts, ids)
+    for d in range(experts):
+        chosen_ref[d * CAP : (d + 1) * CAP, :] = jnp.where(hits[d], 1.0, 0.0).astype(BF16)
     weight = jnp.where(ids[0:1, :] == named, gates[0:1, :], 0.0) + jnp.where(
         ids[1:2, :] == named, gates[1:2, :], 0.0
     )
@@ -247,9 +238,10 @@
     tokens = ids.shape[1]
     return pl.pallas_call(
         functools.partial(spread_kernel, experts),
-        out_shape=[jax.ShapeDtypeStruct((tokens, experts * CAP), BF16)] * 2,
+        out_shape=[jax.ShapeDtypeStruct((tokens, experts * CAP), BF16)] * 2
+        + [jax.ShapeDtypeStruct((experts * CAP, tokens), BF16)],
         in_specs=[VMEM] * 2,
-        out_specs=[VMEM] * 2,
+        out_specs=[VMEM] * 3,
         compiler_params=params(16),
         cost_estimate=cost(0, 4 * tokens * experts * CAP),
         name="spread_gates",
@@ -331,14 +323,14 @@
     received = [
         exchange(packed[c * groups : (c + 1) * groups], f"qkv{c}_") for c in range(chunks)
     ]
-    weights = spread(experts, ids, gates)
+    *weights, chosen = spread(experts, ids, gates)
     received[-1][0] = after(received[-1][0], weights)
     heads = [attend(width, head_size, received[c]) for c in range(chunks)]
     kept, arrived = [], [[] for _ in range(experts)]
     for c in range(chunks):
         last = c == chunks - 1
         out = heads[c]
-        *rows, own = select(groups, experts, ids, exchange(out, f"heads{c}_"), kept, last)
+        *rows, own = select(groups, experts, chosen, exchange(out, f"heads{c}_"), kept, last)
         kept.append(own)
         for d in range(half, middle):
             row = rows[d - half] if c == 0 else after(rows[d - half], arrived[d][-1])

time: 80.8 us -> 80.6 us (level)
  no operation moved by 1% of the time
where the time goes in v5:
time: 80.6 us; the launch traced here: 79.3 us
  waiting for transfers between devices  33.9 us (42%)
  starting transfers between devices  31.3 us (39%)
  Pallas kernels  10.9 us (14%)
  local copies, waits for them, and re-layouts  3.15 us (4%)
    ppermute x28, waiting for transfers between devices, swap(): return lax.ppermute(x, axis, [(i, i ^ distance) for i in range(size)])  33.9 us
    ppermute x28, starting transfers between devices, swap(): return lax.ppermute(x, axis, [(i, i ^ distance) for i in range(size)])  31.3 us
    pallas_call x3, Pallas kernels, run_experts(): pl.pallas_call(functools.partial(experts_kernel, groups, chunks, width, h...  5.42 us
    unnamed x18, local copies, waits for them, and re-layouts  3.15 us
    pallas_call x2, Pallas kernels, attend(): pl.pallas_call(functools.partial(attend_kernel, groups, width, head_size)...  1.9 us
  transfers between devices with their start and end apart: 28, of which 12 were waited for; matrix products, arithmetic and copies ran while one was open for 0% of the time, Pallas kernels for 11%

profile of v5, /device:TPU:11, one launch (start us, length us, event | category | flops | bytes accessed | tf_op | source)
XLA Modules:
  0.0 79.3 jit_solution(13171022100083025893)
XLA Ops:
  0.0 1.2 %pack_heads.3 = (bf16[3,128,256]{2,1,0:T(8,128)(2,1)S(1)}, bf16[3,128,256]{2,1,0:T(8,128)(2,1)S(1)}, bf16[3,128,256]{2,1,0:T(8,128)(2,1)S(1)}) custom-call(bf16[1,128,2048]{2,1,0:T(8,128)(2,1)} %q_ref.3, bf16[1,128,2048]{2,1,0:T(8,128)(2,1)} %k_ref.3, bf16[1,128,2048]{2,1,0:T(8,128)(2,1)} %v_ref.3), custom_call_target="tpu_custom_call" | custom-call | bytes 1179648 | tf_op jit(solution)/shard_map/pack_heads/pallas_call | solution.py:55
  1.2 0.3 collective-permute-start
  1.5 1.2 %collective-permute-start.1 = (bf16[3,128,256]{2,1,0:T(8,128)(2,1)S(1)}, bf16[3,128,256]{2,1,0:T(8,128)(2,1)S(1)}, u32[]{:S(2)}, u32[]{:S(2)}) collective-permute-start(bf16[3,128,256]{2,1,0:T(8,128)(2,1)S(1)} %get-tuple-element.52), channel_id=1, source_target_pairs={{0,16},{8,24},{16,0},{24,8},{1,17},{9,25},{17,1},{25,9},{2,18},{10... | collective-permute-start | bytes 589832 | tf_op jit(solution)/shard_map/qkv0_/ppermute | solution.py:23
  2.8 1.2 %collective-permute-start.2 = (bf16[3,128,256]{2,1,0:T(8,128)(2,1)S(1)}, bf16[3,128,256]{2,1,0:T(8,128)(2,1)S(1)}, u32[]{:S(2)}, u32[]{:S(2)}) collective-permute-start(bf16[3,128,256]{2,1,0:T(8,128)(2,1)S(1)} %get-tuple-element.53), channel_id=1, source_target_pairs={{0,24},{8,16},{16,8},{24,0},{1,25},{9,17},{17,9},{25,1},{2,26},{10... | collective-permute-start | bytes 589832 | tf_op jit(solution)/shard_map/qkv0_/ppermute | solution.py:23
  3.9 1.0 %copy-done.3 = bf16[1,128,2048]{2,1,0:T(8,128)(2,1)S(1)} copy-done((bf16[1,128,2048]{2,1,0:T(8,128)(2,1)S(1)}, bf16[1,128,2048]{2,1,0:T(8,128)(2,1)}, u32[]{:S(2)}) %copy-start.3) | copy-done | bytes 524312
  5.0 1.0 %copy-done.4 = bf16[1,128,2048]{2,1,0:T(8,128)(2,1)S(1)} copy-done((bf16[1,128,2048]{2,1,0:T(8,128)(2,1)S(1)}, bf16[1,128,2048]{2,1,0:T(8,128)(2,1)}, u32[]{:S(2)}) %copy-start.4) | copy-done | bytes 524312
  6.0 1.0 %copy-done.5 = bf16[1,128,2048]{2,1,0:T(8,128)(2,1)S(1)} copy-done((bf16[1,128,2048]{2,1,0:T(8,128)(2,1)S(1)}, bf16[1,128,2048]{2,1,0:T(8,128)(2,1)}, u32[]{:S(2)}) %copy-start.5) | copy-done | bytes 524312
  7.1 0.3 pack_heads.2
  7.4 0.3 collective-permute-start.6
  7.7 1.2 %collective-permute-start.7 = (bf16[3,128,256]{2,1,0:T(8,128)(2,1)S(1)}, bf16[3,128,256]{2,1,0:T(8,128)(2,1)S(1)}, u32[]{:S(2)}, u32[]{:S(2)}) collective-permute-start(bf16[3,128,256]{2,1,0:T(8,128)(2,1)S(1)} %get-tuple-element.62), channel_id=1, source_target_pairs={{0,16},{8,24},{16,0},{24,8},{1,17},{9,25},{17,1},{25,9},{2,18},{10... | collective-permute-start | bytes 589832 | tf_op jit(solution)/shard_map/qkv1_/ppermute | solution.py:23
  8.9 0.2 spread_gates.1
  9.2 1.2 %collective-permute-start.8 = (bf16[3,128,256]{2,1,0:T(8,128)(2,1)S(1)}, bf16[3,128,256]{2,1,0:T(8,128)(2,1)S(1)}, u32[]{:S(2)}, u32[]{:S(2)}) collective-permute-start(bf16[3,128,256]{2,1,0:T(8,128)(2,1)S(1)} %get-tuple-element.63), channel_id=1, source_target_pairs={{0,24},{8,16},{16,8},{24,0},{1,25},{9,17},{17,9},{25,1},{2,26},{10... | collective-permute-start | bytes 589832 | tf_op jit(solution)/shard_map/qkv1_/ppermute | solution.py:23
  10.4 1.8 %collective-permute-done.2.rest_3_ = bf16[3,128,256]{2,1,0:T(8,128)(2,1)S(1)} collective-permute-done((bf16[3,128,256]{2,1,0:T(8,128)(2,1)S(1)}, bf16[3,128,256]{2,1,0:T(8,128)(2,1)S(1)}, u32[]{:S(2)}, u32[]{:S(2)}) %collective-permute-start.2) | collective-permute-done | bytes 196640 | tf_op jit(solution)/shard_map/qkv0_/ppermute | solution.py:23
  12.3 0.9 %attend.2 = (bf16[128,256]{1,0:T(8,128)(2,1)S(1)}, bf16[128,256]{1,0:T(8,128)(2,1)S(1)}, bf16[128,256]{1,0:T(8,128)(2,1)S(1)}, bf16[128,256]{1,0:T(8,128)(2,1)S(1)}) custom-call(bf16[3,128,256]{2,1,0:T(8,128)(2,1)S(1)} %get-tuple-element.50.rest_0_, bf16[3,128,256]{2,1,0:T(8,128)(2,1)S(1)} %collective-permute-done.rest_1_, ...), custom_call_target="tpu_custom_call" | custom-call | flops 10737418240 | bytes 10485760 | tf_op jit(solution)/shard_map/attend/pallas_call | solution.py:98
  13.2 0.3 collective-permute-start.3
  13.5 0.2 collective-permute-start.4
  13.8 1.8 %collective-permute-done.6.rest_1_ = bf16[3,128,256]{2,1,0:T(8,128)(2,1)S(1)} collective-permute-done((bf16[3,128,256]{2,1,0:T(8,128)(2,1)S(1)}, bf16[3,128,256]{2,1,0:T(8,128)(2,1)S(1)}, u32[]{:S(2)}, u32[]{:S(2)}) %collective-permute-start.6) | collective-permute-done | bytes 196640 | tf_op jit(solution)/shard_map/qkv1_/ppermute | solution.py:23
  15.5 1.3 %collective-permute-start.5 = (bf16[128,256]{1,0:T(8,128)(2,1)S(1)}, bf16[128,256]{1,0:T(8,128)(2,1)S(1)}, u32[]{:S(2)}, u32[]{:S(2)}) collective-permute-start(bf16[128,256]{1,0:T(8,128)(2,1)S(1)} %get-tuple-element.57), channel_id=1, source_target_pairs={{0,24},{8,16},{16,8},{24,0},{1,25},{9,17},{17,9},{25,1},{2,26},{10... | collective-permute-start | bytes 196616 | tf_op jit(solution)/shard_map/heads0_/ppermute | solution.py:23
  16.8 1.4 %collective-permute-done.7.rest_2_ = bf16[3,128,256]{2,1,0:T(8,128)(2,1)S(1)} collective-permute-done((bf16[3,128,256]{2,1,0:T(8,128)(2,1)S(1)}, bf16[3,128,256]{2,1,0:T(8,128)(2,1)S(1)}, u32[]{:S(2)}, u32[]{:S(2)}) %collective-permute-start.7) | collective-permute-done | bytes 196640 | tf_op jit(solution)/shard_map/qkv1_/ppermute | solution.py:23
  18.2 2.5 %collective-permute-done.8.rest_3_ = bf16[3,128,256]{2,1,0:T(8,128)(2,1)S(1)} collective-permute-done((bf16[3,128,256]{2,1,0:T(8,128)(2,1)S(1)}, bf16[3,128,256]{2,1,0:T(8,128)(2,1)S(1)}, u32[]{:S(2)}, u32[]{:S(2)}) %collective-permute-start.8) | collective-permute-done | bytes 196640 | tf_op jit(solution)/shard_map/qkv1_/ppermute | solution.py:23
  20.7 1.0 %attend.3 = (bf16[128,256]{1,0:T(8,128)(2,1)S(1)}, bf16[128,256]{1,0:T(8,128)(2,1)S(1)}, bf16[128,256]{1,0:T(8,128)(2,1)S(1)}, bf16[128,256]{1,0:T(8,128)(2,1)S(1)}) custom-call(bf16[3,128,256]{2,1,0:T(8,128)(2,1)S(1)} %get-tuple-element.60.rest_0_, bf16[3,128,256]{2,1,0:T(8,128)(2,1)S(1)} %collective-permute-done.6.rest_1_, ...), custom_call_target="tpu_custom_call" | custom-call | flops 10737418240 | bytes 10485760 | tf_op jit(solution)/shard_map/attend/pallas_call | solution.py:98
  21.7 0.3 collective-permute-start.9
  22.0 0.4 collective-permute-start.10
  22.4 2.0 %collective-permute-start.11 = (bf16[128,256]{1,0:T(8,128)(2,1)S(1)}, bf16[128,256]{1,0:T(8,128)(2,1)S(1)}, u32[]{:S(2)}, u32[]{:S(2)}) collective-permute-start(bf16[128,256]{1,0:T(8,128)(2,1)S(1)} %get-tuple-element.67), channel_id=1, source_target_pairs={{0,24},{8,16},{16,8},{24,0},{1,25},{9,17},{17,9},{25,1},{2,26},{10... | collective-permute-start | bytes 196616 | tf_op jit(solution)/shard_map/heads1_/ppermute | solution.py:23
  24.6 2.4 %collective-permute-start.18 = (bf16[32,1024]{1,0:T(8,128)(2,1)S(1)}, bf16[32,1024]{1,0:T(8,128)(2,1)S(1)}, u32[]{:S(2)}, u32[]{:S(2)}) collective-permute-start(bf16[32,1024]{1,0:T(8,128)(2,1)S(1)} %get-tuple-element.77), channel_id=1, source_target_pairs={{0,4},{1,5},{2,6},{3,7},{4,0},{5,1},{6,2},{7,3},{8,12},{9,13},{10,... | collective-permute-start | bytes 196616 | tf_op jit(solution)/shard_map/rows0_4/ppermute | solution.py:23
  27.0 3.8 %collective-permute-start.20 = (bf16[32,1024]{1,0:T(8,128)(2,1)S(1)}, bf16[32,1024]{1,0:T(8,128)(2,1)S(1)}, u32[]{:S(2)}, u32[]{:S(2)}) collective-permute-start(bf16[32,1024]{1,0:T(8,128)(2,1)S(1)} %get-tuple-element.80), channel_id=1, source_target_pairs={{0,5},{1,4},{2,7},{3,6},{4,1},{5,0},{6,3},{7,2},{8,13},{9,12},{10,... | collective-permute-start | bytes 196616 | tf_op jit(solution)/shard_map/rows0_5/ppermute | solution.py:23
  30.8 0.4 select_rows.3
  31.3 2.1 %collective-permute-start.12 = (bf16[32,2048]{1,0:T(8,128)(2,1)S(1)}, bf16[32,2048]{1,0:T(8,128)(2,1)S(1)}, u32[]{:S(2)}, u32[]{:S(2)}) collective-permute-start(bf16[32,2048]{1,0:T(8,128)(2,1)S(1)} %get-tuple-element.70), channel_id=1, source_target_pairs={{0,1},{1,0},{2,3},{3,2},{4,5},{5,4},{6,7},{7,6},{8,9},{9,8},{10,11... | collective-permute-start | bytes 393224 | tf_op jit(solution)/shard_map/rows_1/ppermute | solution.py:23
  33.5 1.2 %collective-permute-done.20.rest_2_ = bf16[32,1024]{1,0:T(8,128)(2,1)S(1)} collective-permute-done((bf16[32,1024]{1,0:T(8,128)(2,1)S(1)}, bf16[32,1024]{1,0:T(8,128)(2,1)S(1)}, u32[]{:S(2)}, u32[]{:S(2)}) %collective-permute-start.20) | collective-permute-done | bytes 65568 | tf_op jit(solution)/shard_map/rows0_5/ppermute | solution.py:23
  34.7 3.4 %collective-permute-start.21 = (bf16[32,1024]{1,0:T(8,128)(2,1)S(1)}, bf16[32,1024]{1,0:T(8,128)(2,1)S(1)}, u32[]{:S(2)}, u32[]{:S(2)}) collective-permute-start(bf16[32,1024]{1,0:T(8,128)(2,1)S(1)} %get-tuple-element.82), channel_id=1, source_target_pairs={{0,5},{1,4},{2,7},{3,6},{4,1},{5,0},{6,3},{7,2},{8,13},{9,12},{10,... | collective-permute-start | bytes 196616 | tf_op jit(solution)/shard_map/rows1_5/ppermute | solution.py:23
  38.3 0.2 collective-permute-start.14
  38.5 3.5 %collective-permute-done.21.rest_3_ = bf16[32,1024]{1,0:T(8,128)(2,1)S(1)} collective-permute-done((bf16[32,1024]{1,0:T(8,128)(2,1)S(1)}, bf16[32,1024]{1,0:T(8,128)(2,1)S(1)}, u32[]{:S(2)}, u32[]{:S(2)}) %collective-permute-start.21) | collective-permute-done | bytes 65568 | tf_op jit(solution)/shard_map/rows1_5/ppermute | solution.py:23
  42.0 1.4 %collective-permute-done.19.rest_1_ = bf16[32,1024]{1,0:T(8,128)(2,1)S(1)} collective-permute-done((bf16[32,1024]{1,0:T(8,128)(2,1)S(1)}, bf16[32,1024]{1,0:T(8,128)(2,1)S(1)}, u32[]{:S(2)}, u32[]{:S(2)}) %collective-permute-start.19) | collective-permute-done | bytes 65568 | tf_op jit(solution)/shard_map/rows1_4/ppermute | solution.py:23
  43.4 0.8 collective-permute-start.25
  44.2 1.9 %experts.4 = (bf16[32,2048]{1,0:T(8,128)(2,1)S(1)}, bf16[32,2048]{1,0:T(8,128)(2,1)S(1)}) custom-call(f32[1,2048]{1,0:T(1,128)S(1)} %bitcast.7, bf16[1,2048,768]{2,1,0:T(8,128)(2,1)S(1)} %copy-done, bf16[1,2048,768]{2,1,0:T(8,128)(2,1)S(1)} %copy-done.1, bf16[1,768,2048]{2,1,0:T(8,128)(2,1)S(1)} %copy-done.2, ...), custom_call_target="tpu_custom_call" | custom-call | flops 131072 | bytes 15728 | tf_op jit(solution)/shard_map/experts/pallas_call | solution.py:208
  46.1 4.9 %collective-permute-start.22 = (bf16[32,2048]{1,0:T(8,128)(2,1)S(1)}, bf16[32,2048]{1,0:T(8,128)(2,1)S(1)}, u32[]{:S(2)}, u32[]{:S(2)}) collective-permute-start(bf16[32,2048]{1,0:T(8,128)(2,1)S(1)} %get-tuple-element.83), channel_id=1, source_target_pairs={{0,4},{1,5},{2,6},{3,7},{4,0},{5,1},{6,2},{7,3},{8,12},{9,13},{10,... | collective-permute-start | bytes 393224 | tf_op jit(solution)/shard_map/back_4/ppermute | solution.py:23
  51.0 1.7 %experts.3 = (bf16[32,2048]{1,0:T(8,128)(2,1)S(1)}, bf16[32,2048]{1,0:T(8,128)(2,1)S(1)}, bf16[32,2048]{1,0:T(8,128)(2,1)S(1)}, bf16[32,2048]{1,0:T(8,128)(2,1)S(1)}) custom-call(f32[1,2048]{1,0:T(1,128)S(1)} %bitcast.8, bf16[1,2048,768]{2,1,0:T(8,128)(2,1)S(1)} %copy-done, bf16[1,2048,768]{2,1,0:T(8,128)(2,1)S(1)} %copy-done.1, ...), custom_call_target="tpu_custom_call" | custom-call | flops 262144 | bytes 15728 | tf_op jit(solution)/shard_map/experts/pallas_call | solution.py:208
  52.6 0.5 collective-permute-start.15
  53.2 1.4 %collective-permute-start.16 = (bf16[32,2048]{1,0:T(8,128)(2,1)S(1)}, bf16[32,2048]{1,0:T(8,128)(2,1)S(1)}, u32[]{:S(2)}, u32[]{:S(2)}) collective-permute-start(bf16[32,2048]{1,0:T(8,128)(2,1)S(1)} %get-tuple-element.75), channel_id=1, source_target_pairs={{0,2},{1,3},{2,0},{3,1},{4,6},{5,7},{6,4},{7,5},{8,10},{9,11},{10,... | collective-permute-start | bytes 393224 | tf_op jit(solution)/shard_map/back_2/ppermute | solution.py:23
  54.6 7.6 %collective-permute-done.25.rest_1_ = bf16[32,2048]{1,0:T(8,128)(2,1)S(1)} collective-permute-done((bf16[32,2048]{1,0:T(8,128)(2,1)S(1)}, bf16[32,2048]{1,0:T(8,128)(2,1)S(1)}, u32[]{:S(2)}, u32[]{:S(2)}) %collective-permute-start.25) | collective-permute-done | bytes 131104 | tf_op jit(solution)/shard_map/rows_7/ppermute | solution.py:23
  62.2 1.9 %experts.5 = (bf16[32,2048]{1,0:T(8,128)(2,1)S(1)}, bf16[32,2048]{1,0:T(8,128)(2,1)S(1)}) custom-call(f32[1,2048]{1,0:T(1,128)S(1)} %bitcast.9, bf16[1,2048,768]{2,1,0:T(8,128)(2,1)S(1)} %copy-done, bf16[1,2048,768]{2,1,0:T(8,128)(2,1)S(1)} %copy-done.1, bf16[1,768,2048]{2,1,0:T(8,128)(2,1)S(1)} %copy-done.2, ...), custom_call_target="tpu_custom_call" | custom-call | flops 131072 | bytes 15728 | tf_op jit(solution)/shard_map/experts/pallas_call | solution.py:208
  64.1 0.5 collective-permute-start.26
  64.6 1.4 %collective-permute-done.23.rest_7_ = bf16[32,2048]{1,0:T(8,128)(2,1)S(1)} collective-permute-done((bf16[32,2048]{1,0:T(8,128)(2,1)S(1)}, bf16[32,2048]{1,0:T(8,128)(2,1)S(1)}, u32[]{:S(2)}, u32[]{:S(2)}) %collective-permute-start.23) | collective-permute-done | bytes 131104 | tf_op jit(solution)/shard_map/back_5/ppermute | solution.py:23
  65.9 1.1 %collective-permute-start.27 = (bf16[32,2048]{1,0:T(8,128)(2,1)S(1)}, bf16[32,2048]{1,0:T(8,128)(2,1)S(1)}, u32[]{:S(2)}, u32[]{:S(2)}) collective-permute-start(bf16[32,2048]{1,0:T(8,128)(2,1)S(1)} %get-tuple-element.88), channel_id=1, source_target_pairs={{0,7},{1,6},{2,5},{3,4},{4,3},{5,2},{6,1},{7,0},{8,15},{9,14},{10,... | collective-permute-start | bytes 393224 | tf_op jit(solution)/shard_map/back_7/ppermute | solution.py:23
  67.0 7.6 %collective-permute-done.17.rest_5_ = bf16[32,2048]{1,0:T(8,128)(2,1)S(1)} collective-permute-done((bf16[32,2048]{1,0:T(8,128)(2,1)S(1)}, bf16[32,2048]{1,0:T(8,128)(2,1)S(1)}, u32[]{:S(2)}, u32[]{:S(2)}) %collective-permute-start.17) | collective-permute-done | bytes 131104 | tf_op jit(solution)/shard_map/back_3/ppermute | solution.py:23
  74.6 0.8 %collective-permute-done.26.rest_8_ = bf16[32,2048]{1,0:T(8,128)(2,1)S(1)} collective-permute-done((bf16[32,2048]{1,0:T(8,128)(2,1)S(1)}, bf16[32,2048]{1,0:T(8,128)(2,1)S(1)}, u32[]{:S(2)}, u32[]{:S(2)}) %collective-permute-start.26) | collective-permute-done | bytes 131104 | tf_op jit(solution)/shard_map/back_6/ppermute | solution.py:23
  75.4 2.8 %collective-permute-done.27.rest_9_ = bf16[32,2048]{1,0:T(8,128)(2,1)S(1)} collective-permute-done((bf16[32,2048]{1,0:T(8,128)(2,1)S(1)}, bf16[32,2048]{1,0:T(8,128)(2,1)S(1)}, u32[]{:S(2)}, u32[]{:S(2)}) %collective-permute-start.27) | collective-permute-done | bytes 131104 | tf_op jit(solution)/shard_map/back_7/ppermute | solution.py:23
  78.2 1.1 %combine.1 = bf16[1,128,2048]{2,1,0:T(8,128)(2,1)} custom-call(bf16[128,256]{1,0:T(8,128)(2,1)S(1)} %get-tuple-element.47.coarse_ref, bf16[128,256]{1,0:T(8,128)(2,1)S(1)} %get-tuple-element.48.fine_ref, bf16[128,1024]{1,0:T(8,128)(2,1)S(1)} %get-tuple-element.58.rest_4_.rest_0_, bf16[128,1024]{1,0:T(8,128)(2,1)S(1)} %get-tuple-element.68.rest_1_, ...), custom_call_target="tpu_custom_call" | custom-call | flops 268435456 | bytes 2097152 | tf_op jit(solution)/shard_map/combine/pallas_call | solution.py:276
  (37 shorter events, 0.7 us)
Async XLA Ops:
  0.0 8.9 %copy-start.8 = (f32[1,128,2]{1,2,0:T(2,128)S(1)}, f32[1,128,2]{1,2,0:T(2,128)}, u32[]{:S(2)}) copy-start(f32[1,128,2]{1,2,0:T(2,128)} %param.14) | copy-start | bytes 3076
  0.0 8.9 %copy-start.7 = (s32[1,128,2]{1,2,0:T(2,128)S(1)}, s32[1,128,2]{1,2,0:T(2,128)}, u32[]{:S(2)}) copy-start(s32[1,128,2]{1,2,0:T(2,128)} %param.13) | copy-start | bytes 3076
  1.2 8.0 %collective-permute-start = (bf16[3,128,256]{2,1,0:T(8,128)(2,1)S(1)}, bf16[3,128,256]{2,1,0:T(8,128)(2,1)S(1)}, u32[]{:S(2)}, u32[]{:S(2)}) collective-permute-start(bf16[3,128,256]{2,1,0:T(8,128)(2,1)S(1)} %get-tuple-element.51), channel_id=1, source_target_pairs={{0,8},{8,0},{16,24},{24,16},{1,9},{9,1},{17,25},{25,17},{2,10},{10... | collective-permute-start | bytes 589832 | tf_op jit(solution)/shard_map/qkv0_/ppermute | solution.py:23
  1.5 8.9 %collective-permute-start.1 = (bf16[3,128,256]{2,1,0:T(8,128)(2,1)S(1)}, bf16[3,128,256]{2,1,0:T(8,128)(2,1)S(1)}, u32[]{:S(2)}, u32[]{:S(2)}) collective-permute-start(bf16[3,128,256]{2,1,0:T(8,128)(2,1)S(1)} %get-tuple-element.52), channel_id=1, source_target_pairs={{0,16},{8,24},{16,0},{24,8},{1,17},{9,25},{17,1},{25,9},{2,18},{10... | collective-permute-start | bytes 589832 | tf_op jit(solution)/shard_map/qkv0_/ppermute | solution.py:23
  2.8 9.5 %collective-permute-start.2 = (bf16[3,128,256]{2,1,0:T(8,128)(2,1)S(1)}, bf16[3,128,256]{2,1,0:T(8,128)(2,1)S(1)}, u32[]{:S(2)}, u32[]{:S(2)}) collective-permute-start(bf16[3,128,256]{2,1,0:T(8,128)(2,1)S(1)} %get-tuple-element.53), channel_id=1, source_target_pairs={{0,24},{8,16},{16,8},{24,0},{1,25},{9,17},{17,9},{25,1},{2,26},{10... | collective-permute-start | bytes 589832 | tf_op jit(solution)/shard_map/qkv0_/ppermute | solution.py:23
  3.9 1.0 %copy-start.3 = (bf16[1,128,2048]{2,1,0:T(8,128)(2,1)S(1)}, bf16[1,128,2048]{2,1,0:T(8,128)(2,1)}, u32[]{:S(2)}) copy-start(bf16[1,128,2048]{2,1,0:T(8,128)(2,1)} %q_ref.3) | copy-start | bytes 1572868
  5.0 1.0 %copy-start.4 = (bf16[1,128,2048]{2,1,0:T(8,128)(2,1)S(1)}, bf16[1,128,2048]{2,1,0:T(8,128)(2,1)}, u32[]{:S(2)}) copy-start(bf16[1,128,2048]{2,1,0:T(8,128)(2,1)} %k_ref.3) | copy-start | bytes 1572868
  6.0 1.0 %copy-start.5 = (bf16[1,128,2048]{2,1,0:T(8,128)(2,1)S(1)}, bf16[1,128,2048]{2,1,0:T(8,128)(2,1)}, u32[]{:S(2)}) copy-start(bf16[1,128,2048]{2,1,0:T(8,128)(2,1)} %v_ref.3) | copy-start | bytes 1572868
  7.4 8.1 %collective-permute-start.6 = (bf16[3,128,256]{2,1,0:T(8,128)(2,1)S(1)}, bf16[3,128,256]{2,1,0:T(8,128)(2,1)S(1)}, u32[]{:S(2)}, u32[]{:S(2)}) collective-permute-start(bf16[3,128,256]{2,1,0:T(8,128)(2,1)S(1)} %get-tuple-element.61), channel_id=1, source_target_pairs={{0,8},{8,0},{16,24},{24,16},{1,9},{9,1},{17,25},{25,17},{2,10},{10... | collective-permute-start | bytes 589832 | tf_op jit(solution)/shard_map/qkv1_/ppermute | solution.py:23
  7.7 10.5 %collective-permute-start.7 = (bf16[3,128,256]{2,1,0:T(8,128)(2,1)S(1)}, bf16[3,128,256]{2,1,0:T(8,128)(2,1)S(1)}, u32[]{:S(2)}, u32[]{:S(2)}) collective-permute-start(bf16[3,128,256]{2,1,0:T(8,128)(2,1)S(1)} %get-tuple-element.62), channel_id=1, source_target_pairs={{0,16},{8,24},{16,0},{24,8},{1,17},{9,25},{17,1},{25,9},{2,18},{10... | collective-permute-start | bytes 589832 | tf_op jit(solution)/shard_map/qkv1_/ppermute | solution.py:23
  9.2 11.5 %collective-permute-start.8 = (bf16[3,128,256]{2,1,0:T(8,128)(2,1)S(1)}, bf16[3,128,256]{2,1,0:T(8,128)(2,1)S(1)}, u32[]{:S(2)}, u32[]{:S(2)}) collective-permute-start(bf16[3,128,256]{2,1,0:T(8,128)(2,1)S(1)} %get-tuple-element.63), channel_id=1, source_target_pairs={{0,24},{8,16},{16,8},{24,0},{1,25},{9,17},{17,9},{25,1},{2,26},{10... | collective-permute-start | bytes 589832 | tf_op jit(solution)/shard_map/qkv1_/ppermute | solution.py:23
  13.2 9.2 %collective-permute-start.3 = (bf16[128,256]{1,0:T(8,128)(2,1)S(1)}, bf16[128,256]{1,0:T(8,128)(2,1)S(1)}, u32[]{:S(2)}, u32[]{:S(2)}) collective-permute-start(bf16[128,256]{1,0:T(8,128)(2,1)S(1)} %get-tuple-element.55), channel_id=1, source_target_pairs={{0,8},{8,0},{16,24},{24,16},{1,9},{9,1},{17,25},{25,17},{2,10},{10... | collective-permute-start | bytes 196616 | tf_op jit(solution)/shard_map/heads0_/ppermute | solution.py:23
  13.5 10.9 %collective-permute-start.4 = (bf16[128,256]{1,0:T(8,128)(2,1)S(1)}, bf16[128,256]{1,0:T(8,128)(2,1)S(1)}, u32[]{:S(2)}, u32[]{:S(2)}) collective-permute-start(bf16[128,256]{1,0:T(8,128)(2,1)S(1)} %get-tuple-element.56), channel_id=1, source_target_pairs={{0,16},{8,24},{16,0},{24,8},{1,17},{9,25},{17,1},{25,9},{2,18},{10... | collective-permute-start | bytes 196616 | tf_op jit(solution)/shard_map/heads0_/ppermute | solution.py:23
  15.5 28.7 %copy-start = (bf16[1,2048,768]{2,1,0:T(8,128)(2,1)S(1)}, bf16[1,2048,768]{2,1,0:T(8,128)(2,1)}, u32[]{:S(2)}) copy-start(bf16[1,2048,768]{2,1,0:T(8,128)(2,1)} %gate_ref.5) | copy-start | bytes 9437188
  15.5 28.7 %copy-start.1 = (bf16[1,2048,768]{2,1,0:T(8,128)(2,1)S(1)}, bf16[1,2048,768]{2,1,0:T(8,128)(2,1)}, u32[]{:S(2)}) copy-start(bf16[1,2048,768]{2,1,0:T(8,128)(2,1)} %up_ref.5) | copy-start | bytes 9437188
  15.5 28.7 %copy-start.2 = (bf16[1,768,2048]{2,1,0:T(8,128)(2,1)S(1)}, bf16[1,768,2048]{2,1,0:T(8,128)(2,1)}, u32[]{:S(2)}) copy-start(bf16[1,768,2048]{2,1,0:T(8,128)(2,1)} %down_ref.5) | copy-start | bytes 9437188
  15.5 28.7 %copy-start.6 = (f32[2048]{0:T(1024)S(1)}, f32[2048]{0:T(1024)}, u32[]{:S(2)}) copy-start(f32[2048]{0:T(1024)} %param.12) | copy-start | bytes 24580
  15.5 8.9 %collective-permute-start.5 = (bf16[128,256]{1,0:T(8,128)(2,1)S(1)}, bf16[128,256]{1,0:T(8,128)(2,1)S(1)}, u32[]{:S(2)}, u32[]{:S(2)}) collective-permute-start(bf16[128,256]{1,0:T(8,128)(2,1)S(1)} %get-tuple-element.57), channel_id=1, source_target_pairs={{0,24},{8,16},{16,8},{24,0},{1,25},{9,17},{17,9},{25,1},{2,26},{10... | collective-permute-start | bytes 196616 | tf_op jit(solution)/shard_map/heads0_/ppermute | solution.py:23
  21.7 9.1 %collective-permute-start.9 = (bf16[128,256]{1,0:T(8,128)(2,1)S(1)}, bf16[128,256]{1,0:T(8,128)(2,1)S(1)}, u32[]{:S(2)}, u32[]{:S(2)}) collective-permute-start(bf16[128,256]{1,0:T(8,128)(2,1)S(1)} %get-tuple-element.65), channel_id=1, source_target_pairs={{0,8},{8,0},{16,24},{24,16},{1,9},{9,1},{17,25},{25,17},{2,10},{10... | collective-permute-start | bytes 196616 | tf_op jit(solution)/shard_map/heads1_/ppermute | solution.py:23
  22.0 8.8 %collective-permute-start.10 = (bf16[128,256]{1,0:T(8,128)(2,1)S(1)}, bf16[128,256]{1,0:T(8,128)(2,1)S(1)}, u32[]{:S(2)}, u32[]{:S(2)}) collective-permute-start(bf16[128,256]{1,0:T(8,128)(2,1)S(1)} %get-tuple-element.66), channel_id=1, source_target_pairs={{0,16},{8,24},{16,0},{24,8},{1,17},{9,25},{17,1},{25,9},{2,18},{10... | collective-permute-start | bytes 196616 | tf_op jit(solution)/shard_map/heads1_/ppermute | solution.py:23
  22.4 8.4 %collective-permute-start.11 = (bf16[128,256]{1,0:T(8,128)(2,1)S(1)}, bf16[128,256]{1,0:T(8,128)(2,1)S(1)}, u32[]{:S(2)}, u32[]{:S(2)}) collective-permute-start(bf16[128,256]{1,0:T(8,128)(2,1)S(1)} %get-tuple-element.67), channel_id=1, source_target_pairs={{0,24},{8,16},{16,8},{24,0},{1,25},{9,17},{17,9},{25,1},{2,26},{10... | collective-permute-start | bytes 196616 | tf_op jit(solution)/shard_map/heads1_/ppermute | solution.py:23
  24.6 13.4 %collective-permute-start.18 = (bf16[32,1024]{1,0:T(8,128)(2,1)S(1)}, bf16[32,1024]{1,0:T(8,128)(2,1)S(1)}, u32[]{:S(2)}, u32[]{:S(2)}) collective-permute-start(bf16[32,1024]{1,0:T(8,128)(2,1)S(1)} %get-tuple-element.77), channel_id=1, source_target_pairs={{0,4},{1,5},{2,6},{3,7},{4,0},{5,1},{6,2},{7,3},{8,12},{9,13},{10,... | collective-permute-start | bytes 196616 | tf_op jit(solution)/shard_map/rows0_4/ppermute | solution.py:23
  27.0 7.7 %collective-permute-start.20 = (bf16[32,1024]{1,0:T(8,128)(2,1)S(1)}, bf16[32,1024]{1,0:T(8,128)(2,1)S(1)}, u32[]{:S(2)}, u32[]{:S(2)}) collective-permute-start(bf16[32,1024]{1,0:T(8,128)(2,1)S(1)} %get-tuple-element.80), channel_id=1, source_target_pairs={{0,5},{1,4},{2,7},{3,6},{4,1},{5,0},{6,3},{7,2},{8,13},{9,12},{10,... | collective-permute-start | bytes 196616 | tf_op jit(solution)/shard_map/rows0_5/ppermute | solution.py:23
  31.3 14.8 %collective-permute-start.12 = (bf16[32,2048]{1,0:T(8,128)(2,1)S(1)}, bf16[32,2048]{1,0:T(8,128)(2,1)S(1)}, u32[]{:S(2)}, u32[]{:S(2)}) collective-permute-start(bf16[32,2048]{1,0:T(8,128)(2,1)S(1)} %get-tuple-element.70), channel_id=1, source_target_pairs={{0,1},{1,0},{2,3},{3,2},{4,5},{5,4},{6,7},{7,6},{8,9},{9,8},{10,11... | collective-permute-start | bytes 393224 | tf_op jit(solution)/shard_map/rows_1/ppermute | solution.py:23
  33.3 17.7 %collective-permute-start.13 = (bf16[32,2048]{1,0:T(8,128)(2,1)S(1)}, bf16[32,2048]{1,0:T(8,128)(2,1)S(1)}, u32[]{:S(2)}, u32[]{:S(2)}) collective-permute-start(bf16[32,2048]{1,0:T(8,128)(2,1)S(1)} %get-tuple-element.71), channel_id=1, source_target_pairs={{0,2},{1,3},{2,0},{3,1},{4,6},{5,7},{6,4},{7,5},{8,10},{9,11},{10,... | collective-permute-start | bytes 393224 | tf_op jit(solution)/shard_map/rows_2/ppermute | solution.py:23
  34.7 7.3 %collective-permute-start.21 = (bf16[32,1024]{1,0:T(8,128)(2,1)S(1)}, bf16[32,1024]{1,0:T(8,128)(2,1)S(1)}, u32[]{:S(2)}, u32[]{:S(2)}) collective-permute-start(bf16[32,1024]{1,0:T(8,128)(2,1)S(1)} %get-tuple-element.82), channel_id=1, source_target_pairs={{0,5},{1,4},{2,7},{3,6},{4,1},{5,0},{6,3},{7,2},{8,13},{9,12},{10,... | collective-permute-start | bytes 196616 | tf_op jit(solution)/shard_map/rows1_5/ppermute | solution.py:23
  38.1 5.4 %collective-permute-start.19 = (bf16[32,1024]{1,0:T(8,128)(2,1)S(1)}, bf16[32,1024]{1,0:T(8,128)(2,1)S(1)}, u32[]{:S(2)}, u32[]{:S(2)}) collective-permute-start(bf16[32,1024]{1,0:T(8,128)(2,1)S(1)} %get-tuple-element.79), channel_id=1, source_target_pairs={{0,4},{1,5},{2,6},{3,7},{4,0},{5,1},{6,2},{7,3},{8,12},{9,13},{10,... | collective-permute-start | bytes 196616 | tf_op jit(solution)/shard_map/rows1_4/ppermute | solution.py:23
  38.3 12.7 %collective-permute-start.14 = (bf16[32,2048]{1,0:T(8,128)(2,1)S(1)}, bf16[32,2048]{1,0:T(8,128)(2,1)S(1)}, u32[]{:S(2)}, u32[]{:S(2)}) collective-permute-start(bf16[32,2048]{1,0:T(8,128)(2,1)S(1)} %get-tuple-element.72), channel_id=1, source_target_pairs={{0,3},{1,2},{2,1},{3,0},{4,7},{5,6},{6,5},{7,4},{8,11},{9,10},{10,... | collective-permute-start | bytes 393224 | tf_op jit(solution)/shard_map/rows_3/ppermute | solution.py:23
  42.0 11.2 %collective-permute-start.24 = (bf16[32,2048]{1,0:T(8,128)(2,1)S(1)}, bf16[32,2048]{1,0:T(8,128)(2,1)S(1)}, u32[]{:S(2)}, u32[]{:S(2)}) collective-permute-start(bf16[32,2048]{1,0:T(8,128)(2,1)S(1)} %get-tuple-element.85), channel_id=1, source_target_pairs={{0,6},{1,7},{2,4},{3,5},{4,2},{5,3},{6,0},{7,1},{8,14},{9,15},{10,... | collective-permute-start | bytes 393224 | tf_op jit(solution)/shard_map/rows_6/ppermute | solution.py:23
  43.4 18.8 %collective-permute-start.25 = (bf16[32,2048]{1,0:T(8,128)(2,1)S(1)}, bf16[32,2048]{1,0:T(8,128)(2,1)S(1)}, u32[]{:S(2)}, u32[]{:S(2)}) collective-permute-start(bf16[32,2048]{1,0:T(8,128)(2,1)S(1)} %get-tuple-element.86), channel_id=1, source_target_pairs={{0,7},{1,6},{2,5},{3,4},{4,3},{5,2},{6,1},{7,0},{8,15},{9,14},{10,... | collective-permute-start | bytes 393224 | tf_op jit(solution)/shard_map/rows_7/ppermute | solution.py:23
  46.1 18.0 %collective-permute-start.22 = (bf16[32,2048]{1,0:T(8,128)(2,1)S(1)}, bf16[32,2048]{1,0:T(8,128)(2,1)S(1)}, u32[]{:S(2)}, u32[]{:S(2)}) collective-permute-start(bf16[32,2048]{1,0:T(8,128)(2,1)S(1)} %get-tuple-element.83), channel_id=1, source_target_pairs={{0,4},{1,5},{2,6},{3,7},{4,0},{5,1},{6,2},{7,3},{8,12},{9,13},{10,... | collective-permute-start | bytes 393224 | tf_op jit(solution)/shard_map/back_4/ppermute | solution.py:23
  51.0 15.0 %collective-permute-start.23 = (bf16[32,2048]{1,0:T(8,128)(2,1)S(1)}, bf16[32,2048]{1,0:T(8,128)(2,1)S(1)}, u32[]{:S(2)}, u32[]{:S(2)}) collective-permute-start(bf16[32,2048]{1,0:T(8,128)(2,1)S(1)} %get-tuple-element.84), channel_id=1, source_target_pairs={{0,5},{1,4},{2,7},{3,6},{4,1},{5,0},{6,3},{7,2},{8,13},{9,12},{10,... | collective-permute-start | bytes 393224 | tf_op jit(solution)/shard_map/back_5/ppermute | solution.py:23
  52.6 14.3 %collective-permute-start.15 = (bf16[32,2048]{1,0:T(8,128)(2,1)S(1)}, bf16[32,2048]{1,0:T(8,128)(2,1)S(1)}, u32[]{:S(2)}, u32[]{:S(2)}) collective-permute-start(bf16[32,2048]{1,0:T(8,128)(2,1)S(1)} %get-tuple-element.74), channel_id=1, source_target_pairs={{0,1},{1,0},{2,3},{3,2},{4,5},{5,4},{6,7},{7,6},{8,9},{9,8},{10,11... | collective-permute-start | bytes 393224 | tf_op jit(solution)/shard_map/back_1/ppermute | solution.py:23
  53.2 13.8 %collective-permute-start.16 = (bf16[32,2048]{1,0:T(8,128)(2,1)S(1)}, bf16[32,2048]{1,0:T(8,128)(2,1)S(1)}, u32[]{:S(2)}, u32[]{:S(2)}) collective-permute-start(bf16[32,2048]{1,0:T(8,128)(2,1)S(1)} %get-tuple-element.75), channel_id=1, source_target_pairs={{0,2},{1,3},{2,0},{3,1},{4,6},{5,7},{6,4},{7,5},{8,10},{9,11},{10,... | collective-permute-start | bytes 393224 | tf_op jit(solution)/shard_map/back_2/ppermute | solution.py:23
  62.2 12.4 %collective-permute-start.17 = (bf16[32,2048]{1,0:T(8,128)(2,1)S(1)}, bf16[32,2048]{1,0:T(8,128)(2,1)S(1)}, u32[]{:S(2)}, u32[]{:S(2)}) collective-permute-start(bf16[32,2048]{1,0:T(8,128)(2,1)S(1)} %get-tuple-element.76), channel_id=1, source_target_pairs={{0,3},{1,2},{2,1},{3,0},{4,7},{5,6},{6,5},{7,4},{8,11},{9,10},{10,... | collective-permute-start | bytes 393224 | tf_op jit(solution)/shard_map/back_3/ppermute | solution.py:23
  64.1 11.3 %collective-permute-start.26 = (bf16[32,2048]{1,0:T(8,128)(2,1)S(1)}, bf16[32,2048]{1,0:T(8,128)(2,1)S(1)}, u32[]{:S(2)}, u32[]{:S(2)}) collective-permute-start(bf16[32,2048]{1,0:T(8,128)(2,1)S(1)} %get-tuple-element.87), channel_id=1, source_target_pairs={{0,6},{1,7},{2,4},{3,5},{4,2},{5,3},{6,0},{7,1},{8,14},{9,15},{10,... | collective-permute-start | bytes 393224 | tf_op jit(solution)/shard_map/back_6/ppermute | solution.py:23
  65.9 12.3 %collective-permute-start.27 = (bf16[32,2048]{1,0:T(8,128)(2,1)S(1)}, bf16[32,2048]{1,0:T(8,128)(2,1)S(1)}, u32[]{:S(2)}, u32[]{:S(2)}) collective-permute-start(bf16[32,2048]{1,0:T(8,128)(2,1)S(1)} %get-tuple-element.88), channel_id=1, source_target_pairs={{0,7},{1,6},{2,5},{3,4},{4,3},{5,2},{6,1},{7,0},{8,15},{9,14},{10,... | collective-permute-start | bytes 393224 | tf_op jit(solution)/shard_map/back_7/ppermute | solution.py:23

commit v6 on v5

--- a/solution.py
+++ b/solution.py
@@ -220,7 +220,7 @@
     )(gain, w_gate, w_up, w_down, *flat)
 
 
-def spread_kernel(experts, ids_ref, gates_ref, coarse_ref, fine_ref, chosen_ref):
+def spread_kernel(experts, ids_ref, gates_ref, weight_ref, chosen_ref):
     ids, gates = ids_ref[...], gates_ref[...]
     hits, named = slot_matrix(experts, ids)
     for d in range(experts):
@@ -228,27 +228,27 @@
     weight = jnp.where(ids[0:1, :] == named, gates[0:1, :], 0.0) + jnp.where(
         ids[1:2, :] == named, gates[1:2, :], 0.0
     )
-    coarse = weight.astype(BF16).astype(F32)
-    for ref, part in ((coarse_ref, coarse), (fine_ref, weight - coarse)):
-        slots = [jnp.where(hits[d], part[d : d + 1, :], 0.0) for d in range(experts)]
-        ref[...] = jnp.concatenate(slots, axis=0).T.astype(BF16)
+    slots = [jnp.where(hits[d], weight[d : d + 1, :], 0.0) for d in range(experts)]
+    weight_ref[...] = jnp.concatenate(slots, axis=0).T.astype(BF16)
 
 
 def spread(experts, ids, gates):
     tokens = ids.shape[1]
     return pl.pallas_call(
         functools.partial(spread_kernel, experts),
-        out_shape=[jax.ShapeDtypeStruct((tokens, experts * CAP), BF16)] * 2
-        + [jax.ShapeDtypeStruct((experts * CAP, tokens), BF16)],
+        out_shape=[
+            jax.ShapeDtypeStruct((tokens, experts * CAP), BF16),
+            jax.ShapeDtypeStruct((experts * CAP, tokens), BF16),
+        ],
         in_specs=[VMEM] * 2,
-        out_specs=[VMEM] * 3,
+        out_specs=[VMEM] * 2,
         compiler_params=params(16),
         cost_estimate=cost(0, 4 * tokens * experts * CAP),
         name="spread_gates",
     )(ids, gates)
 
 
-def combine_kernel(groups, experts, chunks, coarse_ref, fine_ref, *rest):
+def combine_kernel(groups, experts, chunks, weight_ref, *rest):
     kept, blocks = rest[:chunks], rest[chunks : chunks + experts]
     out_ref, made_ref, sems = rest[chunks + experts :]
     width = kept[0].shape[1] // groups
@@ -259,8 +259,7 @@
         total = jnp.concatenate(
             [ref[:, g * width : (g + 1) * width] for ref in kept], axis=1
         ).astype(F32)
-        total += jnp.dot(coarse_ref[...], rows, preferred_element_type=F32)
-        total += jnp.dot(fine_ref[...], rows, preferred_element_type=F32)
+        total += jnp.dot(weight_ref[...], rows, preferred_element_type=F32)
         made_ref[:, span] = total.astype(BF16)
         copies.append(
             pltpu.make_async_copy(made_ref.at[:, span], out_ref.at[0, :, span], sems.at[g])
@@ -271,12 +270,12 @@
 
 
 def combine(groups, weights, kept, blocks):
-    tokens, features = weights[0].shape[0], blocks[0].shape[1]
+    tokens, features = weights.shape[0], blocks[0].shape[1]
     experts = len(blocks)
     return pl.pallas_call(
         functools.partial(combine_kernel, groups, experts, len(kept)),
         out_shape=jax.ShapeDtypeStruct((1, tokens, features), BF16),
-        in_specs=[VMEM] * (2 + len(kept) + experts),
+        in_specs=[VMEM] * (1 + len(kept) + experts),
         out_specs=HBM,
         scratch_shapes=[
             pltpu.VMEM((tokens, features), BF16),
@@ -285,7 +284,7 @@
         compiler_params=params(24),
         cost_estimate=cost(4 * experts * CAP * tokens * features, 8 * tokens * features),
         name="combine",
-    )(*weights, *kept, *blocks)
+    )(weights, *kept, *blocks)
 
 
 def after(values, *earlier):
@@ -323,7 +322,7 @@
     received = [
         exchange(packed[c * groups : (c + 1) * groups], f"qkv{c}_") for c in range(chunks)
     ]
-    *weights, chosen = spread(experts, ids, gates)
+    weights, chosen = spread(experts, ids, gates)
     received[-1][0] = after(received[-1][0], weights)
     heads = [attend(width, head_size, received[c]) for c in range(chunks)]
     kept, arrived = [], [[] for _ in range(experts)]

time: 80.6 us -> 80.5 us (level)
  no operation moved by 1% of the time
where the time goes in v6:
time: 80.5 us; the launch traced here: 79.2 us
  waiting for transfers between devices  33.9 us (42%)
  starting transfers between devices  31.3 us (39%)
  Pallas kernels  10.7 us (13%)
  local copies, waits for them, and re-layouts  3.15 us (4%)
    ppermute x28, waiting for transfers between devices, swap(): return lax.ppermute(x, axis, [(i, i ^ distance) for i in range(size)])  33.9 us
    ppermute x28, starting transfers between devices, swap(): return lax.ppermute(x, axis, [(i, i ^ distance) for i in range(size)])  31.3 us
    pallas_call x3, Pallas kernels, run_experts(): pl.pallas_call(functools.partial(experts_kernel, groups, chunks, width, h...  5.42 us
    unnamed x18, local copies, waits for them, and re-layouts  3.15 us
    pallas_call x2, Pallas kernels, attend(): pl.pallas_call(functools.partial(attend_kernel, groups, width, head_size)...  1.9 us
  transfers between devices with their start and end apart: 28, of which 12 were waited for; matrix products, arithmetic and copies ran while one was open for 0% of the time, Pallas kernels for 11%

profile of v6, /device:TPU:11, one launch (start us, length us, event | category | flops | bytes accessed | tf_op | source)
XLA Modules:
  0.0 79.2 jit_solution(5081257879607264693)
XLA Ops:
  0.0 1.2 %pack_heads.3 = (bf16[3,128,256]{2,1,0:T(8,128)(2,1)S(1)}, bf16[3,128,256]{2,1,0:T(8,128)(2,1)S(1)}, bf16[3,128,256]{2,1,0:T(8,128)(2,1)S(1)}) custom-call(bf16[1,128,2048]{2,1,0:T(8,128)(2,1)} %q_ref.3, bf16[1,128,2048]{2,1,0:T(8,128)(2,1)} %k_ref.3, bf16[1,128,2048]{2,1,0:T(8,128)(2,1)} %v_ref.3), custom_call_target="tpu_custom_call" | custom-call | bytes 1179648 | tf_op jit(solution)/shard_map/pack_heads/pallas_call | solution.py:55
  1.2 0.3 collective-permute-start
  1.5 1.2 %collective-permute-start.1 = (bf16[3,128,256]{2,1,0:T(8,128)(2,1)S(1)}, bf16[3,128,256]{2,1,0:T(8,128)(2,1)S(1)}, u32[]{:S(2)}, u32[]{:S(2)}) collective-permute-start(bf16[3,128,256]{2,1,0:T(8,128)(2,1)S(1)} %get-tuple-element.50), channel_id=1, source_target_pairs={{0,16},{8,24},{16,0},{24,8},{1,17},{9,25},{17,1},{25,9},{2,18},{10... | collective-permute-start | bytes 589832 | tf_op jit(solution)/shard_map/qkv0_/ppermute | solution.py:23
  2.8 1.2 %collective-permute-start.2 = (bf16[3,128,256]{2,1,0:T(8,128)(2,1)S(1)}, bf16[3,128,256]{2,1,0:T(8,128)(2,1)S(1)}, u32[]{:S(2)}, u32[]{:S(2)}) collective-permute-start(bf16[3,128,256]{2,1,0:T(8,128)(2,1)S(1)} %get-tuple-element.51), channel_id=1, source_target_pairs={{0,24},{8,16},{16,8},{24,0},{1,25},{9,17},{17,9},{25,1},{2,26},{10... | collective-permute-start | bytes 589832 | tf_op jit(solution)/shard_map/qkv0_/ppermute | solution.py:23
  3.9 1.0 %copy-done.3 = bf16[1,128,2048]{2,1,0:T(8,128)(2,1)S(1)} copy-done((bf16[1,128,2048]{2,1,0:T(8,128)(2,1)S(1)}, bf16[1,128,2048]{2,1,0:T(8,128)(2,1)}, u32[]{:S(2)}) %copy-start.3) | copy-done | bytes 524312
  5.0 1.0 %copy-done.4 = bf16[1,128,2048]{2,1,0:T(8,128)(2,1)S(1)} copy-done((bf16[1,128,2048]{2,1,0:T(8,128)(2,1)S(1)}, bf16[1,128,2048]{2,1,0:T(8,128)(2,1)}, u32[]{:S(2)}) %copy-start.4) | copy-done | bytes 524312
  6.0 1.0 %copy-done.5 = bf16[1,128,2048]{2,1,0:T(8,128)(2,1)S(1)} copy-done((bf16[1,128,2048]{2,1,0:T(8,128)(2,1)S(1)}, bf16[1,128,2048]{2,1,0:T(8,128)(2,1)}, u32[]{:S(2)}) %copy-start.5) | copy-done | bytes 524312
  7.1 0.3 pack_heads.2
  7.4 0.3 collective-permute-start.6
  7.7 1.2 %collective-permute-start.7 = (bf16[3,128,256]{2,1,0:T(8,128)(2,1)S(1)}, bf16[3,128,256]{2,1,0:T(8,128)(2,1)S(1)}, u32[]{:S(2)}, u32[]{:S(2)}) collective-permute-start(bf16[3,128,256]{2,1,0:T(8,128)(2,1)S(1)} %get-tuple-element.60), channel_id=1, source_target_pairs={{0,16},{8,24},{16,0},{24,8},{1,17},{9,25},{17,1},{25,9},{2,18},{10... | collective-permute-start | bytes 589832 | tf_op jit(solution)/shard_map/qkv1_/ppermute | solution.py:23
  8.9 0.2 spread_gates.1
  9.2 1.2 %collective-permute-start.8 = (bf16[3,128,256]{2,1,0:T(8,128)(2,1)S(1)}, bf16[3,128,256]{2,1,0:T(8,128)(2,1)S(1)}, u32[]{:S(2)}, u32[]{:S(2)}) collective-permute-start(bf16[3,128,256]{2,1,0:T(8,128)(2,1)S(1)} %get-tuple-element.61), channel_id=1, source_target_pairs={{0,24},{8,16},{16,8},{24,0},{1,25},{9,17},{17,9},{25,1},{2,26},{10... | collective-permute-start | bytes 589832 | tf_op jit(solution)/shard_map/qkv1_/ppermute | solution.py:23
  10.4 1.8 %collective-permute-done.2.rest_3_ = bf16[3,128,256]{2,1,0:T(8,128)(2,1)S(1)} collective-permute-done((bf16[3,128,256]{2,1,0:T(8,128)(2,1)S(1)}, bf16[3,128,256]{2,1,0:T(8,128)(2,1)S(1)}, u32[]{:S(2)}, u32[]{:S(2)}) %collective-permute-start.2) | collective-permute-done | bytes 196640 | tf_op jit(solution)/shard_map/qkv0_/ppermute | solution.py:23
  12.3 0.9 %attend.2 = (bf16[128,256]{1,0:T(8,128)(2,1)S(1)}, bf16[128,256]{1,0:T(8,128)(2,1)S(1)}, bf16[128,256]{1,0:T(8,128)(2,1)S(1)}, bf16[128,256]{1,0:T(8,128)(2,1)S(1)}) custom-call(bf16[3,128,256]{2,1,0:T(8,128)(2,1)S(1)} %get-tuple-element.48.rest_0_, bf16[3,128,256]{2,1,0:T(8,128)(2,1)S(1)} %collective-permute-done.rest_1_, ...), custom_call_target="tpu_custom_call" | custom-call | flops 10737418240 | bytes 10485760 | tf_op jit(solution)/shard_map/attend/pallas_call | solution.py:98
  13.2 0.3 collective-permute-start.3
  13.5 0.2 collective-permute-start.4
  13.8 1.8 %collective-permute-done.6.rest_1_ = bf16[3,128,256]{2,1,0:T(8,128)(2,1)S(1)} collective-permute-done((bf16[3,128,256]{2,1,0:T(8,128)(2,1)S(1)}, bf16[3,128,256]{2,1,0:T(8,128)(2,1)S(1)}, u32[]{:S(2)}, u32[]{:S(2)}) %collective-permute-start.6) | collective-permute-done | bytes 196640 | tf_op jit(solution)/shard_map/qkv1_/ppermute | solution.py:23
  15.5 1.3 %collective-permute-start.5 = (bf16[128,256]{1,0:T(8,128)(2,1)S(1)}, bf16[128,256]{1,0:T(8,128)(2,1)S(1)}, u32[]{:S(2)}, u32[]{:S(2)}) collective-permute-start(bf16[128,256]{1,0:T(8,128)(2,1)S(1)} %get-tuple-element.55), channel_id=1, source_target_pairs={{0,24},{8,16},{16,8},{24,0},{1,25},{9,17},{17,9},{25,1},{2,26},{10... | collective-permute-start | bytes 196616 | tf_op jit(solution)/shard_map/heads0_/ppermute | solution.py:23
  16.8 1.4 %collective-permute-done.7.rest_2_ = bf16[3,128,256]{2,1,0:T(8,128)(2,1)S(1)} collective-permute-done((bf16[3,128,256]{2,1,0:T(8,128)(2,1)S(1)}, bf16[3,128,256]{2,1,0:T(8,128)(2,1)S(1)}, u32[]{:S(2)}, u32[]{:S(2)}) %collective-permute-start.7) | collective-permute-done | bytes 196640 | tf_op jit(solution)/shard_map/qkv1_/ppermute | solution.py:23
  18.2 2.5 %collective-permute-done.8.rest_3_ = bf16[3,128,256]{2,1,0:T(8,128)(2,1)S(1)} collective-permute-done((bf16[3,128,256]{2,1,0:T(8,128)(2,1)S(1)}, bf16[3,128,256]{2,1,0:T(8,128)(2,1)S(1)}, u32[]{:S(2)}, u32[]{:S(2)}) %collective-permute-start.8) | collective-permute-done | bytes 196640 | tf_op jit(solution)/shard_map/qkv1_/ppermute | solution.py:23
  20.7 1.0 %attend.3 = (bf16[128,256]{1,0:T(8,128)(2,1)S(1)}, bf16[128,256]{1,0:T(8,128)(2,1)S(1)}, bf16[128,256]{1,0:T(8,128)(2,1)S(1)}, bf16[128,256]{1,0:T(8,128)(2,1)S(1)}) custom-call(bf16[3,128,256]{2,1,0:T(8,128)(2,1)S(1)} %get-tuple-element.58.rest_0_, bf16[3,128,256]{2,1,0:T(8,128)(2,1)S(1)} %collective-permute-done.6.rest_1_, ...), custom_call_target="tpu_custom_call" | custom-call | flops 10737418240 | bytes 10485760 | tf_op jit(solution)/shard_map/attend/pallas_call | solution.py:98
  21.7 0.3 collective-permute-start.9
  22.0 0.4 collective-permute-start.10
  22.4 2.0 %collective-permute-start.11 = (bf16[128,256]{1,0:T(8,128)(2,1)S(1)}, bf16[128,256]{1,0:T(8,128)(2,1)S(1)}, u32[]{:S(2)}, u32[]{:S(2)}) collective-permute-start(bf16[128,256]{1,0:T(8,128)(2,1)S(1)} %get-tuple-element.65), channel_id=1, source_target_pairs={{0,24},{8,16},{16,8},{24,0},{1,25},{9,17},{17,9},{25,1},{2,26},{10... | collective-permute-start | bytes 196616 | tf_op jit(solution)/shard_map/heads1_/ppermute | solution.py:23
  24.6 2.4 %collective-permute-start.18 = (bf16[32,1024]{1,0:T(8,128)(2,1)S(1)}, bf16[32,1024]{1,0:T(8,128)(2,1)S(1)}, u32[]{:S(2)}, u32[]{:S(2)}) collective-permute-start(bf16[32,1024]{1,0:T(8,128)(2,1)S(1)} %get-tuple-element.75), channel_id=1, source_target_pairs={{0,4},{1,5},{2,6},{3,7},{4,0},{5,1},{6,2},{7,3},{8,12},{9,13},{10,... | collective-permute-start | bytes 196616 | tf_op jit(solution)/shard_map/rows0_4/ppermute | solution.py:23
  27.0 3.8 %collective-permute-start.20 = (bf16[32,1024]{1,0:T(8,128)(2,1)S(1)}, bf16[32,1024]{1,0:T(8,128)(2,1)S(1)}, u32[]{:S(2)}, u32[]{:S(2)}) collective-permute-start(bf16[32,1024]{1,0:T(8,128)(2,1)S(1)} %get-tuple-element.78), channel_id=1, source_target_pairs={{0,5},{1,4},{2,7},{3,6},{4,1},{5,0},{6,3},{7,2},{8,13},{9,12},{10,... | collective-permute-start | bytes 196616 | tf_op jit(solution)/shard_map/rows0_5/ppermute | solution.py:23
  30.8 0.4 select_rows.3
  31.3 2.1 %collective-permute-start.12 = (bf16[32,2048]{1,0:T(8,128)(2,1)S(1)}, bf16[32,2048]{1,0:T(8,128)(2,1)S(1)}, u32[]{:S(2)}, u32[]{:S(2)}) collective-permute-start(bf16[32,2048]{1,0:T(8,128)(2,1)S(1)} %get-tuple-element.68), channel_id=1, source_target_pairs={{0,1},{1,0},{2,3},{3,2},{4,5},{5,4},{6,7},{7,6},{8,9},{9,8},{10,11... | collective-permute-start | bytes 393224 | tf_op jit(solution)/shard_map/rows_1/ppermute | solution.py:23
  33.5 1.2 %collective-permute-done.20.rest_2_ = bf16[32,1024]{1,0:T(8,128)(2,1)S(1)} collective-permute-done((bf16[32,1024]{1,0:T(8,128)(2,1)S(1)}, bf16[32,1024]{1,0:T(8,128)(2,1)S(1)}, u32[]{:S(2)}, u32[]{:S(2)}) %collective-permute-start.20) | collective-permute-done | bytes 65568 | tf_op jit(solution)/shard_map/rows0_5/ppermute | solution.py:23
  34.7 3.4 %collective-permute-start.21 = (bf16[32,1024]{1,0:T(8,128)(2,1)S(1)}, bf16[32,1024]{1,0:T(8,128)(2,1)S(1)}, u32[]{:S(2)}, u32[]{:S(2)}) collective-permute-start(bf16[32,1024]{1,0:T(8,128)(2,1)S(1)} %get-tuple-element.80), channel_id=1, source_target_pairs={{0,5},{1,4},{2,7},{3,6},{4,1},{5,0},{6,3},{7,2},{8,13},{9,12},{10,... | collective-permute-start | bytes 196616 | tf_op jit(solution)/shard_map/rows1_5/ppermute | solution.py:23
  38.3 0.2 collective-permute-start.14
  38.5 3.5 %collective-permute-done.21.rest_3_ = bf16[32,1024]{1,0:T(8,128)(2,1)S(1)} collective-permute-done((bf16[32,1024]{1,0:T(8,128)(2,1)S(1)}, bf16[32,1024]{1,0:T(8,128)(2,1)S(1)}, u32[]{:S(2)}, u32[]{:S(2)}) %collective-permute-start.21) | collective-permute-done | bytes 65568 | tf_op jit(solution)/shard_map/rows1_5/ppermute | solution.py:23
  42.0 1.4 %collective-permute-done.19.rest_1_ = bf16[32,1024]{1,0:T(8,128)(2,1)S(1)} collective-permute-done((bf16[32,1024]{1,0:T(8,128)(2,1)S(1)}, bf16[32,1024]{1,0:T(8,128)(2,1)S(1)}, u32[]{:S(2)}, u32[]{:S(2)}) %collective-permute-start.19) | collective-permute-done | bytes 65568 | tf_op jit(solution)/shard_map/rows1_4/ppermute | solution.py:23
  43.4 0.8 collective-permute-start.25
  44.2 1.9 %experts.4 = (bf16[32,2048]{1,0:T(8,128)(2,1)S(1)}, bf16[32,2048]{1,0:T(8,128)(2,1)S(1)}) custom-call(f32[1,2048]{1,0:T(1,128)S(1)} %bitcast.7, bf16[1,2048,768]{2,1,0:T(8,128)(2,1)S(1)} %copy-done, bf16[1,2048,768]{2,1,0:T(8,128)(2,1)S(1)} %copy-done.1, bf16[1,768,2048]{2,1,0:T(8,128)(2,1)S(1)} %copy-done.2, ...), custom_call_target="tpu_custom_call" | custom-call | flops 131072 | bytes 15728 | tf_op jit(solution)/shard_map/experts/pallas_call | solution.py:208
  46.1 4.9 %collective-permute-start.22 = (bf16[32,2048]{1,0:T(8,128)(2,1)S(1)}, bf16[32,2048]{1,0:T(8,128)(2,1)S(1)}, u32[]{:S(2)}, u32[]{:S(2)}) collective-permute-start(bf16[32,2048]{1,0:T(8,128)(2,1)S(1)} %get-tuple-element.81), channel_id=1, source_target_pairs={{0,4},{1,5},{2,6},{3,7},{4,0},{5,1},{6,2},{7,3},{8,12},{9,13},{10,... | collective-permute-start | bytes 393224 | tf_op jit(solution)/shard_map/back_4/ppermute | solution.py:23
  51.0 1.7 %experts.3 = (bf16[32,2048]{1,0:T(8,128)(2,1)S(1)}, bf16[32,2048]{1,0:T(8,128)(2,1)S(1)}, bf16[32,2048]{1,0:T(8,128)(2,1)S(1)}, bf16[32,2048]{1,0:T(8,128)(2,1)S(1)}) custom-call(f32[1,2048]{1,0:T(1,128)S(1)} %bitcast.8, bf16[1,2048,768]{2,1,0:T(8,128)(2,1)S(1)} %copy-done, bf16[1,2048,768]{2,1,0:T(8,128)(2,1)S(1)} %copy-done.1, ...), custom_call_target="tpu_custom_call" | custom-call | flops 262144 | bytes 15728 | tf_op jit(solution)/shard_map/experts/pallas_call | solution.py:208
  52.6 0.5 collective-permute-start.15
  53.2 1.4 %collective-permute-start.16 = (bf16[32,2048]{1,0:T(8,128)(2,1)S(1)}, bf16[32,2048]{1,0:T(8,128)(2,1)S(1)}, u32[]{:S(2)}, u32[]{:S(2)}) collective-permute-start(bf16[32,2048]{1,0:T(8,128)(2,1)S(1)} %get-tuple-element.73), channel_id=1, source_target_pairs={{0,2},{1,3},{2,0},{3,1},{4,6},{5,7},{6,4},{7,5},{8,10},{9,11},{10,... | collective-permute-start | bytes 393224 | tf_op jit(solution)/shard_map/back_2/ppermute | solution.py:23
  54.6 7.6 %collective-permute-done.25.rest_1_ = bf16[32,2048]{1,0:T(8,128)(2,1)S(1)} collective-permute-done((bf16[32,2048]{1,0:T(8,128)(2,1)S(1)}, bf16[32,2048]{1,0:T(8,128)(2,1)S(1)}, u32[]{:S(2)}, u32[]{:S(2)}) %collective-permute-start.25) | collective-permute-done | bytes 131104 | tf_op jit(solution)/shard_map/rows_7/ppermute | solution.py:23
  62.2 1.9 %experts.5 = (bf16[32,2048]{1,0:T(8,128)(2,1)S(1)}, bf16[32,2048]{1,0:T(8,128)(2,1)S(1)}) custom-call(f32[1,2048]{1,0:T(1,128)S(1)} %bitcast.9, bf16[1,2048,768]{2,1,0:T(8,128)(2,1)S(1)} %copy-done, bf16[1,2048,768]{2,1,0:T(8,128)(2,1)S(1)} %copy-done.1, bf16[1,768,2048]{2,1,0:T(8,128)(2,1)S(1)} %copy-done.2, ...), custom_call_target="tpu_custom_call" | custom-call | flops 131072 | bytes 15728 | tf_op jit(solution)/shard_map/experts/pallas_call | solution.py:208
  64.1 0.5 collective-permute-start.26
  64.6 1.4 %collective-permute-done.23.rest_7_ = bf16[32,2048]{1,0:T(8,128)(2,1)S(1)} collective-permute-done((bf16[32,2048]{1,0:T(8,128)(2,1)S(1)}, bf16[32,2048]{1,0:T(8,128)(2,1)S(1)}, u32[]{:S(2)}, u32[]{:S(2)}) %collective-permute-start.23) | collective-permute-done | bytes 131104 | tf_op jit(solution)/shard_map/back_5/ppermute | solution.py:23
  65.9 1.1 %collective-permute-start.27 = (bf16[32,2048]{1,0:T(8,128)(2,1)S(1)}, bf16[32,2048]{1,0:T(8,128)(2,1)S(1)}, u32[]{:S(2)}, u32[]{:S(2)}) collective-permute-start(bf16[32,2048]{1,0:T(8,128)(2,1)S(1)} %get-tuple-element.86), channel_id=1, source_target_pairs={{0,7},{1,6},{2,5},{3,4},{4,3},{5,2},{6,1},{7,0},{8,15},{9,14},{10,... | collective-permute-start | bytes 393224 | tf_op jit(solution)/shard_map/back_7/ppermute | solution.py:23
  67.0 7.6 %collective-permute-done.17.rest_5_ = bf16[32,2048]{1,0:T(8,128)(2,1)S(1)} collective-permute-done((bf16[32,2048]{1,0:T(8,128)(2,1)S(1)}, bf16[32,2048]{1,0:T(8,128)(2,1)S(1)}, u32[]{:S(2)}, u32[]{:S(2)}) %collective-permute-start.17) | collective-permute-done | bytes 131104 | tf_op jit(solution)/shard_map/back_3/ppermute | solution.py:23
  74.6 0.8 %collective-permute-done.26.rest_8_ = bf16[32,2048]{1,0:T(8,128)(2,1)S(1)} collective-permute-done((bf16[32,2048]{1,0:T(8,128)(2,1)S(1)}, bf16[32,2048]{1,0:T(8,128)(2,1)S(1)}, u32[]{:S(2)}, u32[]{:S(2)}) %collective-permute-start.26) | collective-permute-done | bytes 131104 | tf_op jit(solution)/shard_map/back_6/ppermute | solution.py:23
  75.4 2.8 %collective-permute-done.27.rest_9_ = bf16[32,2048]{1,0:T(8,128)(2,1)S(1)} collective-permute-done((bf16[32,2048]{1,0:T(8,128)(2,1)S(1)}, bf16[32,2048]{1,0:T(8,128)(2,1)S(1)}, u32[]{:S(2)}, u32[]{:S(2)}) %collective-permute-start.27) | collective-permute-done | bytes 131104 | tf_op jit(solution)/shard_map/back_7/ppermute | solution.py:23
  78.2 1.0 %combine.1 = bf16[1,128,2048]{2,1,0:T(8,128)(2,1)} custom-call(bf16[128,256]{1,0:T(8,128)(2,1)S(1)} %get-tuple-element.46.weight_ref, bf16[128,1024]{1,0:T(8,128)(2,1)S(1)} %get-tuple-element.56.rest_4_.rest_0_, bf16[128,1024]{1,0:T(8,128)(2,1)S(1)} %get-tuple-element.66.rest_1_, bf16[32,2048]{1,0:T(8,128)(2,1)S(1)} %get-tuple-element.71.rest_2_, ...), custom_call_target="tpu_custom_call" | custom-call | flops 268435456 | bytes 2097152 | tf_op jit(solution)/shard_map/combine/pallas_call | solution.py:275
  (37 shorter events, 0.7 us)
Async XLA Ops:
  0.0 8.9 %copy-start.8 = (f32[1,128,2]{1,2,0:T(2,128)S(1)}, f32[1,128,2]{1,2,0:T(2,128)}, u32[]{:S(2)}) copy-start(f32[1,128,2]{1,2,0:T(2,128)} %param.14) | copy-start | bytes 3076
  0.0 8.9 %copy-start.7 = (s32[1,128,2]{1,2,0:T(2,128)S(1)}, s32[1,128,2]{1,2,0:T(2,128)}, u32[]{:S(2)}) copy-start(s32[1,128,2]{1,2,0:T(2,128)} %param.13) | copy-start | bytes 3076
  1.2 8.0 %collective-permute-start = (bf16[3,128,256]{2,1,0:T(8,128)(2,1)S(1)}, bf16[3,128,256]{2,1,0:T(8,128)(2,1)S(1)}, u32[]{:S(2)}, u32[]{:S(2)}) collective-permute-start(bf16[3,128,256]{2,1,0:T(8,128)(2,1)S(1)} %get-tuple-element.49), channel_id=1, source_target_pairs={{0,8},{8,0},{16,24},{24,16},{1,9},{9,1},{17,25},{25,17},{2,10},{10... | collective-permute-start | bytes 589832 | tf_op jit(solution)/shard_map/qkv0_/ppermute | solution.py:23
  1.5 8.9 %collective-permute-start.1 = (bf16[3,128,256]{2,1,0:T(8,128)(2,1)S(1)}, bf16[3,128,256]{2,1,0:T(8,128)(2,1)S(1)}, u32[]{:S(2)}, u32[]{:S(2)}) collective-permute-start(bf16[3,128,256]{2,1,0:T(8,128)(2,1)S(1)} %get-tuple-element.50), channel_id=1, source_target_pairs={{0,16},{8,24},{16,0},{24,8},{1,17},{9,25},{17,1},{25,9},{2,18},{10... | collective-permute-start | bytes 589832 | tf_op jit(solution)/shard_map/qkv0_/ppermute | solution.py:23
  2.8 9.5 %collective-permute-start.2 = (bf16[3,128,256]{2,1,0:T(8,128)(2,1)S(1)}, bf16[3,128,256]{2,1,0:T(8,128)(2,1)S(1)}, u32[]{:S(2)}, u32[]{:S(2)}) collective-permute-start(bf16[3,128,256]{2,1,0:T(8,128)(2,1)S(1)} %get-tuple-element.51), channel_id=1, source_target_pairs={{0,24},{8,16},{16,8},{24,0},{1,25},{9,17},{17,9},{25,1},{2,26},{10... | collective-permute-start | bytes 589832 | tf_op jit(solution)/shard_map/qkv0_/ppermute | solution.py:23
  3.9 1.0 %copy-start.3 = (bf16[1,128,2048]{2,1,0:T(8,128)(2,1)S(1)}, bf16[1,128,2048]{2,1,0:T(8,128)(2,1)}, u32[]{:S(2)}) copy-start(bf16[1,128,2048]{2,1,0:T(8,128)(2,1)} %q_ref.3) | copy-start | bytes 1572868
  5.0 1.0 %copy-start.4 = (bf16[1,128,2048]{2,1,0:T(8,128)(2,1)S(1)}, bf16[1,128,2048]{2,1,0:T(8,128)(2,1)}, u32[]{:S(2)}) copy-start(bf16[1,128,2048]{2,1,0:T(8,128)(2,1)} %k_ref.3) | copy-start | bytes 1572868
  6.0 1.0 %copy-start.5 = (bf16[1,128,2048]{2,1,0:T(8,128)(2,1)S(1)}, bf16[1,128,2048]{2,1,0:T(8,128)(2,1)}, u32[]{:S(2)}) copy-start(bf16[1,128,2048]{2,1,0:T(8,128)(2,1)} %v_ref.3) | copy-start | bytes 1572868
  7.4 8.1 %collective-permute-start.6 = (bf16[3,128,256]{2,1,0:T(8,128)(2,1)S(1)}, bf16[3,128,256]{2,1,0:T(8,128)(2,1)S(1)}, u32[]{:S(2)}, u32[]{:S(2)}) collective-permute-start(bf16[3,128,256]{2,1,0:T(8,128)(2,1)S(1)} %get-tuple-element.59), channel_id=1, source_target_pairs={{0,8},{8,0},{16,24},{24,16},{1,9},{9,1},{17,25},{25,17},{2,10},{10... | collective-permute-start | bytes 589832 | tf_op jit(solution)/shard_map/qkv1_/ppermute | solution.py:23
  7.7 10.5 %collective-permute-start.7 = (bf16[3,128,256]{2,1,0:T(8,128)(2,1)S(1)}, bf16[3,128,256]{2,1,0:T(8,128)(2,1)S(1)}, u32[]{:S(2)}, u32[]{:S(2)}) collective-permute-start(bf16[3,128,256]{2,1,0:T(8,128)(2,1)S(1)} %get-tuple-element.60), channel_id=1, source_target_pairs={{0,16},{8,24},{16,0},{24,8},{1,17},{9,25},{17,1},{25,9},{2,18},{10... | collective-permute-start | bytes 589832 | tf_op jit(solution)/shard_map/qkv1_/ppermute | solution.py:23
  9.2 11.5 %collective-permute-start.8 = (bf16[3,128,256]{2,1,0:T(8,128)(2,1)S(1)}, bf16[3,128,256]{2,1,0:T(8,128)(2,1)S(1)}, u32[]{:S(2)}, u32[]{:S(2)}) collective-permute-start(bf16[3,128,256]{2,1,0:T(8,128)(2,1)S(1)} %get-tuple-element.61), channel_id=1, source_target_pairs={{0,24},{8,16},{16,8},{24,0},{1,25},{9,17},{17,9},{25,1},{2,26},{10... | collective-permute-start | bytes 589832 | tf_op jit(solution)/shard_map/qkv1_/ppermute | solution.py:23
  13.2 9.2 %collective-permute-start.3 = (bf16[128,256]{1,0:T(8,128)(2,1)S(1)}, bf16[128,256]{1,0:T(8,128)(2,1)S(1)}, u32[]{:S(2)}, u32[]{:S(2)}) collective-permute-start(bf16[128,256]{1,0:T(8,128)(2,1)S(1)} %get-tuple-element.53), channel_id=1, source_target_pairs={{0,8},{8,0},{16,24},{24,16},{1,9},{9,1},{17,25},{25,17},{2,10},{10... | collective-permute-start | bytes 196616 | tf_op jit(solution)/shard_map/heads0_/ppermute | solution.py:23
  13.5 10.9 %collective-permute-start.4 = (bf16[128,256]{1,0:T(8,128)(2,1)S(1)}, bf16[128,256]{1,0:T(8,128)(2,1)S(1)}, u32[]{:S(2)}, u32[]{:S(2)}) collective-permute-start(bf16[128,256]{1,0:T(8,128)(2,1)S(1)} %get-tuple-element.54), channel_id=1, source_target_pairs={{0,16},{8,24},{16,0},{24,8},{1,17},{9,25},{17,1},{25,9},{2,18},{10... | collective-permute-start | bytes 196616 | tf_op jit(solution)/shard_map/heads0_/ppermute | solution.py:23
  15.5 28.7 %copy-start = (bf16[1,2048,768]{2,1,0:T(8,128)(2,1)S(1)}, bf16[1,2048,768]{2,1,0:T(8,128)(2,1)}, u32[]{:S(2)}) copy-start(bf16[1,2048,768]{2,1,0:T(8,128)(2,1)} %gate_ref.5) | copy-start | bytes 9437188
  15.5 28.7 %copy-start.1 = (bf16[1,2048,768]{2,1,0:T(8,128)(2,1)S(1)}, bf16[1,2048,768]{2,1,0:T(8,128)(2,1)}, u32[]{:S(2)}) copy-start(bf16[1,2048,768]{2,1,0:T(8,128)(2,1)} %up_ref.5) | copy-start | bytes 9437188
  15.5 28.7 %copy-start.2 = (bf16[1,768,2048]{2,1,0:T(8,128)(2,1)S(1)}, bf16[1,768,2048]{2,1,0:T(8,128)(2,1)}, u32[]{:S(2)}) copy-start(bf16[1,768,2048]{2,1,0:T(8,128)(2,1)} %down_ref.5) | copy-start | bytes 9437188
  15.5 28.7 %copy-start.6 = (f32[2048]{0:T(1024)S(1)}, f32[2048]{0:T(1024)}, u32[]{:S(2)}) copy-start(f32[2048]{0:T(1024)} %param.12) | copy-start | bytes 24580
  15.5 8.9 %collective-permute-start.5 = (bf16[128,256]{1,0:T(8,128)(2,1)S(1)}, bf16[128,256]{1,0:T(8,128)(2,1)S(1)}, u32[]{:S(2)}, u32[]{:S(2)}) collective-permute-start(bf16[128,256]{1,0:T(8,128)(2,1)S(1)} %get-tuple-element.55), channel_id=1, source_target_pairs={{0,24},{8,16},{16,8},{24,0},{1,25},{9,17},{17,9},{25,1},{2,26},{10... | collective-permute-start | bytes 196616 | tf_op jit(solution)/shard_map/heads0_/ppermute | solution.py:23
  21.7 9.1 %collective-permute-start.9 = (bf16[128,256]{1,0:T(8,128)(2,1)S(1)}, bf16[128,256]{1,0:T(8,128)(2,1)S(1)}, u32[]{:S(2)}, u32[]{:S(2)}) collective-permute-start(bf16[128,256]{1,0:T(8,128)(2,1)S(1)} %get-tuple-element.63), channel_id=1, source_target_pairs={{0,8},{8,0},{16,24},{24,16},{1,9},{9,1},{17,25},{25,17},{2,10},{10... | collective-permute-start | bytes 196616 | tf_op jit(solution)/shard_map/heads1_/ppermute | solution.py:23
  22.0 8.8 %collective-permute-start.10 = (bf16[128,256]{1,0:T(8,128)(2,1)S(1)}, bf16[128,256]{1,0:T(8,128)(2,1)S(1)}, u32[]{:S(2)}, u32[]{:S(2)}) collective-permute-start(bf16[128,256]{1,0:T(8,128)(2,1)S(1)} %get-tuple-element.64), channel_id=1, source_target_pairs={{0,16},{8,24},{16,0},{24,8},{1,17},{9,25},{17,1},{25,9},{2,18},{10... | collective-permute-start | bytes 196616 | tf_op jit(solution)/shard_map/heads1_/ppermute | solution.py:23
  22.4 8.4 %collective-permute-start.11 = (bf16[128,256]{1,0:T(8,128)(2,1)S(1)}, bf16[128,256]{1,0:T(8,128)(2,1)S(1)}, u32[]{:S(2)}, u32[]{:S(2)}) collective-permute-start(bf16[128,256]{1,0:T(8,128)(2,1)S(1)} %get-tuple-element.65), channel_id=1, source_target_pairs={{0,24},{8,16},{16,8},{24,0},{1,25},{9,17},{17,9},{25,1},{2,26},{10... | collective-permute-start | bytes 196616 | tf_op jit(solution)/shard_map/heads1_/ppermute | solution.py:23
  24.6 13.4 %collective-permute-start.18 = (bf16[32,1024]{1,0:T(8,128)(2,1)S(1)}, bf16[32,1024]{1,0:T(8,128)(2,1)S(1)}, u32[]{:S(2)}, u32[]{:S(2)}) collective-permute-start(bf16[32,1024]{1,0:T(8,128)(2,1)S(1)} %get-tuple-element.75), channel_id=1, source_target_pairs={{0,4},{1,5},{2,6},{3,7},{4,0},{5,1},{6,2},{7,3},{8,12},{9,13},{10,... | collective-permute-start | bytes 196616 | tf_op jit(solution)/shard_map/rows0_4/ppermute | solution.py:23
  27.0 7.7 %collective-permute-start.20 = (bf16[32,1024]{1,0:T(8,128)(2,1)S(1)}, bf16[32,1024]{1,0:T(8,128)(2,1)S(1)}, u32[]{:S(2)}, u32[]{:S(2)}) collective-permute-start(bf16[32,1024]{1,0:T(8,128)(2,1)S(1)} %get-tuple-element.78), channel_id=1, source_target_pairs={{0,5},{1,4},{2,7},{3,6},{4,1},{5,0},{6,3},{7,2},{8,13},{9,12},{10,... | collective-permute-start | bytes 196616 | tf_op jit(solution)/shard_map/rows0_5/ppermute | solution.py:23
  31.3 14.8 %collective-permute-start.12 = (bf16[32,2048]{1,0:T(8,128)(2,1)S(1)}, bf16[32,2048]{1,0:T(8,128)(2,1)S(1)}, u32[]{:S(2)}, u32[]{:S(2)}) collective-permute-start(bf16[32,2048]{1,0:T(8,128)(2,1)S(1)} %get-tuple-element.68), channel_id=1, source_target_pairs={{0,1},{1,0},{2,3},{3,2},{4,5},{5,4},{6,7},{7,6},{8,9},{9,8},{10,11... | collective-permute-start | bytes 393224 | tf_op jit(solution)/shard_map/rows_1/ppermute | solution.py:23
  33.3 17.7 %collective-permute-start.13 = (bf16[32,2048]{1,0:T(8,128)(2,1)S(1)}, bf16[32,2048]{1,0:T(8,128)(2,1)S(1)}, u32[]{:S(2)}, u32[]{:S(2)}) collective-permute-start(bf16[32,2048]{1,0:T(8,128)(2,1)S(1)} %get-tuple-element.69), channel_id=1, source_target_pairs={{0,2},{1,3},{2,0},{3,1},{4,6},{5,7},{6,4},{7,5},{8,10},{9,11},{10,... | collective-permute-start | bytes 393224 | tf_op jit(solution)/shard_map/rows_2/ppermute | solution.py:23
  34.7 7.3 %collective-permute-start.21 = (bf16[32,1024]{1,0:T(8,128)(2,1)S(1)}, bf16[32,1024]{1,0:T(8,128)(2,1)S(1)}, u32[]{:S(2)}, u32[]{:S(2)}) collective-permute-start(bf16[32,1024]{1,0:T(8,128)(2,1)S(1)} %get-tuple-element.80), channel_id=1, source_target_pairs={{0,5},{1,4},{2,7},{3,6},{4,1},{5,0},{6,3},{7,2},{8,13},{9,12},{10,... | collective-permute-start | bytes 196616 | tf_op jit(solution)/shard_map/rows1_5/ppermute | solution.py:23
  38.1 5.4 %collective-permute-start.19 = (bf16[32,1024]{1,0:T(8,128)(2,1)S(1)}, bf16[32,1024]{1,0:T(8,128)(2,1)S(1)}, u32[]{:S(2)}, u32[]{:S(2)}) collective-permute-start(bf16[32,1024]{1,0:T(8,128)(2,1)S(1)} %get-tuple-element.77), channel_id=1, source_target_pairs={{0,4},{1,5},{2,6},{3,7},{4,0},{5,1},{6,2},{7,3},{8,12},{9,13},{10,... | collective-permute-start | bytes 196616 | tf_op jit(solution)/shard_map/rows1_4/ppermute | solution.py:23
  38.3 12.7 %collective-permute-start.14 = (bf16[32,2048]{1,0:T(8,128)(2,1)S(1)}, bf16[32,2048]{1,0:T(8,128)(2,1)S(1)}, u32[]{:S(2)}, u32[]{:S(2)}) collective-permute-start(bf16[32,2048]{1,0:T(8,128)(2,1)S(1)} %get-tuple-element.70), channel_id=1, source_target_pairs={{0,3},{1,2},{2,1},{3,0},{4,7},{5,6},{6,5},{7,4},{8,11},{9,10},{10,... | collective-permute-start | bytes 393224 | tf_op jit(solution)/shard_map/rows_3/ppermute | solution.py:23
  42.0 11.2 %collective-permute-start.24 = (bf16[32,2048]{1,0:T(8,128)(2,1)S(1)}, bf16[32,2048]{1,0:T(8,128)(2,1)S(1)}, u32[]{:S(2)}, u32[]{:S(2)}) collective-permute-start(bf16[32,2048]{1,0:T(8,128)(2,1)S(1)} %get-tuple-element.83), channel_id=1, source_target_pairs={{0,6},{1,7},{2,4},{3,5},{4,2},{5,3},{6,0},{7,1},{8,14},{9,15},{10,... | collective-permute-start | bytes 393224 | tf_op jit(solution)/shard_map/rows_6/ppermute | solution.py:23
  43.4 18.8 %collective-permute-start.25 = (bf16[32,2048]{1,0:T(8,128)(2,1)S(1)}, bf16[32,2048]{1,0:T(8,128)(2,1)S(1)}, u32[]{:S(2)}, u32[]{:S(2)}) collective-permute-start(bf16[32,2048]{1,0:T(8,128)(2,1)S(1)} %get-tuple-element.84), channel_id=1, source_target_pairs={{0,7},{1,6},{2,5},{3,4},{4,3},{5,2},{6,1},{7,0},{8,15},{9,14},{10,... | collective-permute-start | bytes 393224 | tf_op jit(solution)/shard_map/rows_7/ppermute | solution.py:23
  46.1 18.0 %collective-permute-start.22 = (bf16[32,2048]{1,0:T(8,128)(2,1)S(1)}, bf16[32,2048]{1,0:T(8,128)(2,1)S(1)}, u32[]{:S(2)}, u32[]{:S(2)}) collective-permute-start(bf16[32,2048]{1,0:T(8,128)(2,1)S(1)} %get-tuple-element.81), channel_id=1, source_target_pairs={{0,4},{1,5},{2,6},{3,7},{4,0},{5,1},{6,2},{7,3},{8,12},{9,13},{10,... | collective-permute-start | bytes 393224 | tf_op jit(solution)/shard_map/back_4/ppermute | solution.py:23
  51.0 15.0 %collective-permute-start.23 = (bf16[32,2048]{1,0:T(8,128)(2,1)S(1)}, bf16[32,2048]{1,0:T(8,128)(2,1)S(1)}, u32[]{:S(2)}, u32[]{:S(2)}) collective-permute-start(bf16[32,2048]{1,0:T(8,128)(2,1)S(1)} %get-tuple-element.82), channel_id=1, source_target_pairs={{0,5},{1,4},{2,7},{3,6},{4,1},{5,0},{6,3},{7,2},{8,13},{9,12},{10,... | collective-permute-start | bytes 393224 | tf_op jit(solution)/shard_map/back_5/ppermute | solution.py:23
  52.6 14.3 %collective-permute-start.15 = (bf16[32,2048]{1,0:T(8,128)(2,1)S(1)}, bf16[32,2048]{1,0:T(8,128)(2,1)S(1)}, u32[]{:S(2)}, u32[]{:S(2)}) collective-permute-start(bf16[32,2048]{1,0:T(8,128)(2,1)S(1)} %get-tuple-element.72), channel_id=1, source_target_pairs={{0,1},{1,0},{2,3},{3,2},{4,5},{5,4},{6,7},{7,6},{8,9},{9,8},{10,11... | collective-permute-start | bytes 393224 | tf_op jit(solution)/shard_map/back_1/ppermute | solution.py:23
  53.2 13.8 %collective-permute-start.16 = (bf16[32,2048]{1,0:T(8,128)(2,1)S(1)}, bf16[32,2048]{1,0:T(8,128)(2,1)S(1)}, u32[]{:S(2)}, u32[]{:S(2)}) collective-permute-start(bf16[32,2048]{1,0:T(8,128)(2,1)S(1)} %get-tuple-element.73), channel_id=1, source_target_pairs={{0,2},{1,3},{2,0},{3,1},{4,6},{5,7},{6,4},{7,5},{8,10},{9,11},{10,... | collective-permute-start | bytes 393224 | tf_op jit(solution)/shard_map/back_2/ppermute | solution.py:23
  62.2 12.4 %collective-permute-start.17 = (bf16[32,2048]{1,0:T(8,128)(2,1)S(1)}, bf16[32,2048]{1,0:T(8,128)(2,1)S(1)}, u32[]{:S(2)}, u32[]{:S(2)}) collective-permute-start(bf16[32,2048]{1,0:T(8,128)(2,1)S(1)} %get-tuple-element.74), channel_id=1, source_target_pairs={{0,3},{1,2},{2,1},{3,0},{4,7},{5,6},{6,5},{7,4},{8,11},{9,10},{10,... | collective-permute-start | bytes 393224 | tf_op jit(solution)/shard_map/back_3/ppermute | solution.py:23
  64.1 11.3 %collective-permute-start.26 = (bf16[32,2048]{1,0:T(8,128)(2,1)S(1)}, bf16[32,2048]{1,0:T(8,128)(2,1)S(1)}, u32[]{:S(2)}, u32[]{:S(2)}) collective-permute-start(bf16[32,2048]{1,0:T(8,128)(2,1)S(1)} %get-tuple-element.85), channel_id=1, source_target_pairs={{0,6},{1,7},{2,4},{3,5},{4,2},{5,3},{6,0},{7,1},{8,14},{9,15},{10,... | collective-permute-start | bytes 393224 | tf_op jit(solution)/shard_map/back_6/ppermute | solution.py:23
  65.9 12.3 %collective-permute-start.27 = (bf16[32,2048]{1,0:T(8,128)(2,1)S(1)}, bf16[32,2048]{1,0:T(8,128)(2,1)S(1)}, u32[]{:S(2)}, u32[]{:S(2)}) collective-permute-start(bf16[32,2048]{1,0:T(8,128)(2,1)S(1)} %get-tuple-element.86), channel_id=1, source_target_pairs={{0,7},{1,6},{2,5},{3,4},{4,3},{5,2},{6,1},{7,0},{8,15},{9,14},{10,... | collective-permute-start | bytes 393224 | tf_op jit(solution)/shard_map/back_7/ppermute | solution.py:23

commit v7 on v6

--- a/solution.py
+++ b/solution.py
@@ -328,7 +328,7 @@
     kept, arrived = [], [[] for _ in range(experts)]
     for c in range(chunks):
         last = c == chunks - 1
-        out = heads[c]
+        out = heads[c] if c == 0 else [*heads[c][:-1], after(heads[c][-1], kept[-1])]
         *rows, own = select(groups, experts, chosen, exchange(out, f"heads{c}_"), kept, last)
         kept.append(own)
         for d in range(half, middle):

time: 80.5 us -> 80.5 us (level)
  waiting for transfers between devices: 33.9 us -> 35.3 us
  starting transfers between devices: 31.3 us -> 30.3 us
    ppermute x28, waiting for transfers between devices: 33.9 us -> 35.3 us  [swap(): return lax.ppermute(x, axis, [(i, i ^ distance) for i in range(size)])]
    ppermute x28, starting transfers between devices: 31.3 us -> 30.3 us  [swap(): return lax.ppermute(x, axis, [(i, i ^ distance) for i in range(size)])]
  transfers between devices with their start and end apart: 28 -> 28, of which waited for: 12 -> 13; matrix products, arithmetic and copies ran while one was open for 0% -> 0% of each run, Pallas kernels for 11% -> 11%
where the time goes in v7:
time: 80.5 us; the launch traced here: 79.6 us
  waiting for transfers between devices  35.3 us (44%)
  starting transfers between devices  30.3 us (38%)
  Pallas kernels  10.8 us (13%)
  local copies, waits for them, and re-layouts  3.15 us (4%)
    ppermute x28, waiting for transfers between devices, swap(): return lax.ppermute(x, axis, [(i, i ^ distance) for i in range(size)])  35.3 us
    ppermute x28, starting transfers between devices, swap(): return lax.ppermute(x, axis, [(i, i ^ distance) for i in range(size)])  30.3 us
    pallas_call x3, Pallas kernels, run_experts(): pl.pallas_call(functools.partial(experts_kernel, groups, chunks, width, h...  5.42 us
    unnamed x18, local copies, waits for them, and re-layouts  3.15 us
    pallas_call x2, Pallas kernels, attend(): pl.pallas_call(functools.partial(attend_kernel, groups, width, head_size)...  1.9 us
  transfers between devices with their start and end apart: 28, of which 13 were waited for; matrix products, arithmetic and copies ran while one was open for 0% of the time, Pallas kernels for 11%

profile of v7, /device:TPU:11, one launch (start us, length us, event | category | flops | bytes accessed | tf_op | source)
XLA Modules:
  0.0 79.6 jit_solution(7335245942905914914)
XLA Ops:
  0.0 1.2 %pack_heads.3 = (bf16[3,128,256]{2,1,0:T(8,128)(2,1)S(1)}, bf16[3,128,256]{2,1,0:T(8,128)(2,1)S(1)}, bf16[3,128,256]{2,1,0:T(8,128)(2,1)S(1)}) custom-call(bf16[1,128,2048]{2,1,0:T(8,128)(2,1)} %q_ref.3, bf16[1,128,2048]{2,1,0:T(8,128)(2,1)} %k_ref.3, bf16[1,128,2048]{2,1,0:T(8,128)(2,1)} %v_ref.3), custom_call_target="tpu_custom_call" | custom-call | bytes 1179648 | tf_op jit(solution)/shard_map/pack_heads/pallas_call | solution.py:55
  1.2 0.3 collective-permute-start
  1.5 1.2 %collective-permute-start.1 = (bf16[3,128,256]{2,1,0:T(8,128)(2,1)S(1)}, bf16[3,128,256]{2,1,0:T(8,128)(2,1)S(1)}, u32[]{:S(2)}, u32[]{:S(2)}) collective-permute-start(bf16[3,128,256]{2,1,0:T(8,128)(2,1)S(1)} %get-tuple-element.51), channel_id=1, source_target_pairs={{0,16},{8,24},{16,0},{24,8},{1,17},{9,25},{17,1},{25,9},{2,18},{10... | collective-permute-start | bytes 589832 | tf_op jit(solution)/shard_map/qkv0_/ppermute | solution.py:23
  2.8 1.2 %collective-permute-start.2 = (bf16[3,128,256]{2,1,0:T(8,128)(2,1)S(1)}, bf16[3,128,256]{2,1,0:T(8,128)(2,1)S(1)}, u32[]{:S(2)}, u32[]{:S(2)}) collective-permute-start(bf16[3,128,256]{2,1,0:T(8,128)(2,1)S(1)} %get-tuple-element.52), channel_id=1, source_target_pairs={{0,24},{8,16},{16,8},{24,0},{1,25},{9,17},{17,9},{25,1},{2,26},{10... | collective-permute-start | bytes 589832 | tf_op jit(solution)/shard_map/qkv0_/ppermute | solution.py:23
  3.9 1.0 %copy-done.3 = bf16[1,128,2048]{2,1,0:T(8,128)(2,1)S(1)} copy-done((bf16[1,128,2048]{2,1,0:T(8,128)(2,1)S(1)}, bf16[1,128,2048]{2,1,0:T(8,128)(2,1)}, u32[]{:S(2)}) %copy-start.3) | copy-done | bytes 524312
  5.0 1.0 %copy-done.4 = bf16[1,128,2048]{2,1,0:T(8,128)(2,1)S(1)} copy-done((bf16[1,128,2048]{2,1,0:T(8,128)(2,1)S(1)}, bf16[1,128,2048]{2,1,0:T(8,128)(2,1)}, u32[]{:S(2)}) %copy-start.4) | copy-done | bytes 524312
  6.0 1.0 %copy-done.5 = bf16[1,128,2048]{2,1,0:T(8,128)(2,1)S(1)} copy-done((bf16[1,128,2048]{2,1,0:T(8,128)(2,1)S(1)}, bf16[1,128,2048]{2,1,0:T(8,128)(2,1)}, u32[]{:S(2)}) %copy-start.5) | copy-done | bytes 524312
  7.1 0.3 pack_heads.2
  7.4 0.3 collective-permute-start.6
  7.7 1.2 %collective-permute-start.7 = (bf16[3,128,256]{2,1,0:T(8,128)(2,1)S(1)}, bf16[3,128,256]{2,1,0:T(8,128)(2,1)S(1)}, u32[]{:S(2)}, u32[]{:S(2)}) collective-permute-start(bf16[3,128,256]{2,1,0:T(8,128)(2,1)S(1)} %get-tuple-element.61), channel_id=1, source_target_pairs={{0,16},{8,24},{16,0},{24,8},{1,17},{9,25},{17,1},{25,9},{2,18},{10... | collective-permute-start | bytes 589832 | tf_op jit(solution)/shard_map/qkv1_/ppermute | solution.py:23
  8.9 0.2 spread_gates.1
  9.2 1.2 %collective-permute-start.8 = (bf16[3,128,256]{2,1,0:T(8,128)(2,1)S(1)}, bf16[3,128,256]{2,1,0:T(8,128)(2,1)S(1)}, u32[]{:S(2)}, u32[]{:S(2)}) collective-permute-start(bf16[3,128,256]{2,1,0:T(8,128)(2,1)S(1)} %get-tuple-element.62), channel_id=1, source_target_pairs={{0,24},{8,16},{16,8},{24,0},{1,25},{9,17},{17,9},{25,1},{2,26},{10... | collective-permute-start | bytes 589832 | tf_op jit(solution)/shard_map/qkv1_/ppermute | solution.py:23
  10.4 1.8 %collective-permute-done.2.rest_3_ = bf16[3,128,256]{2,1,0:T(8,128)(2,1)S(1)} collective-permute-done((bf16[3,128,256]{2,1,0:T(8,128)(2,1)S(1)}, bf16[3,128,256]{2,1,0:T(8,128)(2,1)S(1)}, u32[]{:S(2)}, u32[]{:S(2)}) %collective-permute-start.2) | collective-permute-done | bytes 196640 | tf_op jit(solution)/shard_map/qkv0_/ppermute | solution.py:23
  12.3 0.9 %attend.2 = (bf16[128,256]{1,0:T(8,128)(2,1)S(1)}, bf16[128,256]{1,0:T(8,128)(2,1)S(1)}, bf16[128,256]{1,0:T(8,128)(2,1)S(1)}, bf16[128,256]{1,0:T(8,128)(2,1)S(1)}) custom-call(bf16[3,128,256]{2,1,0:T(8,128)(2,1)S(1)} %get-tuple-element.49.rest_0_, bf16[3,128,256]{2,1,0:T(8,128)(2,1)S(1)} %collective-permute-done.rest_1_, ...), custom_call_target="tpu_custom_call" | custom-call | flops 10737418240 | bytes 10485760 | tf_op jit(solution)/shard_map/attend/pallas_call | solution.py:98
  13.2 0.3 collective-permute-start.3
  13.8 1.8 %collective-permute-done.6.rest_1_ = bf16[3,128,256]{2,1,0:T(8,128)(2,1)S(1)} collective-permute-done((bf16[3,128,256]{2,1,0:T(8,128)(2,1)S(1)}, bf16[3,128,256]{2,1,0:T(8,128)(2,1)S(1)}, u32[]{:S(2)}, u32[]{:S(2)}) %collective-permute-start.6) | collective-permute-done | bytes 196640 | tf_op jit(solution)/shard_map/qkv1_/ppermute | solution.py:23
  15.5 1.3 %collective-permute-start.5 = (bf16[128,256]{1,0:T(8,128)(2,1)S(1)}, bf16[128,256]{1,0:T(8,128)(2,1)S(1)}, u32[]{:S(2)}, u32[]{:S(2)}) collective-permute-start(bf16[128,256]{1,0:T(8,128)(2,1)S(1)} %get-tuple-element.56), channel_id=1, source_target_pairs={{0,24},{8,16},{16,8},{24,0},{1,25},{9,17},{17,9},{25,1},{2,26},{10... | collective-permute-start | bytes 196616 | tf_op jit(solution)/shard_map/heads0_/ppermute | solution.py:23
  16.8 1.4 %collective-permute-done.7.rest_2_ = bf16[3,128,256]{2,1,0:T(8,128)(2,1)S(1)} collective-permute-done((bf16[3,128,256]{2,1,0:T(8,128)(2,1)S(1)}, bf16[3,128,256]{2,1,0:T(8,128)(2,1)S(1)}, u32[]{:S(2)}, u32[]{:S(2)}) %collective-permute-start.7) | collective-permute-done | bytes 196640 | tf_op jit(solution)/shard_map/qkv1_/ppermute | solution.py:23
  18.2 2.5 %collective-permute-done.8.rest_3_ = bf16[3,128,256]{2,1,0:T(8,128)(2,1)S(1)} collective-permute-done((bf16[3,128,256]{2,1,0:T(8,128)(2,1)S(1)}, bf16[3,128,256]{2,1,0:T(8,128)(2,1)S(1)}, u32[]{:S(2)}, u32[]{:S(2)}) %collective-permute-start.8) | collective-permute-done | bytes 196640 | tf_op jit(solution)/shard_map/qkv1_/ppermute | solution.py:23
  20.7 1.0 %attend.3 = (bf16[128,256]{1,0:T(8,128)(2,1)S(1)}, bf16[128,256]{1,0:T(8,128)(2,1)S(1)}, bf16[128,256]{1,0:T(8,128)(2,1)S(1)}, bf16[128,256]{1,0:T(8,128)(2,1)S(1)}) custom-call(bf16[3,128,256]{2,1,0:T(8,128)(2,1)S(1)} %get-tuple-element.59.rest_0_, bf16[3,128,256]{2,1,0:T(8,128)(2,1)S(1)} %collective-permute-done.6.rest_1_, ...), custom_call_target="tpu_custom_call" | custom-call | flops 10737418240 | bytes 10485760 | tf_op jit(solution)/shard_map/attend/pallas_call | solution.py:98
  21.7 0.3 collective-permute-start.9
  22.0 0.4 collective-permute-start.10
  22.4 1.3 %collective-permute-done.4.rest_2_ = bf16[128,256]{1,0:T(8,128)(2,1)S(1)} collective-permute-done((bf16[128,256]{1,0:T(8,128)(2,1)S(1)}, bf16[128,256]{1,0:T(8,128)(2,1)S(1)}, u32[]{:S(2)}, u32[]{:S(2)}) %collective-permute-start.4) | collective-permute-done | bytes 65568 | tf_op jit(solution)/shard_map/heads0_/ppermute | solution.py:23
  23.9 0.8 %collective-permute-start.11 = (bf16[128,256]{1,0:T(8,128)(2,1)S(1)}, bf16[128,256]{1,0:T(8,128)(2,1)S(1)}, u32[]{:S(2)}, u32[]{:S(2)}) collective-permute-start(bf16[128,256]{1,0:T(8,128)(2,1)S(1)} %get-tuple-element.67), channel_id=1, source_target_pairs={{0,24},{8,16},{16,8},{24,0},{1,25},{9,17},{17,9},{25,1},{2,26},{10... | collective-permute-start | bytes 196616 | tf_op jit(solution)/shard_map/heads1_/ppermute | solution.py:23
  24.7 2.3 %collective-permute-start.18 = (bf16[32,1024]{1,0:T(8,128)(2,1)S(1)}, bf16[32,1024]{1,0:T(8,128)(2,1)S(1)}, u32[]{:S(2)}, u32[]{:S(2)}) collective-permute-start(bf16[32,1024]{1,0:T(8,128)(2,1)S(1)} %get-tuple-element.77), channel_id=1, source_target_pairs={{0,4},{1,5},{2,6},{3,7},{4,0},{5,1},{6,2},{7,3},{8,12},{9,13},{10,... | collective-permute-start | bytes 196616 | tf_op jit(solution)/shard_map/rows0_4/ppermute | solution.py:23
  27.0 3.8 %collective-permute-start.20 = (bf16[32,1024]{1,0:T(8,128)(2,1)S(1)}, bf16[32,1024]{1,0:T(8,128)(2,1)S(1)}, u32[]{:S(2)}, u32[]{:S(2)}) collective-permute-start(bf16[32,1024]{1,0:T(8,128)(2,1)S(1)} %get-tuple-element.80), channel_id=1, source_target_pairs={{0,5},{1,4},{2,7},{3,6},{4,1},{5,0},{6,3},{7,2},{8,13},{9,12},{10,... | collective-permute-start | bytes 196616 | tf_op jit(solution)/shard_map/rows0_5/ppermute | solution.py:23
  30.8 0.4 select_rows.3
  31.3 2.3 %collective-permute-start.12 = (bf16[32,2048]{1,0:T(8,128)(2,1)S(1)}, bf16[32,2048]{1,0:T(8,128)(2,1)S(1)}, u32[]{:S(2)}, u32[]{:S(2)}) collective-permute-start(bf16[32,2048]{1,0:T(8,128)(2,1)S(1)} %get-tuple-element.70), channel_id=1, source_target_pairs={{0,1},{1,0},{2,3},{3,2},{4,5},{5,4},{6,7},{7,6},{8,9},{9,8},{10,11... | collective-permute-start | bytes 393224 | tf_op jit(solution)/shard_map/rows_1/ppermute | solution.py:23
  33.8 0.9 %collective-permute-done.20.rest_2_ = bf16[32,1024]{1,0:T(8,128)(2,1)S(1)} collective-permute-done((bf16[32,1024]{1,0:T(8,128)(2,1)S(1)}, bf16[32,1024]{1,0:T(8,128)(2,1)S(1)}, u32[]{:S(2)}, u32[]{:S(2)}) %collective-permute-start.20) | collective-permute-done | bytes 65568 | tf_op jit(solution)/shard_map/rows0_5/ppermute | solution.py:23
  34.7 3.4 %collective-permute-start.21 = (bf16[32,1024]{1,0:T(8,128)(2,1)S(1)}, bf16[32,1024]{1,0:T(8,128)(2,1)S(1)}, u32[]{:S(2)}, u32[]{:S(2)}) collective-permute-start(bf16[32,1024]{1,0:T(8,128)(2,1)S(1)} %get-tuple-element.82), channel_id=1, source_target_pairs={{0,5},{1,4},{2,7},{3,6},{4,1},{5,0},{6,3},{7,2},{8,13},{9,12},{10,... | collective-permute-start | bytes 196616 | tf_op jit(solution)/shard_map/rows1_5/ppermute | solution.py:23
  38.2 0.2 collective-permute-start.14
  38.5 3.8 %collective-permute-done.21.rest_3_ = bf16[32,1024]{1,0:T(8,128)(2,1)S(1)} collective-permute-done((bf16[32,1024]{1,0:T(8,128)(2,1)S(1)}, bf16[32,1024]{1,0:T(8,128)(2,1)S(1)}, u32[]{:S(2)}, u32[]{:S(2)}) %collective-permute-start.21) | collective-permute-done | bytes 65568 | tf_op jit(solution)/shard_map/rows1_5/ppermute | solution.py:23
  42.3 1.4 %collective-permute-done.19.rest_1_ = bf16[32,1024]{1,0:T(8,128)(2,1)S(1)} collective-permute-done((bf16[32,1024]{1,0:T(8,128)(2,1)S(1)}, bf16[32,1024]{1,0:T(8,128)(2,1)S(1)}, u32[]{:S(2)}, u32[]{:S(2)}) %collective-permute-start.19) | collective-permute-done | bytes 65568 | tf_op jit(solution)/shard_map/rows1_4/ppermute | solution.py:23
  43.7 0.8 collective-permute-start.25
  44.5 1.9 %experts.4 = (bf16[32,2048]{1,0:T(8,128)(2,1)S(1)}, bf16[32,2048]{1,0:T(8,128)(2,1)S(1)}) custom-call(f32[1,2048]{1,0:T(1,128)S(1)} %bitcast.7, bf16[1,2048,768]{2,1,0:T(8,128)(2,1)S(1)} %copy-done, bf16[1,2048,768]{2,1,0:T(8,128)(2,1)S(1)} %copy-done.1, bf16[1,768,2048]{2,1,0:T(8,128)(2,1)S(1)} %copy-done.2, ...), custom_call_target="tpu_custom_call" | custom-call | flops 131072 | bytes 15728 | tf_op jit(solution)/shard_map/experts/pallas_call | solution.py:208
  46.4 4.9 %collective-permute-start.22 = (bf16[32,2048]{1,0:T(8,128)(2,1)S(1)}, bf16[32,2048]{1,0:T(8,128)(2,1)S(1)}, u32[]{:S(2)}, u32[]{:S(2)}) collective-permute-start(bf16[32,2048]{1,0:T(8,128)(2,1)S(1)} %get-tuple-element.83), channel_id=1, source_target_pairs={{0,4},{1,5},{2,6},{3,7},{4,0},{5,1},{6,2},{7,3},{8,12},{9,13},{10,... | collective-permute-start | bytes 393224 | tf_op jit(solution)/shard_map/back_4/ppermute | solution.py:23
  51.3 1.7 %experts.3 = (bf16[32,2048]{1,0:T(8,128)(2,1)S(1)}, bf16[32,2048]{1,0:T(8,128)(2,1)S(1)}, bf16[32,2048]{1,0:T(8,128)(2,1)S(1)}, bf16[32,2048]{1,0:T(8,128)(2,1)S(1)}) custom-call(f32[1,2048]{1,0:T(1,128)S(1)} %bitcast.8, bf16[1,2048,768]{2,1,0:T(8,128)(2,1)S(1)} %copy-done, bf16[1,2048,768]{2,1,0:T(8,128)(2,1)S(1)} %copy-done.1, ...), custom_call_target="tpu_custom_call" | custom-call | flops 262144 | bytes 15728 | tf_op jit(solution)/shard_map/experts/pallas_call | solution.py:208
  52.9 0.5 collective-permute-start.15
  53.5 1.4 %collective-permute-start.16 = (bf16[32,2048]{1,0:T(8,128)(2,1)S(1)}, bf16[32,2048]{1,0:T(8,128)(2,1)S(1)}, u32[]{:S(2)}, u32[]{:S(2)}) collective-permute-start(bf16[32,2048]{1,0:T(8,128)(2,1)S(1)} %get-tuple-element.75), channel_id=1, source_target_pairs={{0,2},{1,3},{2,0},{3,1},{4,6},{5,7},{6,4},{7,5},{8,10},{9,11},{10,... | collective-permute-start | bytes 393224 | tf_op jit(solution)/shard_map/back_2/ppermute | solution.py:23
  54.9 7.7 %collective-permute-done.25.rest_1_ = bf16[32,2048]{1,0:T(8,128)(2,1)S(1)} collective-permute-done((bf16[32,2048]{1,0:T(8,128)(2,1)S(1)}, bf16[32,2048]{1,0:T(8,128)(2,1)S(1)}, u32[]{:S(2)}, u32[]{:S(2)}) %collective-permute-start.25) | collective-permute-done | bytes 131104 | tf_op jit(solution)/shard_map/rows_7/ppermute | solution.py:23
  62.6 1.9 %experts.5 = (bf16[32,2048]{1,0:T(8,128)(2,1)S(1)}, bf16[32,2048]{1,0:T(8,128)(2,1)S(1)}) custom-call(f32[1,2048]{1,0:T(1,128)S(1)} %bitcast.9, bf16[1,2048,768]{2,1,0:T(8,128)(2,1)S(1)} %copy-done, bf16[1,2048,768]{2,1,0:T(8,128)(2,1)S(1)} %copy-done.1, bf16[1,768,2048]{2,1,0:T(8,128)(2,1)S(1)} %copy-done.2, ...), custom_call_target="tpu_custom_call" | custom-call | flops 131072 | bytes 15728 | tf_op jit(solution)/shard_map/experts/pallas_call | solution.py:208
  64.5 0.4 collective-permute-start.26
  64.9 1.4 %collective-permute-done.23.rest_7_ = bf16[32,2048]{1,0:T(8,128)(2,1)S(1)} collective-permute-done((bf16[32,2048]{1,0:T(8,128)(2,1)S(1)}, bf16[32,2048]{1,0:T(8,128)(2,1)S(1)}, u32[]{:S(2)}, u32[]{:S(2)}) %collective-permute-start.23) | collective-permute-done | bytes 131104 | tf_op jit(solution)/shard_map/back_5/ppermute | solution.py:23
  66.2 1.0 %collective-permute-start.27 = (bf16[32,2048]{1,0:T(8,128)(2,1)S(1)}, bf16[32,2048]{1,0:T(8,128)(2,1)S(1)}, u32[]{:S(2)}, u32[]{:S(2)}) collective-permute-start(bf16[32,2048]{1,0:T(8,128)(2,1)S(1)} %get-tuple-element.88), channel_id=1, source_target_pairs={{0,7},{1,6},{2,5},{3,4},{4,3},{5,2},{6,1},{7,0},{8,15},{9,14},{10,... | collective-permute-start | bytes 393224 | tf_op jit(solution)/shard_map/back_7/ppermute | solution.py:23
  67.2 7.6 %collective-permute-done.17.rest_5_ = bf16[32,2048]{1,0:T(8,128)(2,1)S(1)} collective-permute-done((bf16[32,2048]{1,0:T(8,128)(2,1)S(1)}, bf16[32,2048]{1,0:T(8,128)(2,1)S(1)}, u32[]{:S(2)}, u32[]{:S(2)}) %collective-permute-start.17) | collective-permute-done | bytes 131104 | tf_op jit(solution)/shard_map/back_3/ppermute | solution.py:23
  74.9 0.8 %collective-permute-done.26.rest_8_ = bf16[32,2048]{1,0:T(8,128)(2,1)S(1)} collective-permute-done((bf16[32,2048]{1,0:T(8,128)(2,1)S(1)}, bf16[32,2048]{1,0:T(8,128)(2,1)S(1)}, u32[]{:S(2)}, u32[]{:S(2)}) %collective-permute-start.26) | collective-permute-done | bytes 131104 | tf_op jit(solution)/shard_map/back_6/ppermute | solution.py:23
  75.7 2.8 %collective-permute-done.27.rest_9_ = bf16[32,2048]{1,0:T(8,128)(2,1)S(1)} collective-permute-done((bf16[32,2048]{1,0:T(8,128)(2,1)S(1)}, bf16[32,2048]{1,0:T(8,128)(2,1)S(1)}, u32[]{:S(2)}, u32[]{:S(2)}) %collective-permute-start.27) | collective-permute-done | bytes 131104 | tf_op jit(solution)/shard_map/back_7/ppermute | solution.py:23
  78.5 1.0 %combine.1 = bf16[1,128,2048]{2,1,0:T(8,128)(2,1)} custom-call(bf16[128,256]{1,0:T(8,128)(2,1)S(1)} %get-tuple-element.47.weight_ref, bf16[128,1024]{1,0:T(8,128)(2,1)S(1)} %get-tuple-element.57.rest_4_.rest_0_, bf16[128,1024]{1,0:T(8,128)(2,1)S(1)} %get-tuple-element.68.rest_1_, bf16[32,2048]{1,0:T(8,128)(2,1)S(1)} %get-tuple-element.73.rest_2_, ...), custom_call_target="tpu_custom_call" | custom-call | flops 268435456 | bytes 2097152 | tf_op jit(solution)/shard_map/combine/pallas_call | solution.py:275
  (37 shorter events, 0.9 us)
Async XLA Ops:
  0.0 8.9 %copy-start.8 = (f32[1,128,2]{1,2,0:T(2,128)S(1)}, f32[1,128,2]{1,2,0:T(2,128)}, u32[]{:S(2)}) copy-start(f32[1,128,2]{1,2,0:T(2,128)} %param.14) | copy-start | bytes 3076
  0.0 8.9 %copy-start.7 = (s32[1,128,2]{1,2,0:T(2,128)S(1)}, s32[1,128,2]{1,2,0:T(2,128)}, u32[]{:S(2)}) copy-start(s32[1,128,2]{1,2,0:T(2,128)} %param.13) | copy-start | bytes 3076
  1.2 8.0 %collective-permute-start = (bf16[3,128,256]{2,1,0:T(8,128)(2,1)S(1)}, bf16[3,128,256]{2,1,0:T(8,128)(2,1)S(1)}, u32[]{:S(2)}, u32[]{:S(2)}) collective-permute-start(bf16[3,128,256]{2,1,0:T(8,128)(2,1)S(1)} %get-tuple-element.50), channel_id=1, source_target_pairs={{0,8},{8,0},{16,24},{24,16},{1,9},{9,1},{17,25},{25,17},{2,10},{10... | collective-permute-start | bytes 589832 | tf_op jit(solution)/shard_map/qkv0_/ppermute | solution.py:23
  1.5 8.9 %collective-permute-start.1 = (bf16[3,128,256]{2,1,0:T(8,128)(2,1)S(1)}, bf16[3,128,256]{2,1,0:T(8,128)(2,1)S(1)}, u32[]{:S(2)}, u32[]{:S(2)}) collective-permute-start(bf16[3,128,256]{2,1,0:T(8,128)(2,1)S(1)} %get-tuple-element.51), channel_id=1, source_target_pairs={{0,16},{8,24},{16,0},{24,8},{1,17},{9,25},{17,1},{25,9},{2,18},{10... | collective-permute-start | bytes 589832 | tf_op jit(solution)/shard_map/qkv0_/ppermute | solution.py:23
  2.8 9.5 %collective-permute-start.2 = (bf16[3,128,256]{2,1,0:T(8,128)(2,1)S(1)}, bf16[3,128,256]{2,1,0:T(8,128)(2,1)S(1)}, u32[]{:S(2)}, u32[]{:S(2)}) collective-permute-start(bf16[3,128,256]{2,1,0:T(8,128)(2,1)S(1)} %get-tuple-element.52), channel_id=1, source_target_pairs={{0,24},{8,16},{16,8},{24,0},{1,25},{9,17},{17,9},{25,1},{2,26},{10... | collective-permute-start | bytes 589832 | tf_op jit(solution)/shard_map/qkv0_/ppermute | solution.py:23
  3.9 1.0 %copy-start.3 = (bf16[1,128,2048]{2,1,0:T(8,128)(2,1)S(1)}, bf16[1,128,2048]{2,1,0:T(8,128)(2,1)}, u32[]{:S(2)}) copy-start(bf16[1,128,2048]{2,1,0:T(8,128)(2,1)} %q_ref.3) | copy-start | bytes 1572868
  5.0 1.0 %copy-start.4 = (bf16[1,128,2048]{2,1,0:T(8,128)(2,1)S(1)}, bf16[1,128,2048]{2,1,0:T(8,128)(2,1)}, u32[]{:S(2)}) copy-start(bf16[1,128,2048]{2,1,0:T(8,128)(2,1)} %k_ref.3) | copy-start | bytes 1572868
  6.0 1.0 %copy-start.5 = (bf16[1,128,2048]{2,1,0:T(8,128)(2,1)S(1)}, bf16[1,128,2048]{2,1,0:T(8,128)(2,1)}, u32[]{:S(2)}) copy-start(bf16[1,128,2048]{2,1,0:T(8,128)(2,1)} %v_ref.3) | copy-start | bytes 1572868
  7.4 8.1 %collective-permute-start.6 = (bf16[3,128,256]{2,1,0:T(8,128)(2,1)S(1)}, bf16[3,128,256]{2,1,0:T(8,128)(2,1)S(1)}, u32[]{:S(2)}, u32[]{:S(2)}) collective-permute-start(bf16[3,128,256]{2,1,0:T(8,128)(2,1)S(1)} %get-tuple-element.60), channel_id=1, source_target_pairs={{0,8},{8,0},{16,24},{24,16},{1,9},{9,1},{17,25},{25,17},{2,10},{10... | collective-permute-start | bytes 589832 | tf_op jit(solution)/shard_map/qkv1_/ppermute | solution.py:23
  7.7 10.5 %collective-permute-start.7 = (bf16[3,128,256]{2,1,0:T(8,128)(2,1)S(1)}, bf16[3,128,256]{2,1,0:T(8,128)(2,1)S(1)}, u32[]{:S(2)}, u32[]{:S(2)}) collective-permute-start(bf16[3,128,256]{2,1,0:T(8,128)(2,1)S(1)} %get-tuple-element.61), channel_id=1, source_target_pairs={{0,16},{8,24},{16,0},{24,8},{1,17},{9,25},{17,1},{25,9},{2,18},{10... | collective-permute-start | bytes 589832 | tf_op jit(solution)/shard_map/qkv1_/ppermute | solution.py:23
  9.2 11.5 %collective-permute-start.8 = (bf16[3,128,256]{2,1,0:T(8,128)(2,1)S(1)}, bf16[3,128,256]{2,1,0:T(8,128)(2,1)S(1)}, u32[]{:S(2)}, u32[]{:S(2)}) collective-permute-start(bf16[3,128,256]{2,1,0:T(8,128)(2,1)S(1)} %get-tuple-element.62), channel_id=1, source_target_pairs={{0,24},{8,16},{16,8},{24,0},{1,25},{9,17},{17,9},{25,1},{2,26},{10... | collective-permute-start | bytes 589832 | tf_op jit(solution)/shard_map/qkv1_/ppermute | solution.py:23
  13.2 9.2 %collective-permute-start.3 = (bf16[128,256]{1,0:T(8,128)(2,1)S(1)}, bf16[128,256]{1,0:T(8,128)(2,1)S(1)}, u32[]{:S(2)}, u32[]{:S(2)}) collective-permute-start(bf16[128,256]{1,0:T(8,128)(2,1)S(1)} %get-tuple-element.54), channel_id=1, source_target_pairs={{0,8},{8,0},{16,24},{24,16},{1,9},{9,1},{17,25},{25,17},{2,10},{10... | collective-permute-start | bytes 196616 | tf_op jit(solution)/shard_map/heads0_/ppermute | solution.py:23
  13.5 10.1 %collective-permute-start.4 = (bf16[128,256]{1,0:T(8,128)(2,1)S(1)}, bf16[128,256]{1,0:T(8,128)(2,1)S(1)}, u32[]{:S(2)}, u32[]{:S(2)}) collective-permute-start(bf16[128,256]{1,0:T(8,128)(2,1)S(1)} %get-tuple-element.55), channel_id=1, source_target_pairs={{0,16},{8,24},{16,0},{24,8},{1,17},{9,25},{17,1},{25,9},{2,18},{10... | collective-permute-start | bytes 196616 | tf_op jit(solution)/shard_map/heads0_/ppermute | solution.py:23
  15.5 29.0 %copy-start = (bf16[1,2048,768]{2,1,0:T(8,128)(2,1)S(1)}, bf16[1,2048,768]{2,1,0:T(8,128)(2,1)}, u32[]{:S(2)}) copy-start(bf16[1,2048,768]{2,1,0:T(8,128)(2,1)} %gate_ref.5) | copy-start | bytes 9437188
  15.5 29.0 %copy-start.1 = (bf16[1,2048,768]{2,1,0:T(8,128)(2,1)S(1)}, bf16[1,2048,768]{2,1,0:T(8,128)(2,1)}, u32[]{:S(2)}) copy-start(bf16[1,2048,768]{2,1,0:T(8,128)(2,1)} %up_ref.5) | copy-start | bytes 9437188
  15.5 29.0 %copy-start.2 = (bf16[1,768,2048]{2,1,0:T(8,128)(2,1)S(1)}, bf16[1,768,2048]{2,1,0:T(8,128)(2,1)}, u32[]{:S(2)}) copy-start(bf16[1,768,2048]{2,1,0:T(8,128)(2,1)} %down_ref.5) | copy-start | bytes 9437188
  15.5 29.0 %copy-start.6 = (f32[2048]{0:T(1024)S(1)}, f32[2048]{0:T(1024)}, u32[]{:S(2)}) copy-start(f32[2048]{0:T(1024)} %param.12) | copy-start | bytes 24580
  15.5 8.1 %collective-permute-start.5 = (bf16[128,256]{1,0:T(8,128)(2,1)S(1)}, bf16[128,256]{1,0:T(8,128)(2,1)S(1)}, u32[]{:S(2)}, u32[]{:S(2)}) collective-permute-start(bf16[128,256]{1,0:T(8,128)(2,1)S(1)} %get-tuple-element.56), channel_id=1, source_target_pairs={{0,24},{8,16},{16,8},{24,0},{1,25},{9,17},{17,9},{25,1},{2,26},{10... | collective-permute-start | bytes 196616 | tf_op jit(solution)/shard_map/heads0_/ppermute | solution.py:23
  21.7 9.1 %collective-permute-start.9 = (bf16[128,256]{1,0:T(8,128)(2,1)S(1)}, bf16[128,256]{1,0:T(8,128)(2,1)S(1)}, u32[]{:S(2)}, u32[]{:S(2)}) collective-permute-start(bf16[128,256]{1,0:T(8,128)(2,1)S(1)} %get-tuple-element.64), channel_id=1, source_target_pairs={{0,8},{8,0},{16,24},{24,16},{1,9},{9,1},{17,25},{25,17},{2,10},{10... | collective-permute-start | bytes 196616 | tf_op jit(solution)/shard_map/heads1_/ppermute | solution.py:23
  22.0 8.8 %collective-permute-start.10 = (bf16[128,256]{1,0:T(8,128)(2,1)S(1)}, bf16[128,256]{1,0:T(8,128)(2,1)S(1)}, u32[]{:S(2)}, u32[]{:S(2)}) collective-permute-start(bf16[128,256]{1,0:T(8,128)(2,1)S(1)} %get-tuple-element.65), channel_id=1, source_target_pairs={{0,16},{8,24},{16,0},{24,8},{1,17},{9,25},{17,1},{25,9},{2,18},{10... | collective-permute-start | bytes 196616 | tf_op jit(solution)/shard_map/heads1_/ppermute | solution.py:23
  23.9 6.9 %collective-permute-start.11 = (bf16[128,256]{1,0:T(8,128)(2,1)S(1)}, bf16[128,256]{1,0:T(8,128)(2,1)S(1)}, u32[]{:S(2)}, u32[]{:S(2)}) collective-permute-start(bf16[128,256]{1,0:T(8,128)(2,1)S(1)} %get-tuple-element.67), channel_id=1, source_target_pairs={{0,24},{8,16},{16,8},{24,0},{1,25},{9,17},{17,9},{25,1},{2,26},{10... | collective-permute-start | bytes 196616 | tf_op jit(solution)/shard_map/heads1_/ppermute | solution.py:23
  24.7 13.4 %collective-permute-start.18 = (bf16[32,1024]{1,0:T(8,128)(2,1)S(1)}, bf16[32,1024]{1,0:T(8,128)(2,1)S(1)}, u32[]{:S(2)}, u32[]{:S(2)}) collective-permute-start(bf16[32,1024]{1,0:T(8,128)(2,1)S(1)} %get-tuple-element.77), channel_id=1, source_target_pairs={{0,4},{1,5},{2,6},{3,7},{4,0},{5,1},{6,2},{7,3},{8,12},{9,13},{10,... | collective-permute-start | bytes 196616 | tf_op jit(solution)/shard_map/rows0_4/ppermute | solution.py:23
  27.0 7.7 %collective-permute-start.20 = (bf16[32,1024]{1,0:T(8,128)(2,1)S(1)}, bf16[32,1024]{1,0:T(8,128)(2,1)S(1)}, u32[]{:S(2)}, u32[]{:S(2)}) collective-permute-start(bf16[32,1024]{1,0:T(8,128)(2,1)S(1)} %get-tuple-element.80), channel_id=1, source_target_pairs={{0,5},{1,4},{2,7},{3,6},{4,1},{5,0},{6,3},{7,2},{8,13},{9,12},{10,... | collective-permute-start | bytes 196616 | tf_op jit(solution)/shard_map/rows0_5/ppermute | solution.py:23
  31.3 15.1 %collective-permute-start.12 = (bf16[32,2048]{1,0:T(8,128)(2,1)S(1)}, bf16[32,2048]{1,0:T(8,128)(2,1)S(1)}, u32[]{:S(2)}, u32[]{:S(2)}) collective-permute-start(bf16[32,2048]{1,0:T(8,128)(2,1)S(1)} %get-tuple-element.70), channel_id=1, source_target_pairs={{0,1},{1,0},{2,3},{3,2},{4,5},{5,4},{6,7},{7,6},{8,9},{9,8},{10,11... | collective-permute-start | bytes 393224 | tf_op jit(solution)/shard_map/rows_1/ppermute | solution.py:23
  33.6 17.7 %collective-permute-start.13 = (bf16[32,2048]{1,0:T(8,128)(2,1)S(1)}, bf16[32,2048]{1,0:T(8,128)(2,1)S(1)}, u32[]{:S(2)}, u32[]{:S(2)}) collective-permute-start(bf16[32,2048]{1,0:T(8,128)(2,1)S(1)} %get-tuple-element.71), channel_id=1, source_target_pairs={{0,2},{1,3},{2,0},{3,1},{4,6},{5,7},{6,4},{7,5},{8,10},{9,11},{10,... | collective-permute-start | bytes 393224 | tf_op jit(solution)/shard_map/rows_2/ppermute | solution.py:23
  34.7 7.6 %collective-permute-start.21 = (bf16[32,1024]{1,0:T(8,128)(2,1)S(1)}, bf16[32,1024]{1,0:T(8,128)(2,1)S(1)}, u32[]{:S(2)}, u32[]{:S(2)}) collective-permute-start(bf16[32,1024]{1,0:T(8,128)(2,1)S(1)} %get-tuple-element.82), channel_id=1, source_target_pairs={{0,5},{1,4},{2,7},{3,6},{4,1},{5,0},{6,3},{7,2},{8,13},{9,12},{10,... | collective-permute-start | bytes 196616 | tf_op jit(solution)/shard_map/rows1_5/ppermute | solution.py:23
  38.1 5.6 %collective-permute-start.19 = (bf16[32,1024]{1,0:T(8,128)(2,1)S(1)}, bf16[32,1024]{1,0:T(8,128)(2,1)S(1)}, u32[]{:S(2)}, u32[]{:S(2)}) collective-permute-start(bf16[32,1024]{1,0:T(8,128)(2,1)S(1)} %get-tuple-element.79), channel_id=1, source_target_pairs={{0,4},{1,5},{2,6},{3,7},{4,0},{5,1},{6,2},{7,3},{8,12},{9,13},{10,... | collective-permute-start | bytes 196616 | tf_op jit(solution)/shard_map/rows1_4/ppermute | solution.py:23
  38.2 13.0 %collective-permute-start.14 = (bf16[32,2048]{1,0:T(8,128)(2,1)S(1)}, bf16[32,2048]{1,0:T(8,128)(2,1)S(1)}, u32[]{:S(2)}, u32[]{:S(2)}) collective-permute-start(bf16[32,2048]{1,0:T(8,128)(2,1)S(1)} %get-tuple-element.72), channel_id=1, source_target_pairs={{0,3},{1,2},{2,1},{3,0},{4,7},{5,6},{6,5},{7,4},{8,11},{9,10},{10,... | collective-permute-start | bytes 393224 | tf_op jit(solution)/shard_map/rows_3/ppermute | solution.py:23
  42.3 11.2 %collective-permute-start.24 = (bf16[32,2048]{1,0:T(8,128)(2,1)S(1)}, bf16[32,2048]{1,0:T(8,128)(2,1)S(1)}, u32[]{:S(2)}, u32[]{:S(2)}) collective-permute-start(bf16[32,2048]{1,0:T(8,128)(2,1)S(1)} %get-tuple-element.85), channel_id=1, source_target_pairs={{0,6},{1,7},{2,4},{3,5},{4,2},{5,3},{6,0},{7,1},{8,14},{9,15},{10,... | collective-permute-start | bytes 393224 | tf_op jit(solution)/shard_map/rows_6/ppermute | solution.py:23
  43.7 18.8 %collective-permute-start.25 = (bf16[32,2048]{1,0:T(8,128)(2,1)S(1)}, bf16[32,2048]{1,0:T(8,128)(2,1)S(1)}, u32[]{:S(2)}, u32[]{:S(2)}) collective-permute-start(bf16[32,2048]{1,0:T(8,128)(2,1)S(1)} %get-tuple-element.86), channel_id=1, source_target_pairs={{0,7},{1,6},{2,5},{3,4},{4,3},{5,2},{6,1},{7,0},{8,15},{9,14},{10,... | collective-permute-start | bytes 393224 | tf_op jit(solution)/shard_map/rows_7/ppermute | solution.py:23
  46.4 18.1 %collective-permute-start.22 = (bf16[32,2048]{1,0:T(8,128)(2,1)S(1)}, bf16[32,2048]{1,0:T(8,128)(2,1)S(1)}, u32[]{:S(2)}, u32[]{:S(2)}) collective-permute-start(bf16[32,2048]{1,0:T(8,128)(2,1)S(1)} %get-tuple-element.83), channel_id=1, source_target_pairs={{0,4},{1,5},{2,6},{3,7},{4,0},{5,1},{6,2},{7,3},{8,12},{9,13},{10,... | collective-permute-start | bytes 393224 | tf_op jit(solution)/shard_map/back_4/ppermute | solution.py:23
  51.3 15.0 %collective-permute-start.23 = (bf16[32,2048]{1,0:T(8,128)(2,1)S(1)}, bf16[32,2048]{1,0:T(8,128)(2,1)S(1)}, u32[]{:S(2)}, u32[]{:S(2)}) collective-permute-start(bf16[32,2048]{1,0:T(8,128)(2,1)S(1)} %get-tuple-element.84), channel_id=1, source_target_pairs={{0,5},{1,4},{2,7},{3,6},{4,1},{5,0},{6,3},{7,2},{8,13},{9,12},{10,... | collective-permute-start | bytes 393224 | tf_op jit(solution)/shard_map/back_5/ppermute | solution.py:23
  52.9 14.3 %collective-permute-start.15 = (bf16[32,2048]{1,0:T(8,128)(2,1)S(1)}, bf16[32,2048]{1,0:T(8,128)(2,1)S(1)}, u32[]{:S(2)}, u32[]{:S(2)}) collective-permute-start(bf16[32,2048]{1,0:T(8,128)(2,1)S(1)} %get-tuple-element.74), channel_id=1, source_target_pairs={{0,1},{1,0},{2,3},{3,2},{4,5},{5,4},{6,7},{7,6},{8,9},{9,8},{10,11... | collective-permute-start | bytes 393224 | tf_op jit(solution)/shard_map/back_1/ppermute | solution.py:23
  53.5 13.7 %collective-permute-start.16 = (bf16[32,2048]{1,0:T(8,128)(2,1)S(1)}, bf16[32,2048]{1,0:T(8,128)(2,1)S(1)}, u32[]{:S(2)}, u32[]{:S(2)}) collective-permute-start(bf16[32,2048]{1,0:T(8,128)(2,1)S(1)} %get-tuple-element.75), channel_id=1, source_target_pairs={{0,2},{1,3},{2,0},{3,1},{4,6},{5,7},{6,4},{7,5},{8,10},{9,11},{10,... | collective-permute-start | bytes 393224 | tf_op jit(solution)/shard_map/back_2/ppermute | solution.py:23
  62.6 12.3 %collective-permute-start.17 = (bf16[32,2048]{1,0:T(8,128)(2,1)S(1)}, bf16[32,2048]{1,0:T(8,128)(2,1)S(1)}, u32[]{:S(2)}, u32[]{:S(2)}) collective-permute-start(bf16[32,2048]{1,0:T(8,128)(2,1)S(1)} %get-tuple-element.76), channel_id=1, source_target_pairs={{0,3},{1,2},{2,1},{3,0},{4,7},{5,6},{6,5},{7,4},{8,11},{9,10},{10,... | collective-permute-start | bytes 393224 | tf_op jit(solution)/shard_map/back_3/ppermute | solution.py:23
  64.5 11.3 %collective-permute-start.26 = (bf16[32,2048]{1,0:T(8,128)(2,1)S(1)}, bf16[32,2048]{1,0:T(8,128)(2,1)S(1)}, u32[]{:S(2)}, u32[]{:S(2)}) collective-permute-start(bf16[32,2048]{1,0:T(8,128)(2,1)S(1)} %get-tuple-element.87), channel_id=1, source_target_pairs={{0,6},{1,7},{2,4},{3,5},{4,2},{5,3},{6,0},{7,1},{8,14},{9,15},{10,... | collective-permute-start | bytes 393224 | tf_op jit(solution)/shard_map/back_6/ppermute | solution.py:23
  66.2 12.3 %collective-permute-start.27 = (bf16[32,2048]{1,0:T(8,128)(2,1)S(1)}, bf16[32,2048]{1,0:T(8,128)(2,1)S(1)}, u32[]{:S(2)}, u32[]{:S(2)}) collective-permute-start(bf16[32,2048]{1,0:T(8,128)(2,1)S(1)} %get-tuple-element.88), channel_id=1, source_target_pairs={{0,7},{1,6},{2,5},{3,4},{4,3},{5,2},{6,1},{7,0},{8,15},{9,14},{10,... | collective-permute-start | bytes 393224 | tf_op jit(solution)/shard_map/back_7/ppermute | solution.py:23

commit v8 on v6

--- a/solution.py
+++ b/solution.py
@@ -252,17 +252,19 @@
     kept, blocks = rest[:chunks], rest[chunks : chunks + experts]
     out_ref, made_ref, sems = rest[chunks + experts :]
     width = kept[0].shape[1] // groups
+    step = 2 if groups % 2 == 0 else 1
     copies = []
-    for g in range(groups):
-        span = slice(g * chunks * width, (g + 1) * chunks * width)
+    for first in range(0, groups, step):
+        members = range(first, first + step)
+        span = slice(first * chunks * width, (first + step) * chunks * width)
         rows = jnp.concatenate([block[:, span] for block in blocks], axis=0)
         total = jnp.concatenate(
-            [ref[:, g * width : (g + 1) * width] for ref in kept], axis=1
+            [ref[:, g * width : (g + 1) * width] for g in members for ref in kept], axis=1
         ).astype(F32)
         total += jnp.dot(weight_ref[...], rows, preferred_element_type=F32)
         made_ref[:, span] = total.astype(BF16)
         copies.append(
-            pltpu.make_async_copy(made_ref.at[:, span], out_ref.at[0, :, span], sems.at[g])
+            pltpu.make_async_copy(made_ref.at[:, span], out_ref.at[0, :, span], sems.at[first])
         )
         copies[-1].start()
     for copy in copies:

time: 80.5 us -> 80.5 us (level)
  no operation moved by 1% of the time
where the time goes in v8:
time: 80.5 us; the launch traced here: 79.3 us
  waiting for transfers between devices  33.9 us (42%)
  starting transfers between devices  31.3 us (39%)
  Pallas kernels  10.8 us (13%)
  local copies, waits for them, and re-layouts  3.15 us (4%)
    ppermute x28, waiting for transfers between devices, swap(): return lax.ppermute(x, axis, [(i, i ^ distance) for i in range(size)])  33.9 us
    ppermute x28, starting transfers between devices, swap(): return lax.ppermute(x, axis, [(i, i ^ distance) for i in range(size)])  31.3 us
    pallas_call x3, Pallas kernels, run_experts(): pl.pallas_call(functools.partial(experts_kernel, groups, chunks, width, h...  5.42 us
    unnamed x18, local copies, waits for them, and re-layouts  3.15 us
    pallas_call x2, Pallas kernels, attend(): pl.pallas_call(functools.partial(attend_kernel, groups, width, head_size)...  1.9 us
  transfers between devices with their start and end apart: 28, of which 12 were waited for; matrix products, arithmetic and copies ran while one was open for 0% of the time, Pallas kernels for 11%

profile of v8, /device:TPU:11, one launch (start us, length us, event | category | flops | bytes accessed | tf_op | source)
XLA Modules:
  0.0 79.3 jit_solution(4548298223910298866)
XLA Ops:
  0.0 1.2 %pack_heads.3 = (bf16[3,128,256]{2,1,0:T(8,128)(2,1)S(1)}, bf16[3,128,256]{2,1,0:T(8,128)(2,1)S(1)}, bf16[3,128,256]{2,1,0:T(8,128)(2,1)S(1)}) custom-call(bf16[1,128,2048]{2,1,0:T(8,128)(2,1)} %q_ref.3, bf16[1,128,2048]{2,1,0:T(8,128)(2,1)} %k_ref.3, bf16[1,128,2048]{2,1,0:T(8,128)(2,1)} %v_ref.3), custom_call_target="tpu_custom_call" | custom-call | bytes 1179648 | tf_op jit(solution)/shard_map/pack_heads/pallas_call | solution.py:55
  1.2 0.3 collective-permute-start
  1.5 1.2 %collective-permute-start.1 = (bf16[3,128,256]{2,1,0:T(8,128)(2,1)S(1)}, bf16[3,128,256]{2,1,0:T(8,128)(2,1)S(1)}, u32[]{:S(2)}, u32[]{:S(2)}) collective-permute-start(bf16[3,128,256]{2,1,0:T(8,128)(2,1)S(1)} %get-tuple-element.50), channel_id=1, source_target_pairs={{0,16},{8,24},{16,0},{24,8},{1,17},{9,25},{17,1},{25,9},{2,18},{10... | collective-permute-start | bytes 589832 | tf_op jit(solution)/shard_map/qkv0_/ppermute | solution.py:23
  2.8 1.2 %collective-permute-start.2 = (bf16[3,128,256]{2,1,0:T(8,128)(2,1)S(1)}, bf16[3,128,256]{2,1,0:T(8,128)(2,1)S(1)}, u32[]{:S(2)}, u32[]{:S(2)}) collective-permute-start(bf16[3,128,256]{2,1,0:T(8,128)(2,1)S(1)} %get-tuple-element.51), channel_id=1, source_target_pairs={{0,24},{8,16},{16,8},{24,0},{1,25},{9,17},{17,9},{25,1},{2,26},{10... | collective-permute-start | bytes 589832 | tf_op jit(solution)/shard_map/qkv0_/ppermute | solution.py:23
  3.9 1.0 %copy-done.3 = bf16[1,128,2048]{2,1,0:T(8,128)(2,1)S(1)} copy-done((bf16[1,128,2048]{2,1,0:T(8,128)(2,1)S(1)}, bf16[1,128,2048]{2,1,0:T(8,128)(2,1)}, u32[]{:S(2)}) %copy-start.3) | copy-done | bytes 524312
  5.0 1.0 %copy-done.4 = bf16[1,128,2048]{2,1,0:T(8,128)(2,1)S(1)} copy-done((bf16[1,128,2048]{2,1,0:T(8,128)(2,1)S(1)}, bf16[1,128,2048]{2,1,0:T(8,128)(2,1)}, u32[]{:S(2)}) %copy-start.4) | copy-done | bytes 524312
  6.0 1.0 %copy-done.5 = bf16[1,128,2048]{2,1,0:T(8,128)(2,1)S(1)} copy-done((bf16[1,128,2048]{2,1,0:T(8,128)(2,1)S(1)}, bf16[1,128,2048]{2,1,0:T(8,128)(2,1)}, u32[]{:S(2)}) %copy-start.5) | copy-done | bytes 524312
  7.1 0.3 pack_heads.2
  7.4 0.3 collective-permute-start.6
  7.7 1.2 %collective-permute-start.7 = (bf16[3,128,256]{2,1,0:T(8,128)(2,1)S(1)}, bf16[3,128,256]{2,1,0:T(8,128)(2,1)S(1)}, u32[]{:S(2)}, u32[]{:S(2)}) collective-permute-start(bf16[3,128,256]{2,1,0:T(8,128)(2,1)S(1)} %get-tuple-element.60), channel_id=1, source_target_pairs={{0,16},{8,24},{16,0},{24,8},{1,17},{9,25},{17,1},{25,9},{2,18},{10... | collective-permute-start | bytes 589832 | tf_op jit(solution)/shard_map/qkv1_/ppermute | solution.py:23
  8.9 0.2 spread_gates.1
  9.2 1.2 %collective-permute-start.8 = (bf16[3,128,256]{2,1,0:T(8,128)(2,1)S(1)}, bf16[3,128,256]{2,1,0:T(8,128)(2,1)S(1)}, u32[]{:S(2)}, u32[]{:S(2)}) collective-permute-start(bf16[3,128,256]{2,1,0:T(8,128)(2,1)S(1)} %get-tuple-element.61), channel_id=1, source_target_pairs={{0,24},{8,16},{16,8},{24,0},{1,25},{9,17},{17,9},{25,1},{2,26},{10... | collective-permute-start | bytes 589832 | tf_op jit(solution)/shard_map/qkv1_/ppermute | solution.py:23
  10.4 1.8 %collective-permute-done.2.rest_3_ = bf16[3,128,256]{2,1,0:T(8,128)(2,1)S(1)} collective-permute-done((bf16[3,128,256]{2,1,0:T(8,128)(2,1)S(1)}, bf16[3,128,256]{2,1,0:T(8,128)(2,1)S(1)}, u32[]{:S(2)}, u32[]{:S(2)}) %collective-permute-start.2) | collective-permute-done | bytes 196640 | tf_op jit(solution)/shard_map/qkv0_/ppermute | solution.py:23
  12.3 0.9 %attend.2 = (bf16[128,256]{1,0:T(8,128)(2,1)S(1)}, bf16[128,256]{1,0:T(8,128)(2,1)S(1)}, bf16[128,256]{1,0:T(8,128)(2,1)S(1)}, bf16[128,256]{1,0:T(8,128)(2,1)S(1)}) custom-call(bf16[3,128,256]{2,1,0:T(8,128)(2,1)S(1)} %get-tuple-element.48.rest_0_, bf16[3,128,256]{2,1,0:T(8,128)(2,1)S(1)} %collective-permute-done.rest_1_, ...), custom_call_target="tpu_custom_call" | custom-call | flops 10737418240 | bytes 10485760 | tf_op jit(solution)/shard_map/attend/pallas_call | solution.py:98
  13.2 0.3 collective-permute-start.3
  13.5 0.2 collective-permute-start.4
  13.8 1.8 %collective-permute-done.6.rest_1_ = bf16[3,128,256]{2,1,0:T(8,128)(2,1)S(1)} collective-permute-done((bf16[3,128,256]{2,1,0:T(8,128)(2,1)S(1)}, bf16[3,128,256]{2,1,0:T(8,128)(2,1)S(1)}, u32[]{:S(2)}, u32[]{:S(2)}) %collective-permute-start.6) | collective-permute-done | bytes 196640 | tf_op jit(solution)/shard_map/qkv1_/ppermute | solution.py:23
  15.5 1.3 %collective-permute-start.5 = (bf16[128,256]{1,0:T(8,128)(2,1)S(1)}, bf16[128,256]{1,0:T(8,128)(2,1)S(1)}, u32[]{:S(2)}, u32[]{:S(2)}) collective-permute-start(bf16[128,256]{1,0:T(8,128)(2,1)S(1)} %get-tuple-element.55), channel_id=1, source_target_pairs={{0,24},{8,16},{16,8},{24,0},{1,25},{9,17},{17,9},{25,1},{2,26},{10... | collective-permute-start | bytes 196616 | tf_op jit(solution)/shard_map/heads0_/ppermute | solution.py:23
  16.8 1.4 %collective-permute-done.7.rest_2_ = bf16[3,128,256]{2,1,0:T(8,128)(2,1)S(1)} collective-permute-done((bf16[3,128,256]{2,1,0:T(8,128)(2,1)S(1)}, bf16[3,128,256]{2,1,0:T(8,128)(2,1)S(1)}, u32[]{:S(2)}, u32[]{:S(2)}) %collective-permute-start.7) | collective-permute-done | bytes 196640 | tf_op jit(solution)/shard_map/qkv1_/ppermute | solution.py:23
  18.2 2.5 %collective-permute-done.8.rest_3_ = bf16[3,128,256]{2,1,0:T(8,128)(2,1)S(1)} collective-permute-done((bf16[3,128,256]{2,1,0:T(8,128)(2,1)S(1)}, bf16[3,128,256]{2,1,0:T(8,128)(2,1)S(1)}, u32[]{:S(2)}, u32[]{:S(2)}) %collective-permute-start.8) | collective-permute-done | bytes 196640 | tf_op jit(solution)/shard_map/qkv1_/ppermute | solution.py:23
  20.7 1.0 %attend.3 = (bf16[128,256]{1,0:T(8,128)(2,1)S(1)}, bf16[128,256]{1,0:T(8,128)(2,1)S(1)}, bf16[128,256]{1,0:T(8,128)(2,1)S(1)}, bf16[128,256]{1,0:T(8,128)(2,1)S(1)}) custom-call(bf16[3,128,256]{2,1,0:T(8,128)(2,1)S(1)} %get-tuple-element.58.rest_0_, bf16[3,128,256]{2,1,0:T(8,128)(2,1)S(1)} %collective-permute-done.6.rest_1_, ...), custom_call_target="tpu_custom_call" | custom-call | flops 10737418240 | bytes 10485760 | tf_op jit(solution)/shard_map/attend/pallas_call | solution.py:98
  21.7 0.3 collective-permute-start.9
  22.0 0.4 collective-permute-start.10
  22.4 2.0 %collective-permute-start.11 = (bf16[128,256]{1,0:T(8,128)(2,1)S(1)}, bf16[128,256]{1,0:T(8,128)(2,1)S(1)}, u32[]{:S(2)}, u32[]{:S(2)}) collective-permute-start(bf16[128,256]{1,0:T(8,128)(2,1)S(1)} %get-tuple-element.65), channel_id=1, source_target_pairs={{0,24},{8,16},{16,8},{24,0},{1,25},{9,17},{17,9},{25,1},{2,26},{10... | collective-permute-start | bytes 196616 | tf_op jit(solution)/shard_map/heads1_/ppermute | solution.py:23
  24.6 2.4 %collective-permute-start.18 = (bf16[32,1024]{1,0:T(8,128)(2,1)S(1)}, bf16[32,1024]{1,0:T(8,128)(2,1)S(1)}, u32[]{:S(2)}, u32[]{:S(2)}) collective-permute-start(bf16[32,1024]{1,0:T(8,128)(2,1)S(1)} %get-tuple-element.75), channel_id=1, source_target_pairs={{0,4},{1,5},{2,6},{3,7},{4,0},{5,1},{6,2},{7,3},{8,12},{9,13},{10,... | collective-permute-start | bytes 196616 | tf_op jit(solution)/shard_map/rows0_4/ppermute | solution.py:23
  27.0 3.8 %collective-permute-start.20 = (bf16[32,1024]{1,0:T(8,128)(2,1)S(1)}, bf16[32,1024]{1,0:T(8,128)(2,1)S(1)}, u32[]{:S(2)}, u32[]{:S(2)}) collective-permute-start(bf16[32,1024]{1,0:T(8,128)(2,1)S(1)} %get-tuple-element.78), channel_id=1, source_target_pairs={{0,5},{1,4},{2,7},{3,6},{4,1},{5,0},{6,3},{7,2},{8,13},{9,12},{10,... | collective-permute-start | bytes 196616 | tf_op jit(solution)/shard_map/rows0_5/ppermute | solution.py:23
  30.8 0.4 select_rows.3
  31.3 2.1 %collective-permute-start.12 = (bf16[32,2048]{1,0:T(8,128)(2,1)S(1)}, bf16[32,2048]{1,0:T(8,128)(2,1)S(1)}, u32[]{:S(2)}, u32[]{:S(2)}) collective-permute-start(bf16[32,2048]{1,0:T(8,128)(2,1)S(1)} %get-tuple-element.68), channel_id=1, source_target_pairs={{0,1},{1,0},{2,3},{3,2},{4,5},{5,4},{6,7},{7,6},{8,9},{9,8},{10,11... | collective-permute-start | bytes 393224 | tf_op jit(solution)/shard_map/rows_1/ppermute | solution.py:23
  33.5 1.2 %collective-permute-done.20.rest_2_ = bf16[32,1024]{1,0:T(8,128)(2,1)S(1)} collective-permute-done((bf16[32,1024]{1,0:T(8,128)(2,1)S(1)}, bf16[32,1024]{1,0:T(8,128)(2,1)S(1)}, u32[]{:S(2)}, u32[]{:S(2)}) %collective-permute-start.20) | collective-permute-done | bytes 65568 | tf_op jit(solution)/shard_map/rows0_5/ppermute | solution.py:23
  34.7 3.4 %collective-permute-start.21 = (bf16[32,1024]{1,0:T(8,128)(2,1)S(1)}, bf16[32,1024]{1,0:T(8,128)(2,1)S(1)}, u32[]{:S(2)}, u32[]{:S(2)}) collective-permute-start(bf16[32,1024]{1,0:T(8,128)(2,1)S(1)} %get-tuple-element.80), channel_id=1, source_target_pairs={{0,5},{1,4},{2,7},{3,6},{4,1},{5,0},{6,3},{7,2},{8,13},{9,12},{10,... | collective-permute-start | bytes 196616 | tf_op jit(solution)/shard_map/rows1_5/ppermute | solution.py:23
  38.3 0.2 collective-permute-start.14
  38.5 3.5 %collective-permute-done.21.rest_3_ = bf16[32,1024]{1,0:T(8,128)(2,1)S(1)} collective-permute-done((bf16[32,1024]{1,0:T(8,128)(2,1)S(1)}, bf16[32,1024]{1,0:T(8,128)(2,1)S(1)}, u32[]{:S(2)}, u32[]{:S(2)}) %collective-permute-start.21) | collective-permute-done | bytes 65568 | tf_op jit(solution)/shard_map/rows1_5/ppermute | solution.py:23
  42.0 1.4 %collective-permute-done.19.rest_1_ = bf16[32,1024]{1,0:T(8,128)(2,1)S(1)} collective-permute-done((bf16[32,1024]{1,0:T(8,128)(2,1)S(1)}, bf16[32,1024]{1,0:T(8,128)(2,1)S(1)}, u32[]{:S(2)}, u32[]{:S(2)}) %collective-permute-start.19) | collective-permute-done | bytes 65568 | tf_op jit(solution)/shard_map/rows1_4/ppermute | solution.py:23
  43.4 0.8 collective-permute-start.25
  44.2 1.9 %experts.4 = (bf16[32,2048]{1,0:T(8,128)(2,1)S(1)}, bf16[32,2048]{1,0:T(8,128)(2,1)S(1)}) custom-call(f32[1,2048]{1,0:T(1,128)S(1)} %bitcast.7, bf16[1,2048,768]{2,1,0:T(8,128)(2,1)S(1)} %copy-done, bf16[1,2048,768]{2,1,0:T(8,128)(2,1)S(1)} %copy-done.1, bf16[1,768,2048]{2,1,0:T(8,128)(2,1)S(1)} %copy-done.2, ...), custom_call_target="tpu_custom_call" | custom-call | flops 131072 | bytes 15728 | tf_op jit(solution)/shard_map/experts/pallas_call | solution.py:208
  46.1 4.9 %collective-permute-start.22 = (bf16[32,2048]{1,0:T(8,128)(2,1)S(1)}, bf16[32,2048]{1,0:T(8,128)(2,1)S(1)}, u32[]{:S(2)}, u32[]{:S(2)}) collective-permute-start(bf16[32,2048]{1,0:T(8,128)(2,1)S(1)} %get-tuple-element.81), channel_id=1, source_target_pairs={{0,4},{1,5},{2,6},{3,7},{4,0},{5,1},{6,2},{7,3},{8,12},{9,13},{10,... | collective-permute-start | bytes 393224 | tf_op jit(solution)/shard_map/back_4/ppermute | solution.py:23
  51.0 1.7 %experts.3 = (bf16[32,2048]{1,0:T(8,128)(2,1)S(1)}, bf16[32,2048]{1,0:T(8,128)(2,1)S(1)}, bf16[32,2048]{1,0:T(8,128)(2,1)S(1)}, bf16[32,2048]{1,0:T(8,128)(2,1)S(1)}) custom-call(f32[1,2048]{1,0:T(1,128)S(1)} %bitcast.8, bf16[1,2048,768]{2,1,0:T(8,128)(2,1)S(1)} %copy-done, bf16[1,2048,768]{2,1,0:T(8,128)(2,1)S(1)} %copy-done.1, ...), custom_call_target="tpu_custom_call" | custom-call | flops 262144 | bytes 15728 | tf_op jit(solution)/shard_map/experts/pallas_call | solution.py:208
  52.6 0.5 collective-permute-start.15
  53.2 1.4 %collective-permute-start.16 = (bf16[32,2048]{1,0:T(8,128)(2,1)S(1)}, bf16[32,2048]{1,0:T(8,128)(2,1)S(1)}, u32[]{:S(2)}, u32[]{:S(2)}) collective-permute-start(bf16[32,2048]{1,0:T(8,128)(2,1)S(1)} %get-tuple-element.73), channel_id=1, source_target_pairs={{0,2},{1,3},{2,0},{3,1},{4,6},{5,7},{6,4},{7,5},{8,10},{9,11},{10,... | collective-permute-start | bytes 393224 | tf_op jit(solution)/shard_map/back_2/ppermute | solution.py:23
  54.6 7.6 %collective-permute-done.25.rest_1_ = bf16[32,2048]{1,0:T(8,128)(2,1)S(1)} collective-permute-done((bf16[32,2048]{1,0:T(8,128)(2,1)S(1)}, bf16[32,2048]{1,0:T(8,128)(2,1)S(1)}, u32[]{:S(2)}, u32[]{:S(2)}) %collective-permute-start.25) | collective-permute-done | bytes 131104 | tf_op jit(solution)/shard_map/rows_7/ppermute | solution.py:23
  62.2 1.9 %experts.5 = (bf16[32,2048]{1,0:T(8,128)(2,1)S(1)}, bf16[32,2048]{1,0:T(8,128)(2,1)S(1)}) custom-call(f32[1,2048]{1,0:T(1,128)S(1)} %bitcast.9, bf16[1,2048,768]{2,1,0:T(8,128)(2,1)S(1)} %copy-done, bf16[1,2048,768]{2,1,0:T(8,128)(2,1)S(1)} %copy-done.1, bf16[1,768,2048]{2,1,0:T(8,128)(2,1)S(1)} %copy-done.2, ...), custom_call_target="tpu_custom_call" | custom-call | flops 131072 | bytes 15728 | tf_op jit(solution)/shard_map/experts/pallas_call | solution.py:208
  64.1 0.5 collective-permute-start.26
  64.6 1.4 %collective-permute-done.23.rest_7_ = bf16[32,2048]{1,0:T(8,128)(2,1)S(1)} collective-permute-done((bf16[32,2048]{1,0:T(8,128)(2,1)S(1)}, bf16[32,2048]{1,0:T(8,128)(2,1)S(1)}, u32[]{:S(2)}, u32[]{:S(2)}) %collective-permute-start.23) | collective-permute-done | bytes 131104 | tf_op jit(solution)/shard_map/back_5/ppermute | solution.py:23
  65.9 1.1 %collective-permute-start.27 = (bf16[32,2048]{1,0:T(8,128)(2,1)S(1)}, bf16[32,2048]{1,0:T(8,128)(2,1)S(1)}, u32[]{:S(2)}, u32[]{:S(2)}) collective-permute-start(bf16[32,2048]{1,0:T(8,128)(2,1)S(1)} %get-tuple-element.86), channel_id=1, source_target_pairs={{0,7},{1,6},{2,5},{3,4},{4,3},{5,2},{6,1},{7,0},{8,15},{9,14},{10,... | collective-permute-start | bytes 393224 | tf_op jit(solution)/shard_map/back_7/ppermute | solution.py:23
  67.0 7.6 %collective-permute-done.17.rest_5_ = bf16[32,2048]{1,0:T(8,128)(2,1)S(1)} collective-permute-done((bf16[32,2048]{1,0:T(8,128)(2,1)S(1)}, bf16[32,2048]{1,0:T(8,128)(2,1)S(1)}, u32[]{:S(2)}, u32[]{:S(2)}) %collective-permute-start.17) | collective-permute-done | bytes 131104 | tf_op jit(solution)/shard_map/back_3/ppermute | solution.py:23
  74.6 0.8 %collective-permute-done.26.rest_8_ = bf16[32,2048]{1,0:T(8,128)(2,1)S(1)} collective-permute-done((bf16[32,2048]{1,0:T(8,128)(2,1)S(1)}, bf16[32,2048]{1,0:T(8,128)(2,1)S(1)}, u32[]{:S(2)}, u32[]{:S(2)}) %collective-permute-start.26) | collective-permute-done | bytes 131104 | tf_op jit(solution)/shard_map/back_6/ppermute | solution.py:23
  75.4 2.8 %collective-permute-done.27.rest_9_ = bf16[32,2048]{1,0:T(8,128)(2,1)S(1)} collective-permute-done((bf16[32,2048]{1,0:T(8,128)(2,1)S(1)}, bf16[32,2048]{1,0:T(8,128)(2,1)S(1)}, u32[]{:S(2)}, u32[]{:S(2)}) %collective-permute-start.27) | collective-permute-done | bytes 131104 | tf_op jit(solution)/shard_map/back_7/ppermute | solution.py:23
  78.2 1.1 %combine.1 = bf16[1,128,2048]{2,1,0:T(8,128)(2,1)} custom-call(bf16[128,256]{1,0:T(8,128)(2,1)S(1)} %get-tuple-element.46.weight_ref, bf16[128,1024]{1,0:T(8,128)(2,1)S(1)} %get-tuple-element.56.rest_4_.rest_0_, bf16[128,1024]{1,0:T(8,128)(2,1)S(1)} %get-tuple-element.66.rest_1_, bf16[32,2048]{1,0:T(8,128)(2,1)S(1)} %get-tuple-element.71.rest_2_, ...), custom_call_target="tpu_custom_call" | custom-call | flops 268435456 | bytes 2097152 | tf_op jit(solution)/shard_map/combine/pallas_call | solution.py:277
  (37 shorter events, 0.7 us)
Async XLA Ops:
  0.0 8.9 %copy-start.8 = (f32[1,128,2]{1,2,0:T(2,128)S(1)}, f32[1,128,2]{1,2,0:T(2,128)}, u32[]{:S(2)}) copy-start(f32[1,128,2]{1,2,0:T(2,128)} %param.14) | copy-start | bytes 3076
  0.0 8.9 %copy-start.7 = (s32[1,128,2]{1,2,0:T(2,128)S(1)}, s32[1,128,2]{1,2,0:T(2,128)}, u32[]{:S(2)}) copy-start(s32[1,128,2]{1,2,0:T(2,128)} %param.13) | copy-start | bytes 3076
  1.2 8.0 %collective-permute-start = (bf16[3,128,256]{2,1,0:T(8,128)(2,1)S(1)}, bf16[3,128,256]{2,1,0:T(8,128)(2,1)S(1)}, u32[]{:S(2)}, u32[]{:S(2)}) collective-permute-start(bf16[3,128,256]{2,1,0:T(8,128)(2,1)S(1)} %get-tuple-element.49), channel_id=1, source_target_pairs={{0,8},{8,0},{16,24},{24,16},{1,9},{9,1},{17,25},{25,17},{2,10},{10... | collective-permute-start | bytes 589832 | tf_op jit(solution)/shard_map/qkv0_/ppermute | solution.py:23
  1.5 8.9 %collective-permute-start.1 = (bf16[3,128,256]{2,1,0:T(8,128)(2,1)S(1)}, bf16[3,128,256]{2,1,0:T(8,128)(2,1)S(1)}, u32[]{:S(2)}, u32[]{:S(2)}) collective-permute-start(bf16[3,128,256]{2,1,0:T(8,128)(2,1)S(1)} %get-tuple-element.50), channel_id=1, source_target_pairs={{0,16},{8,24},{16,0},{24,8},{1,17},{9,25},{17,1},{25,9},{2,18},{10... | collective-permute-start | bytes 589832 | tf_op jit(solution)/shard_map/qkv0_/ppermute | solution.py:23
  2.8 9.5 %collective-permute-start.2 = (bf16[3,128,256]{2,1,0:T(8,128)(2,1)S(1)}, bf16[3,128,256]{2,1,0:T(8,128)(2,1)S(1)}, u32[]{:S(2)}, u32[]{:S(2)}) collective-permute-start(bf16[3,128,256]{2,1,0:T(8,128)(2,1)S(1)} %get-tuple-element.51), channel_id=1, source_target_pairs={{0,24},{8,16},{16,8},{24,0},{1,25},{9,17},{17,9},{25,1},{2,26},{10... | collective-permute-start | bytes 589832 | tf_op jit(solution)/shard_map/qkv0_/ppermute | solution.py:23
  3.9 1.0 %copy-start.3 = (bf16[1,128,2048]{2,1,0:T(8,128)(2,1)S(1)}, bf16[1,128,2048]{2,1,0:T(8,128)(2,1)}, u32[]{:S(2)}) copy-start(bf16[1,128,2048]{2,1,0:T(8,128)(2,1)} %q_ref.3) | copy-start | bytes 1572868
  5.0 1.0 %copy-start.4 = (bf16[1,128,2048]{2,1,0:T(8,128)(2,1)S(1)}, bf16[1,128,2048]{2,1,0:T(8,128)(2,1)}, u32[]{:S(2)}) copy-start(bf16[1,128,2048]{2,1,0:T(8,128)(2,1)} %k_ref.3) | copy-start | bytes 1572868
  6.0 1.0 %copy-start.5 = (bf16[1,128,2048]{2,1,0:T(8,128)(2,1)S(1)}, bf16[1,128,2048]{2,1,0:T(8,128)(2,1)}, u32[]{:S(2)}) copy-start(bf16[1,128,2048]{2,1,0:T(8,128)(2,1)} %v_ref.3) | copy-start | bytes 1572868
  7.4 8.1 %collective-permute-start.6 = (bf16[3,128,256]{2,1,0:T(8,128)(2,1)S(1)}, bf16[3,128,256]{2,1,0:T(8,128)(2,1)S(1)}, u32[]{:S(2)}, u32[]{:S(2)}) collective-permute-start(bf16[3,128,256]{2,1,0:T(8,128)(2,1)S(1)} %get-tuple-element.59), channel_id=1, source_target_pairs={{0,8},{8,0},{16,24},{24,16},{1,9},{9,1},{17,25},{25,17},{2,10},{10... | collective-permute-start | bytes 589832 | tf_op jit(solution)/shard_map/qkv1_/ppermute | solution.py:23
  7.7 10.5 %collective-permute-start.7 = (bf16[3,128,256]{2,1,0:T(8,128)(2,1)S(1)}, bf16[3,128,256]{2,1,0:T(8,128)(2,1)S(1)}, u32[]{:S(2)}, u32[]{:S(2)}) collective-permute-start(bf16[3,128,256]{2,1,0:T(8,128)(2,1)S(1)} %get-tuple-element.60), channel_id=1, source_target_pairs={{0,16},{8,24},{16,0},{24,8},{1,17},{9,25},{17,1},{25,9},{2,18},{10... | collective-permute-start | bytes 589832 | tf_op jit(solution)/shard_map/qkv1_/ppermute | solution.py:23
  9.2 11.5 %collective-permute-start.8 = (bf16[3,128,256]{2,1,0:T(8,128)(2,1)S(1)}, bf16[3,128,256]{2,1,0:T(8,128)(2,1)S(1)}, u32[]{:S(2)}, u32[]{:S(2)}) collective-permute-start(bf16[3,128,256]{2,1,0:T(8,128)(2,1)S(1)} %get-tuple-element.61), channel_id=1, source_target_pairs={{0,24},{8,16},{16,8},{24,0},{1,25},{9,17},{17,9},{25,1},{2,26},{10... | collective-permute-start | bytes 589832 | tf_op jit(solution)/shard_map/qkv1_/ppermute | solution.py:23
  13.2 9.2 %collective-permute-start.3 = (bf16[128,256]{1,0:T(8,128)(2,1)S(1)}, bf16[128,256]{1,0:T(8,128)(2,1)S(1)}, u32[]{:S(2)}, u32[]{:S(2)}) collective-permute-start(bf16[128,256]{1,0:T(8,128)(2,1)S(1)} %get-tuple-element.53), channel_id=1, source_target_pairs={{0,8},{8,0},{16,24},{24,16},{1,9},{9,1},{17,25},{25,17},{2,10},{10... | collective-permute-start | bytes 196616 | tf_op jit(solution)/shard_map/heads0_/ppermute | solution.py:23
  13.5 10.9 %collective-permute-start.4 = (bf16[128,256]{1,0:T(8,128)(2,1)S(1)}, bf16[128,256]{1,0:T(8,128)(2,1)S(1)}, u32[]{:S(2)}, u32[]{:S(2)}) collective-permute-start(bf16[128,256]{1,0:T(8,128)(2,1)S(1)} %get-tuple-element.54), channel_id=1, source_target_pairs={{0,16},{8,24},{16,0},{24,8},{1,17},{9,25},{17,1},{25,9},{2,18},{10... | collective-permute-start | bytes 196616 | tf_op jit(solution)/shard_map/heads0_/ppermute | solution.py:23
  15.5 28.7 %copy-start = (bf16[1,2048,768]{2,1,0:T(8,128)(2,1)S(1)}, bf16[1,2048,768]{2,1,0:T(8,128)(2,1)}, u32[]{:S(2)}) copy-start(bf16[1,2048,768]{2,1,0:T(8,128)(2,1)} %gate_ref.5) | copy-start | bytes 9437188
  15.5 28.7 %copy-start.1 = (bf16[1,2048,768]{2,1,0:T(8,128)(2,1)S(1)}, bf16[1,2048,768]{2,1,0:T(8,128)(2,1)}, u32[]{:S(2)}) copy-start(bf16[1,2048,768]{2,1,0:T(8,128)(2,1)} %up_ref.5) | copy-start | bytes 9437188
  15.5 28.7 %copy-start.2 = (bf16[1,768,2048]{2,1,0:T(8,128)(2,1)S(1)}, bf16[1,768,2048]{2,1,0:T(8,128)(2,1)}, u32[]{:S(2)}) copy-start(bf16[1,768,2048]{2,1,0:T(8,128)(2,1)} %down_ref.5) | copy-start | bytes 9437188
  15.5 28.7 %copy-start.6 = (f32[2048]{0:T(1024)S(1)}, f32[2048]{0:T(1024)}, u32[]{:S(2)}) copy-start(f32[2048]{0:T(1024)} %param.12) | copy-start | bytes 24580
  15.5 8.9 %collective-permute-start.5 = (bf16[128,256]{1,0:T(8,128)(2,1)S(1)}, bf16[128,256]{1,0:T(8,128)(2,1)S(1)}, u32[]{:S(2)}, u32[]{:S(2)}) collective-permute-start(bf16[128,256]{1,0:T(8,128)(2,1)S(1)} %get-tuple-element.55), channel_id=1, source_target_pairs={{0,24},{8,16},{16,8},{24,0},{1,25},{9,17},{17,9},{25,1},{2,26},{10... | collective-permute-start | bytes 196616 | tf_op jit(solution)/shard_map/heads0_/ppermute | solution.py:23
  21.7 9.1 %collective-permute-start.9 = (bf16[128,256]{1,0:T(8,128)(2,1)S(1)}, bf16[128,256]{1,0:T(8,128)(2,1)S(1)}, u32[]{:S(2)}, u32[]{:S(2)}) collective-permute-start(bf16[128,256]{1,0:T(8,128)(2,1)S(1)} %get-tuple-element.63), channel_id=1, source_target_pairs={{0,8},{8,0},{16,24},{24,16},{1,9},{9,1},{17,25},{25,17},{2,10},{10... | collective-permute-start | bytes 196616 | tf_op jit(solution)/shard_map/heads1_/ppermute | solution.py:23
  22.0 8.8 %collective-permute-start.10 = (bf16[128,256]{1,0:T(8,128)(2,1)S(1)}, bf16[128,256]{1,0:T(8,128)(2,1)S(1)}, u32[]{:S(2)}, u32[]{:S(2)}) collective-permute-start(bf16[128,256]{1,0:T(8,128)(2,1)S(1)} %get-tuple-element.64), channel_id=1, source_target_pairs={{0,16},{8,24},{16,0},{24,8},{1,17},{9,25},{17,1},{25,9},{2,18},{10... | collective-permute-start | bytes 196616 | tf_op jit(solution)/shard_map/heads1_/ppermute | solution.py:23
  22.4 8.4 %collective-permute-start.11 = (bf16[128,256]{1,0:T(8,128)(2,1)S(1)}, bf16[128,256]{1,0:T(8,128)(2,1)S(1)}, u32[]{:S(2)}, u32[]{:S(2)}) collective-permute-start(bf16[128,256]{1,0:T(8,128)(2,1)S(1)} %get-tuple-element.65), channel_id=1, source_target_pairs={{0,24},{8,16},{16,8},{24,0},{1,25},{9,17},{17,9},{25,1},{2,26},{10... | collective-permute-start | bytes 196616 | tf_op jit(solution)/shard_map/heads1_/ppermute | solution.py:23
  24.6 13.4 %collective-permute-start.18 = (bf16[32,1024]{1,0:T(8,128)(2,1)S(1)}, bf16[32,1024]{1,0:T(8,128)(2,1)S(1)}, u32[]{:S(2)}, u32[]{:S(2)}) collective-permute-start(bf16[32,1024]{1,0:T(8,128)(2,1)S(1)} %get-tuple-element.75), channel_id=1, source_target_pairs={{0,4},{1,5},{2,6},{3,7},{4,0},{5,1},{6,2},{7,3},{8,12},{9,13},{10,... | collective-permute-start | bytes 196616 | tf_op jit(solution)/shard_map/rows0_4/ppermute | solution.py:23
  27.0 7.7 %collective-permute-start.20 = (bf16[32,1024]{1,0:T(8,128)(2,1)S(1)}, bf16[32,1024]{1,0:T(8,128)(2,1)S(1)}, u32[]{:S(2)}, u32[]{:S(2)}) collective-permute-start(bf16[32,1024]{1,0:T(8,128)(2,1)S(1)} %get-tuple-element.78), channel_id=1, source_target_pairs={{0,5},{1,4},{2,7},{3,6},{4,1},{5,0},{6,3},{7,2},{8,13},{9,12},{10,... | collective-permute-start | bytes 196616 | tf_op jit(solution)/shard_map/rows0_5/ppermute | solution.py:23
  31.3 14.8 %collective-permute-start.12 = (bf16[32,2048]{1,0:T(8,128)(2,1)S(1)}, bf16[32,2048]{1,0:T(8,128)(2,1)S(1)}, u32[]{:S(2)}, u32[]{:S(2)}) collective-permute-start(bf16[32,2048]{1,0:T(8,128)(2,1)S(1)} %get-tuple-element.68), channel_id=1, source_target_pairs={{0,1},{1,0},{2,3},{3,2},{4,5},{5,4},{6,7},{7,6},{8,9},{9,8},{10,11... | collective-permute-start | bytes 393224 | tf_op jit(solution)/shard_map/rows_1/ppermute | solution.py:23
  33.3 17.7 %collective-permute-start.13 = (bf16[32,2048]{1,0:T(8,128)(2,1)S(1)}, bf16[32,2048]{1,0:T(8,128)(2,1)S(1)}, u32[]{:S(2)}, u32[]{:S(2)}) collective-permute-start(bf16[32,2048]{1,0:T(8,128)(2,1)S(1)} %get-tuple-element.69), channel_id=1, source_target_pairs={{0,2},{1,3},{2,0},{3,1},{4,6},{5,7},{6,4},{7,5},{8,10},{9,11},{10,... | collective-permute-start | bytes 393224 | tf_op jit(solution)/shard_map/rows_2/ppermute | solution.py:23
  34.7 7.3 %collective-permute-start.21 = (bf16[32,1024]{1,0:T(8,128)(2,1)S(1)}, bf16[32,1024]{1,0:T(8,128)(2,1)S(1)}, u32[]{:S(2)}, u32[]{:S(2)}) collective-permute-start(bf16[32,1024]{1,0:T(8,128)(2,1)S(1)} %get-tuple-element.80), channel_id=1, source_target_pairs={{0,5},{1,4},{2,7},{3,6},{4,1},{5,0},{6,3},{7,2},{8,13},{9,12},{10,... | collective-permute-start | bytes 196616 | tf_op jit(solution)/shard_map/rows1_5/ppermute | solution.py:23
  38.1 5.4 %collective-permute-start.19 = (bf16[32,1024]{1,0:T(8,128)(2,1)S(1)}, bf16[32,1024]{1,0:T(8,128)(2,1)S(1)}, u32[]{:S(2)}, u32[]{:S(2)}) collective-permute-start(bf16[32,1024]{1,0:T(8,128)(2,1)S(1)} %get-tuple-element.77), channel_id=1, source_target_pairs={{0,4},{1,5},{2,6},{3,7},{4,0},{5,1},{6,2},{7,3},{8,12},{9,13},{10,... | collective-permute-start | bytes 196616 | tf_op jit(solution)/shard_map/rows1_4/ppermute | solution.py:23
  38.3 12.7 %collective-permute-start.14 = (bf16[32,2048]{1,0:T(8,128)(2,1)S(1)}, bf16[32,2048]{1,0:T(8,128)(2,1)S(1)}, u32[]{:S(2)}, u32[]{:S(2)}) collective-permute-start(bf16[32,2048]{1,0:T(8,128)(2,1)S(1)} %get-tuple-element.70), channel_id=1, source_target_pairs={{0,3},{1,2},{2,1},{3,0},{4,7},{5,6},{6,5},{7,4},{8,11},{9,10},{10,... | collective-permute-start | bytes 393224 | tf_op jit(solution)/shard_map/rows_3/ppermute | solution.py:23
  42.0 11.2 %collective-permute-start.24 = (bf16[32,2048]{1,0:T(8,128)(2,1)S(1)}, bf16[32,2048]{1,0:T(8,128)(2,1)S(1)}, u32[]{:S(2)}, u32[]{:S(2)}) collective-permute-start(bf16[32,2048]{1,0:T(8,128)(2,1)S(1)} %get-tuple-element.83), channel_id=1, source_target_pairs={{0,6},{1,7},{2,4},{3,5},{4,2},{5,3},{6,0},{7,1},{8,14},{9,15},{10,... | collective-permute-start | bytes 393224 | tf_op jit(solution)/shard_map/rows_6/ppermute | solution.py:23
  43.4 18.8 %collective-permute-start.25 = (bf16[32,2048]{1,0:T(8,128)(2,1)S(1)}, bf16[32,2048]{1,0:T(8,128)(2,1)S(1)}, u32[]{:S(2)}, u32[]{:S(2)}) collective-permute-start(bf16[32,2048]{1,0:T(8,128)(2,1)S(1)} %get-tuple-element.84), channel_id=1, source_target_pairs={{0,7},{1,6},{2,5},{3,4},{4,3},{5,2},{6,1},{7,0},{8,15},{9,14},{10,... | collective-permute-start | bytes 393224 | tf_op jit(solution)/shard_map/rows_7/ppermute | solution.py:23
  46.1 18.0 %collective-permute-start.22 = (bf16[32,2048]{1,0:T(8,128)(2,1)S(1)}, bf16[32,2048]{1,0:T(8,128)(2,1)S(1)}, u32[]{:S(2)}, u32[]{:S(2)}) collective-permute-start(bf16[32,2048]{1,0:T(8,128)(2,1)S(1)} %get-tuple-element.81), channel_id=1, source_target_pairs={{0,4},{1,5},{2,6},{3,7},{4,0},{5,1},{6,2},{7,3},{8,12},{9,13},{10,... | collective-permute-start | bytes 393224 | tf_op jit(solution)/shard_map/back_4/ppermute | solution.py:23
  51.0 15.0 %collective-permute-start.23 = (bf16[32,2048]{1,0:T(8,128)(2,1)S(1)}, bf16[32,2048]{1,0:T(8,128)(2,1)S(1)}, u32[]{:S(2)}, u32[]{:S(2)}) collective-permute-start(bf16[32,2048]{1,0:T(8,128)(2,1)S(1)} %get-tuple-element.82), channel_id=1, source_target_pairs={{0,5},{1,4},{2,7},{3,6},{4,1},{5,0},{6,3},{7,2},{8,13},{9,12},{10,... | collective-permute-start | bytes 393224 | tf_op jit(solution)/shard_map/back_5/ppermute | solution.py:23
  52.6 14.3 %collective-permute-start.15 = (bf16[32,2048]{1,0:T(8,128)(2,1)S(1)}, bf16[32,2048]{1,0:T(8,128)(2,1)S(1)}, u32[]{:S(2)}, u32[]{:S(2)}) collective-permute-start(bf16[32,2048]{1,0:T(8,128)(2,1)S(1)} %get-tuple-element.72), channel_id=1, source_target_pairs={{0,1},{1,0},{2,3},{3,2},{4,5},{5,4},{6,7},{7,6},{8,9},{9,8},{10,11... | collective-permute-start | bytes 393224 | tf_op jit(solution)/shard_map/back_1/ppermute | solution.py:23
  53.2 13.8 %collective-permute-start.16 = (bf16[32,2048]{1,0:T(8,128)(2,1)S(1)}, bf16[32,2048]{1,0:T(8,128)(2,1)S(1)}, u32[]{:S(2)}, u32[]{:S(2)}) collective-permute-start(bf16[32,2048]{1,0:T(8,128)(2,1)S(1)} %get-tuple-element.73), channel_id=1, source_target_pairs={{0,2},{1,3},{2,0},{3,1},{4,6},{5,7},{6,4},{7,5},{8,10},{9,11},{10,... | collective-permute-start | bytes 393224 | tf_op jit(solution)/shard_map/back_2/ppermute | solution.py:23
  62.2 12.4 %collective-permute-start.17 = (bf16[32,2048]{1,0:T(8,128)(2,1)S(1)}, bf16[32,2048]{1,0:T(8,128)(2,1)S(1)}, u32[]{:S(2)}, u32[]{:S(2)}) collective-permute-start(bf16[32,2048]{1,0:T(8,128)(2,1)S(1)} %get-tuple-element.74), channel_id=1, source_target_pairs={{0,3},{1,2},{2,1},{3,0},{4,7},{5,6},{6,5},{7,4},{8,11},{9,10},{10,... | collective-permute-start | bytes 393224 | tf_op jit(solution)/shard_map/back_3/ppermute | solution.py:23
  64.1 11.3 %collective-permute-start.26 = (bf16[32,2048]{1,0:T(8,128)(2,1)S(1)}, bf16[32,2048]{1,0:T(8,128)(2,1)S(1)}, u32[]{:S(2)}, u32[]{:S(2)}) collective-permute-start(bf16[32,2048]{1,0:T(8,128)(2,1)S(1)} %get-tuple-element.85), channel_id=1, source_target_pairs={{0,6},{1,7},{2,4},{3,5},{4,2},{5,3},{6,0},{7,1},{8,14},{9,15},{10,... | collective-permute-start | bytes 393224 | tf_op jit(solution)/shard_map/back_6/ppermute | solution.py:23
  65.9 12.3 %collective-permute-start.27 = (bf16[32,2048]{1,0:T(8,128)(2,1)S(1)}, bf16[32,2048]{1,0:T(8,128)(2,1)S(1)}, u32[]{:S(2)}, u32[]{:S(2)}) collective-permute-start(bf16[32,2048]{1,0:T(8,128)(2,1)S(1)} %get-tuple-element.86), channel_id=1, source_target_pairs={{0,7},{1,6},{2,5},{3,4},{4,3},{5,2},{6,1},{7,0},{8,15},{9,14},{10,... | collective-permute-start | bytes 393224 | tf_op jit(solution)/shard_map/back_7/ppermute | solution.py:23
